TPU v7x, 32 devices: a whole 2x2x4 slice. The times are simulated.
32 devices in a mesh: dp: 2 (over core), expert: 4 (over z), tensor: 4 (over y, x).
Axes of the slice: x: 2, y: 2, z: 4, core: 2. Of those that a mesh axis runs over, the one named last changes fastest.
Arguments:
- tokens: bfloat16 [12288, 768], P(('dp', 'expert', 'tensor')), may hold values from -6 to 6
- cotangent: bfloat16 [12288, 768], P(('dp', 'expert', 'tensor')), may hold values from -6 to 6
- query_key_value_weight: bfloat16 [3, 768, 768], P(None, ('dp', 'expert'), 'tensor'), may hold values from -0.21875 to 0.21875
- attention_output_weight: bfloat16 [768, 768], P('tensor', ('dp', 'expert')), may hold values from -2 to 2
- rel_bias: bfloat16 [12, 32], P('tensor'), may hold values from -6 to 6
- gain_attn: bfloat16 [768], P(('dp', 'expert', 'tensor')), may hold values from 0.5 to 1.5
- gain_moe: bfloat16 [768], P(('dp', 'expert', 'tensor')), may hold values from 0.5 to 1.5
- w_router: bfloat16 [768, 16], P(('dp', 'expert', 'tensor')), may hold values from -0.109375 to 0.109375
- w_in: bfloat16 [16, 768, 3072], P('expert', 'dp', 'tensor'), may hold values from -0.21875 to 0.21875
- w_out: bfloat16 [16, 3072, 768], P('expert', 'tensor', 'dp'), may hold values from -3 to 3
- expert_index: int32 [12288], P(('dp', 'expert', 'tensor')), may hold values from 0 to 15, as said below
- slot_index: int32 [12288], P(('dp', 'expert', 'tensor')), may hold values from 0 to 35, as said below
- kept_mask: int32 [12288], P(('dp', 'expert', 'tensor')), may hold values from 0 to 1, as said below
Outputs:
- output: bfloat16 [12288, 768], P(('dp', 'expert', 'tensor'))
- grad_tokens: float32 [12288, 768], P(('dp', 'expert', 'tensor'))
- grad_w_qkv: float32 [3, 768, 768], P(None, ('dp', 'expert'), 'tensor')
- grad_w_attn_out: float32 [768, 768], P('tensor', ('dp', 'expert'))
- grad_rel_bias: float32 [12, 32], P('tensor')
- grad_gain_attn: float32 [768], P(('dp', 'expert', 'tensor'))
- grad_gain_moe: float32 [768], P(('dp', 'expert', 'tensor'))
- grad_w_router: float32 [768, 16], P(('dp', 'expert', 'tensor'))
- grad_w_in: float32 [16, 768, 3072], P('expert', 'dp', 'tensor')
- grad_w_out: float32 [16, 3072, 768], P('expert', 'tensor', 'dp')
Inputs may be any that keep to these rules, and one draw needn't show every extreme that they name: `expert_index`: in every aligned block of 384 rows (the rows of one device) some expert is named by more than 36 rows. `slot_index`: the number of earlier rows of the same block of 384 rows (the rows of one device) with the same expert, or 35 where that number is 36 or more. `kept_mask`: 1 where that number of earlier rows is below 36, else 0.
All inputs are finite; a program needn't handle non-finite values.
Results may differ from a plain program's by a relative error of at most 0.024.
Values may be sent and summed in bfloat16 or wider, within the bound.
No kernel may reach another device: no remote copies, remote signals or barrier semaphores. Data moves between devices by JAX's collectives and lax.ppermute only.
A program may use at most 128 MiB of HBM per device.

v0:
```python
import jax
import jax.numpy as jnp
from jax import lax
from jax.sharding import PartitionSpec as P

HEAD_DIM = 64
BUCKETS = 32
LENGTH = 512


EPSILON = 1e-06
BORDERS = (12, 16, 23, 32, 46, 64, 91)


def bucket_table(length):
    places = jnp.arange(length, dtype=jnp.int32)
    offset = places[None, :] - places[:, None]
    distance = jnp.abs(offset)
    bucket = jnp.minimum(distance, 8)
    for border in BORDERS:
        bucket = bucket + (distance >= border).astype(jnp.int32)
    bucket = bucket + jnp.where(offset > 0, 16, 0).astype(jnp.int32)
    return (bucket[:, :, None] == jnp.arange(BUCKETS, dtype=jnp.int32)[None, None, :]).astype(
        jnp.bfloat16
    )


def rms_scaled(values, scaling):
    return values * lax.rsqrt(jnp.mean(values * values, axis=-1, keepdims=True) + EPSILON) * scaling


def rows_over_tensor(value):
    return lax.all_gather(value, "tensor", axis=1, tiled=True)


def sum_over_tensor(value):
    return lax.psum_scatter(
        value.astype(jnp.bfloat16), "tensor", scatter_dimension=1, tiled=True
    ).astype(jnp.float32)


def to_experts(buffer):
    grouped = rows_over_tensor(buffer)
    return lax.all_to_all(grouped, "expert", split_axis=0, concat_axis=1, tiled=True)


def from_experts(partial_value):
    returned = lax.all_to_all(
        partial_value.astype(jnp.bfloat16), "expert", split_axis=1, concat_axis=0, tiled=True
    ).astype(partial_value.dtype)
    return sum_over_tensor(returned)


def on_device(
    tokens,
    cotangent,
    query_key_value_weight,
    attention_output_weight,
    rel_bias,
    gain_attn,
    gain_moe,
    w_router,
    w_in,
    w_out,
    expert_index,
    slot_index,
    kept_mask,
):
    tok_rows, width = tokens.shape
    experts_all = w_router.shape[1]
    capacity = max(2, 3 * tok_rows // (2 * experts_all))
    head_local = rel_bias.shape[0]
    score_scale = HEAD_DIM ** (-0.5)
    gain_one, gain_two, router_full = (
        lax.all_gather(gain_attn, ("dp", "expert", "tensor"), axis=0, tiled=True),
        lax.all_gather(gain_moe, ("dp", "expert", "tensor"), axis=0, tiled=True),
        lax.all_gather(w_router, ("dp", "expert", "tensor"), axis=0, tiled=True),
    )
    qkv_full, attn_out_full = (
        lax.all_gather(query_key_value_weight, ("dp", "expert"), axis=1, tiled=True),
        lax.all_gather(attention_output_weight, ("dp", "expert"), axis=1, tiled=True),
    )
    win_full, wout_full = (
        lax.all_gather(w_in, "dp", axis=1, tiled=True),
        lax.all_gather(w_out, "dp", axis=2, tiled=True),
    )
    gain_one = gain_one.astype(jnp.float32)
    gain_two = gain_two.astype(jnp.float32)
    inputs = tokens.astype(jnp.float32)
    normed = rms_scaled(inputs, gain_one).astype(jnp.bfloat16)
    group_normed = rows_over_tensor(normed[None])[0]
    grouped_token_rows = group_normed.shape[0]
    seq_count = grouped_token_rows // LENGTH
    output_projected = jnp.einsum(
        "td,cde->cte", group_normed, qkv_full, preferred_element_type=jnp.float32
    ).astype(jnp.bfloat16)
    heads_view = output_projected.reshape(3, seq_count, LENGTH, head_local, HEAD_DIM)
    onehot_table = bucket_table(LENGTH)
    bias_full = jnp.einsum(
        "qkb,hb->hqk", onehot_table, rel_bias, preferred_element_type=jnp.float32
    )

    def score_block(query_rows, key_rows):
        return (
            jnp.einsum("qhe,khe->hqk", query_rows, key_rows, preferred_element_type=jnp.float32)
            * score_scale
            + bias_full
        )

    def attend(packed):
        query_rows, key_rows, value_rows = packed
        scores = score_block(query_rows, key_rows)
        row_max = jnp.max(scores, axis=-1, keepdims=True)
        exponent = jnp.exp(scores - row_max)
        totals = jnp.sum(exponent, axis=-1, keepdims=True)
        attention = (exponent / totals).astype(jnp.bfloat16)
        mixed_part = jnp.einsum(
            "hqk,khe->qhe", attention, value_rows, preferred_element_type=jnp.float32
        )
        return (mixed_part.astype(jnp.bfloat16), row_max + jnp.log(totals))

    mixed_all, log_totals = lax.map(attend, (heads_view[0], heads_view[1], heads_view[2]))
    attention_mixed_rows = mixed_all.reshape(grouped_token_rows, head_local * HEAD_DIM)
    attn_partial = jnp.dot(attention_mixed_rows, attn_out_full, preferred_element_type=jnp.float32)
    hidden_one = inputs + sum_over_tensor(attn_partial[None])[0]
    moe_in = rms_scaled(hidden_one, gain_two).astype(jnp.bfloat16)
    logits = jnp.dot(moe_in, router_full, preferred_element_type=jnp.float32)
    logit_max = jnp.max(logits, axis=-1, keepdims=True)
    logit_exp = jnp.exp(logits - logit_max)
    router_probs = logit_exp / jnp.sum(logit_exp, axis=-1, keepdims=True)
    chosen = (expert_index[:, None] == jnp.arange(experts_all, dtype=jnp.int32)[None, :]).astype(
        jnp.float32
    )
    kept_float = kept_mask.astype(jnp.float32)
    picked = jnp.sum(router_probs * chosen, axis=1)
    gate_value = picked * kept_float
    target = jnp.where(kept_mask > 0, expert_index * capacity + slot_index, experts_all * capacity)
    source = jnp.minimum(target, experts_all * capacity - 1)
    dispatched = (
        jnp.zeros((experts_all * capacity, width), jnp.bfloat16).at[target].set(moe_in, mode="drop")
    )
    arrived = to_experts(dispatched.reshape(experts_all, capacity, width))
    inner_rows = jnp.einsum("erd,edf->erf", arrived, win_full, preferred_element_type=jnp.float32)
    activated, gelu_back = jax.vjp(jax.nn.gelu, inner_rows)
    hidden_units = activated.astype(jnp.bfloat16)
    partial_value = jnp.einsum(
        "erf,efd->erd", hidden_units, wout_full, preferred_element_type=jnp.float32
    )
    returned = from_experts(partial_value).reshape(experts_all * capacity, width)
    expert_rows = returned[source]
    output = (hidden_one + gate_value[:, None] * expert_rows).astype(jnp.bfloat16)
    grad_out = cotangent.astype(jnp.float32)
    grad_expert = (gate_value[:, None] * grad_out).astype(jnp.bfloat16)
    grad_dispatch = (
        jnp.zeros((experts_all * capacity, width), jnp.bfloat16)
        .at[target]
        .set(grad_expert, mode="drop")
    )
    grad_arrived = to_experts(grad_dispatch.reshape(experts_all, capacity, width))
    grad_units = jnp.einsum(
        "erd,efd->erf", grad_arrived, wout_full, preferred_element_type=jnp.float32
    )
    grad_inner = gelu_back(grad_units)[0].astype(jnp.bfloat16)
    grad_wout_full = jnp.einsum(
        "erf,erd->efd", hidden_units, grad_arrived, preferred_element_type=jnp.float32
    )
    grad_win_full = jnp.einsum(
        "erd,erf->edf", arrived, grad_inner, preferred_element_type=jnp.float32
    )
    grad_partial = jnp.einsum(
        "erf,edf->erd", grad_inner, win_full, preferred_element_type=jnp.float32
    )
    grad_back = from_experts(grad_partial).reshape(experts_all * capacity, width)
    grad_gate = jnp.sum(grad_out * expert_rows, axis=1) * kept_float
    grad_logits = (grad_gate[:, None] * router_probs * (chosen - picked[:, None])).astype(
        jnp.bfloat16
    )
    grad_router_full = jnp.einsum(
        "td,te->de", moe_in, grad_logits, preferred_element_type=jnp.float32
    )
    grad_moe_in = grad_back[source] * kept_float[:, None]
    grad_moe_in = grad_moe_in + jnp.einsum(
        "te,de->td", grad_logits, router_full, preferred_element_type=jnp.float32
    )
    norm_two_back = jax.vjp(rms_scaled, hidden_one, gain_two)[1]
    grad_hidden_part, grad_gain_two = norm_two_back(grad_moe_in)
    grad_hidden = grad_out + grad_hidden_part
    grad_attn = grad_hidden.astype(jnp.bfloat16)
    group_grad = rows_over_tensor(grad_attn[None])[0]
    grad_mixed = jnp.einsum(
        "td,ed->te", group_grad, attn_out_full, preferred_element_type=jnp.float32
    ).astype(jnp.bfloat16)
    grad_attn_out_full = jnp.einsum(
        "te,td->ed", attention_mixed_rows, group_grad, preferred_element_type=jnp.float32
    )
    grad_mixed_view = grad_mixed.reshape(seq_count, LENGTH, head_local, HEAD_DIM)

    def attend_back(carried, packed):
        query_rows, key_rows, value_rows, log_total, grad_rows = packed
        attention = jnp.exp(score_block(query_rows, key_rows) - log_total)
        grad_weights = jnp.einsum(
            "qhe,khe->hqk", grad_rows, value_rows, preferred_element_type=jnp.float32
        )
        inner_sum = jnp.sum(attention * grad_weights, axis=-1, keepdims=True)
        grad_scores = (attention * (grad_weights - inner_sum)).astype(jnp.bfloat16)
        grad_query = (
            jnp.einsum("hqk,khe->qhe", grad_scores, key_rows, preferred_element_type=jnp.float32)
            * score_scale
        ).astype(jnp.bfloat16)
        grad_key = (
            jnp.einsum("hqk,qhe->khe", grad_scores, query_rows, preferred_element_type=jnp.float32)
            * score_scale
        ).astype(jnp.bfloat16)
        grad_value = jnp.einsum(
            "hqk,qhe->khe",
            attention.astype(jnp.bfloat16),
            grad_rows,
            preferred_element_type=jnp.float32,
        ).astype(jnp.bfloat16)
        bias_step = jnp.einsum(
            "hqk,qkb->hb", grad_scores, onehot_table, preferred_element_type=jnp.float32
        )
        return (carried + bias_step, (grad_query, grad_key, grad_value))

    bias_part, grads_qkv = lax.scan(
        attend_back,
        jnp.zeros((head_local, BUCKETS), jnp.float32),
        (heads_view[0], heads_view[1], heads_view[2], log_totals, grad_mixed_view),
    )
    grad_projected = jnp.stack([grads_qkv[0], grads_qkv[1], grads_qkv[2]]).reshape(
        3, grouped_token_rows, head_local * HEAD_DIM
    )
    grad_qkv_full = jnp.einsum(
        "td,cte->cde", group_normed, grad_projected, preferred_element_type=jnp.float32
    )
    grad_normed_part = jnp.einsum(
        "cte,cde->td", grad_projected, qkv_full, preferred_element_type=jnp.float32
    )
    grad_normed = sum_over_tensor(grad_normed_part[None])[0]
    norm_one_back = jax.vjp(rms_scaled, inputs, gain_one)[1]
    grad_input_part, grad_gain_one = norm_one_back(grad_normed)
    grad_tokens = grad_hidden + grad_input_part
    grad_w_qkv, grad_w_attn_out = (
        lax.psum_scatter(grad_qkv_full, ("dp", "expert"), scatter_dimension=1, tiled=True),
        lax.psum_scatter(grad_attn_out_full, ("dp", "expert"), scatter_dimension=1, tiled=True),
    )
    grad_rel_bias = lax.psum(bias_part, ("dp", "expert"))
    grad_gain_attn, grad_gain_moe, grad_w_router = (
        lax.psum_scatter(
            grad_gain_one, ("dp", "expert", "tensor"), scatter_dimension=0, tiled=True
        ),
        lax.psum_scatter(
            grad_gain_two, ("dp", "expert", "tensor"), scatter_dimension=0, tiled=True
        ),
        lax.psum_scatter(
            grad_router_full, ("dp", "expert", "tensor"), scatter_dimension=0, tiled=True
        ),
    )
    grad_w_in, grad_w_out = (
        lax.psum_scatter(
            grad_win_full.astype(jnp.bfloat16), "dp", scatter_dimension=1, tiled=True
        ).astype(jnp.float32),
        lax.psum_scatter(
            grad_wout_full.astype(jnp.bfloat16), "dp", scatter_dimension=2, tiled=True
        ).astype(jnp.float32),
    )
    return (
        output,
        grad_tokens,
        grad_w_qkv,
        grad_w_attn_out,
        grad_rel_bias,
        grad_gain_attn,
        grad_gain_moe,
        grad_w_router,
        grad_w_in,
        grad_w_out,
    )


def solution(mesh):
    placed = (
        P(("dp", "expert", "tensor"), None),
        P(("dp", "expert", "tensor"), None),
        P(None, ("dp", "expert"), "tensor"),
        P("tensor", ("dp", "expert")),
        P("tensor", None),
        P(("dp", "expert", "tensor")),
        P(("dp", "expert", "tensor")),
        P(("dp", "expert", "tensor"), None),
        P("expert", "dp", "tensor"),
        P("expert", "tensor", "dp"),
        P(("dp", "expert", "tensor")),
        P(("dp", "expert", "tensor")),
        P(("dp", "expert", "tensor")),
    )
    return jax.shard_map(
        on_device,
        mesh=mesh,
        in_specs=placed,
        out_specs=(
            P(("dp", "expert", "tensor"), None),
            P(("dp", "expert", "tensor"), None),
            P(None, ("dp", "expert"), "tensor"),
            P("tensor", ("dp", "expert")),
            P("tensor", None),
            P(("dp", "expert", "tensor")),
            P(("dp", "expert", "tensor")),
            P(("dp", "expert", "tensor"), None),
            P("expert", "dp", "tensor"),
            P("expert", "tensor", "dp"),
        ),
        check_vma=False,
    )
```

profile of v0, /device:TPU:0, one launch (start us, length us, event | category | flops | bytes accessed | tf_op | source)
XLA Modules:
  0.0 1131.7 jit_solution(15127313171151331822)
XLA Ops:
  10.2 42.0 %all-reduce.6 = (bf16[768]{0:T(1024)(128)(2,1)S(1)}, bf16[768]{0:T(1024)(128)(2,1)S(1)}) all-reduce(bf16[768]{0:T(1024)(128)(2,1)S(1)} %dynamic-update-slice, bf16[768]{0:T(1024)(128)(2,1)S(1)} %dynamic-update-slice.1), channel_id=1, replica_groups=mesh['dp'=2,'expert'=4,'tensor'=4] {'dp','expert','tensor'}, use_global_device_ids=true, to_apply=%add | all-reduce | flops 1536 | bytes 6144
  58.7 34.2 %all_gather.35 = bf16[3,768,192]{2,0,1:T(4,128)(2,1)S(1)} all-gather(bf16[3,96,192]{2,0,1:T(4,128)(2,1)S(1)} %copy.113), channel_id=1, replica_groups=mesh['dp'=2,'expert'=4,'tensor'=4] {'dp','expert'}, dimensions={1}, use_global_device_ids=true | all-gather | bytes 995328 | tf_op jit(solution)/shard_map/all_gather | solution.py:80
  104.8 26.2 %all_gather.36 = bf16[192,768]{0,1:T(8,128)(2,1)S(1)} all-gather(bf16[192,96]{0,1:T(8,128)(2,1)} %copy.121), channel_id=1, replica_groups=mesh['dp'=2,'expert'=4,'tensor'=4] {'dp','expert'}, dimensions={1}, use_global_device_ids=true | all-gather | bytes 331776 | tf_op jit(solution)/shard_map/all_gather | solution.py:81
  149.4 14.9 %while.29 = (s32[]{:T(128)}, bf16[3,512,3,64]{1,3,2,0:T(8,128)(2,1)}, f32[3,3,512,1]{2,1,3,0:T(4,128)}, bf16[3,512,3,64]{1,3,2,0:T(8,128)(2,1)}, bf16[3,512,3,64...) while((s32[]{:T(128)}, ...), condition=%wide.region_4.5_spmd, body=%wide.region_1.4_spmd.sunk | while | flops 207714816 | bytes 13422689 | solution.py:122
  170.8 36.4 %reduce-scatter.16.cloned.1.call-done = bf16[1,384,768]{2,1,0:T(8,128)(2,1)} async-done(((bf16[1,1536,768]{2,1,0:T(8,128)(2,1)}), bf16[1,384,768]{2,1,0:T(8,128)(2,1)}) %reduce-scatter.16.cloned.1.call-update) | async-done | bytes 589840 | tf_op jit(solution)/shard_map/reduce_scatter | solution.py:37
  220.2 46.8 %all-gather.10.cloned.1.call-done = bf16[16,144,768]{2,0,1:T(8,128)(2,1)} async-done(((bf16[16,36,768]{2,0,1:T(8,128)(2,1)}), bf16[16,144,768]{2,0,1:T(8,128)(2,1)}) %all-gather.10.cloned.1.call-update) | async-done | bytes 3538960 | tf_op jit(solution)/shard_map/all_gather | solution.py:33
  277.4 78.8 %all-to-all-done = bf16[16,144,768]{2,1,0:T(8,128)(2,1)} async-done(((bf16[16,144,768]{2,1,0:T(8,128)(2,1)}), bf16[16,144,768]{2,1,0:T(8,128)(2,1)}, u32[]{:S(2)}, u32[]{:S(2)}) %all-to-all-start) | async-done | bytes 3538976 | tf_op jit(solution)/shard_map/all_to_all | solution.py:44
  360.2 9.2 fusion.119
  369.4 7.6 convolution_convert_fusion.5
  379.8 81.2 %all_to_all.72 = bf16[4,576,768]{2,0,1:T(4,128)(2,1)S(1)} all-to-all(bf16[4,576,768]{2,0,1:T(4,128)(2,1)S(1)} %copy.126), channel_id=1, replica_groups=mesh['dp'=2,'expert'=4,'tensor'=4] {'expert'}, dimensions={1} | all-to-all | bytes 7077888 | tf_op jit(solution)/shard_map/all_to_all | solution.py:48
  465.4 66.8 %all-gather.2 = bf16[32,24,16]{1,2,0:T(8,128)(2,1)S(1)} all-gather(bf16[1,24,16]{1,2,0:T(8,128)(2,1)S(1)} %bitcast.247), channel_id=1, replica_groups=mesh['dp'=2,'expert'=4,'tensor'=4] {'dp','expert','tensor'}, dimensions={0}, use_global_device_ids=true | all-gather | bytes 25344 | tf_op jit(solution)/shard_map/all_gather | solution.py:77
  559.5 43.9 %all-gather.16.cloned.1.call-done = bf16[16,144,768]{2,0,1:T(8,128)(2,1)} async-done(((bf16[16,36,768]{2,0,1:T(8,128)(2,1)}), bf16[16,144,768]{2,0,1:T(8,128)(2,1)}) %all-gather.16.cloned.1.call-update) | async-done | bytes 3538960 | tf_op jit(solution)/shard_map/all_gather | solution.py:33
  606.7 83.9 %all_to_all.73 = bf16[16,144,768]{2,1,0:T(8,128)(2,1)S(1)} all-to-all(bf16[16,144,768]{2,1,0:T(8,128)(2,1)S(1)} %copy.132), channel_id=1, replica_groups=mesh['dp'=2,'expert'=4,'tensor'=4] {'expert'}, dimensions={0} | all-to-all | bytes 7077888 | tf_op jit(solution)/shard_map/all_to_all | solution.py:44
  692.7 8.0 fusion.75
  708.4 81.4 %all_to_all.74 = bf16[4,576,768]{2,0,1:T(4,128)(2,1)S(1)} all-to-all(bf16[4,576,768]{2,0,1:T(4,128)(2,1)S(1)} %copy.134), channel_id=1, replica_groups=mesh['dp'=2,'expert'=4,'tensor'=4] {'expert'}, dimensions={1} | all-to-all | bytes 7077888 | tf_op jit(solution)/shard_map/all_to_all | solution.py:48
  793.8 45.2 %reduce-scatter.20.cloned.1.call-done = bf16[16,36,768]{2,0,1:T(8,128)(2,1)} async-done(((bf16[16,144,768]{2,0,1:T(8,128)(2,1)}), bf16[16,36,768]{2,0,1:T(8,128)(2,1)}) %reduce-scatter.20.cloned.1.call-update) | async-done | bytes 884752 | tf_op jit(solution)/shard_map/reduce_scatter | solution.py:37
  854.5 11.0 convolution_convert_fusion.1
  865.5 8.5 copy.159
  879.7 9.2 convolution_convert_fusion.2
  902.4 41.3 %while.30 = (s32[]{:T(128)}, f32[3,32]{1,0:T(4,128)S(1)}, bf16[3,512,3,64]{1,3,2,0:T(8,128)(2,1)}, bf16[3,512,3,64]{1,3,2,0:T(8,128)(2,1)}, bf16[3,512,3,64]{1,3...) while((s32[]{:T(128)}, f32[3,32]{1,0:T(4,128)S(1)}, ...), condition=%wide.region_18.19_spmd.clone, body=%wide.region_16.18_spmd.clone.sunk | while | flops 577993408 | bytes 40277996 | solution.py:225
  992.4 17.5 %psum.7 = f32[3,32]{1,0:T(4,128)} all-reduce(f32[3,32]{1,0:T(4,128)S(1)} %get-tuple-element.118), channel_id=1, replica_groups=mesh['dp'=2,'expert'=4,'tensor'=4] {'dp','expert'}, use_global_device_ids=true, to_apply=%region_23.24 | all-reduce | flops 96 | bytes 768 | tf_op jit(solution)/shard_map/psum | solution.py:247
  1011.5 27.3 %reduce-scatter.26.cloned.1.call-done = f32[96,576]{1,0:T(8,128)} async-done(((f32[768,576]{1,0:T(8,128)}), f32[96,576]{1,0:T(8,128)}) %reduce-scatter.26.cloned.1.call-update) | async-done | bytes 221200
  1040.7 37.4 %reduce-scatter.22.cloned.1.call-done = bf16[1,384,768]{2,1,0:T(8,128)(2,1)} async-done(((bf16[1,1536,768]{2,1,0:T(8,128)(2,1)}), bf16[1,384,768]{2,1,0:T(8,128)(2,1)}) %reduce-scatter.22.cloned.1.call-update) | async-done | bytes 589840 | tf_op jit(solution)/shard_map/reduce_scatter | solution.py:37
  1079.7 39.9 %all-reduce.5 = (f32[768]{0:T(1024)S(1)}, f32[768]{0:T(1024)S(1)}, f32[768,16]{0,1:T(8,128)S(1)}) all-reduce(f32[768]{0:T(1024)S(1)} %get-tuple-element.279, f32[768]{0:T(1024)S(1)} %copy-done.37, f32[768,16]{0,1:T(8,128)S(1)} %fusion.113), channel_id=10, replica_groups=mesh['dp'=2,'expert'=4,'tensor'=4] {'dp','expert','tensor'}, use_global_device_ids=true, to_apply=%region_25.26.clone | all-reduce | flops 13824 | bytes 110592
  (288 shorter events, 274.3 us)
Async XLA Ops:
  7.2 123.8 %all-gather.18.cloned.1.call-start = ((), (), s32[]{:S(2)}) async-start(), calls=%async_computation.21 | async-start | bytes 2949120 | tf_op jit(solution)/shard_map/all_gather | solution.py:33
  54.4 152.8 %reduce-scatter.16.cloned.1.call-start = ((), (), s32[]{:S(2)}) async-start(), calls=%async_computation.12 | async-start | bytes 2949120 | tf_op jit(solution)/shard_map/reduce_scatter | solution.py:37
  169.2 97.8 %all-gather.10.cloned.1.call-start = ((), (), s32[]{:S(2)}) async-start(), calls=%async_computation.13 | async-start | bytes 4423680 | tf_op jit(solution)/shard_map/all_gather | solution.py:33
  219.6 140.6 %all-gather.12.cloned.1.call-start = ((), (), s32[]{:S(2)}) async-start(), calls=%async_computation.14 | async-start | bytes 7077888 | tf_op jit(solution)/shard_map/all_gather | solution.py:84
  271.9 84.3 %all-to-all-start = ((bf16[16,144,768]{2,1,0:T(8,128)(2,1)}), bf16[16,144,768]{2,1,0:T(8,128)(2,1)}, u32[]{:S(2)}, u32[]{:S(2)}) async-start(bf16[16,144,768]{2,1,0:T(8,128)(2,1)} %copy.124), calls=%async_computation.1 | async-start | bytes 7077888 | tf_op jit(solution)/shard_map/all_to_all | solution.py:44
  276.8 92.6 %all-gather.14.cloned.1.call-start = ((), (), s32[]{:S(2)}) async-start(), calls=%async_computation.15 | async-start | bytes 7077888 | tf_op jit(solution)/shard_map/all_gather | solution.py:85
  277.4 261.0 %reduce-scatter.18.cloned.1.call-start = ((), (), s32[]{:S(2)}) async-start(), calls=%async_computation.16 | async-start | bytes 4423680 | tf_op jit(solution)/shard_map/reduce_scatter | solution.py:37
  464.7 138.7 %all-gather.16.cloned.1.call-start = ((), (), s32[]{:S(2)}) async-start(), calls=%async_computation.17 | async-start | bytes 4423680 | tf_op jit(solution)/shard_map/all_gather | solution.py:33
  559.4 279.6 %reduce-scatter.20.cloned.1.call-start = ((), (), s32[]{:S(2)}) async-start(), calls=%async_computation.18 | async-start | bytes 4423680 | tf_op jit(solution)/shard_map/reduce_scatter | solution.py:37
  793.5 98.5 %all-gather.20.cloned.1.call-start = ((), (), s32[]{:S(2)}) async-start(), calls=%async_computation.22 | async-start | bytes 2949120 | tf_op jit(solution)/shard_map/all_gather | solution.py:33
  854.4 121.3 %reduce-scatter.30.cloned.1.call-start = ((), (), s32[]{:S(2)}) async-start(), calls=%async_computation.25 | async-start | bytes 7077888
  879.6 108.4 %reduce-scatter.24.cloned.1.call-start = ((), (), s32[]{:S(2)}) async-start(), calls=%async_computation.20 | async-start | bytes 7077888 | tf_op jit(solution)/shard_map/reduce_scatter | solution.py:260
  888.8 121.0 %reduce-scatter.28.cloned.1.call-start = ((), (), s32[]{:S(2)}) async-start(), calls=%async_computation.24 | async-start | bytes 884736
  956.3 82.5 %reduce-scatter.26.cloned.1.call-start = ((), (), s32[]{:S(2)}) async-start(), calls=%async_computation.23 | async-start | bytes 2211840
  970.2 107.9 %reduce-scatter.22.cloned.1.call-start = ((), (), s32[]{:S(2)}) async-start(), calls=%async_computation.19 | async-start | bytes 2949120 | tf_op jit(solution)/shard_map/reduce_scatter | solution.py:37
  988.0 90.2 %copy-start.23 = (f32[768]{0:T(1024)S(1)}, f32[768]{0:T(1024)}, u32[]{:S(2)}) copy-start(f32[768]{0:T(1024)} %copy-done.22) | copy-start | bytes 9220
  988.0 90.2 %copy-start.28 = (f32[384]{0:T(512)S(1)}, f32[384]{0:T(512)}, u32[]{:S(2)}) copy-start(f32[384]{0:T(512)} %copy-done.27) | copy-start | bytes 4612
  988.0 91.7 %copy-start.34 = (f32[384]{0:T(512)S(1)}, f32[384]{0:T(512)}, u32[]{:S(2)}) copy-start(f32[384]{0:T(512)} %copy-done.33) | copy-start | bytes 4612
  988.0 91.8 %copy-start.37 = (f32[768]{0:T(1024)S(1)}, f32[768]{0:T(1024)}, u32[]{:S(2)}) copy-start(f32[768]{0:T(1024)} %get-tuple-element.277) | copy-start | bytes 9220
  988.0 133.5 %copy-start.31 = (f32[384]{0:T(512)S(1)}, f32[384]{0:T(512)}, u32[]{:S(2)}) copy-start(f32[384]{0:T(512)} %copy-done.30) | copy-start | bytes 4612
  988.0 133.5 %copy-start.32 = (f32[384]{0:T(512)S(1)}, f32[384]{0:T(512)}, u32[]{:S(2)}) copy-start(f32[384]{0:T(512)} %get-tuple-element.336) | copy-start | bytes 4612
  992.3 129.2 %copy-start.7 = (bf16[1,384,768]{2,1,0:T(8,128)(2,1)S(1)}, bf16[1,384,768]{2,1,0:T(8,128)(2,1)}, u32[]{:S(2)}) copy-start(bf16[1,384,768]{2,1,0:T(8,128)(2,1)} %reduce-scatter.16.cloned.1.call-done) | copy-start | bytes 1769476
  992.3 129.2 %copy-start.9 = (f32[384,768]{1,0:T(8,128)S(1)}, f32[384,768]{1,0:T(8,128)}, u32[]{:S(2)}) copy-start(f32[384,768]{1,0:T(8,128)} %copy-done.8) | copy-start | bytes 3538948
  992.3 129.2 %copy-start.11 = (bf16[384,768]{1,0:T(8,128)(2,1)S(1)}, bf16[384,768]{1,0:T(8,128)(2,1)}, u32[]{:S(2)}) copy-start(bf16[384,768]{1,0:T(8,128)(2,1)} %param.18) | copy-start | bytes 1769476
  (44 other events, 746.3 us)
Sparse Core Ops, SparseCore 0:
  54.5 37.2 all-gather.17
  169.3 37.8 reduce-scatter.15
  219.7 47.2 all-gather.9
  268.4 14.4 all-gather.11
  284.2 15.4 all-gather.13
  464.8 46.4 reduce-scatter.17
  559.6 43.7 all-gather.15
  793.7 45.3 reduce-scatter.19
  854.6 37.4 all-gather.19
  894.8 12.5 reduce-scatter.29
  910.4 13.7 reduce-scatter.23
  956.4 33.8 reduce-scatter.27
  992.8 45.9 reduce-scatter.25
  1041.7 36.3 reduce-scatter.21
where the time goes:
time: 1140 us; the launch traced here: 1130 us
  blocking collectives  473 us (41%)
  waiting for transfers between devices  320 us (28%)
  local copies, waits for them, and re-layouts  150 us (13%)
  matrix products  131 us (11%)
  other arithmetic  36.4 us (3%)
  between operations  14.7 us (1%)
    all_to_all x2, blocking collectives, from_experts(): lax.all_to_all(partial_value.astype(jnp.bfloat16), 'expert', split_axis=1...  163 us
    reduce_scatter x4, waiting for transfers between devices, sum_over_tensor(): lax.psum_scatter(value.astype(jnp.bfloat16), 'tensor', scatter_dimension=...  119 us
    all_gather x4, waiting for transfers between devices, rows_over_tensor(): return lax.all_gather(value, 'tensor', axis=1, tiled=True)  93.5 us
    all_to_all x1, blocking collectives, to_experts(): lax.all_to_all(grouped, 'expert', split_axis=0, concat_axis=1, tiled=True)  83.9 us
    unnamed x2, blocking collectives  82 us
    all_to_all x1, waiting for transfers between devices, to_experts(): lax.all_to_all(grouped, 'expert', split_axis=0, concat_axis=1, tiled=True)  78.8 us
    all_gather x1, blocking collectives, on_device(): lax.all_gather(w_router, ('dp', 'expert', 'tensor'), axis=0, tiled=True)  66.8 us
    unnamed x111, local copies, waits for them, and re-layouts  53.1 us
  transfers between devices with their start and end apart: 15, of which 8 were waited for; matrix products, arithmetic and copies ran while one was open for 16% of the time, Pallas kernels for 0%

commit v1 on v0

v1 whole, which is shorter than its diff:
```python
import functools

import jax
import jax.numpy as jnp
from jax import lax
from jax.experimental import pallas as pl
from jax.experimental.pallas import tpu as pltpu
from jax.sharding import PartitionSpec as P

HEAD_DIM = 64
BUCKETS = 32
LENGTH = 512
TILE = 128
EPSILON = 1e-06
BORDERS = (12, 16, 23, 32, 46, 64, 91)
F32 = jnp.float32
BF16 = jnp.bfloat16
GELU_A = 0.7978845608028654
GELU_B = 0.044715
ROWS_NN = (((1,), (0,)), ((), ()))
ROWS_NT = (((1,), (1,)), ((), ()))
ROWS_TN = (((0,), (0,)), ((), ()))
VMEM_BYTES = 56 * 1024 * 1024
GROUPS = 1


def dot(a, b, dims=ROWS_NN):
    return lax.dot_general(a, b, dims, preferred_element_type=F32)


def params(**more):
    return pltpu.CompilerParams(vmem_limit_bytes=VMEM_BYTES, **more)


def cost(flops, moved, special=0):
    return pl.CostEstimate(flops=int(flops), bytes_accessed=int(moved), transcendentals=int(special))


def whole(shape):
    return pl.BlockSpec(shape, lambda *_: (0,) * len(shape))


def tile_bucket(step):
    rows = lax.broadcasted_iota(jnp.int32, (TILE, TILE), 0)
    cols = lax.broadcasted_iota(jnp.int32, (TILE, TILE), 1)
    offset = cols - rows + step * TILE
    distance = jnp.abs(offset)
    bucket = jnp.minimum(distance, 8)
    for border in BORDERS:
        bucket = bucket + jnp.where(distance >= border, 1, 0)
    return bucket + jnp.where(offset > 0, 16, 0)


def tile_range(step):
    return {-1: range(1, 16), 0: range(0, 32), 1: range(17, 32)}[step]


def fill_bias(bias_ref, table, heads):
    blocks = LENGTH // TILE
    buckets = {step: tile_bucket(step) for step in (-1, 0, 1)}
    for head in range(heads):
        near = {}
        for step in (-1, 0, 1):
            value = jnp.zeros((TILE, TILE), F32)
            for k in tile_range(step):
                value = jnp.where(buckets[step] == k, bias_ref[head, k], value)
            near[step] = value
        low = jnp.full((TILE, TILE), bias_ref[head, 15], F32)
        high = jnp.full((TILE, TILE), bias_ref[head, 31], F32)
        for i in range(blocks):
            for j in range(blocks):
                step = j - i
                value = near[step] if abs(step) <= 1 else (low if step < 0 else high)
                table[head, i * TILE : (i + 1) * TILE, j * TILE : (j + 1) * TILE] = value


def unit_rows(values):
    scale = lax.rsqrt(jnp.mean(values * values, axis=-1, keepdims=True) + EPSILON)
    return values * scale, scale


def attend_kernel(heads, bias_ref, tok_ref, gain_ref, w_ref, part_ref, qkv_ref, mixed_ref, log_ref, table, wo):
    inner = heads * HEAD_DIM

    @pl.when(pl.program_id(0) == 0)
    def _():
        fill_bias(bias_ref, table, heads)
        wo[...] = w_ref[:, 3 * inner :]

    unit, _ = unit_rows(tok_ref[...].astype(F32))
    normed = (unit * gain_ref[...]).astype(BF16)
    qkv_ref[...] = dot(normed, w_ref[:, : 3 * inner]).astype(BF16)
    lanes = lax.broadcasted_iota(jnp.int32, (LENGTH, TILE), 1)
    logs = jnp.zeros((LENGTH, TILE), F32)
    for head in range(heads):
        at = head * HEAD_DIM
        query = qkv_ref[:, at : at + HEAD_DIM] * HEAD_DIM ** (-0.5)
        key = qkv_ref[:, inner + at : inner + at + HEAD_DIM]
        value = qkv_ref[:, 2 * inner + at : 2 * inner + at + HEAD_DIM]
        scores = dot(query.astype(BF16), key, ROWS_NT) + table[head]
        top = jnp.max(scores, axis=-1, keepdims=True)
        exponent = jnp.exp(scores - top)
        total = jnp.sum(exponent, axis=-1, keepdims=True)
        attention = (exponent * (1.0 / total)).astype(BF16)
        mixed_ref[:, at : at + HEAD_DIM] = dot(attention, value).astype(BF16)
        logs = jnp.where(lanes == head, top + jnp.log(total), logs)
    log_ref[...] = logs
    part_ref[...] = dot(mixed_ref[...], wo[...], ROWS_NT).astype(BF16)


def attend(bias, tokens, gain, weights):
    rows, width = tokens.shape
    heads = bias.shape[0]
    inner = heads * HEAD_DIM
    seqs = rows // LENGTH
    by_seq = lambda cols: pl.BlockSpec((LENGTH, cols), lambda s: (s, 0))
    return pl.pallas_call(
        functools.partial(attend_kernel, heads),
        grid=(seqs,),
        in_specs=[
            pl.BlockSpec(memory_space=pltpu.SMEM),
            by_seq(width),
            whole((1, width)),
            whole((width, 4 * inner)),
        ],
        out_specs=[by_seq(width), by_seq(3 * inner), by_seq(inner), by_seq(TILE)],
        out_shape=[
            jax.ShapeDtypeStruct((rows, width), BF16),
            jax.ShapeDtypeStruct((rows, 3 * inner), BF16),
            jax.ShapeDtypeStruct((rows, inner), BF16),
            jax.ShapeDtypeStruct((rows, TILE), F32),
        ],
        scratch_shapes=[pltpu.VMEM((heads, LENGTH, LENGTH), F32), pltpu.VMEM((width, inner), BF16)],
        compiler_params=params(),
        cost_estimate=cost(8 * rows * width * inner + 4 * rows * LENGTH * inner, rows * width * 8, rows * LENGTH * heads),
        name="attend",
    )(bias, tokens, gain, weights)


def attend_back_kernel(
    heads, bias_ref, tok_ref, gain_ref, w_ref, qkv_ref, mixed_ref, log_ref, grad_ref,
    normed_ref, weight_ref, buckets_ref, gain_out, table, wo, gmix, gproj, near, far, rows_s,
):
    inner = heads * HEAD_DIM
    blocks = LENGTH // TILE
    step_id = pl.program_id(0)

    @pl.when(step_id == 0)
    def _():
        fill_bias(bias_ref, table, heads)
        wo[...] = w_ref[:, 3 * inner :]
        near[...] = jnp.zeros_like(near)
        far[...] = jnp.zeros_like(far)
        weight_ref[...] = jnp.zeros_like(weight_ref)
        gain_out[...] = jnp.zeros_like(gain_out)

    gmix[...] = dot(grad_ref[...], wo[...]).astype(BF16)
    for head in range(heads):
        at = head * HEAD_DIM
        query = (qkv_ref[:, at : at + HEAD_DIM] * HEAD_DIM ** (-0.5)).astype(BF16)
        key = qkv_ref[:, inner + at : inner + at + HEAD_DIM]
        value = qkv_ref[:, 2 * inner + at : 2 * inner + at + HEAD_DIM]
        grad_rows = gmix[:, at : at + HEAD_DIM]
        scores = dot(query, key, ROWS_NT) + table[head]
        attention = jnp.exp(scores - log_ref[:, head : head + 1])
        grad_weights = dot(grad_rows, value, ROWS_NT)
        inner_sum = jnp.sum(attention * grad_weights, axis=-1, keepdims=True)
        grad_scores = attention * (grad_weights - inner_sum)
        low = jnp.zeros((TILE, TILE), F32)
        high = jnp.zeros((TILE, TILE), F32)
        mid = [jnp.zeros((TILE, TILE), F32) for _ in range(3)]
        for i in range(blocks):
            for j in range(blocks):
                piece = grad_scores[i * TILE : (i + 1) * TILE, j * TILE : (j + 1) * TILE]
                if abs(j - i) <= 1:
                    mid[j - i + 1] = mid[j - i + 1] + piece
                elif j < i:
                    low = low + piece
                else:
                    high = high + piece
        for k in range(3):
            near[head * 3 + k] += mid[k]
        far[head * 2] += low
        far[head * 2 + 1] += high
        rounded = grad_scores.astype(BF16)
        gproj[:, at : at + HEAD_DIM] = (dot(rounded, key) * HEAD_DIM ** (-0.5)).astype(BF16)
        gproj[:, inner + at : inner + at + HEAD_DIM] = dot(rounded, query, ROWS_TN).astype(BF16)
        gproj[:, 2 * inner + at : 2 * inner + at + HEAD_DIM] = dot(
            attention.astype(BF16), grad_rows, ROWS_TN
        ).astype(BF16)
    unit, _ = unit_rows(tok_ref[...].astype(F32))
    normed = (unit * gain_ref[...]).astype(BF16)
    grad_normed = dot(gproj[...], w_ref[:, : 3 * inner], ROWS_NT)
    normed_ref[...] = grad_normed.astype(BF16)
    gain_out[...] += jnp.sum(grad_normed * unit, axis=0, keepdims=True)
    weight_ref[:, : 3 * inner] += dot(normed, gproj[...], ROWS_TN)
    weight_ref[:, 3 * inner :] += dot(grad_ref[...], mixed_ref[...], ROWS_TN)

    @pl.when(step_id == pl.num_programs(0) - 1)
    def _():
        ids = [tile_bucket(step) for step in (-1, 0, 1)]
        for head in range(heads):
            for k in range(BUCKETS):
                total = jnp.zeros((TILE, TILE), F32)
                for step in (-1, 0, 1):
                    if k in tile_range(step):
                        total = total + jnp.where(ids[step + 1] == k, near[head * 3 + step + 1], 0.0)
                if k == 15:
                    total = total + far[head * 2]
                if k == 31:
                    total = total + far[head * 2 + 1]
                at = head * BUCKETS + k
                rows_s[at : at + 1, :] = jnp.sum(total, axis=0, keepdims=True)
        buckets_ref[...] = jnp.sum(rows_s[...], axis=1, keepdims=True)


def attend_back(bias, tokens, gain, weights, projected, mixed, logs, grad):
    rows, width = tokens.shape
    heads = bias.shape[0]
    inner = heads * HEAD_DIM
    seqs = rows // LENGTH
    by_seq = lambda cols: pl.BlockSpec((LENGTH, cols), lambda s: (s, 0))
    return pl.pallas_call(
        functools.partial(attend_back_kernel, heads),
        grid=(seqs,),
        in_specs=[
            pl.BlockSpec(memory_space=pltpu.SMEM),
            by_seq(width),
            whole((1, width)),
            whole((width, 4 * inner)),
            by_seq(3 * inner),
            by_seq(inner),
            by_seq(TILE),
            by_seq(width),
        ],
        out_specs=[
            by_seq(width),
            whole((width, 4 * inner)),
            whole((heads * BUCKETS, 1)),
            whole((1, width)),
        ],
        out_shape=[
            jax.ShapeDtypeStruct((rows, width), BF16),
            jax.ShapeDtypeStruct((width, 4 * inner), F32),
            jax.ShapeDtypeStruct((heads * BUCKETS, 1), F32),
            jax.ShapeDtypeStruct((1, width), F32),
        ],
        scratch_shapes=[
            pltpu.VMEM((heads, LENGTH, LENGTH), F32),
            pltpu.VMEM((width, inner), BF16),
            pltpu.VMEM((LENGTH, inner), BF16),
            pltpu.VMEM((LENGTH, 3 * inner), BF16),
            pltpu.VMEM((heads * 3, TILE, TILE), F32),
            pltpu.VMEM((heads * 2, TILE, TILE), F32),
            pltpu.VMEM((heads * BUCKETS, TILE), F32),
        ],
        compiler_params=params(),
        cost_estimate=cost(18 * rows * width * inner + 10 * rows * LENGTH * inner, rows * width * 12, rows * LENGTH * heads),
        name="attend_back",
    )(bias, tokens, gain, weights, projected, mixed, logs, grad)


def place_kernel(target_ref, rows_ref, out_ref):
    count = out_ref.shape[0]
    rows = lax.broadcasted_iota(jnp.int32, (count, rows_ref.shape[0]), 0)
    chosen = jnp.where(rows == target_ref[...], 1.0, 0.0).astype(BF16)
    out_ref[...] = dot(chosen, rows_ref[...]).astype(BF16)


def place(target_row, rows, count):
    return pl.pallas_call(
        place_kernel,
        out_shape=jax.ShapeDtypeStruct((count, rows.shape[1]), BF16),
        compiler_params=params(),
        cost_estimate=cost(2 * count * rows.size, 4 * rows.size),
        name="place",
    )(target_row, rows)


def softmax_rows(logits):
    exponent = jnp.exp(logits - jnp.max(logits, axis=-1, keepdims=True))
    return exponent * (1.0 / jnp.sum(exponent, axis=-1, keepdims=True))


def route_kernel(tok_ref, attn_ref, gain_ref, router_ref, target_ref, index_ref, kept_ref, hidden_ref, sent_ref, gate_ref):
    hidden = tok_ref[...].astype(F32) + attn_ref[...].astype(F32)
    hidden_ref[...] = hidden
    unit, _ = unit_rows(hidden)
    moe_in = (unit * gain_ref[...]).astype(BF16)
    count = sent_ref.shape[0]
    rows = lax.broadcasted_iota(jnp.int32, (count, hidden.shape[0]), 0)
    chosen = jnp.where(rows == target_ref[...], 1.0, 0.0).astype(BF16)
    sent_ref[...] = dot(chosen, moe_in).astype(BF16)
    probs = softmax_rows(dot(moe_in, router_ref[...]))
    lanes = lax.broadcasted_iota(jnp.int32, probs.shape, 1)
    picked = jnp.sum(jnp.where(lanes == index_ref[...], probs, 0.0), axis=-1, keepdims=True)
    gate_ref[...] = picked * kept_ref[...].astype(F32)


def route(tokens, attn, gain, router, target_row, index_col, kept_col, count):
    rows, width = tokens.shape
    return pl.pallas_call(
        route_kernel,
        out_shape=[
            jax.ShapeDtypeStruct((rows, width), F32),
            jax.ShapeDtypeStruct((count, width), BF16),
            jax.ShapeDtypeStruct((rows, 1), F32),
        ],
        compiler_params=params(),
        cost_estimate=cost(2 * count * rows * width, 12 * rows * width),
        name="route",
    )(tokens, attn, gain, router, target_row, index_col, kept_col)


def rest_choice(blocks, locals_, rest, expert):
    rows = lax.broadcasted_iota(jnp.int32, (blocks * rest, blocks * locals_ * rest), 0)
    cols = lax.broadcasted_iota(jnp.int32, (blocks * rest, blocks * locals_ * rest), 1)
    block = lax.div(rows, rest)
    wanted = block * (locals_ * rest) + expert * rest + (rows - block * rest)
    return jnp.where(cols == wanted, 1.0, 0.0).astype(BF16)


def pick_rows(out_ref, main_refs, rest_refs, choice, main_rows):
    at = 0
    for ref in main_refs:
        count = ref.shape[0] * ref.shape[1]
        out_ref[at : at + count, :] = ref[...].reshape(count, ref.shape[2])
        at += count
    pieces = [ref[...].reshape(ref.shape[0] * ref.shape[1], ref.shape[2]) for ref in rest_refs]
    together = pieces[0] if len(pieces) == 1 else jnp.concatenate(pieces, axis=0)
    out_ref[main_rows:, :] = dot(choice, together).astype(BF16)


def put_rows(out_refs, value_ref, choice, main_rows, main, locals_, rest, expert):
    at = 0
    spread = dot(choice, value_ref[main_rows:, :], ROWS_TN).astype(BF16)
    rest_at = 0
    for ref in out_refs:
        blocks, _, width = ref.shape
        if main:
            count = blocks * main
            start = pl.multiple_of(expert * main, main)
            ref[:, pl.ds(start, main), :] = value_ref[at : at + count, :].reshape(blocks, main, width)
            at += count
        part = spread[rest_at : rest_at + blocks * locals_ * rest].reshape(blocks, locals_ * rest, width)
        rest_at += blocks * locals_ * rest

        @pl.when(expert == 0)
        def _():
            ref[:, locals_ * main :, :] = part

        @pl.when(expert > 0)
        def _():
            ref[:, locals_ * main :, :] = ref[:, locals_ * main :, :] + part


def join_halves(place_ref, own_in, peer_in, own_out, peer_out, win, wout):
    half = own_in.shape[1]
    mine = pl.multiple_of(place_ref[0] * half, half)
    other = pl.multiple_of((1 - place_ref[0]) * half, half)
    if win is not None:
        win[pl.ds(mine, half), :] = own_in[0]
        win[pl.ds(other, half), :] = peer_in[0]
    half_out = own_out.shape[2]
    mine = pl.multiple_of(place_ref[0] * half_out, half_out)
    other = pl.multiple_of((1 - place_ref[0]) * half_out, half_out)
    wout[:, pl.ds(mine, half_out)] = own_out[0]
    wout[:, pl.ds(other, half_out)] = peer_out[0]


def expert_kernel(groups, main, locals_, rest, place_ref, *refs):
    take = lambda n: [refs_iter.pop(0) for _ in range(n)]
    refs_iter = list(refs)
    mains = groups if main else 0
    x_main, x_rest = take(mains), take(groups)
    g_main, g_rest = take(mains), take(groups)
    own_in, peer_in, own_out, peer_out, router = take(5)
    back_refs = take(groups)
    x_ref, ge_ref, hid_ref, gi_ref, gl_ref = take(5)
    win, wout, grows, inner, gunits, gate_s, dots, back = take(8)
    expert = pl.program_id(0)
    blocks = sum(ref.shape[0] for ref in x_rest)
    main_rows = blocks * main
    rows, width = x_ref.shape[1:]
    choice = rest_choice(blocks, locals_, rest, expert)
    pick_rows(x_ref.at[0], x_main, x_rest, choice, main_rows)
    pick_rows(grows, g_main, g_rest, choice, main_rows)
    join_halves(place_ref, own_in, peer_in, own_out, peer_out, win, wout)
    inner[...] = dot(x_ref[0], win[...])
    gunits[...] = dot(grows[...], wout[...], ROWS_NT)
    probs = softmax_rows(dot(x_ref[0], router[...]))
    lanes = lax.broadcasted_iota(jnp.int32, probs.shape, 1)
    mine = lanes == place_ref[1] * locals_ + expert
    picked = jnp.sum(jnp.where(mine, probs, 0.0), axis=-1, keepdims=True)
    gate_s[...] = picked
    chunk = 64

    def body(step, _):
        at = pl.ds(pl.multiple_of(step * chunk, chunk), chunk)
        value = inner[at, :]
        square = value * value
        wave = jnp.tanh(GELU_A * value * (1.0 + GELU_B * square))
        half = 0.5 * (1.0 + wave)
        hidden = (value * half).astype(BF16)
        slope = half + (0.5 * GELU_A) * value * (1.0 - wave * wave) * (1.0 + 3.0 * GELU_B * square)
        units = gunits[at, :]
        gate = gate_s[at, :]
        hid_ref[0, at, :] = hidden
        gi_ref[0, at, :] = (gate * units * slope).astype(BF16)
        ge_ref[0, at, :] = (gate * grows[at, :].astype(F32)).astype(BF16)
        dots[at, :] = jnp.sum(hidden.astype(F32) * units, axis=-1, keepdims=True)
        return 0

    lax.fori_loop(0, rows // chunk, body, 0)
    grad_logits = (dots[...] * probs * (jnp.where(mine, 1.0, 0.0) - picked)).astype(BF16)
    gl_ref[0] = grad_logits
    back[...] = (dot(gi_ref[0], win[...], ROWS_NT) + dot(grad_logits, router[...], ROWS_NT)).astype(BF16)
    put_rows(back_refs, back, choice, main_rows, main, locals_, rest, expert)


def group_specs(arrays, main, locals_, rest):
    mains, rests = [], []
    for array in arrays:
        blocks, _, width = array.shape
        if main:
            mains.append(pl.BlockSpec((blocks, main, width), lambda e, *_: (0, e, 0)))
        at = locals_ * main // (locals_ * rest)
        rests.append(pl.BlockSpec((blocks, locals_ * rest, width), lambda e, *_, at=at: (0, at, 0)))
    return mains, rests


def expert_forward_back(places, xs, gs, own_in, peer_in, own_out, peer_out, router, main, rest):
    locals_, half, wide = own_in.shape
    width, experts = router.shape
    groups = len(xs)
    blocks = sum(x.shape[0] for x in xs)
    rows = blocks * (main + rest)
    mains, rests = group_specs(xs, main, locals_, rest)
    per = lambda *shape: pl.BlockSpec((1,) + shape, lambda e, *_: (e, 0, 0))
    repeated = list(xs) if main else []
    saved = jax.ShapeDtypeStruct((locals_, rows, width), BF16)
    saved_wide = jax.ShapeDtypeStruct((locals_, rows, wide), BF16)
    result = pl.pallas_call(
        functools.partial(expert_kernel, groups, main, locals_, rest),
        grid_spec=pltpu.PrefetchScalarGridSpec(
            num_scalar_prefetch=1,
            grid=(locals_,),
            in_specs=mains + rests + mains + rests
            + [per(half, wide)] * 2 + [per(wide, half)] * 2 + [whole((width, experts))],
            out_specs=[whole(x.shape) for x in xs]
            + [per(rows, width), per(rows, width), per(rows, wide), per(rows, wide), per(rows, experts)],
            scratch_shapes=[
                pltpu.VMEM((width, wide), BF16),
                pltpu.VMEM((wide, width), BF16),
                pltpu.VMEM((rows, width), BF16),
                pltpu.VMEM((rows, wide), F32),
                pltpu.VMEM((rows, wide), F32),
                pltpu.VMEM((rows, 1), F32),
                pltpu.VMEM((rows, 1), F32),
                pltpu.VMEM((rows, width), BF16),
            ],
        ),
        out_shape=[jax.ShapeDtypeStruct(x.shape, BF16) for x in xs]
        + [saved, saved, saved_wide, saved_wide, jax.ShapeDtypeStruct((locals_, rows, experts), BF16)],
        compiler_params=params(),
        cost_estimate=cost(6 * locals_ * rows * width * wide, locals_ * rows * width * 14, locals_ * rows * wide),
        name="experts",
    )(places, *repeated, *xs, *(list(gs) if main else []), *gs, own_in, peer_in, own_out, peer_out, router)
    return result[:groups], result[groups:]


def expert_weights_kernel(groups, main, locals_, rest, place_ref, x_ref, ge_ref, hid_ref, gi_ref, gl_ref, own_out, peer_out, *refs):
    forward_refs = refs[:groups]
    in_own, in_send, out_own, out_send, router_ref, wout, value = refs[groups:]
    expert = pl.program_id(0)
    blocks = sum(ref.shape[0] for ref in forward_refs)
    choice = rest_choice(blocks, locals_, rest, expert)
    join_halves(place_ref, own_out, peer_out, own_out, peer_out, None, wout)
    value[...] = dot(hid_ref[0], wout[...]).astype(BF16)
    put_rows(forward_refs, value, choice, blocks * main, main, locals_, rest, expert)
    half = in_own.shape[1]
    mine = pl.ds(pl.multiple_of(place_ref[0] * half, half), half)
    other = pl.ds(pl.multiple_of((1 - place_ref[0]) * half, half), half)
    in_own[0] = dot(x_ref[0, :, mine], gi_ref[0], ROWS_TN)
    in_send[0] = dot(x_ref[0, :, other], gi_ref[0], ROWS_TN).astype(BF16)
    out_own[0] = dot(hid_ref[0], ge_ref[0, :, mine], ROWS_TN)
    out_send[0] = dot(hid_ref[0], ge_ref[0, :, other], ROWS_TN).astype(BF16)

    @pl.when(expert == 0)
    def _():
        router_ref[...] = jnp.zeros_like(router_ref)

    router_ref[...] += dot(x_ref[0], gl_ref[0], ROWS_TN)


def expert_weights(places, saved, own_out, peer_out, shapes, main, rest):
    x, ge, hidden, gi, gl = saved
    locals_, rows, width = x.shape
    wide = hidden.shape[2]
    experts = gl.shape[2]
    half = own_out.shape[2]
    groups = len(shapes)
    per = lambda *shape: pl.BlockSpec((1,) + shape, lambda e, *_: (e, 0, 0))
    result = pl.pallas_call(
        functools.partial(expert_weights_kernel, groups, main, locals_, rest),
        grid_spec=pltpu.PrefetchScalarGridSpec(
            num_scalar_prefetch=1,
            grid=(locals_,),
            in_specs=[per(rows, width), per(rows, width), per(rows, wide), per(rows, wide), per(rows, experts)]
            + [per(wide, half)] * 2,
            out_specs=[whole(s) for s in shapes]
            + [per(half, wide), per(half, wide), per(wide, half), per(wide, half), whole((width, experts))],
            scratch_shapes=[pltpu.VMEM((wide, width), BF16), pltpu.VMEM((rows, width), BF16)],
        ),
        out_shape=[jax.ShapeDtypeStruct(s, BF16) for s in shapes]
        + [
            jax.ShapeDtypeStruct((locals_, half, wide), F32),
            jax.ShapeDtypeStruct((locals_, half, wide), BF16),
            jax.ShapeDtypeStruct((locals_, wide, half), F32),
            jax.ShapeDtypeStruct((locals_, wide, half), BF16),
            jax.ShapeDtypeStruct((width, experts), F32),
        ],
        compiler_params=params(),
        cost_estimate=cost(6 * locals_ * rows * width * wide, locals_ * rows * width * 14),
        name="expert_weights",
    )(places, x, ge, hidden, gi, gl, own_out, peer_out)
    return result[:groups], result[groups:]


def hidden_back_kernel(target_ref, back_ref, hidden_ref, cot_ref, gain_ref, grad_ref, attn_ref, gain_out):
    count = back_ref.shape[0]
    cols = lax.broadcasted_iota(jnp.int32, (target_ref.shape[0], count), 1)
    chosen = jnp.where(cols == target_ref[...], 1.0, 0.0).astype(BF16)
    grad_in = dot(chosen, back_ref[...])
    unit, scale = unit_rows(hidden_ref[...])
    gain_out[...] = jnp.sum(grad_in * unit, axis=0, keepdims=True)
    scaled = grad_in * gain_ref[...]
    inside = jnp.mean(unit * scaled, axis=-1, keepdims=True)
    grad = cot_ref[...].astype(F32) + scale * (scaled - unit * inside)
    grad_ref[...] = grad
    attn_ref[...] = grad.astype(BF16)


def hidden_back(target_col, back, hidden, cotangent, gain):
    rows, width = hidden.shape
    return pl.pallas_call(
        hidden_back_kernel,
        out_shape=[
            jax.ShapeDtypeStruct((rows, width), F32),
            jax.ShapeDtypeStruct((rows, width), BF16),
            jax.ShapeDtypeStruct((1, width), F32),
        ],
        compiler_params=params(),
        cost_estimate=cost(2 * back.shape[0] * rows * width, 16 * rows * width),
        name="hidden_back",
    )(target_col, back, hidden, cotangent, gain)


def output_kernel(target_ref, rows_ref, hidden_ref, gate_ref, out_ref):
    count = rows_ref.shape[0]
    cols = lax.broadcasted_iota(jnp.int32, (target_ref.shape[0], count), 1)
    chosen = jnp.where(cols == target_ref[...], 1.0, 0.0).astype(BF16)
    out_ref[...] = (hidden_ref[...] + gate_ref[...] * dot(chosen, rows_ref[...])).astype(BF16)


def output_rows(target_col, expert_rows, hidden, gate):
    return pl.pallas_call(
        output_kernel,
        out_shape=jax.ShapeDtypeStruct(hidden.shape, BF16),
        compiler_params=params(),
        cost_estimate=cost(2 * expert_rows.shape[0] * hidden.size, 10 * hidden.size),
        name="output_rows",
    )(target_col, expert_rows, hidden, gate)


def tokens_back_kernel(tok_ref, normed_ref, gain_ref, hidden_ref, out_ref):
    unit, scale = unit_rows(tok_ref[...].astype(F32))
    scaled = normed_ref[...].astype(F32) * gain_ref[...]
    inside = jnp.mean(unit * scaled, axis=-1, keepdims=True)
    out_ref[...] = hidden_ref[...] + scale * (scaled - unit * inside)


def tokens_back(tokens, grad_normed, gain, grad_hidden):
    return pl.pallas_call(
        tokens_back_kernel,
        out_shape=jax.ShapeDtypeStruct(tokens.shape, F32),
        compiler_params=params(),
        cost_estimate=cost(10 * tokens.size, 12 * tokens.size),
        name="tokens_back",
    )(tokens, grad_normed, gain, grad_hidden)


def shifted(value, axis, count, step):
    return lax.ppermute(value, axis, [(s, (s + step) % count) for s in range(count)])


def gather_ring(value, axis, count):
    me = lax.axis_index(axis)
    parts = [value] + [shifted(value, axis, count, -k) for k in range(1, count)]
    return jnp.roll(jnp.stack(parts), me, axis=0)


def send_chunks(chunks, axis, count):
    return [chunks[0]] + [shifted(chunks[k], axis, count, k) for k in range(1, count)]


def return_chunks(chunks, axis, count):
    return [chunks[0]] + [shifted(chunks[k], axis, count, -k) for k in range(1, count)]


def grouped(count):
    bounds = [count * i // GROUPS for i in range(GROUPS + 1)]
    return [range(a, b) for a, b in zip(bounds[:-1], bounds[1:]) if b > a]


def on_device(
    sizes,
    tokens,
    cotangent,
    query_key_value_weight,
    attention_output_weight,
    rel_bias,
    gain_attn,
    gain_moe,
    w_router,
    w_in,
    w_out,
    expert_index,
    slot_index,
    kept_mask,
):
    dp_count, z_count, t_count = sizes
    tok_rows, width = tokens.shape
    experts_all = w_router.shape[1]
    capacity = max(2, 3 * tok_rows // (2 * experts_all))
    locals_ = w_in.shape[0]
    main = capacity // 16 * 16
    rest = capacity - main
    block = locals_ * capacity
    heads = rel_bias.shape[0]
    inner = heads * HEAD_DIM
    part = query_key_value_weight.shape[1]
    fine = w_router.shape[0]
    my_dp = lax.axis_index("dp")
    my_z = lax.axis_index("expert")
    bias = rel_bias.astype(F32)

    group_tokens = lax.all_gather(tokens, "tensor", axis=0, tiled=True)

    small = jnp.concatenate([gain_attn[:, None], gain_moe[:, None], w_router], axis=1)
    small = gather_ring(small, "tensor", t_count).reshape(-1)
    extra = -(-small.shape[0] // (16 * width)) * 16
    packed = jnp.concatenate(
        [
            query_key_value_weight.transpose(1, 0, 2).reshape(part, 3 * inner),
            attention_output_weight.T,
        ],
        axis=1,
    )
    packed = jnp.concatenate(
        [packed, jnp.pad(small, (0, extra * width - small.shape[0])).reshape(extra, width)], axis=0
    )
    packed = gather_ring(packed, "expert", z_count)
    packed = gather_ring(packed, "dp", dp_count).reshape(dp_count * z_count, part + extra, width)
    weights = packed[:, :part].reshape(width, 4 * inner)
    smalls = packed[:, part:].reshape(dp_count * z_count, -1)[:, : small.shape[0]].reshape(width, 2 + experts_all)
    gain_one = smalls[:, 0].astype(F32)[None]
    gain_two = smalls[:, 1].astype(F32)[None]
    router = smalls[:, 2:]

    peer_in = shifted(w_in, "dp", dp_count, 1)
    peer_out = shifted(w_out, "dp", dp_count, 1)

    z_of = expert_index // locals_
    local = expert_index - z_of * locals_
    inside = jnp.where(
        slot_index < main, local * main + slot_index, locals_ * main + local * rest + slot_index - main
    )
    target = lax.rem(z_of - my_z + z_count, z_count) * block + inside
    target = jnp.where(kept_mask > 0, target, -1)
    target_row, target_col = target[None, :], target[:, None]
    count = z_count * block
    split = grouped(z_count)

    def to_experts(rows):
        chunks = send_chunks(list(rows.reshape(z_count, block, width)), "expert", z_count)
        gathered = []
        for members in split:
            joined = jnp.concatenate([chunks[k] for k in members], axis=0)
            full = lax.all_gather(joined, "tensor", axis=0, tiled=True)
            gathered.append(full.reshape(t_count * len(members), block, width))
        return gathered

    def from_experts(parts):
        chunks = [None] * z_count
        for members, value in zip(split, parts):
            value = value.reshape(t_count * len(members) * block, width)
            summed = lax.psum_scatter(value, "tensor", scatter_dimension=0, tiled=True)
            for place_, k in enumerate(members):
                chunks[k] = summed[place_ * block : (place_ + 1) * block]
        return jnp.concatenate(return_chunks(chunks, "expert", z_count), axis=0)

    grad_arrived = to_experts(place(target_row, cotangent, count))

    partial_, projected, mixed, logs = attend(bias, group_tokens, gain_one, weights)
    attn = lax.psum_scatter(partial_, "tensor", scatter_dimension=0, tiled=True)
    hidden_one, sent, gate = route(
        tokens, attn, gain_two, router, target_row, expert_index[:, None], kept_mask[:, None], count
    )
    arrived = to_experts(sent)
    places = jnp.stack([my_dp, my_z]).astype(jnp.int32)
    back_parts, saved = expert_forward_back(
        places, arrived, grad_arrived, w_in, peer_in, w_out, peer_out, router, main, rest
    )
    grad_back = from_experts(back_parts)
    forward_parts, (in_own, in_send, out_own, out_send, router_part) = expert_weights(
        places, saved, w_out, peer_out, [x.shape for x in arrived], main, rest
    )
    grad_w_in = in_own + shifted(in_send, "dp", dp_count, 1).astype(F32)
    grad_w_out = out_own + shifted(out_send, "dp", dp_count, 1).astype(F32)
    grad_hidden, grad_attn, gain_two_part = hidden_back(target_col, grad_back, hidden_one, cotangent, gain_two)
    group_grad = lax.all_gather(grad_attn, "tensor", axis=0, tiled=True)
    grad_normed_part, weight_part, bucket_part, gain_one_part = attend_back(
        bias, group_tokens, gain_one, weights, projected, mixed, logs, group_grad
    )
    grad_normed = lax.psum_scatter(grad_normed_part, "tensor", scatter_dimension=0, tiled=True)
    output = output_rows(target_col, from_experts(forward_parts), hidden_one, gate)
    grad_tokens = tokens_back(tokens, grad_normed, gain_one, grad_hidden)

    owners = dp_count * z_count
    smalls = jnp.concatenate(
        [
            gain_one_part.reshape(owners, part),
            gain_two_part.reshape(owners, part),
            router_part.reshape(owners, part * experts_all),
            jnp.broadcast_to(bucket_part.reshape(1, heads * BUCKETS), (owners, heads * BUCKETS)),
        ],
        axis=1,
    )
    extra = -(-smalls.shape[1] // (16 * width)) * 16
    smalls = jnp.pad(smalls, ((0, 0), (0, extra * width - smalls.shape[1]))).reshape(owners, extra, width)
    payload = jnp.concatenate([weight_part.reshape(owners, part, width), smalls], axis=1)
    payload = payload.reshape(dp_count, z_count, part + extra, width)
    own = lax.dynamic_index_in_dim(payload, my_dp, 0, keepdims=False)
    other = lax.dynamic_index_in_dim(payload, 1 - my_dp, 0, keepdims=False)
    summed = own + shifted(other.astype(BF16), "dp", dp_count, 1).astype(F32)
    turned = jnp.roll(summed, -my_z, axis=0)
    pieces = send_chunks(
        [turned[0]] + [turned[k].astype(BF16) for k in range(1, z_count)], "expert", z_count
    )
    total = pieces[0]
    for piece in pieces[1:]:
        total = total + piece.astype(F32)
    weight_total = total[:part].reshape(part, 4, inner)
    grad_w_qkv = weight_total[:, :3].transpose(1, 0, 2)
    grad_w_attn_out = weight_total[:, 3].T
    flat = total[part:].reshape(-1)
    ends = [part, 2 * part, 2 * part + part * experts_all]
    grad_rel_bias = flat[ends[2] : ends[2] + heads * BUCKETS].reshape(heads, BUCKETS)
    rows_left = jnp.concatenate(
        [
            flat[: ends[0]].reshape(t_count, fine),
            flat[ends[0] : ends[1]].reshape(t_count, fine),
            flat[ends[1] : ends[2]].reshape(t_count, fine * experts_all),
        ],
        axis=1,
    )
    turned = jnp.roll(rows_left, -lax.axis_index("tensor"), axis=0)
    left = turned[0]
    for piece in send_chunks([turned[k] for k in range(t_count)], "tensor", t_count)[1:]:
        left = left + piece
    grad_gain_attn = left[:fine]
    grad_gain_moe = left[fine : 2 * fine]
    grad_w_router = left[2 * fine :].reshape(fine, experts_all)
    return (
        output,
        grad_tokens,
        grad_w_qkv,
        grad_w_attn_out,
        grad_rel_bias,
        grad_gain_attn,
        grad_gain_moe,
        grad_w_router,
        grad_w_in,
        grad_w_out,
    )


def solution(mesh):
    placed = (
        P(("dp", "expert", "tensor"), None),
        P(("dp", "expert", "tensor"), None),
        P(None, ("dp", "expert"), "tensor"),
        P("tensor", ("dp", "expert")),
        P("tensor", None),
        P(("dp", "expert", "tensor")),
        P(("dp", "expert", "tensor")),
        P(("dp", "expert", "tensor"), None),
        P("expert", "dp", "tensor"),
        P("expert", "tensor", "dp"),
        P(("dp", "expert", "tensor")),
        P(("dp", "expert", "tensor")),
        P(("dp", "expert", "tensor")),
    )
    sizes = tuple(mesh.shape[name] for name in ("dp", "expert", "tensor"))
    return jax.shard_map(
        functools.partial(on_device, sizes),
        mesh=mesh,
        in_specs=placed,
        out_specs=(
            P(("dp", "expert", "tensor"), None),
            P(("dp", "expert", "tensor"), None),
            P(None, ("dp", "expert"), "tensor"),
            P("tensor", ("dp", "expert")),
            P("tensor", None),
            P(("dp", "expert", "tensor")),
            P(("dp", "expert", "tensor")),
            P(("dp", "expert", "tensor"), None),
            P("expert", "dp", "tensor"),
            P("expert", "tensor", "dp"),
        ),
        check_vma=False,
    )
```

time: 1140 us -> 459 us (0.40)
  blocking collectives: 473 us -> 0 us
  matrix products: 131 us -> 0 us
  local copies, waits for them, and re-layouts: 150 us -> 22.1 us
  Pallas kernels: 0 us -> 110 us
  waiting for transfers between devices: 320 us -> 240 us
  starting transfers between devices: 6.25 us -> 49.6 us
  other arithmetic: 36.4 us -> 21.3 us
    all_to_all x3 -> x0, blocking collectives: 246 us -> none  [the longest x2 163 us: from_experts(): lax.all_to_all(partial_value.astype(jnp.bfloat16), 'expert', split_axis=1...]
    all_gather x3 -> x0, blocking collectives: 127 us -> none  [the longest x1 66.8 us: on_device(): lax.all_gather(w_router, ('dp', 'expert', 'tensor'), axis=0, tiled=True)]
    dot_general x38 -> x0, matrix products: 124 us -> none  [the longest x3 13.7 us: attend_back(): jnp.einsum('hqk,qkb->hb', grad_scores, onehot_table, preferred_element_ty...]
    pallas_call x0 -> x9, Pallas kernels: none -> 110 us  [the longest x1 35.7 us: expert_forward_back(): pl.pallas_call(functools.partial(expert_kernel, groups, main, locals_, re...]
    ppermute x0 -> x30, waiting for transfers between devices: none -> 82.2 us  [shifted(): lax.ppermute(value, axis, [(s, (s + step) % count) for s in range(count)])]
    unnamed x2 -> x0, blocking collectives: 82 us -> none
    all_to_all x1 -> x0, waiting for transfers between devices: 78.8 us -> none  [to_experts(): lax.all_to_all(grouped, 'expert', split_axis=0, concat_axis=1, tiled=True)]
    ppermute x0 -> x30, starting transfers between devices: none -> 48.9 us  [shifted(): lax.ppermute(value, axis, [(s, (s + step) % count) for s in range(count)])]
  transfers between devices with their start and end apart: 15 -> 38, of which waited for: 8 -> 20; matrix products, arithmetic and copies ran while one was open for 16% -> 8% of each run, Pallas kernels for 0% -> 12%
where the time goes in v1:
time: 459 us; the launch traced here: 458 us
  waiting for transfers between devices  240 us (52%)
  Pallas kernels  110 us (24%)
  starting transfers between devices  49.6 us (11%)
  local copies, waits for them, and re-layouts  22.1 us (5%)
  other arithmetic  21.3 us (5%)
  between operations  14.7 us (3%)
    ppermute x30, waiting for transfers between devices, shifted(): lax.ppermute(value, axis, [(s, (s + step) % count) for s in range(count)])  82.2 us
    reduce_scatter x2, waiting for transfers between devices, from_experts(): summed = lax.psum_scatter(value, 'tensor', scatter_dimension=0, tiled=True)  66.8 us
    all_gather x2, waiting for transfers between devices, to_experts(): full = lax.all_gather(joined, 'tensor', axis=0, tiled=True)  62.3 us
    ppermute x30, starting transfers between devices, shifted(): lax.ppermute(value, axis, [(s, (s + step) % count) for s in range(count)])  48.9 us
    pallas_call x1, Pallas kernels, expert_forward_back(): pl.pallas_call(functools.partial(expert_kernel, groups, main, locals_, re...  35.7 us
    pallas_call x1, Pallas kernels, expert_weights(): pl.pallas_call(functools.partial(expert_weights_kernel, groups, main, loc...  23.8 us
    pallas_call x1, Pallas kernels, attend_back(): pl.pallas_call(functools.partial(attend_back_kernel, heads), grid=(seqs,)...  22.1 us
    all_gather x1, waiting for transfers between devices, on_device(): group_grad = lax.all_gather(grad_attn, 'tensor', axis=0, tiled=True)  15.7 us
  transfers between devices with their start and end apart: 38, of which 20 were waited for; matrix products, arithmetic and copies ran while one was open for 8% of the time, Pallas kernels for 12%

profile of v1, /device:TPU:0, one launch (start us, length us, event | category | flops | bytes accessed | tf_op | source)
XLA Modules:
  0.0 457.9 jit_solution(14098402207071141934)
XLA Ops:
  23.8 4.4 collective-permute-done.3
  28.2 10.3 %collective-permute-done.4 = bf16[112,768]{0,1:T(8,128)(2,1)S(1)} collective-permute-done((bf16[112,768]{0,1:T(8,128)(2,1)S(1)}, bf16[112,768]{0,1:T(8,128)(2,1)S(1)}, u32[]{:S(2)}, u32[]{:S(2)}) %collective-permute-start.4) | collective-permute-done | bytes 172064 | tf_op jit(solution)/shard_map/ppermute | solution.py:594
  44.7 7.1 %all-gather.5.cloned.1.call-done.tok_ref = bf16[1536,768]{1,0:T(8,128)(2,1)} async-done(((bf16[384,768]{1,0:T(8,128)(2,1)}), bf16[1536,768]{1,0:T(8,128)(2,1)}) %all-gather.5.cloned.1.call-update) | async-done | bytes 2359312 | tf_op jit(solution)/shard_map/all_gather | solution.py:648
  51.9 12.2 %attend.1 = (bf16[1536,768]{1,0:T(8,128)(2,1)}, bf16[1536,576]{1,0:T(8,128)(2,1)}, bf16[1536,192]{1,0:T(8,128)(2,1)}, f32[1536,128]{1,0:T(8,128)}) custom-call(f32[3,32]{1,0:T(4,128)} %convert_element_type.69.bias_ref, bf16[1536,768]{1,0:T(8,128)(2,1)} %all-gather.5.cloned.1.call-done.tok_ref, f32[1,768]{1,0:T(1,128)} %reshape.161.gain_ref, ...), custom_call_target="tpu_custom_call" | custom-call | flops 2415919104 | bytes 9437184 | tf_op jit(solution)/shard_map/attend/pallas_call | solution.py:117
  73.8 4.8 %collective-permute-done.12 = bf16[144,768]{1,0:T(8,128)(2,1)S(1)} collective-permute-done((bf16[144,768]{1,0:T(8,128)(2,1)S(1)}, bf16[144,768]{1,0:T(8,128)(2,1)S(1)}, u32[]{:S(2)}, u32[]{:S(2)}) %collective-permute-start.12) | collective-permute-done | bytes 221216 | tf_op jit(solution)/shard_map/ppermute | solution.py:594
  78.5 13.1 %collective-permute-done.11 = bf16[144,768]{1,0:T(8,128)(2,1)S(1)} collective-permute-done((bf16[144,768]{1,0:T(8,128)(2,1)S(1)}, bf16[144,768]{1,0:T(8,128)(2,1)S(1)}, u32[]{:S(2)}, u32[]{:S(2)}) %collective-permute-start.11) | collective-permute-done | bytes 221216 | tf_op jit(solution)/shard_map/ppermute | solution.py:594
  95.6 6.0 %reduce-scatter.5.cloned.1.call-done.attn_ref = bf16[384,768]{1,0:T(8,128)(2,1)} async-done(((bf16[1536,768]{1,0:T(8,128)(2,1)}), bf16[384,768]{1,0:T(8,128)(2,1)}) %reduce-scatter.5.cloned.1.call-update) | async-done | bytes 589840 | tf_op jit(solution)/shard_map/reduce_scatter | solution.py:706
  110.9 4.8 %collective-permute-done.9 = bf16[144,768]{1,0:T(8,128)(2,1)S(1)} collective-permute-done((bf16[144,768]{1,0:T(8,128)(2,1)S(1)}, bf16[144,768]{1,0:T(8,128)(2,1)S(1)}, u32[]{:S(2)}, u32[]{:S(2)}) %collective-permute-start.9) | collective-permute-done | bytes 221216 | tf_op jit(solution)/shard_map/ppermute | solution.py:594
  115.7 13.1 %collective-permute-done.8 = bf16[144,768]{1,0:T(8,128)(2,1)S(1)} collective-permute-done((bf16[144,768]{1,0:T(8,128)(2,1)S(1)}, bf16[144,768]{1,0:T(8,128)(2,1)S(1)}, u32[]{:S(2)}, u32[]{:S(2)}) %collective-permute-start.8) | collective-permute-done | bytes 221216 | tf_op jit(solution)/shard_map/ppermute | solution.py:594
  131.2 6.0 %collective-permute-done.13.refs_5_ = bf16[4,384,768]{2,1,0:T(8,128)(2,1)S(1)} collective-permute-done((bf16[4,384,768]{2,1,0:T(8,128)(2,1)S(1)}, bf16[4,384,768]{2,1,0:T(8,128)(2,1)S(1)}, u32[]{:S(2)}, u32[]{:S(2)}) %collective-permute-start.13) | collective-permute-done | bytes 2359328 | tf_op jit(solution)/shard_map/ppermute | solution.py:594
  138.6 12.7 %all-gather.9.cloned.1.call-done = bf16[2304,768]{1,0:T(8,128)(2,1)} async-done(((bf16[576,768]{1,0:T(8,128)(2,1)}), bf16[2304,768]{1,0:T(8,128)(2,1)}) %all-gather.9.cloned.1.call-update) | async-done | bytes 3538960 | tf_op jit(solution)/shard_map/all_gather | solution.py:690
  151.3 49.6 %all-gather.7.cloned.1.call-done = bf16[2304,768]{1,0:T(8,128)(2,1)} async-done(((bf16[576,768]{1,0:T(8,128)(2,1)}), bf16[2304,768]{1,0:T(8,128)(2,1)}) %all-gather.7.cloned.1.call-update) | async-done | bytes 3538960 | tf_op jit(solution)/shard_map/all_gather | solution.py:690
  200.9 35.7 %experts.1 = (bf16[16,144,768]{2,1,0:T(8,128)(2,1)}, bf16[4,576,768]{2,1,0:T(8,128)(2,1)}, bf16[4,576,768]{2,1,0:T(8,128)(2,1)}, bf16[4,576,768]{2,1,0:T(8,128)(...) custom-call(s32[2]{0:T(128)} %pad_add_fusion.place_ref, bf16[16,144,768]{2,1,0:T(8,128)(2,1)} %bitcast.110, ...), custom_call_target="tpu_custom_call" | custom-call | flops 8153726976 | bytes 24772608 | tf_op jit(solution)/shard_map/experts/pallas_call | solution.py:443
  236.7 47.3 %reduce-scatter.9.cloned.1.call-done = bf16[576,768]{1,0:T(8,128)(2,1)} async-done(((bf16[2304,768]{1,0:T(8,128)(2,1)}), bf16[576,768]{1,0:T(8,128)(2,1)}) %reduce-scatter.9.cloned.1.call-update) | async-done | bytes 884752 | tf_op jit(solution)/shard_map/reduce_scatter | solution.py:698
  291.5 4.1 collective-permute-done.20
  295.7 8.3 %collective-permute-done.19 = bf16[144,768]{1,0:T(8,128)(2,1)S(1)} collective-permute-done((bf16[144,768]{1,0:T(8,128)(2,1)S(1)}, bf16[144,768]{1,0:T(8,128)(2,1)S(1)}, u32[]{:S(2)}, u32[]{:S(2)}) %collective-permute-start.19) | collective-permute-done | bytes 221216 | tf_op jit(solution)/shard_map/ppermute | solution.py:594
  309.0 23.8 %expert_weights.1 = (bf16[16,144,768]{2,1,0:T(8,128)(2,1)}, f32[4,384,768]{2,1,0:T(8,128)}, bf16[4,384,768]{2,1,0:T(8,128)(2,1)}, f32[4,768,384]{2,1,0:T(8,128)}...) custom-call(s32[2]{0:T(128)} %pad_add_fusion.place_ref, bf16[4,576,768]{2,1,0:T(8,128)(2,1)} %get-tuple-element.38.x_ref, ...), custom_call_target="tpu_custom_call" | custom-call | flops 8153726976 | bytes 24772608 | tf_op jit(solution)/shard_map/expert_weights/pallas_call | solution.py:504
  333.7 15.7 %all-gather.11.cloned.1.call-done.grad_ref = bf16[1536,768]{1,0:T(8,128)(2,1)} async-done(((bf16[384,768]{1,0:T(8,128)(2,1)}), bf16[1536,768]{1,0:T(8,128)(2,1)}) %all-gather.11.cloned.1.call-update) | async-done | bytes 2359312 | tf_op jit(solution)/shard_map/all_gather | solution.py:722
  349.4 22.1 %attend_back.1 = (bf16[1536,768]{1,0:T(8,128)(2,1)}, f32[768,768]{1,0:T(8,128)}, f32[96,1]{1,0:T(8,128)}, f32[1,768]{1,0:T(1,128)}) custom-call(f32[3,32]{1,0:T(4,128)} %convert_element_type.69.bias_ref, bf16[1536,768]{1,0:T(8,128)(2,1)} %all-gather.5.cloned.1.call-done.tok_ref, f32[1,768]{1,0:T(1,128)} %reshape.161.gain_ref, bf16[768,768]{1,0:T(8,128)(2,1)} %bitcast.92, ...), custom_call_target="tpu_custom_call" | custom-call | flops 5586812928 | bytes 14155776 | tf_op jit(solution)/shard_map/attend_back/pallas_call | solution.py:223
  374.4 5.8 %convert_add_fusion.1 = f32[4,384,768]{2,1,0:T(8,128)} fusion(f32[4,384,768]{2,1,0:T(8,128)} %get-tuple-element.58, bf16[4,384,768]{2,1,0:T(8,128)(2,1)} %collective-permute-done.28), kind=kLoop, calls=%fused_computation.1 | loop fusion | flops 2359296 | bytes 11796480 | tf_op jit(solution)/shard_map/add | solution.py:719
  380.3 19.5 %reduce-scatter.7.cloned.1.call-done = bf16[576,768]{1,0:T(8,128)(2,1)} async-done(((bf16[2304,768]{1,0:T(8,128)(2,1)}), bf16[576,768]{1,0:T(8,128)(2,1)}) %reduce-scatter.7.cloned.1.call-update) | async-done | bytes 884752 | tf_op jit(solution)/shard_map/reduce_scatter | solution.py:698
  411.4 9.9 %collective-permute-start.23 = (bf16[112,768]{1,0:T(8,128)(2,1)S(1)}, bf16[112,768]{1,0:T(8,128)(2,1)S(1)}, u32[]{:S(2)}, u32[]{:S(2)}) collective-permute-start(bf16[112,768]{1,0:T(8,128)(2,1)S(1)} %get-tuple-element.136), channel_id=1, source_target_pairs={{0,8},{4,12},{8,0},{12,4},{1,9},{5,13},{9,1},{13,5},{2,10},{6,14},... | collective-permute-start | bytes 516104 | tf_op jit(solution)/shard_map/ppermute | solution.py:594
  421.3 4.4 convert_add_fusion
  429.8 9.3 %collective-permute-done.23 = bf16[112,768]{1,0:T(8,128)(2,1)S(1)} collective-permute-done((bf16[112,768]{1,0:T(8,128)(2,1)S(1)}, bf16[112,768]{1,0:T(8,128)(2,1)S(1)}, u32[]{:S(2)}, u32[]{:S(2)}) %collective-permute-start.23) | collective-permute-done | bytes 172064 | tf_op jit(solution)/shard_map/ppermute | solution.py:594
  (184 shorter events, 93.1 us)
Async XLA Ops:
  7.2 44.7 %all-gather.5.cloned.1.call-start = ((), (), s32[]{:S(2)}) async-start(), calls=%async_computation.4 | async-start | bytes 2949120 | tf_op jit(solution)/shard_map/all_gather | solution.py:648
  13.0 88.6 %reduce-scatter.5.cloned.1.call-start = ((), (), s32[]{:S(2)}) async-start(), calls=%async_computation.5 | async-start | bytes 2949120 | tf_op jit(solution)/shard_map/reduce_scatter | solution.py:706
  22.8 15.8 %collective-permute-start.5 = (bf16[112,768]{0,1:T(8,128)(2,1)S(1)}, bf16[112,768]{0,1:T(8,128)(2,1)S(1)}, u32[]{:S(2)}, u32[]{:S(2)}) collective-permute-start(bf16[112,768]{0,1:T(8,128)(2,1)S(1)} %get-tuple-element.117), channel_id=1, source_target_pairs={{0,4},{4,8},{8,12},{12,0},{1,5},{5,9},{9,13},{13,1},{2,6},{6,10},{... | collective-permute-start | bytes 516104 | tf_op jit(solution)/shard_map/ppermute | solution.py:594
  22.8 15.7 %collective-permute-start.4 = (bf16[112,768]{0,1:T(8,128)(2,1)S(1)}, bf16[112,768]{0,1:T(8,128)(2,1)S(1)}, u32[]{:S(2)}, u32[]{:S(2)}) collective-permute-start(bf16[112,768]{0,1:T(8,128)(2,1)S(1)} %get-tuple-element.117), channel_id=1, source_target_pairs={{0,8},{4,12},{8,0},{12,4},{1,9},{5,13},{9,1},{13,5},{2,10},{6,14},... | collective-permute-start | bytes 516104 | tf_op jit(solution)/shard_map/ppermute | solution.py:594
  64.1 87.3 %all-gather.9.cloned.1.call-start = ((), (), s32[]{:S(2)}) async-start(), calls=%async_computation.7 | async-start | bytes 4423680 | tf_op jit(solution)/shard_map/all_gather | solution.py:690
  72.6 19.0 %collective-permute-start.11 = (bf16[144,768]{1,0:T(8,128)(2,1)S(1)}, bf16[144,768]{1,0:T(8,128)(2,1)S(1)}, u32[]{:S(2)}, u32[]{:S(2)}) collective-permute-start(bf16[144,768]{1,0:T(8,128)(2,1)S(1)} %get-tuple-element.128), channel_id=1, source_target_pairs={{0,8},{4,12},{8,0},{12,4},{1,9},{5,13},{9,1},{13,5},{2,10},{6,14},... | collective-permute-start | bytes 663560 | tf_op jit(solution)/shard_map/ppermute | solution.py:594
  72.6 19.0 %collective-permute-start.10 = (bf16[144,768]{1,0:T(8,128)(2,1)S(1)}, bf16[144,768]{1,0:T(8,128)(2,1)S(1)}, u32[]{:S(2)}, u32[]{:S(2)}) collective-permute-start(bf16[144,768]{1,0:T(8,128)(2,1)S(1)} %get-tuple-element.129), channel_id=1, source_target_pairs={{0,4},{4,8},{8,12},{12,0},{1,5},{5,9},{9,13},{13,1},{2,6},{6,10},{... | collective-permute-start | bytes 663560 | tf_op jit(solution)/shard_map/ppermute | solution.py:594
  92.6 108.3 %all-gather.7.cloned.1.call-start = ((), (), s32[]{:S(2)}) async-start(), calls=%async_computation.6 | async-start | bytes 4423680 | tf_op jit(solution)/shard_map/all_gather | solution.py:690
  109.8 19.0 %collective-permute-start.8 = (bf16[144,768]{1,0:T(8,128)(2,1)S(1)}, bf16[144,768]{1,0:T(8,128)(2,1)S(1)}, u32[]{:S(2)}, u32[]{:S(2)}) collective-permute-start(bf16[144,768]{1,0:T(8,128)(2,1)S(1)} %get-tuple-element.132), channel_id=1, source_target_pairs={{0,8},{4,12},{8,0},{12,4},{1,9},{5,13},{9,1},{13,5},{2,10},{6,14},... | collective-permute-start | bytes 663560 | tf_op jit(solution)/shard_map/ppermute | solution.py:594
  109.8 19.0 %collective-permute-start.7 = (bf16[144,768]{1,0:T(8,128)(2,1)S(1)}, bf16[144,768]{1,0:T(8,128)(2,1)S(1)}, u32[]{:S(2)}, u32[]{:S(2)}) collective-permute-start(bf16[144,768]{1,0:T(8,128)(2,1)S(1)} %get-tuple-element.133), channel_id=1, source_target_pairs={{0,4},{4,8},{8,12},{12,0},{1,5},{5,9},{9,13},{13,1},{2,6},{6,10},{... | collective-permute-start | bytes 663560 | tf_op jit(solution)/shard_map/ppermute | solution.py:594
  129.8 154.3 %reduce-scatter.9.cloned.1.call-start = ((), (), s32[]{:S(2)}) async-start(), calls=%async_computation.9 | async-start | bytes 4423680 | tf_op jit(solution)/shard_map/reduce_scatter | solution.py:698
  236.7 112.7 %all-gather.11.cloned.1.call-start = ((), (), s32[]{:S(2)}) async-start(), calls=%async_computation.10 | async-start | bytes 2949120 | tf_op jit(solution)/shard_map/all_gather | solution.py:722
  286.9 17.1 %collective-permute-start.19 = (bf16[144,768]{1,0:T(8,128)(2,1)S(1)}, bf16[144,768]{1,0:T(8,128)(2,1)S(1)}, u32[]{:S(2)}, u32[]{:S(2)}) collective-permute-start(bf16[144,768]{1,0:T(8,128)(2,1)S(1)} %get-tuple-element.120), channel_id=1, source_target_pairs={{0,8},{4,12},{8,0},{12,4},{1,9},{5,13},{9,1},{13,5},{2,10},{6,14},... | collective-permute-start | bytes 663560 | tf_op jit(solution)/shard_map/ppermute | solution.py:594
  289.3 14.7 %collective-permute-start.18 = (bf16[144,768]{1,0:T(8,128)(2,1)S(1)}, bf16[144,768]{1,0:T(8,128)(2,1)S(1)}, u32[]{:S(2)}, u32[]{:S(2)}) collective-permute-start(bf16[144,768]{1,0:T(8,128)(2,1)S(1)} %get-tuple-element.121), channel_id=1, source_target_pairs={{0,12},{4,0},{8,4},{12,8},{1,13},{5,1},{9,5},{13,9},{2,14},{6,2},{... | collective-permute-start | bytes 663560 | tf_op jit(solution)/shard_map/ppermute | solution.py:594
  309.0 90.7 %reduce-scatter.7.cloned.1.call-start = ((), (), s32[]{:S(2)}) async-start(), calls=%async_computation.8 | async-start | bytes 4423680 | tf_op jit(solution)/shard_map/reduce_scatter | solution.py:698
  332.9 115.0 %reduce-scatter.11.cloned.1.call-start = ((), (), s32[]{:S(2)}) async-start(), calls=%async_computation.11 | async-start | bytes 2949120 | tf_op jit(solution)/shard_map/reduce_scatter | solution.py:726
  333.2 41.3 %collective-permute-start.28 = (bf16[4,384,768]{2,1,0:T(8,128)(2,1)}, bf16[4,384,768]{2,1,0:T(8,128)(2,1)}, u32[]{:S(2)}, u32[]{:S(2)}) collective-permute-start(bf16[4,384,768]{2,1,0:T(8,128)(2,1)} %get-tuple-element.59), channel_id=1, source_target_pairs={{0,16},{16,0},{1,17},{17,1},{2,18},{18,2},{3,19},{19,3},{4,20},{20... | collective-permute-start | bytes 7077896 | tf_op jit(solution)/shard_map/ppermute | solution.py:594
  333.2 74.3 %collective-permute-start.29 = (bf16[4,768,384]{2,1,0:T(8,128)(2,1)}, bf16[4,768,384]{2,1,0:T(8,128)(2,1)}, u32[]{:S(2)}, u32[]{:S(2)}) collective-permute-start(bf16[4,768,384]{2,1,0:T(8,128)(2,1)} %get-tuple-element.61), channel_id=1, source_target_pairs={{0,16},{16,0},{1,17},{17,1},{2,18},{18,2},{3,19},{19,3},{4,20},{20... | collective-permute-start | bytes 7077896 | tf_op jit(solution)/shard_map/ppermute | solution.py:594
  374.4 32.0 %collective-permute-start.21 = (bf16[4,112,768]{2,1,0:T(8,128)(2,1)}, bf16[4,112,768]{2,1,0:T(8,128)(2,1)S(1)}, u32[]{:S(2)}, u32[]{:S(2)}) collective-permute-start(bf16[4,112,768]{2,1,0:T(8,128)(2,1)} %fusion.9), channel_id=1, source_target_pairs={{0,16},{16,0},{1,17},{17,1},{2,18},{18,2},{3,19},{19,3},{4,20},{20... | collective-permute-start | bytes 2064392 | tf_op jit(solution)/shard_map/ppermute | solution.py:594
  402.6 23.1 %collective-permute-start.16 = (bf16[144,768]{1,0:T(8,128)(2,1)S(1)}, bf16[144,768]{1,0:T(8,128)(2,1)S(1)}, u32[]{:S(2)}, u32[]{:S(2)}) collective-permute-start(bf16[144,768]{1,0:T(8,128)(2,1)S(1)} %get-tuple-element.124), channel_id=1, source_target_pairs={{0,8},{4,12},{8,0},{12,4},{1,9},{5,13},{9,1},{13,5},{2,10},{6,14},... | collective-permute-start | bytes 663560 | tf_op jit(solution)/shard_map/ppermute | solution.py:594
  405.0 20.7 %collective-permute-start.15 = (bf16[144,768]{1,0:T(8,128)(2,1)S(1)}, bf16[144,768]{1,0:T(8,128)(2,1)S(1)}, u32[]{:S(2)}, u32[]{:S(2)}) collective-permute-start(bf16[144,768]{1,0:T(8,128)(2,1)S(1)} %get-tuple-element.125), channel_id=1, source_target_pairs={{0,12},{4,0},{8,4},{12,8},{1,13},{5,1},{9,5},{13,9},{2,14},{6,2},{... | collective-permute-start | bytes 663560 | tf_op jit(solution)/shard_map/ppermute | solution.py:594
  406.9 22.9 %collective-permute-start.22 = (bf16[112,768]{1,0:T(8,128)(2,1)S(1)}, bf16[112,768]{1,0:T(8,128)(2,1)S(1)}, u32[]{:S(2)}, u32[]{:S(2)}) collective-permute-start(bf16[112,768]{1,0:T(8,128)(2,1)S(1)} %get-tuple-element.134), channel_id=1, source_target_pairs={{0,4},{4,8},{8,12},{12,0},{1,5},{5,9},{9,13},{13,1},{2,6},{6,10},{... | collective-permute-start | bytes 516104 | tf_op jit(solution)/shard_map/ppermute | solution.py:594
  407.6 22.3 %collective-permute-start.24 = (bf16[112,768]{1,0:T(8,128)(2,1)S(1)}, bf16[112,768]{1,0:T(8,128)(2,1)S(1)}, u32[]{:S(2)}, u32[]{:S(2)}) collective-permute-start(bf16[112,768]{1,0:T(8,128)(2,1)S(1)} %get-tuple-element.135), channel_id=1, source_target_pairs={{0,12},{4,0},{8,4},{12,8},{1,13},{5,1},{9,5},{13,9},{2,14},{6,2},{... | collective-permute-start | bytes 516104 | tf_op jit(solution)/shard_map/ppermute | solution.py:594
  411.4 27.8 %collective-permute-start.23 = (bf16[112,768]{1,0:T(8,128)(2,1)S(1)}, bf16[112,768]{1,0:T(8,128)(2,1)S(1)}, u32[]{:S(2)}, u32[]{:S(2)}) collective-permute-start(bf16[112,768]{1,0:T(8,128)(2,1)S(1)} %get-tuple-element.136), channel_id=1, source_target_pairs={{0,8},{4,12},{8,0},{12,4},{1,9},{5,13},{9,1},{13,5},{2,10},{6,14},... | collective-permute-start | bytes 516104 | tf_op jit(solution)/shard_map/ppermute | solution.py:594
  (27 other events, 165.3 us)
Sparse Core Ops, SparseCore 0:
  13.1 38.6 all-gather.4
  64.2 37.3 reduce-scatter.4
  104.1 47.2 all-gather.8
  153.6 47.2 all-gather.6
  236.8 47.2 reduce-scatter.8
  309.1 40.2 all-gather.10
  352.5 47.2 reduce-scatter.6
  402.8 37.3 reduce-scatter.10

commit v2 on v1

--- a/solution.py
+++ b/solution.py
@@ -21,7 +21,6 @@
 ROWS_NT = (((1,), (1,)), ((), ()))
 ROWS_TN = (((0,), (0,)), ((), ()))
 VMEM_BYTES = 56 * 1024 * 1024
-GROUPS = 1
 
 
 def dot(a, b, dims=ROWS_NN):
@@ -79,14 +78,36 @@
     return values * scale, scale
 
 
-def attend_kernel(heads, bias_ref, tok_ref, gain_ref, w_ref, part_ref, qkv_ref, mixed_ref, log_ref, table, wo):
+def group_rows(place_ref, out, pieces):
+    rows = pieces[0].shape[0]
+    for j, piece in enumerate(pieces):
+        at = pl.multiple_of((place_ref[2] ^ j) * rows, rows)
+        out[pl.ds(at, rows), :] = piece[...]
+
+
+def part_rows(place_ref, pieces, source):
+    rows = pieces[0].shape[0]
+    for j, piece in enumerate(pieces):
+        at = pl.multiple_of((place_ref[2] ^ j) * rows, rows)
+        piece[...] = source[pl.ds(at, rows), :]
+
+
+def attend_kernel(heads, tensors, place_ref, bias_ref, *refs):
+    pieces = refs[:tensors]
+    gain_ref, w_ref = refs[tensors : tensors + 2]
+    parts = refs[tensors + 2 : 2 * tensors + 2]
+    tok_ref, qkv_ref, mixed_ref, log_ref, table, wo, group, result = refs[2 * tensors + 2 :]
     inner = heads * HEAD_DIM
-
-    @pl.when(pl.program_id(0) == 0)
+    step_id = pl.program_id(0)
+
+    @pl.when(step_id == 0)
     def _():
         fill_bias(bias_ref, table, heads)
         wo[...] = w_ref[:, 3 * inner :]
-
+        group_rows(place_ref, group, pieces)
+
+    here = pl.ds(pl.multiple_of(step_id * LENGTH, LENGTH), LENGTH)
+    tok_ref[...] = group[here, :]
     unit, _ = unit_rows(tok_ref[...].astype(F32))
     normed = (unit * gain_ref[...]).astype(BF16)
     qkv_ref[...] = dot(normed, w_ref[:, : 3 * inner]).astype(BF16)
@@ -105,42 +126,57 @@
         mixed_ref[:, at : at + HEAD_DIM] = dot(attention, value).astype(BF16)
         logs = jnp.where(lanes == head, top + jnp.log(total), logs)
     log_ref[...] = logs
-    part_ref[...] = dot(mixed_ref[...], wo[...], ROWS_NT).astype(BF16)
-
-
-def attend(bias, tokens, gain, weights):
-    rows, width = tokens.shape
+    result[here, :] = dot(mixed_ref[...], wo[...], ROWS_NT).astype(BF16)
+
+    @pl.when(step_id == pl.num_programs(0) - 1)
+    def _():
+        part_rows(place_ref, parts, result)
+
+
+def attend(places, bias, pieces, gain, weights):
+    tensors = len(pieces)
+    piece_rows, width = pieces[0].shape
+    rows = tensors * piece_rows
     heads = bias.shape[0]
     inner = heads * HEAD_DIM
     seqs = rows // LENGTH
-    by_seq = lambda cols: pl.BlockSpec((LENGTH, cols), lambda s: (s, 0))
-    return pl.pallas_call(
-        functools.partial(attend_kernel, heads),
-        grid=(seqs,),
-        in_specs=[
-            pl.BlockSpec(memory_space=pltpu.SMEM),
-            by_seq(width),
-            whole((1, width)),
-            whole((width, 4 * inner)),
-        ],
-        out_specs=[by_seq(width), by_seq(3 * inner), by_seq(inner), by_seq(TILE)],
-        out_shape=[
+    by_seq = lambda cols: pl.BlockSpec((LENGTH, cols), lambda s, *_: (s, 0))
+    result = pl.pallas_call(
+        functools.partial(attend_kernel, heads, tensors),
+        grid_spec=pltpu.PrefetchScalarGridSpec(
+            num_scalar_prefetch=1,
+            grid=(seqs,),
+            in_specs=[pl.BlockSpec(memory_space=pltpu.SMEM)]
+            + [whole((piece_rows, width))] * tensors
+            + [whole((1, width)), whole((width, 4 * inner))],
+            out_specs=[whole((piece_rows, width))] * tensors
+            + [by_seq(width), by_seq(3 * inner), by_seq(inner), by_seq(TILE)],
+            scratch_shapes=[
+                pltpu.VMEM((heads, LENGTH, LENGTH), F32),
+                pltpu.VMEM((width, inner), BF16),
+                pltpu.VMEM((rows, width), BF16),
+                pltpu.VMEM((rows, width), BF16),
+            ],
+        ),
+        out_shape=[jax.ShapeDtypeStruct((piece_rows, width), BF16)] * tensors
+        + [
             jax.ShapeDtypeStruct((rows, width), BF16),
             jax.ShapeDtypeStruct((rows, 3 * inner), BF16),
             jax.ShapeDtypeStruct((rows, inner), BF16),
             jax.ShapeDtypeStruct((rows, TILE), F32),
         ],
-        scratch_shapes=[pltpu.VMEM((heads, LENGTH, LENGTH), F32), pltpu.VMEM((width, inner), BF16)],
         compiler_params=params(),
         cost_estimate=cost(8 * rows * width * inner + 4 * rows * LENGTH * inner, rows * width * 8, rows * LENGTH * heads),
         name="attend",
-    )(bias, tokens, gain, weights)
+    )(places, bias, *pieces, gain, weights)
+    return result[:tensors], result[tensors:]
 
 
 def attend_back_kernel(
-    heads, bias_ref, tok_ref, gain_ref, w_ref, qkv_ref, mixed_ref, log_ref, grad_ref,
-    normed_ref, weight_ref, buckets_ref, gain_out, table, wo, gmix, gproj, near, far, rows_s,
+    heads, tensors, place_ref, bias_ref, tok_ref, gain_ref, w_ref, qkv_ref, mixed_ref, log_ref, *refs
 ):
+    pieces, parts = refs[:tensors], refs[tensors : 2 * tensors]
+    weight_ref, buckets_ref, gain_out, table, wo, gmix, gproj, near, far, rows_s, group, result = refs[2 * tensors :]
     inner = heads * HEAD_DIM
     blocks = LENGTH // TILE
     step_id = pl.program_id(0)
@@ -153,8 +189,10 @@
         far[...] = jnp.zeros_like(far)
         weight_ref[...] = jnp.zeros_like(weight_ref)
         gain_out[...] = jnp.zeros_like(gain_out)
-
-    gmix[...] = dot(grad_ref[...], wo[...]).astype(BF16)
+        group_rows(place_ref, group, pieces)
+
+    here = pl.ds(pl.multiple_of(step_id * LENGTH, LENGTH), LENGTH)
+    gmix[...] = dot(group[here, :], wo[...]).astype(BF16)
     for head in range(heads):
         at = head * HEAD_DIM
         query = (qkv_ref[:, at : at + HEAD_DIM] * HEAD_DIM ** (-0.5)).astype(BF16)
@@ -191,13 +229,14 @@
     unit, _ = unit_rows(tok_ref[...].astype(F32))
     normed = (unit * gain_ref[...]).astype(BF16)
     grad_normed = dot(gproj[...], w_ref[:, : 3 * inner], ROWS_NT)
-    normed_ref[...] = grad_normed.astype(BF16)
+    result[here, :] = grad_normed.astype(BF16)
     gain_out[...] += jnp.sum(grad_normed * unit, axis=0, keepdims=True)
     weight_ref[:, : 3 * inner] += dot(normed, gproj[...], ROWS_TN)
-    weight_ref[:, 3 * inner :] += dot(grad_ref[...], mixed_ref[...], ROWS_TN)
+    weight_ref[:, 3 * inner :] += dot(group[here, :], mixed_ref[...], ROWS_TN)
 
     @pl.when(step_id == pl.num_programs(0) - 1)
     def _():
+        part_rows(place_ref, parts, result)
         ids = [tile_bucket(step) for step in (-1, 0, 1)]
         for head in range(heads):
             for k in range(BUCKETS):
@@ -214,50 +253,54 @@
         buckets_ref[...] = jnp.sum(rows_s[...], axis=1, keepdims=True)
 
 
-def attend_back(bias, tokens, gain, weights, projected, mixed, logs, grad):
+def attend_back(places, bias, tokens, gain, weights, projected, mixed, logs, pieces):
     rows, width = tokens.shape
+    tensors = len(pieces)
+    piece = whole(pieces[0].shape)
     heads = bias.shape[0]
     inner = heads * HEAD_DIM
     seqs = rows // LENGTH
-    by_seq = lambda cols: pl.BlockSpec((LENGTH, cols), lambda s: (s, 0))
-    return pl.pallas_call(
-        functools.partial(attend_back_kernel, heads),
-        grid=(seqs,),
-        in_specs=[
-            pl.BlockSpec(memory_space=pltpu.SMEM),
-            by_seq(width),
-            whole((1, width)),
-            whole((width, 4 * inner)),
-            by_seq(3 * inner),
-            by_seq(inner),
-            by_seq(TILE),
-            by_seq(width),
-        ],
-        out_specs=[
-            by_seq(width),
-            whole((width, 4 * inner)),
-            whole((heads * BUCKETS, 1)),
-            whole((1, width)),
-        ],
-        out_shape=[
-            jax.ShapeDtypeStruct((rows, width), BF16),
+    by_seq = lambda cols: pl.BlockSpec((LENGTH, cols), lambda s, *_: (s, 0))
+    result = pl.pallas_call(
+        functools.partial(attend_back_kernel, heads, tensors),
+        grid_spec=pltpu.PrefetchScalarGridSpec(
+            num_scalar_prefetch=1,
+            grid=(seqs,),
+            in_specs=[
+                pl.BlockSpec(memory_space=pltpu.SMEM),
+                by_seq(width),
+                whole((1, width)),
+                whole((width, 4 * inner)),
+                by_seq(3 * inner),
+                by_seq(inner),
+                by_seq(TILE),
+            ]
+            + [piece] * tensors,
+            out_specs=[piece] * tensors
+            + [whole((width, 4 * inner)), whole((heads * BUCKETS, 1)), whole((1, width))],
+            scratch_shapes=[
+                pltpu.VMEM((heads, LENGTH, LENGTH), F32),
+                pltpu.VMEM((width, inner), BF16),
+                pltpu.VMEM((LENGTH, inner), BF16),
+                pltpu.VMEM((LENGTH, 3 * inner), BF16),
+                pltpu.VMEM((heads * 3, TILE, TILE), F32),
+                pltpu.VMEM((heads * 2, TILE, TILE), F32),
+                pltpu.VMEM((heads * BUCKETS, TILE), F32),
+                pltpu.VMEM((rows, width), BF16),
+                pltpu.VMEM((rows, width), BF16),
+            ],
+        ),
+        out_shape=[jax.ShapeDtypeStruct(pieces[0].shape, BF16)] * tensors
+        + [
             jax.ShapeDtypeStruct((width, 4 * inner), F32),
             jax.ShapeDtypeStruct((heads * BUCKETS, 1), F32),
             jax.ShapeDtypeStruct((1, width), F32),
         ],
-        scratch_shapes=[
-            pltpu.VMEM((heads, LENGTH, LENGTH), F32),
-            pltpu.VMEM((width, inner), BF16),
-            pltpu.VMEM((LENGTH, inner), BF16),
-            pltpu.VMEM((LENGTH, 3 * inner), BF16),
-            pltpu.VMEM((heads * 3, TILE, TILE), F32),
-            pltpu.VMEM((heads * 2, TILE, TILE), F32),
-            pltpu.VMEM((heads * BUCKETS, TILE), F32),
-        ],
         compiler_params=params(),
         cost_estimate=cost(18 * rows * width * inner + 10 * rows * LENGTH * inner, rows * width * 12, rows * LENGTH * heads),
         name="attend_back",
-    )(bias, tokens, gain, weights, projected, mixed, logs, grad)
+    )(places, bias, tokens, gain, weights, projected, mixed, logs, *pieces)
+    return result[:tensors], result[tensors:]
 
 
 def place_kernel(target_ref, rows_ref, out_ref):
@@ -282,8 +325,17 @@
     return exponent * (1.0 / jnp.sum(exponent, axis=-1, keepdims=True))
 
 
-def route_kernel(tok_ref, attn_ref, gain_ref, router_ref, target_ref, index_ref, kept_ref, hidden_ref, sent_ref, gate_ref):
-    hidden = tok_ref[...].astype(F32) + attn_ref[...].astype(F32)
+def sum_pieces(refs):
+    total = refs[0][...].astype(F32)
+    for ref in refs[1:]:
+        total = total + ref[...].astype(F32)
+    return total
+
+
+def route_kernel(tensors, tok_ref, *refs):
+    attn_refs = refs[:tensors]
+    gain_ref, router_ref, target_ref, index_ref, kept_ref, hidden_ref, sent_ref, gate_ref = refs[tensors:]
+    hidden = tok_ref[...].astype(F32) + sum_pieces(attn_refs)
     hidden_ref[...] = hidden
     unit, _ = unit_rows(hidden)
     moe_in = (unit * gain_ref[...]).astype(BF16)
@@ -300,7 +352,7 @@
 def route(tokens, attn, gain, router, target_row, index_col, kept_col, count):
     rows, width = tokens.shape
     return pl.pallas_call(
-        route_kernel,
+        functools.partial(route_kernel, len(attn)),
         out_shape=[
             jax.ShapeDtypeStruct((rows, width), F32),
             jax.ShapeDtypeStruct((count, width), BF16),
@@ -309,7 +361,7 @@
         compiler_params=params(),
         cost_estimate=cost(2 * count * rows * width, 12 * rows * width),
         name="route",
-    )(tokens, attn, gain, router, target_row, index_col, kept_col)
+    )(tokens, *attn, gain, router, target_row, index_col, kept_col)
 
 
 def rest_choice(blocks, locals_, rest, expert):
@@ -320,38 +372,46 @@
     return jnp.where(cols == wanted, 1.0, 0.0).astype(BF16)
 
 
-def pick_rows(out_ref, main_refs, rest_refs, choice, main_rows):
+def pick_rows(out_ref, views, choice, main_rows, main, expert):
     at = 0
-    for ref in main_refs:
-        count = ref.shape[0] * ref.shape[1]
-        out_ref[at : at + count, :] = ref[...].reshape(count, ref.shape[2])
-        at += count
-    pieces = [ref[...].reshape(ref.shape[0] * ref.shape[1], ref.shape[2]) for ref in rest_refs]
-    together = pieces[0] if len(pieces) == 1 else jnp.concatenate(pieces, axis=0)
-    out_ref[main_rows:, :] = dot(choice, together).astype(BF16)
-
-
-def put_rows(out_refs, value_ref, choice, main_rows, main, locals_, rest, expert):
+    pieces = []
+    for view in views:
+        blocks, size, width = view.shape
+        if main:
+            start = pl.multiple_of(expert * main, main)
+            out_ref[at : at + blocks * main, :] = view[:, pl.ds(start, main), :].reshape(blocks * main, width)
+            at += blocks * main
+        rest = size - size * main_rows // out_ref.shape[0]
+        pieces.append(view[:, size - rest :, :].reshape(blocks * rest, width))
+    out_ref[main_rows:, :] = dot(choice, jnp.concatenate(pieces, axis=0)).astype(BF16)
+
+
+def put_rows(views, value_ref, choice, main_rows, main, locals_, rest, expert):
     at = 0
     spread = dot(choice, value_ref[main_rows:, :], ROWS_TN).astype(BF16)
     rest_at = 0
-    for ref in out_refs:
-        blocks, _, width = ref.shape
+    for view in views:
+        blocks, _, width = view.shape
         if main:
             count = blocks * main
             start = pl.multiple_of(expert * main, main)
-            ref[:, pl.ds(start, main), :] = value_ref[at : at + count, :].reshape(blocks, main, width)
+            view[:, pl.ds(start, main), :] = value_ref[at : at + count, :].reshape(blocks, main, width)
             at += count
         part = spread[rest_at : rest_at + blocks * locals_ * rest].reshape(blocks, locals_ * rest, width)
         rest_at += blocks * locals_ * rest
 
         @pl.when(expert == 0)
         def _():
-            ref[:, locals_ * main :, :] = part
+            view[:, locals_ * main :, :] = part
 
         @pl.when(expert > 0)
         def _():
-            ref[:, locals_ * main :, :] = ref[:, locals_ * main :, :] + part
+            view[:, locals_ * main :, :] = view[:, locals_ * main :, :] + part
+
+
+def group_views(place_ref, ref, tensors, chunks):
+    size = ref.shape[1] // chunks
+    return [ref.at[place_ref[2] ^ j, k * size : (k + 1) * size] for k in range(chunks) for j in range(tensors)]
 
 
 def join_halves(place_ref, own_in, peer_in, own_out, peer_out, win, wout):
@@ -368,23 +428,22 @@
     wout[:, pl.ds(other, half_out)] = peer_out[0]
 
 
-def expert_kernel(groups, main, locals_, rest, place_ref, *refs):
-    take = lambda n: [refs_iter.pop(0) for _ in range(n)]
-    refs_iter = list(refs)
-    mains = groups if main else 0
-    x_main, x_rest = take(mains), take(groups)
-    g_main, g_rest = take(mains), take(groups)
+def expert_kernel(chunks, tensors, main, locals_, rest, place_ref, *refs):
+    refs = list(refs)
+    take = lambda n: [refs.pop(0) for _ in range(n)]
+    xs = take(chunks * tensors)
+    (g_ref,) = take(1)
     own_in, peer_in, own_out, peer_out, router = take(5)
-    back_refs = take(groups)
+    back_refs = take(chunks * tensors)
     x_ref, ge_ref, hid_ref, gi_ref, gl_ref = take(5)
     win, wout, grows, inner, gunits, gate_s, dots, back = take(8)
     expert = pl.program_id(0)
-    blocks = sum(ref.shape[0] for ref in x_rest)
+    blocks = sum(ref.shape[0] for ref in xs)
     main_rows = blocks * main
     rows, width = x_ref.shape[1:]
     choice = rest_choice(blocks, locals_, rest, expert)
-    pick_rows(x_ref.at[0], x_main, x_rest, choice, main_rows)
-    pick_rows(grows, g_main, g_rest, choice, main_rows)
+    pick_rows(x_ref.at[0], xs, choice, main_rows, main, expert)
+    pick_rows(grows, group_views(place_ref, g_ref, tensors, chunks), choice, main_rows, main, expert)
     join_halves(place_ref, own_in, peer_in, own_out, peer_out, win, wout)
     inner[...] = dot(x_ref[0], win[...])
     gunits[...] = dot(grows[...], wout[...], ROWS_NT)
@@ -393,7 +452,7 @@
     mine = lanes == place_ref[1] * locals_ + expert
     picked = jnp.sum(jnp.where(mine, probs, 0.0), axis=-1, keepdims=True)
     gate_s[...] = picked
-    chunk = 64
+    chunk = 16
 
     def body(step, _):
         at = pl.ds(pl.multiple_of(step * chunk, chunk), chunk)
@@ -418,34 +477,21 @@
     put_rows(back_refs, back, choice, main_rows, main, locals_, rest, expert)
 
 
-def group_specs(arrays, main, locals_, rest):
-    mains, rests = [], []
-    for array in arrays:
-        blocks, _, width = array.shape
-        if main:
-            mains.append(pl.BlockSpec((blocks, main, width), lambda e, *_: (0, e, 0)))
-        at = locals_ * main // (locals_ * rest)
-        rests.append(pl.BlockSpec((blocks, locals_ * rest, width), lambda e, *_, at=at: (0, at, 0)))
-    return mains, rests
-
-
-def expert_forward_back(places, xs, gs, own_in, peer_in, own_out, peer_out, router, main, rest):
+def expert_forward_back(places, xs, gs, own_in, peer_in, own_out, peer_out, router, main, rest, chunks):
     locals_, half, wide = own_in.shape
     width, experts = router.shape
-    groups = len(xs)
     blocks = sum(x.shape[0] for x in xs)
     rows = blocks * (main + rest)
-    mains, rests = group_specs(xs, main, locals_, rest)
     per = lambda *shape: pl.BlockSpec((1,) + shape, lambda e, *_: (e, 0, 0))
-    repeated = list(xs) if main else []
     saved = jax.ShapeDtypeStruct((locals_, rows, width), BF16)
     saved_wide = jax.ShapeDtypeStruct((locals_, rows, wide), BF16)
     result = pl.pallas_call(
-        functools.partial(expert_kernel, groups, main, locals_, rest),
+        functools.partial(expert_kernel, chunks, len(xs) // chunks, main, locals_, rest),
         grid_spec=pltpu.PrefetchScalarGridSpec(
             num_scalar_prefetch=1,
             grid=(locals_,),
-            in_specs=mains + rests + mains + rests
+            in_specs=[whole(x.shape) for x in xs]
+            + [whole(gs.shape)]
             + [per(half, wide)] * 2 + [per(wide, half)] * 2 + [whole((width, experts))],
             out_specs=[whole(x.shape) for x in xs]
             + [per(rows, width), per(rows, width), per(rows, wide), per(rows, wide), per(rows, experts)],
@@ -465,15 +511,18 @@
         compiler_params=params(),
         cost_estimate=cost(6 * locals_ * rows * width * wide, locals_ * rows * width * 14, locals_ * rows * wide),
         name="experts",
-    )(places, *repeated, *xs, *(list(gs) if main else []), *gs, own_in, peer_in, own_out, peer_out, router)
-    return result[:groups], result[groups:]
-
-
-def expert_weights_kernel(groups, main, locals_, rest, place_ref, x_ref, ge_ref, hid_ref, gi_ref, gl_ref, own_out, peer_out, *refs):
-    forward_refs = refs[:groups]
-    in_own, in_send, out_own, out_send, router_ref, wout, value = refs[groups:]
+    )(places, *xs, gs, own_in, peer_in, own_out, peer_out, router)
+    return result[: len(xs)], result[len(xs) :]
+
+
+def expert_weights_kernel(
+    chunks, main, locals_, rest, place_ref, x_ref, ge_ref, hid_ref, gi_ref, gl_ref, own_out, peer_out, *refs
+):
+    forward_ref, in_own, in_send, out_own, out_send, router_ref, wout, value = refs
     expert = pl.program_id(0)
-    blocks = sum(ref.shape[0] for ref in forward_refs)
+    tensors = forward_ref.shape[0]
+    blocks = tensors * forward_ref.shape[1]
+    forward_refs = group_views(place_ref, forward_ref, tensors, chunks)
     choice = rest_choice(blocks, locals_, rest, expert)
     join_halves(place_ref, own_out, peer_out, own_out, peer_out, None, wout)
     value[...] = dot(hid_ref[0], wout[...]).astype(BF16)
@@ -493,26 +542,25 @@
     router_ref[...] += dot(x_ref[0], gl_ref[0], ROWS_TN)
 
 
-def expert_weights(places, saved, own_out, peer_out, shapes, main, rest):
+def expert_weights(places, saved, own_out, peer_out, shape, main, rest, chunks):
     x, ge, hidden, gi, gl = saved
     locals_, rows, width = x.shape
     wide = hidden.shape[2]
     experts = gl.shape[2]
     half = own_out.shape[2]
-    groups = len(shapes)
     per = lambda *shape: pl.BlockSpec((1,) + shape, lambda e, *_: (e, 0, 0))
     result = pl.pallas_call(
-        functools.partial(expert_weights_kernel, groups, main, locals_, rest),
+        functools.partial(expert_weights_kernel, chunks, main, locals_, rest),
         grid_spec=pltpu.PrefetchScalarGridSpec(
             num_scalar_prefetch=1,
             grid=(locals_,),
             in_specs=[per(rows, width), per(rows, width), per(rows, wide), per(rows, wide), per(rows, experts)]
             + [per(wide, half)] * 2,
-            out_specs=[whole(s) for s in shapes]
+            out_specs=[whole(shape)]
             + [per(half, wide), per(half, wide), per(wide, half), per(wide, half), whole((width, experts))],
             scratch_shapes=[pltpu.VMEM((wide, width), BF16), pltpu.VMEM((rows, width), BF16)],
         ),
-        out_shape=[jax.ShapeDtypeStruct(s, BF16) for s in shapes]
+        out_shape=[jax.ShapeDtypeStruct(shape, BF16)]
         + [
             jax.ShapeDtypeStruct((locals_, half, wide), F32),
             jax.ShapeDtypeStruct((locals_, half, wide), BF16),
@@ -524,14 +572,24 @@
         cost_estimate=cost(6 * locals_ * rows * width * wide, locals_ * rows * width * 14),
         name="expert_weights",
     )(places, x, ge, hidden, gi, gl, own_out, peer_out)
-    return result[:groups], result[groups:]
-
-
-def hidden_back_kernel(target_ref, back_ref, hidden_ref, cot_ref, gain_ref, grad_ref, attn_ref, gain_out):
-    count = back_ref.shape[0]
-    cols = lax.broadcasted_iota(jnp.int32, (target_ref.shape[0], count), 1)
-    chosen = jnp.where(cols == target_ref[...], 1.0, 0.0).astype(BF16)
-    grad_in = dot(chosen, back_ref[...])
+    return result[0], result[1:]
+
+
+def take_rows(target_ref, refs):
+    total, at = None, 0
+    for ref in refs:
+        count = ref.shape[0]
+        cols = lax.broadcasted_iota(jnp.int32, (target_ref.shape[0], count), 1) + at
+        chosen = jnp.where(cols == target_ref[...], 1.0, 0.0).astype(BF16)
+        part = dot(chosen, ref[...])
+        total = part if total is None else total + part
+        at += count
+    return total
+
+
+def hidden_back_kernel(target_ref, *refs):
+    hidden_ref, cot_ref, gain_ref, grad_ref, attn_ref, gain_out = refs[-6:]
+    grad_in = take_rows(target_ref, refs[:-6])
     unit, scale = unit_rows(hidden_ref[...])
     gain_out[...] = jnp.sum(grad_in * unit, axis=0, keepdims=True)
     scaled = grad_in * gain_ref[...]
@@ -551,16 +609,14 @@
             jax.ShapeDtypeStruct((1, width), F32),
         ],
         compiler_params=params(),
-        cost_estimate=cost(2 * back.shape[0] * rows * width, 16 * rows * width),
+        cost_estimate=cost(3 * rows * rows * width, 16 * rows * width),
         name="hidden_back",
-    )(target_col, back, hidden, cotangent, gain)
-
-
-def output_kernel(target_ref, rows_ref, hidden_ref, gate_ref, out_ref):
-    count = rows_ref.shape[0]
-    cols = lax.broadcasted_iota(jnp.int32, (target_ref.shape[0], count), 1)
-    chosen = jnp.where(cols == target_ref[...], 1.0, 0.0).astype(BF16)
-    out_ref[...] = (hidden_ref[...] + gate_ref[...] * dot(chosen, rows_ref[...])).astype(BF16)
+    )(target_col, *back, hidden, cotangent, gain)
+
+
+def output_kernel(target_ref, *refs):
+    hidden_ref, gate_ref, out_ref = refs[-3:]
+    out_ref[...] = (hidden_ref[...] + gate_ref[...] * take_rows(target_ref, refs[:-3])).astype(BF16)
 
 
 def output_rows(target_col, expert_rows, hidden, gate):
@@ -568,14 +624,15 @@
         output_kernel,
         out_shape=jax.ShapeDtypeStruct(hidden.shape, BF16),
         compiler_params=params(),
-        cost_estimate=cost(2 * expert_rows.shape[0] * hidden.size, 10 * hidden.size),
+        cost_estimate=cost(3 * hidden.shape[0] * hidden.size, 10 * hidden.size),
         name="output_rows",
-    )(target_col, expert_rows, hidden, gate)
-
-
-def tokens_back_kernel(tok_ref, normed_ref, gain_ref, hidden_ref, out_ref):
+    )(target_col, *expert_rows, hidden, gate)
+
+
+def tokens_back_kernel(tok_ref, *refs):
+    gain_ref, hidden_ref, out_ref = refs[-3:]
     unit, scale = unit_rows(tok_ref[...].astype(F32))
-    scaled = normed_ref[...].astype(F32) * gain_ref[...]
+    scaled = sum_pieces(refs[:-3]) * gain_ref[...]
     inside = jnp.mean(unit * scaled, axis=-1, keepdims=True)
     out_ref[...] = hidden_ref[...] + scale * (scaled - unit * inside)
 
@@ -587,7 +644,7 @@
         compiler_params=params(),
         cost_estimate=cost(10 * tokens.size, 12 * tokens.size),
         name="tokens_back",
-    )(tokens, grad_normed, gain, grad_hidden)
+    )(tokens, *grad_normed, gain, grad_hidden)
 
 
 def shifted(value, axis, count, step):
@@ -600,17 +657,16 @@
     return jnp.roll(jnp.stack(parts), me, axis=0)
 
 
-def send_chunks(chunks, axis, count):
-    return [chunks[0]] + [shifted(chunks[k], axis, count, k) for k in range(1, count)]
-
-
-def return_chunks(chunks, axis, count):
-    return [chunks[0]] + [shifted(chunks[k], axis, count, -k) for k in range(1, count)]
-
-
-def grouped(count):
-    bounds = [count * i // GROUPS for i in range(GROUPS + 1)]
-    return [range(a, b) for a, b in zip(bounds[:-1], bounds[1:]) if b > a]
+def swapped(value, axis, count, bits):
+    return lax.ppermute(value, axis, [(s, s ^ bits) for s in range(count)])
+
+
+def gather_pieces(value, axis, count):
+    return [value] + [swapped(value, axis, count, k) for k in range(1, count)]
+
+
+def swap_pieces(pieces, axis, count):
+    return [pieces[0]] + [swapped(pieces[k], axis, count, k) for k in range(1, count)]
 
 
 def on_device(
@@ -645,11 +701,14 @@
     my_z = lax.axis_index("expert")
     bias = rel_bias.astype(F32)
 
-    group_tokens = lax.all_gather(tokens, "tensor", axis=0, tiled=True)
+    my_t = lax.axis_index("tensor")
+    places = jnp.stack([my_dp, my_z, my_t]).astype(jnp.int32)
+    token_pieces = gather_pieces(tokens, "tensor", t_count)
 
     small = jnp.concatenate([gain_attn[:, None], gain_moe[:, None], w_router], axis=1)
-    small = gather_ring(small, "tensor", t_count).reshape(-1)
-    extra = -(-small.shape[0] // (16 * width)) * 16
+    smalls = gather_ring(small, "tensor", t_count)
+    smalls = gather_ring(smalls, "expert", z_count)
+    smalls = gather_ring(smalls, "dp", dp_count).reshape(width, 2 + experts_all)
     packed = jnp.concatenate(
         [
             query_key_value_weight.transpose(1, 0, 2).reshape(part, 3 * inner),
@@ -657,13 +716,8 @@
         ],
         axis=1,
     )
-    packed = jnp.concatenate(
-        [packed, jnp.pad(small, (0, extra * width - small.shape[0])).reshape(extra, width)], axis=0
-    )
     packed = gather_ring(packed, "expert", z_count)
-    packed = gather_ring(packed, "dp", dp_count).reshape(dp_count * z_count, part + extra, width)
-    weights = packed[:, :part].reshape(width, 4 * inner)
-    smalls = packed[:, part:].reshape(dp_count * z_count, -1)[:, : small.shape[0]].reshape(width, 2 + experts_all)
+    weights = gather_ring(packed, "dp", dp_count).reshape(width, 4 * inner)
     gain_one = smalls[:, 0].astype(F32)[None]
     gain_two = smalls[:, 1].astype(F32)[None]
     router = smalls[:, 2:]
@@ -676,55 +730,78 @@
     inside = jnp.where(
         slot_index < main, local * main + slot_index, locals_ * main + local * rest + slot_index - main
     )
-    target = lax.rem(z_of - my_z + z_count, z_count) * block + inside
+    target = (z_of ^ my_z) * block + inside
     target = jnp.where(kept_mask > 0, target, -1)
     target_row, target_col = target[None, :], target[:, None]
     count = z_count * block
-    split = grouped(z_count)
-
-    def to_experts(rows):
-        chunks = send_chunks(list(rows.reshape(z_count, block, width)), "expert", z_count)
-        gathered = []
-        for members in split:
-            joined = jnp.concatenate([chunks[k] for k in members], axis=0)
-            full = lax.all_gather(joined, "tensor", axis=0, tiled=True)
-            gathered.append(full.reshape(t_count * len(members), block, width))
-        return gathered
-
-    def from_experts(parts):
-        chunks = [None] * z_count
-        for members, value in zip(split, parts):
-            value = value.reshape(t_count * len(members) * block, width)
-            summed = lax.psum_scatter(value, "tensor", scatter_dimension=0, tiled=True)
-            for place_, k in enumerate(members):
-                chunks[k] = summed[place_ * block : (place_ + 1) * block]
-        return jnp.concatenate(return_chunks(chunks, "expert", z_count), axis=0)
-
-    grad_arrived = to_experts(place(target_row, cotangent, count))
-
-    partial_, projected, mixed, logs = attend(bias, group_tokens, gain_one, weights)
-    attn = lax.psum_scatter(partial_, "tensor", scatter_dimension=0, tiled=True)
+    chunks = min(z_count, 4)
+    many = z_count // chunks
+
+    def over_expert(rows):
+        pieces = swap_pieces(list(rows.reshape(z_count, block, width)), "expert", z_count)
+        if many == 1:
+            return pieces
+        return [jnp.concatenate(pieces[k * many : (k + 1) * many], axis=0) for k in range(chunks)]
+
+    def back_over_expert(groups):
+        if many > 1:
+            groups = [g[i * block : (i + 1) * block] for g in groups for i in range(many)]
+        pieces = swap_pieces(groups, "expert", z_count)
+        if many == 1:
+            return pieces
+        return [jnp.concatenate(pieces[k * many : (k + 1) * many], axis=0) for k in range(chunks)]
+
+    grad_rows = jnp.concatenate(over_expert(place(target_row, cotangent, count)), axis=0)
+    grad_arrived = lax.all_gather(grad_rows, "tensor", axis=0).reshape(t_count, z_count, block, width)
+
+    parts, (group_tokens, projected, mixed, logs) = attend(places, bias, token_pieces, gain_one, weights)
+    attn = swap_pieces(parts, "tensor", t_count)
     hidden_one, sent, gate = route(
         tokens, attn, gain_two, router, target_row, expert_index[:, None], kept_mask[:, None], count
     )
-    arrived = to_experts(sent)
-    places = jnp.stack([my_dp, my_z]).astype(jnp.int32)
+    arrived = [
+        piece.reshape(many, block, width)
+        for group in over_expert(sent)
+        for piece in gather_pieces(group, "tensor", t_count)
+    ]
     back_parts, saved = expert_forward_back(
-        places, arrived, grad_arrived, w_in, peer_in, w_out, peer_out, router, main, rest
-    )
-    grad_back = from_experts(back_parts)
-    forward_parts, (in_own, in_send, out_own, out_send, router_part) = expert_weights(
-        places, saved, w_out, peer_out, [x.shape for x in arrived], main, rest
-    )
+        places, arrived, grad_arrived, w_in, peer_in, w_out, peer_out, router, main, rest, chunks
+    )
+    back_swapped = [
+        swap_pieces(
+            [piece.reshape(many * block, width) for piece in back_parts[k * t_count : (k + 1) * t_count]],
+            "tensor",
+            t_count,
+        )
+        for k in range(chunks)
+    ]
+    forward_part, (in_own, in_send, out_own, out_send, router_part) = expert_weights(
+        places, saved, w_out, peer_out, grad_arrived.shape, main, rest, chunks
+    )
+    back_swapped, forward_part, in_send, out_send = lax.optimization_barrier(
+        (back_swapped, forward_part, in_send, out_send)
+    )
+
+    def summed(pieces):
+        total = pieces[0].astype(F32)
+        for piece in pieces[1:]:
+            total = total + piece.astype(F32)
+        return total.astype(BF16)
+
+    grad_back = back_over_expert([summed(pieces) for pieces in back_swapped])
     grad_w_in = in_own + shifted(in_send, "dp", dp_count, 1).astype(F32)
     grad_w_out = out_own + shifted(out_send, "dp", dp_count, 1).astype(F32)
     grad_hidden, grad_attn, gain_two_part = hidden_back(target_col, grad_back, hidden_one, cotangent, gain_two)
-    group_grad = lax.all_gather(grad_attn, "tensor", axis=0, tiled=True)
-    grad_normed_part, weight_part, bucket_part, gain_one_part = attend_back(
-        bias, group_tokens, gain_one, weights, projected, mixed, logs, group_grad
-    )
-    grad_normed = lax.psum_scatter(grad_normed_part, "tensor", scatter_dimension=0, tiled=True)
-    output = output_rows(target_col, from_experts(forward_parts), hidden_one, gate)
+    normed_parts, (weight_part, bucket_part, gain_one_part) = attend_back(
+        places, bias, group_tokens, gain_one, weights, projected, mixed, logs,
+        gather_pieces(grad_attn, "tensor", t_count),
+    )
+    grad_normed = swap_pieces(normed_parts, "tensor", t_count)
+    forward_sum = lax.psum_scatter(
+        forward_part.reshape(t_count * z_count * block, width), "tensor", scatter_dimension=0, tiled=True
+    )
+    forward_rows = back_over_expert(list(forward_sum.reshape(chunks, many * block, width)))
+    output = output_rows(target_col, forward_rows, hidden_one, gate)
     grad_tokens = tokens_back(tokens, grad_normed, gain_one, grad_hidden)
 
     owners = dp_count * z_count
@@ -743,11 +820,9 @@
     payload = payload.reshape(dp_count, z_count, part + extra, width)
     own = lax.dynamic_index_in_dim(payload, my_dp, 0, keepdims=False)
     other = lax.dynamic_index_in_dim(payload, 1 - my_dp, 0, keepdims=False)
-    summed = own + shifted(other.astype(BF16), "dp", dp_count, 1).astype(F32)
-    turned = jnp.roll(summed, -my_z, axis=0)
-    pieces = send_chunks(
-        [turned[0]] + [turned[k].astype(BF16) for k in range(1, z_count)], "expert", z_count
-    )
+    summed_half = own + shifted(other.astype(BF16), "dp", dp_count, 1).astype(F32)
+    turned = [lax.dynamic_index_in_dim(summed_half, my_z ^ k, 0, keepdims=False) for k in range(z_count)]
+    pieces = swap_pieces([turned[0]] + [t.astype(BF16) for t in turned[1:]], "expert", z_count)
     total = pieces[0]
     for piece in pieces[1:]:
         total = total + piece.astype(F32)
@@ -765,9 +840,9 @@
         ],
         axis=1,
     )
-    turned = jnp.roll(rows_left, -lax.axis_index("tensor"), axis=0)
+    turned = [lax.dynamic_index_in_dim(rows_left, my_t ^ k, 0, keepdims=False) for k in range(t_count)]
     left = turned[0]
-    for piece in send_chunks([turned[k] for k in range(t_count)], "tensor", t_count)[1:]:
+    for piece in swap_pieces(turned, "tensor", t_count)[1:]:
         left = left + piece
     grad_gain_attn = left[:fine]
     grad_gain_moe = left[fine : 2 * fine]

time: 459 us -> 484 us (1.054)
  waiting for transfers between devices: 240 us -> 188 us
  starting transfers between devices: 49.6 us -> 91.3 us
  Pallas kernels: 110 us -> 129 us
  local copies, waits for them, and re-layouts: 22.1 us -> 28.4 us
  other arithmetic: 21.3 us -> 27.5 us
    ppermute x0 -> x54, waiting for transfers between devices: none -> 174 us  [swapped(): return lax.ppermute(value, axis, [(s, s ^ bits) for s in range(count)])]
    all_gather x4 -> x1, waiting for transfers between devices: 85.1 us -> 0.02 us  [on_device(): lax.all_gather(grad_rows, 'tensor', axis=0)]
    ppermute x0 -> x54, starting transfers between devices: none -> 73.8 us  [swapped(): return lax.ppermute(value, axis, [(s, s ^ bits) for s in range(count)])]
    reduce_scatter x4 -> x1, waiting for transfers between devices: 72.8 us -> 0.01 us  [on_device(): lax.psum_scatter(forward_part.reshape(t_count * z_count * block, width),...]
    ppermute x30 -> x16, waiting for transfers between devices: 82.2 us -> 14.3 us  [shifted(): lax.ppermute(value, axis, [(s, (s + step) % count) for s in range(count)])]
    ppermute x30 -> x16, starting transfers between devices: 48.9 us -> 17.4 us  [shifted(): lax.ppermute(value, axis, [(s, (s + step) % count) for s in range(count)])]
    pallas_call x5, Pallas kernels: 97.2 us -> 115 us  [the longest x1 46.4 us: expert_forward_back(): pl.pallas_call(functools.partial(expert_kernel, chunks, len(xs) // chunks...]
    unnamed x42 -> x106, local copies, waits for them, and re-layouts: 5.36 us -> 11.4 us
  transfers between devices with their start and end apart: 38 -> 72, of which waited for: 20 -> 27; matrix products, arithmetic and copies ran while one was open for 8% -> 10% of each run, Pallas kernels for 12% -> 17%
where the time goes in v2:
time: 484 us; the launch traced here: 479 us
  waiting for transfers between devices  188 us (39%)
  Pallas kernels  129 us (27%)
  starting transfers between devices  91.3 us (19%)
  local copies, waits for them, and re-layouts  28.4 us (6%)
  other arithmetic  27.5 us (6%)
  between operations  15 us (3%)
    ppermute x54, waiting for transfers between devices, swapped(): return lax.ppermute(value, axis, [(s, s ^ bits) for s in range(count)])  174 us
    ppermute x54, starting transfers between devices, swapped(): return lax.ppermute(value, axis, [(s, s ^ bits) for s in range(count)])  73.8 us
    pallas_call x1, Pallas kernels, expert_forward_back(): pl.pallas_call(functools.partial(expert_kernel, chunks, len(xs) // chunks...  46.4 us
    pallas_call x1, Pallas kernels, expert_weights(): pl.pallas_call(functools.partial(expert_weights_kernel, chunks, main, loc...  24.3 us
    pallas_call x1, Pallas kernels, attend_back(): pl.pallas_call(functools.partial(attend_back_kernel, heads, tensors), gri...  24.2 us
    ppermute x16, starting transfers between devices, shifted(): lax.ppermute(value, axis, [(s, (s + step) % count) for s in range(count)])  17.4 us
    pallas_call x1, Pallas kernels, attend(): pl.pallas_call(functools.partial(attend_kernel, heads, tensors), grid_spe...  15.5 us
    ppermute x16, waiting for transfers between devices, shifted(): lax.ppermute(value, axis, [(s, (s + step) % count) for s in range(count)])  14.3 us
  transfers between devices with their start and end apart: 72, of which 27 were waited for; matrix products, arithmetic and copies ran while one was open for 10% of the time, Pallas kernels for 17%

profile of v2, /device:TPU:0, one launch (start us, length us, event | category | flops | bytes accessed | tf_op | source)
XLA Modules:
  0.0 479.4 jit_solution(6603838361186410349)
XLA Ops:
  9.1 5.1 %collective-permute-start.10 = (bf16[96,768]{0,1:T(8,128)(2,1)S(1)}, bf16[96,768]{0,1:T(8,128)(2,1)S(1)}, u32[]{:S(2)}, u32[]{:S(2)}) collective-permute-start(bf16[96,768]{0,1:T(8,128)(2,1)S(1)} %pad_maximum_fusion.1), channel_id=1, source_target_pairs={{0,12},{4,0},{8,4},{12,8},{1,13},{5,1},{9,5},{13,9},{2,14},{6,2},{... | collective-permute-start | bytes 442376 | tf_op jit(solution)/shard_map/ppermute | solution.py:651
  32.1 5.5 %collective-permute-done.6 = bf16[4,24,18]{1,2,0:T(8,128)(2,1)S(1)} collective-permute-done((bf16[4,24,18]{1,2,0:T(8,128)(2,1)S(1)}, bf16[4,24,18]{1,2,0:T(8,128)(2,1)S(1)}, u32[]{:S(2)}, u32[]{:S(2)}) %collective-permute-start.6) | collective-permute-done | bytes 3488 | tf_op jit(solution)/shard_map/ppermute | solution.py:651
  42.5 5.4 %collective-permute-done.8 = bf16[4,24,18]{1,2,0:T(8,128)(2,1)S(1)} collective-permute-done((bf16[4,24,18]{1,2,0:T(8,128)(2,1)S(1)}, bf16[4,24,18]{1,2,0:T(8,128)(2,1)S(1)}, u32[]{:S(2)}, u32[]{:S(2)}) %collective-permute-start.8) | collective-permute-done | bytes 3488 | tf_op jit(solution)/shard_map/ppermute | solution.py:651
  73.0 12.3 %collective-permute-done.1.refs_2_ = bf16[384,768]{1,0:T(8,128)(2,1)} collective-permute-done((bf16[384,768]{1,0:T(8,128)(2,1)S(1)}, bf16[384,768]{1,0:T(8,128)(2,1)}, u32[]{:S(2)}, u32[]{:S(2)}) %collective-permute-start.1) | collective-permute-done | bytes 589856 | tf_op jit(solution)/shard_map/ppermute | solution.py:661
  86.1 15.5 %attend.1 = (bf16[384,768]{1,0:T(8,128)(2,1)}, bf16[384,768]{1,0:T(8,128)(2,1)}, bf16[384,768]{1,0:T(8,128)(2,1)}, bf16[384,768]{1,0:T(8,128)(2,1)}, bf16[1536,7...) custom-call(s32[3]{0:T(128)} %pad_add_fusion.place_ref, ...), custom_call_target="tpu_custom_call" | custom-call | flops 2415919104 | bytes 9437184 | tf_op jit(solution)/shard_map/attend/pallas_call | solution.py:144
  110.3 19.9 %collective-permute-done.14.refs_1_ = bf16[384,768]{1,0:T(8,128)(2,1)S(1)} collective-permute-done((bf16[384,768]{1,0:T(8,128)(2,1)}, bf16[384,768]{1,0:T(8,128)(2,1)S(1)}, u32[]{:S(2)}, u32[]{:S(2)}) %collective-permute-start.14) | collective-permute-done | bytes 589856 | tf_op jit(solution)/shard_map/ppermute | solution.py:661
  130.2 6.4 %collective-permute-done.15.refs_2_ = bf16[384,768]{1,0:T(8,128)(2,1)S(1)} collective-permute-done((bf16[384,768]{1,0:T(8,128)(2,1)}, bf16[384,768]{1,0:T(8,128)(2,1)S(1)}, u32[]{:S(2)}, u32[]{:S(2)}) %collective-permute-start.15) | collective-permute-done | bytes 589856 | tf_op jit(solution)/shard_map/ppermute | solution.py:661
  150.6 6.2 %collective-permute-done.20 = bf16[144,768]{1,0:T(8,128)(2,1)S(1)} collective-permute-done((bf16[144,768]{1,0:T(8,128)(2,1)S(1)}, bf16[144,768]{1,0:T(8,128)(2,1)S(1)}, u32[]{:S(2)}, u32[]{:S(2)}) %collective-permute-start.20) | collective-permute-done | bytes 221216 | tf_op jit(solution)/shard_map/ppermute | solution.py:661
  157.6 5.8 %collective-permute-done.24 = bf16[144,768]{1,0:T(8,128)(2,1)S(1)} collective-permute-done((bf16[144,768]{1,0:T(8,128)(2,1)S(1)}, bf16[144,768]{1,0:T(8,128)(2,1)S(1)}, u32[]{:S(2)}, u32[]{:S(2)}) %collective-permute-start.24) | collective-permute-done | bytes 221216 | tf_op jit(solution)/shard_map/ppermute | solution.py:661
  166.9 6.5 %collective-permute-done.18 = bf16[144,768]{1,0:T(8,128)(2,1)S(1)} collective-permute-done((bf16[144,768]{1,0:T(8,128)(2,1)S(1)}, bf16[144,768]{1,0:T(8,128)(2,1)S(1)}, u32[]{:S(2)}, u32[]{:S(2)}) %collective-permute-start.18) | collective-permute-done | bytes 221216 | tf_op jit(solution)/shard_map/ppermute | solution.py:661
  177.0 6.1 %collective-permute-done.22 = bf16[144,768]{1,0:T(8,128)(2,1)S(1)} collective-permute-done((bf16[144,768]{1,0:T(8,128)(2,1)S(1)}, bf16[144,768]{1,0:T(8,128)(2,1)S(1)}, u32[]{:S(2)}, u32[]{:S(2)}) %collective-permute-start.22) | collective-permute-done | bytes 221216 | tf_op jit(solution)/shard_map/ppermute | solution.py:661
  186.6 5.9 %collective-permute-done.26 = bf16[144,768]{1,0:T(8,128)(2,1)S(1)} collective-permute-done((bf16[144,768]{1,0:T(8,128)(2,1)S(1)}, bf16[144,768]{1,0:T(8,128)(2,1)S(1)}, u32[]{:S(2)}, u32[]{:S(2)}) %collective-permute-start.26) | collective-permute-done | bytes 221216 | tf_op jit(solution)/shard_map/ppermute | solution.py:661
  194.9 7.0 %collective-permute-done.30 = bf16[144,768]{1,0:T(8,128)(2,1)S(1)} collective-permute-done((bf16[144,768]{1,0:T(8,128)(2,1)S(1)}, bf16[144,768]{1,0:T(8,128)(2,1)S(1)}, u32[]{:S(2)}, u32[]{:S(2)}) %collective-permute-start.30) | collective-permute-done | bytes 221216 | tf_op jit(solution)/shard_map/ppermute | solution.py:661
  202.7 46.4 %experts.1 = (bf16[1,144,768]{2,1,0:T(8,128)(2,1)}, bf16[1,144,768]{2,1,0:T(8,128)(2,1)}, bf16[1,144,768]{2,1,0:T(8,128)(2,1)}, bf16[1,144,768]{2,1,0:T(8,128)(2...) custom-call(s32[3]{0:T(128)} %pad_add_fusion.place_ref, ...), custom_call_target="tpu_custom_call" | custom-call | flops 8153726976 | bytes 24772608 | tf_op jit(solution)/shard_map/experts/pallas_call | solution.py:488
  277.1 24.3 %expert_weights.1 = (bf16[4,4,144,768]{3,2,1,0:T(8,128)(2,1)}, f32[4,384,768]{2,1,0:T(8,128)}, bf16[4,384,768]{2,1,0:T(8,128)(2,1)}, f32[4,768,384]{2,1,0:T(8,12...) custom-call(s32[3]{0:T(128)} %pad_add_fusion.place_ref, bf16[4,576,768]{2,1,0:T(8,128)(2,1)} %get-tuple-element.98.x_ref, ...), custom_call_target="tpu_custom_call" | custom-call | flops 8153726976 | bytes 24772608 | tf_op jit(solution)/shard_map/expert_weights/pallas_call | solution.py:552
  311.6 7.8 %collective-permute-done.53.refs_2_ = bf16[144,768]{1,0:T(8,128)(2,1)S(1)} collective-permute-done((bf16[144,768]{1,0:T(8,128)(2,1)S(1)}, bf16[144,768]{1,0:T(8,128)(2,1)S(1)}, u32[]{:S(2)}, u32[]{:S(2)}) %collective-permute-start.53) | collective-permute-done | bytes 221216 | tf_op jit(solution)/shard_map/ppermute | solution.py:661
  329.0 14.3 %collective-permute-done.55.refs_1_ = bf16[384,768]{1,0:T(8,128)(2,1)S(1)} collective-permute-done((bf16[384,768]{1,0:T(8,128)(2,1)}, bf16[384,768]{1,0:T(8,128)(2,1)S(1)}, u32[]{:S(2)}, u32[]{:S(2)}) %collective-permute-start.55) | collective-permute-done | bytes 589856 | tf_op jit(solution)/shard_map/ppermute | solution.py:661
  343.3 21.8 %collective-permute-done.57.refs_3_ = bf16[384,768]{1,0:T(8,128)(2,1)S(1)} collective-permute-done((bf16[384,768]{1,0:T(8,128)(2,1)}, bf16[384,768]{1,0:T(8,128)(2,1)S(1)}, u32[]{:S(2)}, u32[]{:S(2)}) %collective-permute-start.57) | collective-permute-done | bytes 589856 | tf_op jit(solution)/shard_map/ppermute | solution.py:661
  365.9 24.2 %attend_back.1 = (bf16[384,768]{1,0:T(8,128)(2,1)}, bf16[384,768]{1,0:T(8,128)(2,1)}, bf16[384,768]{1,0:T(8,128)(2,1)}, bf16[384,768]{1,0:T(8,128)(2,1)}, f32[76...) custom-call(s32[3]{0:T(128)} %pad_add_fusion.place_ref, f32[3,32]{1,0:T(4,128)} %convert_element_type.133.bias_ref, ...), custom_call_target="tpu_custom_call" | custom-call | flops 5586812928 | bytes 14155776 | tf_op jit(solution)/shard_map/attend_back/pallas_call | solution.py:264
  400.9 10.0 %collective-permute-done.58.refs_1_ = bf16[384,768]{1,0:T(8,128)(2,1)} collective-permute-done((bf16[384,768]{1,0:T(8,128)(2,1)}, bf16[384,768]{1,0:T(8,128)(2,1)}, u32[]{:S(2)}, u32[]{:S(2)}) %collective-permute-start.58) | collective-permute-done | bytes 589856 | tf_op jit(solution)/shard_map/ppermute | solution.py:661
  413.3 10.1 %collective-permute-done.59.refs_2_ = bf16[384,768]{1,0:T(8,128)(2,1)} collective-permute-done((bf16[384,768]{1,0:T(8,128)(2,1)}, bf16[384,768]{1,0:T(8,128)(2,1)}, u32[]{:S(2)}, u32[]{:S(2)}) %collective-permute-start.59) | collective-permute-done | bytes 589856 | tf_op jit(solution)/shard_map/ppermute | solution.py:661
  440.2 5.7 %convert_add_fusion = f32[4,768,384]{2,1,0:T(8,128)} fusion(f32[4,768,384]{2,1,0:T(8,128)} %get-tuple-element.142, bf16[4,768,384]{2,1,0:T(8,128)(2,1)} %collective-permute-done.69), kind=kLoop, calls=%fused_computation | loop fusion | flops 2359296 | bytes 11796480 | tf_op jit(solution)/shard_map/add | solution.py:793
  453.3 5.0 %convert_add_fusion.1 = f32[4,384,768]{2,1,0:T(8,128)} fusion(f32[4,384,768]{2,1,0:T(8,128)} %get-tuple-element.140, bf16[4,384,768]{2,1,0:T(8,128)(2,1)S(1)} %collective-permute-done.68), kind=kLoop, calls=%fused_computation.1 | loop fusion | flops 2359296 | bytes 11796480 | tf_op jit(solution)/shard_map/add | solution.py:792
  458.3 9.9 %collective-permute-done.50.refs_2_ = bf16[144,768]{1,0:T(8,128)(2,1)S(1)} collective-permute-done((bf16[144,768]{1,0:T(8,128)(2,1)S(1)}, bf16[144,768]{1,0:T(8,128)(2,1)S(1)}, u32[]{:S(2)}, u32[]{:S(2)}) %collective-permute-start.50) | collective-permute-done | bytes 221216 | tf_op jit(solution)/shard_map/ppermute | solution.py:661
  (306 shorter events, 177.2 us)
Async XLA Ops:
  7.2 194.8 %all-gather.3.cloned.1.call-start = ((), (), s32[]{:S(2)}) async-start(), calls=%async_computation.2 | async-start | bytes 4423680 | tf_op jit(solution)/shard_map/all_gather | solution.py:755
  9.1 48.8 %collective-permute-start.10 = (bf16[96,768]{0,1:T(8,128)(2,1)S(1)}, bf16[96,768]{0,1:T(8,128)(2,1)S(1)}, u32[]{:S(2)}, u32[]{:S(2)}) collective-permute-start(bf16[96,768]{0,1:T(8,128)(2,1)S(1)} %pad_maximum_fusion.1), channel_id=1, source_target_pairs={{0,12},{4,0},{8,4},{12,8},{1,13},{5,1},{9,5},{13,9},{2,14},{6,2},{... | collective-permute-start | bytes 442376 | tf_op jit(solution)/shard_map/ppermute | solution.py:651
  14.2 47.2 %collective-permute-start.11 = (bf16[96,768]{0,1:T(8,128)(2,1)S(1)}, bf16[96,768]{0,1:T(8,128)(2,1)S(1)}, u32[]{:S(2)}, u32[]{:S(2)}) collective-permute-start(bf16[96,768]{0,1:T(8,128)(2,1)S(1)} %pad_maximum_fusion.1), channel_id=1, source_target_pairs={{0,8},{4,12},{8,0},{12,4},{1,9},{5,13},{9,1},{13,5},{2,10},{6,14},... | collective-permute-start | bytes 442376 | tf_op jit(solution)/shard_map/ppermute | solution.py:651
  26.2 22.5 %collective-permute-start.32 = (bf16[144,768]{1,0:T(8,128)(2,1)S(1)}, bf16[144,768]{1,0:T(8,128)(2,1)S(1)}, u32[]{:S(2)}, u32[]{:S(2)}) collective-permute-start(bf16[144,768]{1,0:T(8,128)(2,1)S(1)} %get-tuple-element.198), channel_id=1, source_target_pairs={{0,4},{4,0},{8,12},{12,8},{1,5},{5,1},{9,13},{13,9},{2,6},{6,2},{1... | collective-permute-start | bytes 663560 | tf_op jit(solution)/shard_map/ppermute | solution.py:661
  27.3 24.4 %collective-permute-start.33 = (bf16[144,768]{1,0:T(8,128)(2,1)S(1)}, bf16[144,768]{1,0:T(8,128)(2,1)S(1)}, u32[]{:S(2)}, u32[]{:S(2)}) collective-permute-start(bf16[144,768]{1,0:T(8,128)(2,1)S(1)} %get-tuple-element.197), channel_id=1, source_target_pairs={{0,8},{4,12},{8,0},{12,4},{1,9},{5,13},{9,1},{13,5},{2,10},{6,14},... | collective-permute-start | bytes 663560 | tf_op jit(solution)/shard_map/ppermute | solution.py:661
  55.7 29.6 %collective-permute-start.1 = (bf16[384,768]{1,0:T(8,128)(2,1)S(1)}, bf16[384,768]{1,0:T(8,128)(2,1)}, u32[]{:S(2)}, u32[]{:S(2)}) collective-permute-start(bf16[384,768]{1,0:T(8,128)(2,1)S(1)} %copy-done.2), channel_id=1, source_target_pairs={{0,2},{1,3},{2,0},{3,1},{4,6},{5,7},{6,4},{7,5},{8,10},{9,11},{10,... | collective-permute-start | bytes 1769480 | tf_op jit(solution)/shard_map/ppermute | solution.py:661
  57.9 388.0 %reduce-scatter.2.cloned.1.call-start = ((), (), s32[]{:S(2)}) async-start(), calls=%async_computation.1 | async-start | bytes 4423680 | tf_op jit(solution)/shard_map/reduce_scatter | solution.py:800
  58.0 27.3 %collective-permute-start.2 = (bf16[384,768]{1,0:T(8,128)(2,1)S(1)}, bf16[384,768]{1,0:T(8,128)(2,1)S(1)}, u32[]{:S(2)}, u32[]{:S(2)}) collective-permute-start(bf16[384,768]{1,0:T(8,128)(2,1)S(1)} %copy-done.2), channel_id=1, source_target_pairs={{0,3},{1,2},{2,1},{3,0},{4,7},{5,6},{6,5},{7,4},{8,11},{9,10},{10,... | collective-permute-start | bytes 1769480 | tf_op jit(solution)/shard_map/ppermute | solution.py:661
  69.3 132.7 %collective-permute-start.36 = (bf16[4,768,384]{2,1,0:T(8,128)(2,1)}, bf16[4,768,384]{2,1,0:T(8,128)(2,1)}, u32[]{:S(2)}, u32[]{:S(2)}) collective-permute-start(bf16[4,768,384]{2,1,0:T(8,128)(2,1)} %own_out.1), channel_id=1, source_target_pairs={{0,16},{16,0},{1,17},{17,1},{2,18},{18,2},{3,19},{19,3},{4,20},{20... | collective-permute-start | bytes 7077896 | tf_op jit(solution)/shard_map/ppermute | solution.py:651
  70.8 131.2 %collective-permute-start.35 = (bf16[4,384,768]{2,1,0:T(8,128)(2,1)}, bf16[4,384,768]{2,1,0:T(8,128)(2,1)}, u32[]{:S(2)}, u32[]{:S(2)}) collective-permute-start(bf16[4,384,768]{2,1,0:T(8,128)(2,1)} %refs_17_.1), channel_id=1, source_target_pairs={{0,16},{16,0},{1,17},{17,1},{2,18},{18,2},{3,19},{19,3},{4,20},{20... | collective-permute-start | bytes 7077896 | tf_op jit(solution)/shard_map/ppermute | solution.py:651
  101.6 28.6 %collective-permute-start.14 = (bf16[384,768]{1,0:T(8,128)(2,1)}, bf16[384,768]{1,0:T(8,128)(2,1)S(1)}, u32[]{:S(2)}, u32[]{:S(2)}) collective-permute-start(bf16[384,768]{1,0:T(8,128)(2,1)} %get-tuple-element.78), channel_id=1, source_target_pairs={{0,1},{1,0},{2,3},{3,2},{4,5},{5,4},{6,7},{7,6},{8,9},{9,8},{10,11... | collective-permute-start | bytes 1769480 | tf_op jit(solution)/shard_map/ppermute | solution.py:661
  105.8 30.8 %collective-permute-start.15 = (bf16[384,768]{1,0:T(8,128)(2,1)}, bf16[384,768]{1,0:T(8,128)(2,1)S(1)}, u32[]{:S(2)}, u32[]{:S(2)}) collective-permute-start(bf16[384,768]{1,0:T(8,128)(2,1)} %get-tuple-element.79), channel_id=1, source_target_pairs={{0,2},{1,3},{2,0},{3,1},{4,6},{5,7},{6,4},{7,5},{8,10},{9,11},{10,... | collective-permute-start | bytes 1769480 | tf_op jit(solution)/shard_map/ppermute | solution.py:661
  105.8 30.8 %collective-permute-start.16 = (bf16[384,768]{1,0:T(8,128)(2,1)}, bf16[384,768]{1,0:T(8,128)(2,1)S(1)}, u32[]{:S(2)}, u32[]{:S(2)}) collective-permute-start(bf16[384,768]{1,0:T(8,128)(2,1)} %get-tuple-element.80), channel_id=1, source_target_pairs={{0,3},{1,2},{2,1},{3,0},{4,7},{5,6},{6,5},{7,4},{8,11},{9,10},{10,... | collective-permute-start | bytes 1769480 | tf_op jit(solution)/shard_map/ppermute | solution.py:661
  264.6 36.8 %collective-permute-start.44 = (bf16[144,768]{1,0:T(8,128)(2,1)}, bf16[144,768]{1,0:T(8,128)(2,1)S(1)}, u32[]{:S(2)}, u32[]{:S(2)}) collective-permute-start(bf16[144,768]{1,0:T(8,128)(2,1)} %bitcast.165), channel_id=1, source_target_pairs={{0,2},{1,3},{2,0},{3,1},{4,6},{5,7},{6,4},{7,5},{8,10},{9,11},{10,... | collective-permute-start | bytes 663560 | tf_op jit(solution)/shard_map/ppermute | solution.py:661
  267.2 34.1 %collective-permute-start.45 = (bf16[144,768]{1,0:T(8,128)(2,1)}, bf16[144,768]{1,0:T(8,128)(2,1)S(1)}, u32[]{:S(2)}, u32[]{:S(2)}) collective-permute-start(bf16[144,768]{1,0:T(8,128)(2,1)} %bitcast.164), channel_id=1, source_target_pairs={{0,3},{1,2},{2,1},{3,0},{4,7},{5,6},{6,5},{7,4},{8,11},{9,10},{10,... | collective-permute-start | bytes 663560 | tf_op jit(solution)/shard_map/ppermute | solution.py:661
  272.2 29.2 %collective-permute-start.46 = (bf16[144,768]{1,0:T(8,128)(2,1)}, bf16[144,768]{1,0:T(8,128)(2,1)S(1)}, u32[]{:S(2)}, u32[]{:S(2)}) collective-permute-start(bf16[144,768]{1,0:T(8,128)(2,1)} %bitcast.162), channel_id=1, source_target_pairs={{0,1},{1,0},{2,3},{3,2},{4,5},{5,4},{6,7},{7,6},{8,9},{9,8},{10,11... | collective-permute-start | bytes 663560 | tf_op jit(solution)/shard_map/ppermute | solution.py:661
  274.1 27.3 %collective-permute-start.47 = (bf16[144,768]{1,0:T(8,128)(2,1)}, bf16[144,768]{1,0:T(8,128)(2,1)S(1)}, u32[]{:S(2)}, u32[]{:S(2)}) collective-permute-start(bf16[144,768]{1,0:T(8,128)(2,1)} %bitcast.161), channel_id=1, source_target_pairs={{0,2},{1,3},{2,0},{3,1},{4,6},{5,7},{6,4},{7,5},{8,10},{9,11},{10,... | collective-permute-start | bytes 663560 | tf_op jit(solution)/shard_map/ppermute | solution.py:661
  276.7 24.7 %collective-permute-start.48 = (bf16[144,768]{1,0:T(8,128)(2,1)}, bf16[144,768]{1,0:T(8,128)(2,1)S(1)}, u32[]{:S(2)}, u32[]{:S(2)}) collective-permute-start(bf16[144,768]{1,0:T(8,128)(2,1)} %bitcast.160), channel_id=1, source_target_pairs={{0,3},{1,2},{2,1},{3,0},{4,7},{5,6},{6,5},{7,4},{8,11},{9,10},{10,... | collective-permute-start | bytes 663560 | tf_op jit(solution)/shard_map/ppermute | solution.py:661
  326.3 38.7 %collective-permute-start.57 = (bf16[384,768]{1,0:T(8,128)(2,1)}, bf16[384,768]{1,0:T(8,128)(2,1)S(1)}, u32[]{:S(2)}, u32[]{:S(2)}) collective-permute-start(bf16[384,768]{1,0:T(8,128)(2,1)} %get-tuple-element.129.refs_0_), channel_id=1, source_target_pairs={{0,3},{1,2},{2,1},{3,0},{4,7},{5,6},{6,5},{7,4},{8,11},{9,10},{10,... | collective-permute-start | bytes 1769480 | tf_op jit(solution)/shard_map/ppermute | solution.py:661
  395.0 28.4 %collective-permute-start.59 = (bf16[384,768]{1,0:T(8,128)(2,1)}, bf16[384,768]{1,0:T(8,128)(2,1)}, u32[]{:S(2)}, u32[]{:S(2)}) collective-permute-start(bf16[384,768]{1,0:T(8,128)(2,1)} %get-tuple-element.132), channel_id=1, source_target_pairs={{0,2},{1,3},{2,0},{3,1},{4,6},{5,7},{6,4},{7,5},{8,10},{9,11},{10,... | collective-permute-start | bytes 1769480 | tf_op jit(solution)/shard_map/ppermute | solution.py:661
  395.4 44.8 %collective-permute-start.69 = (bf16[4,768,384]{2,1,0:T(8,128)(2,1)}, bf16[4,768,384]{2,1,0:T(8,128)(2,1)}, u32[]{:S(2)}, u32[]{:S(2)}) collective-permute-start(bf16[4,768,384]{2,1,0:T(8,128)(2,1)} %get-tuple-element.143), channel_id=1, source_target_pairs={{0,16},{16,0},{1,17},{17,1},{2,18},{18,2},{3,19},{19,3},{4,20},{20... | collective-permute-start | bytes 7077896 | tf_op jit(solution)/shard_map/ppermute | solution.py:651
  395.4 31.3 %collective-permute-start.60 = (bf16[384,768]{1,0:T(8,128)(2,1)}, bf16[384,768]{1,0:T(8,128)(2,1)}, u32[]{:S(2)}, u32[]{:S(2)}) collective-permute-start(bf16[384,768]{1,0:T(8,128)(2,1)} %get-tuple-element.133), channel_id=1, source_target_pairs={{0,3},{1,2},{2,1},{3,0},{4,7},{5,6},{6,5},{7,4},{8,11},{9,10},{10,... | collective-permute-start | bytes 1769480 | tf_op jit(solution)/shard_map/ppermute | solution.py:661
  399.3 31.4 %collective-permute-start.62 = (bf16[112,768]{1,0:T(8,128)(2,1)S(1)}, bf16[112,768]{1,0:T(8,128)(2,1)S(1)}, u32[]{:S(2)}, u32[]{:S(2)}) collective-permute-start(bf16[112,768]{1,0:T(8,128)(2,1)S(1)} %get-tuple-element.188), channel_id=1, source_target_pairs={{0,4},{4,0},{8,12},{12,8},{1,5},{5,1},{9,13},{13,9},{2,6},{6,2},{1... | collective-permute-start | bytes 516104 | tf_op jit(solution)/shard_map/ppermute | solution.py:661
  426.8 26.5 %collective-permute-start.68 = (bf16[4,384,768]{2,1,0:T(8,128)(2,1)}, bf16[4,384,768]{2,1,0:T(8,128)(2,1)S(1)}, u32[]{:S(2)}, u32[]{:S(2)}) collective-permute-start(bf16[4,384,768]{2,1,0:T(8,128)(2,1)} %get-tuple-element.141), channel_id=1, source_target_pairs={{0,16},{16,0},{1,17},{17,1},{2,18},{18,2},{3,19},{19,3},{4,20},{20... | collective-permute-start | bytes 7077896 | tf_op jit(solution)/shard_map/ppermute | solution.py:651
  (91 other events, 1087.0 us)
Sparse Core Ops, SparseCore 0:
  58.0 70.9 all-gather.2
  301.6 64.0 reduce-scatter.1

commit v3 on v2

--- a/solution.py
+++ b/solution.py
@@ -92,19 +92,22 @@
         piece[...] = source[pl.ds(at, rows), :]
 
 
-def attend_kernel(heads, tensors, place_ref, bias_ref, *refs):
-    pieces = refs[:tensors]
-    gain_ref, w_ref = refs[tensors : tensors + 2]
-    parts = refs[tensors + 2 : 2 * tensors + 2]
-    tok_ref, qkv_ref, mixed_ref, log_ref, table, wo, group, result = refs[2 * tensors + 2 :]
+def attend_kernel(heads, tensors, owners, part, place_ref, bias_ref, *refs):
+    refs = list(refs)
+    take = lambda n: [refs.pop(0) for _ in range(n)]
+    pieces, owned, (gain_ref,), parts = take(tensors), take(owners), take(1), take(tensors)
+    tok_ref, qkv_ref, mixed_ref, log_ref, w_ref, table, wo, group, result = refs
     inner = heads * HEAD_DIM
     step_id = pl.program_id(0)
 
     @pl.when(step_id == 0)
     def _():
         fill_bias(bias_ref, table, heads)
+        group_rows(place_ref, group, pieces)
+        for k, piece in enumerate(owned):
+            at = pl.multiple_of((place_ref[3] ^ k) * part, part) if owners > 1 else 0
+            w_ref[pl.ds(at, part), :] = piece[:part, :]
         wo[...] = w_ref[:, 3 * inner :]
-        group_rows(place_ref, group, pieces)
 
     here = pl.ds(pl.multiple_of(step_id * LENGTH, LENGTH), LENGTH)
     tok_ref[...] = group[here, :]
@@ -133,7 +136,7 @@
         part_rows(place_ref, parts, result)
 
 
-def attend(places, bias, pieces, gain, weights):
+def attend(places, bias, pieces, owned, part, gain):
     tensors = len(pieces)
     piece_rows, width = pieces[0].shape
     rows = tensors * piece_rows
@@ -142,15 +145,16 @@
     seqs = rows // LENGTH
     by_seq = lambda cols: pl.BlockSpec((LENGTH, cols), lambda s, *_: (s, 0))
     result = pl.pallas_call(
-        functools.partial(attend_kernel, heads, tensors),
+        functools.partial(attend_kernel, heads, tensors, len(owned), part),
         grid_spec=pltpu.PrefetchScalarGridSpec(
             num_scalar_prefetch=1,
             grid=(seqs,),
             in_specs=[pl.BlockSpec(memory_space=pltpu.SMEM)]
             + [whole((piece_rows, width))] * tensors
-            + [whole((1, width)), whole((width, 4 * inner))],
+            + [whole(o.shape) for o in owned]
+            + [whole((1, width))],
             out_specs=[whole((piece_rows, width))] * tensors
-            + [by_seq(width), by_seq(3 * inner), by_seq(inner), by_seq(TILE)],
+            + [by_seq(width), by_seq(3 * inner), by_seq(inner), by_seq(TILE), whole((width, 4 * inner))],
             scratch_shapes=[
                 pltpu.VMEM((heads, LENGTH, LENGTH), F32),
                 pltpu.VMEM((width, inner), BF16),
@@ -164,11 +168,12 @@
             jax.ShapeDtypeStruct((rows, 3 * inner), BF16),
             jax.ShapeDtypeStruct((rows, inner), BF16),
             jax.ShapeDtypeStruct((rows, TILE), F32),
+            jax.ShapeDtypeStruct((width, 4 * inner), BF16),
         ],
         compiler_params=params(),
         cost_estimate=cost(8 * rows * width * inner + 4 * rows * LENGTH * inner, rows * width * 8, rows * LENGTH * heads),
         name="attend",
-    )(places, bias, *pieces, gain, weights)
+    )(places, bias, *pieces, *owned, gain)
     return result[:tensors], result[tensors:]
 
 
@@ -441,6 +446,7 @@
     blocks = sum(ref.shape[0] for ref in xs)
     main_rows = blocks * main
     rows, width = x_ref.shape[1:]
+    wide = win.shape[1]
     choice = rest_choice(blocks, locals_, rest, expert)
     pick_rows(x_ref.at[0], xs, choice, main_rows, main, expert)
     pick_rows(grows, group_views(place_ref, g_ref, tensors, chunks), choice, main_rows, main, expert)
@@ -451,27 +457,38 @@
     lanes = lax.broadcasted_iota(jnp.int32, probs.shape, 1)
     mine = lanes == place_ref[1] * locals_ + expert
     picked = jnp.sum(jnp.where(mine, probs, 0.0), axis=-1, keepdims=True)
-    gate_s[...] = picked
+    gate_s[...] = jnp.broadcast_to(picked, gate_s.shape)
     chunk = 16
+    half_wide = wide // 2 if wide % (2 * TILE) == 0 else wide
 
     def body(step, _):
         at = pl.ds(pl.multiple_of(step * chunk, chunk), chunk)
-        value = inner[at, :]
-        square = value * value
-        wave = jnp.tanh(GELU_A * value * (1.0 + GELU_B * square))
-        half = 0.5 * (1.0 + wave)
-        hidden = (value * half).astype(BF16)
-        slope = half + (0.5 * GELU_A) * value * (1.0 - wave * wave) * (1.0 + 3.0 * GELU_B * square)
-        units = gunits[at, :]
-        gate = gate_s[at, :]
-        hid_ref[0, at, :] = hidden
-        gi_ref[0, at, :] = (gate * units * slope).astype(BF16)
+        gate_tile = gate_s[at, :]
+        gate = jnp.concatenate([gate_tile] * (half_wide // TILE), axis=1)
+        total = None
+        for start in range(0, wide, half_wide):
+            lanes_at = slice(start, start + half_wide)
+            value = inner[at, lanes_at]
+            square = value * value
+            wave = jnp.tanh(value * (GELU_A + (GELU_A * GELU_B) * square))
+            half = 0.5 + 0.5 * wave
+            hidden = (value * half).astype(BF16)
+            bend = value * (0.5 * GELU_A + (1.5 * GELU_A * GELU_B) * square)
+            slope = half + bend * (1.0 - wave * wave)
+            units = gunits[at, lanes_at]
+            hid_ref[0, at, lanes_at] = hidden
+            gi_ref[0, at, lanes_at] = (gate * (units * slope)).astype(BF16)
+            product = hidden.astype(F32) * units
+            for tile in range(0, half_wide, TILE):
+                part = product[:, tile : tile + TILE]
+                total = part if total is None else total + part
+        dots[at, :] = total
+        gate = jnp.concatenate([gate_tile] * (width // TILE), axis=1)
         ge_ref[0, at, :] = (gate * grows[at, :].astype(F32)).astype(BF16)
-        dots[at, :] = jnp.sum(hidden.astype(F32) * units, axis=-1, keepdims=True)
         return 0
 
-    lax.fori_loop(0, rows // chunk, body, 0)
-    grad_logits = (dots[...] * probs * (jnp.where(mine, 1.0, 0.0) - picked)).astype(BF16)
+    lax.fori_loop(0, rows // chunk, body, 0, unroll=4)
+    grad_logits = (jnp.sum(dots[...], axis=-1, keepdims=True) * probs * (jnp.where(mine, 1.0, 0.0) - picked)).astype(BF16)
     gl_ref[0] = grad_logits
     back[...] = (dot(gi_ref[0], win[...], ROWS_NT) + dot(grad_logits, router[...], ROWS_NT)).astype(BF16)
     put_rows(back_refs, back, choice, main_rows, main, locals_, rest, expert)
@@ -501,8 +518,8 @@
                 pltpu.VMEM((rows, width), BF16),
                 pltpu.VMEM((rows, wide), F32),
                 pltpu.VMEM((rows, wide), F32),
-                pltpu.VMEM((rows, 1), F32),
-                pltpu.VMEM((rows, 1), F32),
+                pltpu.VMEM((rows, TILE), F32),
+                pltpu.VMEM((rows, TILE), F32),
                 pltpu.VMEM((rows, width), BF16),
             ],
         ),
@@ -515,18 +532,40 @@
     return result[: len(xs)], result[len(xs) :]
 
 
-def expert_weights_kernel(
-    chunks, main, locals_, rest, place_ref, x_ref, ge_ref, hid_ref, gi_ref, gl_ref, own_out, peer_out, *refs
-):
-    forward_ref, in_own, in_send, out_own, out_send, router_ref, wout, value = refs
+def expert_rows_kernel(chunks, main, locals_, rest, place_ref, hid_ref, own_out, peer_out, forward_ref, wout, value):
     expert = pl.program_id(0)
     tensors = forward_ref.shape[0]
     blocks = tensors * forward_ref.shape[1]
-    forward_refs = group_views(place_ref, forward_ref, tensors, chunks)
     choice = rest_choice(blocks, locals_, rest, expert)
     join_halves(place_ref, own_out, peer_out, own_out, peer_out, None, wout)
     value[...] = dot(hid_ref[0], wout[...]).astype(BF16)
-    put_rows(forward_refs, value, choice, blocks * main, main, locals_, rest, expert)
+    views = group_views(place_ref, forward_ref, tensors, chunks)
+    put_rows(views, value, choice, blocks * main, main, locals_, rest, expert)
+
+
+def expert_rows(places, hidden, own_out, peer_out, shape, main, rest, chunks):
+    locals_, rows, wide = hidden.shape
+    half = own_out.shape[2]
+    width = shape[-1]
+    per = lambda *shape: pl.BlockSpec((1,) + shape, lambda e, *_: (e, 0, 0))
+    return pl.pallas_call(
+        functools.partial(expert_rows_kernel, chunks, main, locals_, rest),
+        grid_spec=pltpu.PrefetchScalarGridSpec(
+            num_scalar_prefetch=1,
+            grid=(locals_,),
+            in_specs=[per(rows, wide)] + [per(wide, half)] * 2,
+            out_specs=whole(shape),
+            scratch_shapes=[pltpu.VMEM((wide, width), BF16), pltpu.VMEM((rows, width), BF16)],
+        ),
+        out_shape=jax.ShapeDtypeStruct(shape, BF16),
+        compiler_params=params(),
+        cost_estimate=cost(2 * locals_ * rows * width * wide, locals_ * rows * width * 6),
+        name="expert_rows",
+    )(places, hidden, own_out, peer_out)
+
+
+def expert_weights_kernel(place_ref, x_ref, ge_ref, hid_ref, gi_ref, gl_ref, *refs):
+    in_own, in_send, out_own, out_send, router_ref = refs
     half = in_own.shape[1]
     mine = pl.ds(pl.multiple_of(place_ref[0] * half, half), half)
     other = pl.ds(pl.multiple_of((1 - place_ref[0]) * half, half), half)
@@ -535,33 +574,28 @@
     out_own[0] = dot(hid_ref[0], ge_ref[0, :, mine], ROWS_TN)
     out_send[0] = dot(hid_ref[0], ge_ref[0, :, other], ROWS_TN).astype(BF16)
 
-    @pl.when(expert == 0)
+    @pl.when(pl.program_id(0) == 0)
     def _():
         router_ref[...] = jnp.zeros_like(router_ref)
 
     router_ref[...] += dot(x_ref[0], gl_ref[0], ROWS_TN)
 
 
-def expert_weights(places, saved, own_out, peer_out, shape, main, rest, chunks):
+def expert_weights(places, saved, half):
     x, ge, hidden, gi, gl = saved
     locals_, rows, width = x.shape
     wide = hidden.shape[2]
     experts = gl.shape[2]
-    half = own_out.shape[2]
     per = lambda *shape: pl.BlockSpec((1,) + shape, lambda e, *_: (e, 0, 0))
-    result = pl.pallas_call(
-        functools.partial(expert_weights_kernel, chunks, main, locals_, rest),
+    return pl.pallas_call(
+        expert_weights_kernel,
         grid_spec=pltpu.PrefetchScalarGridSpec(
             num_scalar_prefetch=1,
             grid=(locals_,),
-            in_specs=[per(rows, width), per(rows, width), per(rows, wide), per(rows, wide), per(rows, experts)]
-            + [per(wide, half)] * 2,
-            out_specs=[whole(shape)]
-            + [per(half, wide), per(half, wide), per(wide, half), per(wide, half), whole((width, experts))],
-            scratch_shapes=[pltpu.VMEM((wide, width), BF16), pltpu.VMEM((rows, width), BF16)],
+            in_specs=[per(rows, width), per(rows, width), per(rows, wide), per(rows, wide), per(rows, experts)],
+            out_specs=[per(half, wide), per(half, wide), per(wide, half), per(wide, half), whole((width, experts))],
         ),
-        out_shape=[jax.ShapeDtypeStruct(shape, BF16)]
-        + [
+        out_shape=[
             jax.ShapeDtypeStruct((locals_, half, wide), F32),
             jax.ShapeDtypeStruct((locals_, half, wide), BF16),
             jax.ShapeDtypeStruct((locals_, wide, half), F32),
@@ -569,10 +603,9 @@
             jax.ShapeDtypeStruct((width, experts), F32),
         ],
         compiler_params=params(),
-        cost_estimate=cost(6 * locals_ * rows * width * wide, locals_ * rows * width * 14),
+        cost_estimate=cost(4 * locals_ * rows * width * wide, locals_ * rows * width * 14),
         name="expert_weights",
-    )(places, x, ge, hidden, gi, gl, own_out, peer_out)
-    return result[0], result[1:]
+    )(places, x, ge, hidden, gi, gl)
 
 
 def take_rows(target_ref, refs):
@@ -702,13 +735,13 @@
     bias = rel_bias.astype(F32)
 
     my_t = lax.axis_index("tensor")
-    places = jnp.stack([my_dp, my_z, my_t]).astype(jnp.int32)
+    owners = dp_count * z_count
+    my_owner = my_dp * z_count + my_z
+    places = jnp.stack([my_dp, my_z, my_t, my_owner]).astype(jnp.int32)
     token_pieces = gather_pieces(tokens, "tensor", t_count)
 
-    small = jnp.concatenate([gain_attn[:, None], gain_moe[:, None], w_router], axis=1)
-    smalls = gather_ring(small, "tensor", t_count)
-    smalls = gather_ring(smalls, "expert", z_count)
-    smalls = gather_ring(smalls, "dp", dp_count).reshape(width, 2 + experts_all)
+    small = jnp.concatenate([gain_attn[:, None], gain_moe[:, None], w_router], axis=1).reshape(-1)
+    extra = -(-small.shape[0] // (16 * width)) * 16
     packed = jnp.concatenate(
         [
             query_key_value_weight.transpose(1, 0, 2).reshape(part, 3 * inner),
@@ -716,14 +749,24 @@
         ],
         axis=1,
     )
-    packed = gather_ring(packed, "expert", z_count)
-    weights = gather_ring(packed, "dp", dp_count).reshape(width, 4 * inner)
+    packed = jnp.concatenate(
+        [packed, jnp.pad(small, (0, extra * width - small.shape[0])).reshape(extra, width)], axis=0
+    )
+    owned = gather_pieces(packed, "expert", z_count)
+    ring_done = owned
+    owned = owned + [swapped(piece, "dp", dp_count, 1) for piece in owned]
+    smalls = jnp.stack([piece[part:].reshape(-1)[: small.shape[0]] for piece in owned])
+    smalls = jnp.stack(gather_pieces(smalls, "tensor", t_count)).reshape(t_count * owners, -1)
+    owner_ids = jnp.arange(owners, dtype=jnp.int32)[:, None] ^ my_owner
+    t_ids = jnp.arange(t_count, dtype=jnp.int32)[None, :] ^ my_t
+    smalls = smalls[(t_ids * owners + owner_ids).reshape(-1)].reshape(width, 2 + experts_all)
+    if part % 16:
+        order = jnp.arange(owners, dtype=jnp.int32) ^ my_owner
+        owned = [jnp.stack([piece[:part] for piece in owned])[order].reshape(width, 4 * inner)]
+    rows_owned = part if len(owned) > 1 else width
     gain_one = smalls[:, 0].astype(F32)[None]
     gain_two = smalls[:, 1].astype(F32)[None]
     router = smalls[:, 2:]
-
-    peer_in = shifted(w_in, "dp", dp_count, 1)
-    peer_out = shifted(w_out, "dp", dp_count, 1)
 
     z_of = expert_index // locals_
     local = expert_index - z_of * locals_
@@ -751,10 +794,17 @@
             return pieces
         return [jnp.concatenate(pieces[k * many : (k + 1) * many], axis=0) for k in range(chunks)]
 
-    grad_rows = jnp.concatenate(over_expert(place(target_row, cotangent, count)), axis=0)
+    late_cotangent, _ = lax.optimization_barrier((cotangent, ring_done))
+    grad_rows = jnp.concatenate(over_expert(place(target_row, late_cotangent, count)), axis=0)
+    late_in, late_out, token_pieces = lax.optimization_barrier((w_in, w_out, token_pieces))
+    peer_in = shifted(late_in, "dp", dp_count, 1)
+    peer_out = shifted(late_out, "dp", dp_count, 1)
+
+    parts, (group_tokens, projected, mixed, logs, weights) = attend(
+        places, bias, token_pieces, owned, rows_owned, gain_one
+    )
+    parts, peer_in, peer_out, grad_rows = lax.optimization_barrier((parts, peer_in, peer_out, grad_rows))
     grad_arrived = lax.all_gather(grad_rows, "tensor", axis=0).reshape(t_count, z_count, block, width)
-
-    parts, (group_tokens, projected, mixed, logs) = attend(places, bias, token_pieces, gain_one, weights)
     attn = swap_pieces(parts, "tensor", t_count)
     hidden_one, sent, gate = route(
         tokens, attn, gain_two, router, target_row, expert_index[:, None], kept_mask[:, None], count
@@ -767,20 +817,6 @@
     back_parts, saved = expert_forward_back(
         places, arrived, grad_arrived, w_in, peer_in, w_out, peer_out, router, main, rest, chunks
     )
-    back_swapped = [
-        swap_pieces(
-            [piece.reshape(many * block, width) for piece in back_parts[k * t_count : (k + 1) * t_count]],
-            "tensor",
-            t_count,
-        )
-        for k in range(chunks)
-    ]
-    forward_part, (in_own, in_send, out_own, out_send, router_part) = expert_weights(
-        places, saved, w_out, peer_out, grad_arrived.shape, main, rest, chunks
-    )
-    back_swapped, forward_part, in_send, out_send = lax.optimization_barrier(
-        (back_swapped, forward_part, in_send, out_send)
-    )
 
     def summed(pieces):
         total = pieces[0].astype(F32)
@@ -788,23 +824,41 @@
             total = total + piece.astype(F32)
         return total.astype(BF16)
 
-    grad_back = back_over_expert([summed(pieces) for pieces in back_swapped])
+    size = many * block
+
+    def swap_group(group):
+        joined = [
+            jnp.concatenate([back_parts[k * t_count + j].reshape(size, width) for k in group], axis=0)
+            for j in range(t_count)
+        ]
+        return swap_pieces(joined, "tensor", t_count)
+
+    half = chunks // 2
+    far = swap_group(range(half, chunks))
+    forward_part = expert_rows(places, saved[2], w_out, peer_out, grad_arrived.shape, main, rest, chunks)
+    far, forward_part, saved = lax.optimization_barrier((far, forward_part, saved))
+    near = swap_group(range(half))
+    in_own, in_send, out_own, out_send, router_part = expert_weights(places, saved, w_in.shape[1])
+    near, forward_part, in_send, out_send = lax.optimization_barrier((near, forward_part, in_send, out_send))
+    groups = [value[k * size : (k + 1) * size] for value in (summed(near), summed(far)) for k in range(half)]
+    grad_back = back_over_expert(groups)
+    forward_sum = lax.psum_scatter(
+        forward_part.reshape(t_count * z_count * block, width), "tensor", scatter_dimension=0, tiled=True
+    )
+    grad_hidden, grad_attn, gain_two_part = hidden_back(target_col, grad_back, hidden_one, cotangent, gain_two)
     grad_w_in = in_own + shifted(in_send, "dp", dp_count, 1).astype(F32)
     grad_w_out = out_own + shifted(out_send, "dp", dp_count, 1).astype(F32)
-    grad_hidden, grad_attn, gain_two_part = hidden_back(target_col, grad_back, hidden_one, cotangent, gain_two)
+    grad_pieces, grad_w_in, grad_w_out, forward_sum = lax.optimization_barrier(
+        (gather_pieces(grad_attn, "tensor", t_count), grad_w_in, grad_w_out, forward_sum)
+    )
     normed_parts, (weight_part, bucket_part, gain_one_part) = attend_back(
-        places, bias, group_tokens, gain_one, weights, projected, mixed, logs,
-        gather_pieces(grad_attn, "tensor", t_count),
+        places, bias, group_tokens, gain_one, weights, projected, mixed, logs, grad_pieces
     )
     grad_normed = swap_pieces(normed_parts, "tensor", t_count)
-    forward_sum = lax.psum_scatter(
-        forward_part.reshape(t_count * z_count * block, width), "tensor", scatter_dimension=0, tiled=True
-    )
     forward_rows = back_over_expert(list(forward_sum.reshape(chunks, many * block, width)))
     output = output_rows(target_col, forward_rows, hidden_one, gate)
     grad_tokens = tokens_back(tokens, grad_normed, gain_one, grad_hidden)
 
-    owners = dp_count * z_count
     smalls = jnp.concatenate(
         [
             gain_one_part.reshape(owners, part),

time: 484 us -> 448 us (0.926)
  starting transfers between devices: 91.3 us -> 73.1 us
  Pallas kernels: 129 us -> 118 us
    ppermute x16 -> x5, starting transfers between devices: 17.4 us -> 1.09 us  [shifted(): lax.ppermute(value, axis, [(s, (s + step) % count) for s in range(count)])]
    ppermute x16 -> x5, waiting for transfers between devices: 14.3 us -> 0.01 us  [shifted(): lax.ppermute(value, axis, [(s, (s + step) % count) for s in range(count)])]
    ppermute x54 -> x58, waiting for transfers between devices: 174 us -> 187 us  [swapped(): return lax.ppermute(value, axis, [(s, s ^ bits) for s in range(count)])]
    pallas_call x1, Pallas kernels: 46.4 us -> 34.9 us  [expert_forward_back(): pl.pallas_call(functools.partial(expert_kernel, chunks, len(xs) // chunks...]
    unnamed x106 -> x118, local copies, waits for them, and re-layouts: 11.4 us -> 7.79 us
    ppermute x54 -> x58, starting transfers between devices: 73.8 us -> 71.8 us  [swapped(): return lax.ppermute(value, axis, [(s, s ^ bits) for s in range(count)])]
    pallas_call x2 -> x3, Pallas kernels: 39.8 us -> 41.5 us  [the longest x1 16.4 us: expert_weights(): pl.pallas_call(expert_weights_kernel, grid_spec=pltpu.PrefetchScalarGridS...]
  transfers between devices with their start and end apart: 72 -> 65, of which waited for: 27 -> 31; matrix products, arithmetic and copies ran while one was open for 10% -> 9% of each run, Pallas kernels for 17% -> 13%
where the time goes in v3:
time: 448 us; the launch traced here: 447 us
  waiting for transfers between devices  187 us (42%)
  Pallas kernels  118 us (26%)
  starting transfers between devices  73.1 us (16%)
  local copies, waits for them, and re-layouts  27.5 us (6%)
  other arithmetic  25.5 us (6%)
  between operations  15 us (3%)
    ppermute x58, waiting for transfers between devices, swapped(): return lax.ppermute(value, axis, [(s, s ^ bits) for s in range(count)])  187 us
    ppermute x58, starting transfers between devices, swapped(): return lax.ppermute(value, axis, [(s, s ^ bits) for s in range(count)])  71.8 us
    pallas_call x1, Pallas kernels, expert_forward_back(): pl.pallas_call(functools.partial(expert_kernel, chunks, len(xs) // chunks...  34.9 us
    pallas_call x1, Pallas kernels, attend_back(): pl.pallas_call(functools.partial(attend_back_kernel, heads, tensors), gri...  23.8 us
    pallas_call x1, Pallas kernels, expert_weights(): pl.pallas_call(expert_weights_kernel, grid_spec=pltpu.PrefetchScalarGridS...  16.4 us
    pallas_call x1, Pallas kernels, attend(): pl.pallas_call(functools.partial(attend_kernel, heads, tensors, len(owned...  15.5 us
    pallas_call x1, Pallas kernels, expert_rows(): pl.pallas_call(functools.partial(expert_rows_kernel, chunks, main, locals...  9.62 us
  transfers between devices with their start and end apart: 65, of which 31 were waited for; matrix products, arithmetic and copies ran while one was open for 9% of the time, Pallas kernels for 13%

profile of v3, /device:TPU:0, one launch (start us, length us, event | category | flops | bytes accessed | tf_op | source)
XLA Modules:
  0.0 446.8 jit_solution(12953528452700018813)
XLA Ops:
  11.8 13.8 %collective-permute-done.2.refs_3_ = bf16[384,768]{1,0:T(8,128)(2,1)S(1)} collective-permute-done((bf16[384,768]{1,0:T(8,128)(2,1)}, bf16[384,768]{1,0:T(8,128)(2,1)S(1)}, u32[]{:S(2)}, u32[]{:S(2)}) %collective-permute-start.2) | collective-permute-done | bytes 589856 | tf_op jit(solution)/shard_map/ppermute | solution.py:694
  25.6 11.8 %collective-permute-done.1.refs_2_ = bf16[384,768]{1,0:T(8,128)(2,1)S(1)} collective-permute-done((bf16[384,768]{1,0:T(8,128)(2,1)}, bf16[384,768]{1,0:T(8,128)(2,1)S(1)}, u32[]{:S(2)}, u32[]{:S(2)}) %collective-permute-start.1) | collective-permute-done | bytes 589856 | tf_op jit(solution)/shard_map/ppermute | solution.py:694
  50.9 9.8 %collective-permute-done.4.refs_6_ = bf16[112,768]{1,0:T(8,128)(2,1)S(1)} collective-permute-done((bf16[112,768]{1,0:T(8,128)(2,1)S(1)}, bf16[112,768]{1,0:T(8,128)(2,1)S(1)}, u32[]{:S(2)}, u32[]{:S(2)}) %collective-permute-start.4) | collective-permute-done | bytes 172064 | tf_op jit(solution)/shard_map/ppermute | solution.py:694
  81.0 4.4 collective-permute-done.17
  85.3 9.7 %collective-permute-done.16 = bf16[144,768]{1,0:T(8,128)(2,1)} collective-permute-done((bf16[144,768]{1,0:T(8,128)(2,1)S(1)}, bf16[144,768]{1,0:T(8,128)(2,1)}, u32[]{:S(2)}, u32[]{:S(2)}) %collective-permute-start.16) | collective-permute-done | bytes 221216 | tf_op jit(solution)/shard_map/ppermute | solution.py:694
  97.1 15.5 %attend.1 = (bf16[384,768]{1,0:T(8,128)(2,1)}, bf16[384,768]{1,0:T(8,128)(2,1)}, bf16[384,768]{1,0:T(8,128)(2,1)}, bf16[384,768]{1,0:T(8,128)(2,1)}, bf16[1536,7...) custom-call(s32[4]{0:T(128)} %pad_add_fusion.place_ref, ...), custom_call_target="tpu_custom_call" | custom-call | flops 2415919104 | bytes 9437184 | tf_op jit(solution)/shard_map/attend/pallas_call | solution.py:147
  119.4 18.1 %collective-permute-done.18.refs_1_ = bf16[384,768]{1,0:T(8,128)(2,1)S(1)} collective-permute-done((bf16[384,768]{1,0:T(8,128)(2,1)}, bf16[384,768]{1,0:T(8,128)(2,1)S(1)}, u32[]{:S(2)}, u32[]{:S(2)}) %collective-permute-start.18) | collective-permute-done | bytes 589856 | tf_op jit(solution)/shard_map/ppermute | solution.py:694
  140.7 9.2 %collective-permute-done.20.refs_3_ = bf16[384,768]{1,0:T(8,128)(2,1)S(1)} collective-permute-done((bf16[384,768]{1,0:T(8,128)(2,1)}, bf16[384,768]{1,0:T(8,128)(2,1)S(1)}, u32[]{:S(2)}, u32[]{:S(2)}) %collective-permute-start.20) | collective-permute-done | bytes 589856 | tf_op jit(solution)/shard_map/ppermute | solution.py:694
  168.6 6.7 %collective-permute-done.28 = bf16[144,768]{1,0:T(8,128)(2,1)S(1)} collective-permute-done((bf16[144,768]{1,0:T(8,128)(2,1)S(1)}, bf16[144,768]{1,0:T(8,128)(2,1)S(1)}, u32[]{:S(2)}, u32[]{:S(2)}) %collective-permute-start.28) | collective-permute-done | bytes 221216 | tf_op jit(solution)/shard_map/ppermute | solution.py:694
  180.2 5.1 %collective-permute-done.23 = bf16[144,768]{1,0:T(8,128)(2,1)S(1)} collective-permute-done((bf16[144,768]{1,0:T(8,128)(2,1)S(1)}, bf16[144,768]{1,0:T(8,128)(2,1)S(1)}, u32[]{:S(2)}, u32[]{:S(2)}) %collective-permute-start.23) | collective-permute-done | bytes 221216 | tf_op jit(solution)/shard_map/ppermute | solution.py:694
  187.1 5.4 %collective-permute-done.35 = bf16[144,768]{1,0:T(8,128)(2,1)S(1)} collective-permute-done((bf16[144,768]{1,0:T(8,128)(2,1)S(1)}, bf16[144,768]{1,0:T(8,128)(2,1)S(1)}, u32[]{:S(2)}, u32[]{:S(2)}) %collective-permute-start.35) | collective-permute-done | bytes 221216 | tf_op jit(solution)/shard_map/ppermute | solution.py:694
  206.1 5.3 %collective-permute-done.27 = bf16[144,768]{1,0:T(8,128)(2,1)S(1)} collective-permute-done((bf16[144,768]{1,0:T(8,128)(2,1)S(1)}, bf16[144,768]{1,0:T(8,128)(2,1)S(1)}, u32[]{:S(2)}, u32[]{:S(2)}) %collective-permute-start.27) | collective-permute-done | bytes 221216 | tf_op jit(solution)/shard_map/ppermute | solution.py:694
  214.3 34.9 %experts.1 = (bf16[1,144,768]{2,1,0:T(8,128)(2,1)}, bf16[1,144,768]{2,1,0:T(8,128)(2,1)}, bf16[1,144,768]{2,1,0:T(8,128)(2,1)}, bf16[1,144,768]{2,1,0:T(8,128)(2...) custom-call(s32[4]{0:T(128)} %pad_add_fusion.place_ref, ...), custom_call_target="tpu_custom_call" | custom-call | flops 8153726976 | bytes 24772608 | tf_op jit(solution)/shard_map/experts/pallas_call | solution.py:505
  259.7 9.6 %expert_rows.1 = bf16[4,4,144,768]{3,2,1,0:T(8,128)(2,1)} custom-call(s32[4]{0:T(128)} %pad_add_fusion.place_ref, bf16[4,576,768]{2,1,0:T(8,128)(2,1)} %get-tuple-element.139.hid_ref, bf16[4,768,384]{2,1,0:T(8,128)(2,1)} %own_out.1, bf16[4,768,384]{2,1,0:T(8,128)(2,1)} %copy-done.2), custom_call_target="tpu_custom_call" | custom-call | flops 2717908992 | bytes 10616832 | tf_op jit(solution)/shard_map/expert_rows/pallas_call | solution.py:551
  269.9 4.3 collective-permute-done.40
  274.2 16.4 %expert_weights.1 = (f32[4,384,768]{2,1,0:T(8,128)}, bf16[4,384,768]{2,1,0:T(8,128)(2,1)}, f32[4,768,384]{2,1,0:T(8,128)}, bf16[4,768,384]{2,1,0:T(8,128)(2,1)}, f32[768,16]{1,0:T(8,128)}) custom-call(s32[4]{0:T(128)} %pad_add_fusion.place_ref, bf16[4,576,768]{2,1,0:T(8,128)(2,1)} %get-tuple-element.137.x_ref, ...), custom_call_target="tpu_custom_call" | custom-call | flops 5435817984 | bytes 24772608 | tf_op jit(solution)/shard_map/expert_weights/pallas_call | solution.py:590
  306.5 12.4 %collective-permute-done.43.refs_2_ = bf16[144,768]{1,0:T(8,128)(2,1)} collective-permute-done((bf16[144,768]{1,0:T(8,128)(2,1)}, bf16[144,768]{1,0:T(8,128)(2,1)}, u32[]{:S(2)}, u32[]{:S(2)}) %collective-permute-start.43) | collective-permute-done | bytes 221216 | tf_op jit(solution)/shard_map/ppermute | solution.py:694
  328.1 5.9 %convert_add_fusion.1 = f32[4,384,768]{2,1,0:T(8,128)} fusion(f32[4,384,768]{2,1,0:T(8,128)} %get-tuple-element.154, bf16[4,384,768]{2,1,0:T(8,128)(2,1)} %collective-permute-done.48), kind=kLoop, calls=%fused_computation.2 | loop fusion | flops 2359296 | bytes 11796480 | tf_op jit(solution)/shard_map/add | solution.py:849
  336.7 14.0 %collective-permute-done.47.refs_3_ = bf16[384,768]{1,0:T(8,128)(2,1)S(1)} collective-permute-done((bf16[384,768]{1,0:T(8,128)(2,1)}, bf16[384,768]{1,0:T(8,128)(2,1)S(1)}, u32[]{:S(2)}, u32[]{:S(2)}) %collective-permute-start.47) | collective-permute-done | bytes 589856 | tf_op jit(solution)/shard_map/ppermute | solution.py:694
  350.7 11.0 %collective-permute-done.46.refs_2_ = bf16[384,768]{1,0:T(8,128)(2,1)} collective-permute-done((bf16[384,768]{1,0:T(8,128)(2,1)}, bf16[384,768]{1,0:T(8,128)(2,1)}, u32[]{:S(2)}, u32[]{:S(2)}) %collective-permute-start.46) | collective-permute-done | bytes 589856 | tf_op jit(solution)/shard_map/ppermute | solution.py:694
  361.7 23.8 %attend_back.1 = (bf16[384,768]{1,0:T(8,128)(2,1)}, bf16[384,768]{1,0:T(8,128)(2,1)}, bf16[384,768]{1,0:T(8,128)(2,1)}, bf16[384,768]{1,0:T(8,128)(2,1)}, f32[76...) custom-call(s32[4]{0:T(128)} %pad_add_fusion.place_ref, f32[3,32]{1,0:T(4,128)} %convert_element_type.105.bias_ref, ...), custom_call_target="tpu_custom_call" | custom-call | flops 5586812928 | bytes 14155776 | tf_op jit(solution)/shard_map/attend_back/pallas_call | solution.py:269
  396.5 4.3 collective-permute-done.52.refs_3_
  404.9 8.9 %collective-permute-done.51.refs_2_ = bf16[144,768]{1,0:T(8,128)(2,1)} collective-permute-done((bf16[144,768]{1,0:T(8,128)(2,1)}, bf16[144,768]{1,0:T(8,128)(2,1)}, u32[]{:S(2)}, u32[]{:S(2)}) %collective-permute-start.51) | collective-permute-done | bytes 221216 | tf_op jit(solution)/shard_map/ppermute | solution.py:694
  426.1 4.9 %collective-permute-done.58 = bf16[112,768]{1,0:T(8,128)(2,1)S(1)} collective-permute-done((bf16[112,768]{1,0:T(8,128)(2,1)S(1)}, bf16[112,768]{1,0:T(8,128)(2,1)S(1)}, u32[]{:S(2)}, u32[]{:S(2)}) %collective-permute-start.58) | collective-permute-done | bytes 172064 | tf_op jit(solution)/shard_map/ppermute | solution.py:694
  (344 shorter events, 166.6 us)
Async XLA Ops:
  7.2 206.4 %all-gather.3.cloned.1.call-start = ((), (), s32[]{:S(2)}) async-start(), calls=%async_computation.2 | async-start | bytes 4423680 | tf_op jit(solution)/shard_map/all_gather | solution.py:807
  11.2 26.2 %collective-permute-start.1 = (bf16[384,768]{1,0:T(8,128)(2,1)}, bf16[384,768]{1,0:T(8,128)(2,1)S(1)}, u32[]{:S(2)}, u32[]{:S(2)}) collective-permute-start(bf16[384,768]{1,0:T(8,128)(2,1)} %tok_ref.3), channel_id=1, source_target_pairs={{0,2},{1,3},{2,0},{3,1},{4,6},{5,7},{6,4},{7,5},{8,10},{9,11},{10,... | collective-permute-start | bytes 1769480 | tf_op jit(solution)/shard_map/ppermute | solution.py:694
  11.7 26.0 %collective-permute-start = (bf16[384,768]{1,0:T(8,128)(2,1)}, bf16[384,768]{1,0:T(8,128)(2,1)S(1)}, u32[]{:S(2)}, u32[]{:S(2)}) collective-permute-start(bf16[384,768]{1,0:T(8,128)(2,1)} %tok_ref.3), channel_id=1, source_target_pairs={{0,1},{1,0},{2,3},{3,2},{4,5},{5,4},{6,7},{7,6},{8,9},{9,8},{10,11... | collective-permute-start | bytes 1769480 | tf_op jit(solution)/shard_map/ppermute | solution.py:694
  37.7 75.0 %collective-permute-start.13 = (bf16[4,384,768]{2,1,0:T(8,128)(2,1)}, bf16[4,384,768]{2,1,0:T(8,128)(2,1)}, u32[]{:S(2)}, u32[]{:S(2)}) collective-permute-start(bf16[4,384,768]{2,1,0:T(8,128)(2,1)} %refs_17_.1), channel_id=1, source_target_pairs={{0,16},{16,0},{1,17},{17,1},{2,18},{18,2},{3,19},{19,3},{4,20},{20... | collective-permute-start | bytes 7077896 | tf_op jit(solution)/shard_map/ppermute | solution.py:684
  37.7 75.0 %collective-permute-start.14 = (bf16[4,768,384]{2,1,0:T(8,128)(2,1)}, bf16[4,768,384]{2,1,0:T(8,128)(2,1)S(1)}, u32[]{:S(2)}, u32[]{:S(2)}) collective-permute-start(bf16[4,768,384]{2,1,0:T(8,128)(2,1)} %own_out.1), channel_id=1, source_target_pairs={{0,16},{16,0},{1,17},{17,1},{2,18},{18,2},{3,19},{19,3},{4,20},{20... | collective-permute-start | bytes 7077896 | tf_op jit(solution)/shard_map/ppermute | solution.py:684
  112.7 249.0 %reduce-scatter.2.cloned.1.call-start = ((), (), s32[]{:S(2)}) async-start(), calls=%async_computation.1 | async-start | bytes 4423680 | tf_op jit(solution)/shard_map/reduce_scatter | solution.py:845
  112.9 24.6 %collective-permute-start.18 = (bf16[384,768]{1,0:T(8,128)(2,1)}, bf16[384,768]{1,0:T(8,128)(2,1)S(1)}, u32[]{:S(2)}, u32[]{:S(2)}) collective-permute-start(bf16[384,768]{1,0:T(8,128)(2,1)} %get-tuple-element.108), channel_id=1, source_target_pairs={{0,1},{1,0},{2,3},{3,2},{4,5},{5,4},{6,7},{7,6},{8,9},{9,8},{10,11... | collective-permute-start | bytes 1769480 | tf_op jit(solution)/shard_map/ppermute | solution.py:694
  114.5 26.2 %collective-permute-start.19 = (bf16[384,768]{1,0:T(8,128)(2,1)}, bf16[384,768]{1,0:T(8,128)(2,1)S(1)}, u32[]{:S(2)}, u32[]{:S(2)}) collective-permute-start(bf16[384,768]{1,0:T(8,128)(2,1)} %get-tuple-element.109), channel_id=1, source_target_pairs={{0,2},{1,3},{2,0},{3,1},{4,6},{5,7},{6,4},{7,5},{8,10},{9,11},{10,... | collective-permute-start | bytes 1769480 | tf_op jit(solution)/shard_map/ppermute | solution.py:694
  115.3 34.6 %collective-permute-start.20 = (bf16[384,768]{1,0:T(8,128)(2,1)}, bf16[384,768]{1,0:T(8,128)(2,1)S(1)}, u32[]{:S(2)}, u32[]{:S(2)}) collective-permute-start(bf16[384,768]{1,0:T(8,128)(2,1)} %get-tuple-element.110), channel_id=1, source_target_pairs={{0,3},{1,2},{2,1},{3,0},{4,7},{5,6},{6,5},{7,4},{8,11},{9,10},{10,... | collective-permute-start | bytes 1769480 | tf_op jit(solution)/shard_map/ppermute | solution.py:694
  177.5 23.0 %collective-permute-start.33 = (bf16[144,768]{1,0:T(8,128)(2,1)S(1)}, bf16[144,768]{1,0:T(8,128)(2,1)S(1)}, u32[]{:S(2)}, u32[]{:S(2)}) collective-permute-start(bf16[144,768]{1,0:T(8,128)(2,1)S(1)} %collective-permute-done.32), channel_id=1, source_target_pairs={{0,1},{1,0},{2,3},{3,2},{4,5},{5,4},{6,7},{7,6},{8,9},{9,8},{10,11... | collective-permute-start | bytes 663560 | tf_op jit(solution)/shard_map/ppermute | solution.py:694
  178.8 23.2 %collective-permute-start.31 = (bf16[144,768]{1,0:T(8,128)(2,1)S(1)}, bf16[144,768]{1,0:T(8,128)(2,1)S(1)}, u32[]{:S(2)}, u32[]{:S(2)}) collective-permute-start(bf16[144,768]{1,0:T(8,128)(2,1)S(1)} %collective-permute-done.28), channel_id=1, source_target_pairs={{0,3},{1,2},{2,1},{3,0},{4,7},{5,6},{6,5},{7,4},{8,11},{9,10},{10,... | collective-permute-start | bytes 663560 | tf_op jit(solution)/shard_map/ppermute | solution.py:694
  185.3 20.6 %collective-permute-start.30 = (bf16[144,768]{1,0:T(8,128)(2,1)S(1)}, bf16[144,768]{1,0:T(8,128)(2,1)S(1)}, u32[]{:S(2)}, u32[]{:S(2)}) collective-permute-start(bf16[144,768]{1,0:T(8,128)(2,1)S(1)} %collective-permute-done.28), channel_id=1, source_target_pairs={{0,2},{1,3},{2,0},{3,1},{4,6},{5,7},{6,4},{7,5},{8,10},{9,11},{10,... | collective-permute-start | bytes 663560 | tf_op jit(solution)/shard_map/ppermute | solution.py:694
  253.2 21.0 %collective-permute-start.40 = (bf16[288,768]{1,0:T(8,128)(2,1)S(1)}, bf16[288,768]{1,0:T(8,128)(2,1)S(1)}, u32[]{:S(2)}, u32[]{:S(2)}) collective-permute-start(bf16[288,768]{1,0:T(8,128)(2,1)S(1)} %pad_maximum_fusion.7), channel_id=1, source_target_pairs={{0,2},{1,3},{2,0},{3,1},{4,6},{5,7},{6,4},{7,5},{8,10},{9,11},{10,... | collective-permute-start | bytes 1327112 | tf_op jit(solution)/shard_map/ppermute | solution.py:694
  256.4 34.2 %collective-permute-start.38 = (bf16[288,768]{1,0:T(8,128)(2,1)S(1)}, bf16[288,768]{1,0:T(8,128)(2,1)S(1)}, u32[]{:S(2)}, u32[]{:S(2)}) collective-permute-start(bf16[288,768]{1,0:T(8,128)(2,1)S(1)} %pad_maximum_fusion.4), channel_id=1, source_target_pairs={{0,3},{1,2},{2,1},{3,0},{4,7},{5,6},{6,5},{7,4},{8,11},{9,10},{10,... | collective-permute-start | bytes 1327112 | tf_op jit(solution)/shard_map/ppermute | solution.py:694
  258.1 33.5 %collective-permute-start.37 = (bf16[288,768]{1,0:T(8,128)(2,1)S(1)}, bf16[288,768]{1,0:T(8,128)(2,1)S(1)}, u32[]{:S(2)}, u32[]{:S(2)}) collective-permute-start(bf16[288,768]{1,0:T(8,128)(2,1)S(1)} %pad_maximum_fusion.3), channel_id=1, source_target_pairs={{0,2},{1,3},{2,0},{3,1},{4,6},{5,7},{6,4},{7,5},{8,10},{9,11},{10,... | collective-permute-start | bytes 1327112 | tf_op jit(solution)/shard_map/ppermute | solution.py:694
  269.3 22.2 %collective-permute-start.36 = (bf16[288,768]{1,0:T(8,128)(2,1)S(1)}, bf16[288,768]{1,0:T(8,128)(2,1)S(1)}, u32[]{:S(2)}, u32[]{:S(2)}) collective-permute-start(bf16[288,768]{1,0:T(8,128)(2,1)S(1)} %pad_maximum_fusion.2), channel_id=1, source_target_pairs={{0,1},{1,0},{2,3},{3,2},{4,5},{5,4},{6,7},{7,6},{8,9},{9,8},{10,11... | collective-permute-start | bytes 1327112 | tf_op jit(solution)/shard_map/ppermute | solution.py:694
  293.2 34.9 %collective-permute-start.48 = (bf16[4,384,768]{2,1,0:T(8,128)(2,1)}, bf16[4,384,768]{2,1,0:T(8,128)(2,1)}, u32[]{:S(2)}, u32[]{:S(2)}) collective-permute-start(bf16[4,384,768]{2,1,0:T(8,128)(2,1)} %get-tuple-element.155), channel_id=1, source_target_pairs={{0,16},{16,0},{1,17},{17,1},{2,18},{18,2},{3,19},{19,3},{4,20},{20... | collective-permute-start | bytes 7077896 | tf_op jit(solution)/shard_map/ppermute | solution.py:684
  293.3 40.7 %collective-permute-start.49 = (bf16[4,768,384]{2,1,0:T(8,128)(2,1)}, bf16[4,768,384]{2,1,0:T(8,128)(2,1)S(1)}, u32[]{:S(2)}, u32[]{:S(2)}) collective-permute-start(bf16[4,768,384]{2,1,0:T(8,128)(2,1)} %get-tuple-element.157), channel_id=1, source_target_pairs={{0,16},{16,0},{1,17},{17,1},{2,18},{18,2},{3,19},{19,3},{4,20},{20... | collective-permute-start | bytes 7077896 | tf_op jit(solution)/shard_map/ppermute | solution.py:684
  323.8 26.9 %collective-permute-start.47 = (bf16[384,768]{1,0:T(8,128)(2,1)}, bf16[384,768]{1,0:T(8,128)(2,1)S(1)}, u32[]{:S(2)}, u32[]{:S(2)}) collective-permute-start(bf16[384,768]{1,0:T(8,128)(2,1)} %get-tuple-element.166.refs_0_), channel_id=1, source_target_pairs={{0,3},{1,2},{2,1},{3,0},{4,7},{5,6},{6,5},{7,4},{8,11},{9,10},{10,... | collective-permute-start | bytes 1769480 | tf_op jit(solution)/shard_map/ppermute | solution.py:694
  325.3 36.4 %collective-permute-start.46 = (bf16[384,768]{1,0:T(8,128)(2,1)}, bf16[384,768]{1,0:T(8,128)(2,1)}, u32[]{:S(2)}, u32[]{:S(2)}) collective-permute-start(bf16[384,768]{1,0:T(8,128)(2,1)} %get-tuple-element.166.refs_0_), channel_id=1, source_target_pairs={{0,2},{1,3},{2,0},{3,1},{4,6},{5,7},{6,4},{7,5},{8,10},{9,11},{10,... | collective-permute-start | bytes 1769480 | tf_op jit(solution)/shard_map/ppermute | solution.py:694
  326.7 35.0 %collective-permute-start.45 = (bf16[384,768]{1,0:T(8,128)(2,1)}, bf16[384,768]{1,0:T(8,128)(2,1)}, u32[]{:S(2)}, u32[]{:S(2)}) collective-permute-start(bf16[384,768]{1,0:T(8,128)(2,1)} %get-tuple-element.166.refs_0_), channel_id=1, source_target_pairs={{0,1},{1,0},{2,3},{3,2},{4,5},{5,4},{6,7},{7,6},{8,9},{9,8},{10,11... | collective-permute-start | bytes 1769480 | tf_op jit(solution)/shard_map/ppermute | solution.py:694
  393.0 23.1 %collective-permute-start.53 = (bf16[384,768]{1,0:T(8,128)(2,1)}, bf16[384,768]{1,0:T(8,128)(2,1)}, u32[]{:S(2)}, u32[]{:S(2)}) collective-permute-start(bf16[384,768]{1,0:T(8,128)(2,1)} %get-tuple-element.171), channel_id=1, source_target_pairs={{0,1},{1,0},{2,3},{3,2},{4,5},{5,4},{6,7},{7,6},{8,9},{9,8},{10,11... | collective-permute-start | bytes 1769480 | tf_op jit(solution)/shard_map/ppermute | solution.py:694
  394.1 28.1 %collective-permute-start.54 = (bf16[384,768]{1,0:T(8,128)(2,1)}, bf16[384,768]{1,0:T(8,128)(2,1)}, u32[]{:S(2)}, u32[]{:S(2)}) collective-permute-start(bf16[384,768]{1,0:T(8,128)(2,1)} %get-tuple-element.172), channel_id=1, source_target_pairs={{0,2},{1,3},{2,0},{3,1},{4,6},{5,7},{6,4},{7,5},{8,10},{9,11},{10,... | collective-permute-start | bytes 1769480 | tf_op jit(solution)/shard_map/ppermute | solution.py:694
  395.0 27.2 %collective-permute-start.55 = (bf16[384,768]{1,0:T(8,128)(2,1)}, bf16[384,768]{1,0:T(8,128)(2,1)}, u32[]{:S(2)}, u32[]{:S(2)}) collective-permute-start(bf16[384,768]{1,0:T(8,128)(2,1)} %get-tuple-element.173), channel_id=1, source_target_pairs={{0,3},{1,2},{2,1},{3,0},{4,7},{5,6},{6,5},{7,4},{8,11},{9,10},{10,... | collective-permute-start | bytes 1769480 | tf_op jit(solution)/shard_map/ppermute | solution.py:694
  (98 other events, 1272.6 us)
Sparse Core Ops, SparseCore 0:
  112.8 84.0 all-gather.2
  293.3 66.5 reduce-scatter.1

commit v4 on v3

--- a/solution.py
+++ b/solution.py
@@ -78,11 +78,35 @@
     return values * scale, scale
 
 
+HOPS = ((1, 2), (2, 1))
+
+
 def group_rows(place_ref, out, pieces):
     rows = pieces[0].shape[0]
     for j, piece in enumerate(pieces):
         at = pl.multiple_of((place_ref[2] ^ j) * rows, rows)
         out[pl.ds(at, rows), :] = piece[...]
+
+
+def group_halves(place_ref, out, pieces):
+    rows = pieces[0].shape[0]
+    half = rows // 2
+    at = pl.multiple_of(place_ref[2] * rows, rows)
+    out[pl.ds(at, rows), :] = pieces[0][...]
+    for h, (a, b) in enumerate(HOPS):
+        first, second = pieces[1 + 2 * h : 3 + 2 * h]
+        for j, value in ((a, first[...]), (b, second[:half, :]), (a | b, second[half:, :])):
+            at = pl.multiple_of((place_ref[2] ^ j) * rows + h * half, half)
+            out[pl.ds(at, half), :] = value
+
+
+def part_halves(place_ref, pieces, source):
+    half = pieces[0].shape[0] // 2
+    for h, (a, b) in enumerate(HOPS):
+        for piece, order in zip(pieces[2 * h : 2 * h + 2], ((0, b), (a, a | b))):
+            for n, j in enumerate(order):
+                at = pl.multiple_of((place_ref[2] ^ j) * 2 * half + h * half, half)
+                piece[n * half : (n + 1) * half, :] = source[pl.ds(at, half), :]
 
 
 def part_rows(place_ref, pieces, source):
@@ -133,7 +157,7 @@
 
     @pl.when(step_id == pl.num_programs(0) - 1)
     def _():
-        part_rows(place_ref, parts, result)
+        part_halves(place_ref, parts, result)
 
 
 def attend(places, bias, pieces, owned, part, gain):
@@ -180,8 +204,10 @@
 def attend_back_kernel(
     heads, tensors, place_ref, bias_ref, tok_ref, gain_ref, w_ref, qkv_ref, mixed_ref, log_ref, *refs
 ):
-    pieces, parts = refs[:tensors], refs[tensors : 2 * tensors]
-    weight_ref, buckets_ref, gain_out, table, wo, gmix, gproj, near, far, rows_s, group, result = refs[2 * tensors :]
+    refs = list(refs)
+    pieces = [refs.pop(0) for _ in range(5)]
+    parts = [refs.pop(0) for _ in range(tensors)]
+    weight_ref, buckets_ref, gain_out, table, wo, gmix, gproj, near, far, rows_s, group, result = refs
     inner = heads * HEAD_DIM
     blocks = LENGTH // TILE
     step_id = pl.program_id(0)
@@ -194,7 +220,7 @@
         far[...] = jnp.zeros_like(far)
         weight_ref[...] = jnp.zeros_like(weight_ref)
         gain_out[...] = jnp.zeros_like(gain_out)
-        group_rows(place_ref, group, pieces)
+        group_halves(place_ref, group, pieces)
 
     here = pl.ds(pl.multiple_of(step_id * LENGTH, LENGTH), LENGTH)
     gmix[...] = dot(group[here, :], wo[...]).astype(BF16)
@@ -260,7 +286,7 @@
 
 def attend_back(places, bias, tokens, gain, weights, projected, mixed, logs, pieces):
     rows, width = tokens.shape
-    tensors = len(pieces)
+    tensors = rows // pieces[0].shape[0]
     piece = whole(pieces[0].shape)
     heads = bias.shape[0]
     inner = heads * HEAD_DIM
@@ -280,7 +306,7 @@
                 by_seq(inner),
                 by_seq(TILE),
             ]
-            + [piece] * tensors,
+            + [whole(p.shape) for p in pieces],
             out_specs=[piece] * tensors
             + [whole((width, 4 * inner)), whole((heads * BUCKETS, 1)), whole((1, width))],
             scratch_shapes=[
@@ -337,11 +363,15 @@
     return total
 
 
-def route_kernel(tensors, tok_ref, *refs):
-    attn_refs = refs[:tensors]
-    gain_ref, router_ref, target_ref, index_ref, kept_ref, hidden_ref, sent_ref, gate_ref = refs[tensors:]
-    hidden = tok_ref[...].astype(F32) + sum_pieces(attn_refs)
-    hidden_ref[...] = hidden
+def route_kernel(tok_ref, *refs):
+    gain_ref, router_ref, target_ref, index_ref, kept_ref, hidden_ref, sent_ref, gate_ref = refs[6:]
+    half = tok_ref.shape[0] // 2
+    for h in range(2):
+        keep, got, last = refs[3 * h : 3 * h + 3]
+        here = slice(h * half, (h + 1) * half)
+        added = keep[:half, :].astype(F32) + got[:half, :].astype(F32) + last[...].astype(F32)
+        hidden_ref[here, :] = tok_ref[here, :].astype(F32) + added
+    hidden = hidden_ref[...]
     unit, _ = unit_rows(hidden)
     moe_in = (unit * gain_ref[...]).astype(BF16)
     count = sent_ref.shape[0]
@@ -357,7 +387,7 @@
 def route(tokens, attn, gain, router, target_row, index_col, kept_col, count):
     rows, width = tokens.shape
     return pl.pallas_call(
-        functools.partial(route_kernel, len(attn)),
+        route_kernel,
         out_shape=[
             jax.ShapeDtypeStruct((rows, width), F32),
             jax.ShapeDtypeStruct((count, width), BF16),
@@ -416,7 +446,11 @@
 
 def group_views(place_ref, ref, tensors, chunks):
     size = ref.shape[1] // chunks
-    return [ref.at[place_ref[2] ^ j, k * size : (k + 1) * size] for k in range(chunks) for j in range(tensors)]
+    views = []
+    for k in range(chunks):
+        a, b = HOPS[k % 2]
+        views += [ref.at[place_ref[2] ^ j, k * size : (k + 1) * size] for j in (0, a, b, a | b)]
+    return views
 
 
 def join_halves(place_ref, own_in, peer_in, own_out, peer_out, win, wout):
@@ -436,10 +470,10 @@
 def expert_kernel(chunks, tensors, main, locals_, rest, place_ref, *refs):
     refs = list(refs)
     take = lambda n: [refs.pop(0) for _ in range(n)]
-    xs = take(chunks * tensors)
+    xs = take(3 * chunks)
     (g_ref,) = take(1)
     own_in, peer_in, own_out, peer_out, router = take(5)
-    back_refs = take(chunks * tensors)
+    backs = take(2 * chunks)
     x_ref, ge_ref, hid_ref, gi_ref, gl_ref = take(5)
     win, wout, grows, inner, gunits, gate_s, dots, back = take(8)
     expert = pl.program_id(0)
@@ -448,6 +482,11 @@
     rows, width = x_ref.shape[1:]
     wide = win.shape[1]
     choice = rest_choice(blocks, locals_, rest, expert)
+    many = xs[0].shape[0]
+    back_refs = []
+    for k in range(chunks):
+        keep, send = backs[2 * k : 2 * k + 2]
+        back_refs += [ref.at[n * many : (n + 1) * many] for n in range(2) for ref in (keep, send)]
     pick_rows(x_ref.at[0], xs, choice, main_rows, main, expert)
     pick_rows(grows, group_views(place_ref, g_ref, tensors, chunks), choice, main_rows, main, expert)
     join_halves(place_ref, own_in, peer_in, own_out, peer_out, win, wout)
@@ -497,20 +536,23 @@
 def expert_forward_back(places, xs, gs, own_in, peer_in, own_out, peer_out, router, main, rest, chunks):
     locals_, half, wide = own_in.shape
     width, experts = router.shape
-    blocks = sum(x.shape[0] for x in xs)
+    many, block = xs[0].shape[:2]
+    tensors = gs.shape[0]
+    blocks = tensors * chunks * many
+    back = (2 * many, block, width)
     rows = blocks * (main + rest)
     per = lambda *shape: pl.BlockSpec((1,) + shape, lambda e, *_: (e, 0, 0))
     saved = jax.ShapeDtypeStruct((locals_, rows, width), BF16)
     saved_wide = jax.ShapeDtypeStruct((locals_, rows, wide), BF16)
     result = pl.pallas_call(
-        functools.partial(expert_kernel, chunks, len(xs) // chunks, main, locals_, rest),
+        functools.partial(expert_kernel, chunks, tensors, main, locals_, rest),
         grid_spec=pltpu.PrefetchScalarGridSpec(
             num_scalar_prefetch=1,
             grid=(locals_,),
             in_specs=[whole(x.shape) for x in xs]
             + [whole(gs.shape)]
             + [per(half, wide)] * 2 + [per(wide, half)] * 2 + [whole((width, experts))],
-            out_specs=[whole(x.shape) for x in xs]
+            out_specs=[whole(back)] * (2 * chunks)
             + [per(rows, width), per(rows, width), per(rows, wide), per(rows, wide), per(rows, experts)],
             scratch_shapes=[
                 pltpu.VMEM((width, wide), BF16),
@@ -523,13 +565,13 @@
                 pltpu.VMEM((rows, width), BF16),
             ],
         ),
-        out_shape=[jax.ShapeDtypeStruct(x.shape, BF16) for x in xs]
+        out_shape=[jax.ShapeDtypeStruct(back, BF16)] * (2 * chunks)
         + [saved, saved, saved_wide, saved_wide, jax.ShapeDtypeStruct((locals_, rows, experts), BF16)],
         compiler_params=params(),
         cost_estimate=cost(6 * locals_ * rows * width * wide, locals_ * rows * width * 14, locals_ * rows * wide),
         name="experts",
     )(places, *xs, gs, own_in, peer_in, own_out, peer_out, router)
-    return result[: len(xs)], result[len(xs) :]
+    return result[: 2 * chunks], result[2 * chunks :]
 
 
 def expert_rows_kernel(chunks, main, locals_, rest, place_ref, hid_ref, own_out, peer_out, forward_ref, wout, value):
@@ -696,6 +738,17 @@
 
 def gather_pieces(value, axis, count):
     return [value] + [swapped(value, axis, count, k) for k in range(1, count)]
+
+
+def gather_hops(value, hops):
+    a, b = hops
+    first = swapped(value, "tensor", 4, a)
+    second = swapped(jnp.concatenate([value, first], axis=0), "tensor", 4, b)
+    return first, second
+
+
+def added(a, b):
+    return (a.astype(F32) + b.astype(F32)).astype(BF16)
 
 
 def swap_pieces(pieces, axis, count):
@@ -796,7 +849,7 @@
 
     late_cotangent, _ = lax.optimization_barrier((cotangent, ring_done))
     grad_rows = jnp.concatenate(over_expert(place(target_row, late_cotangent, count)), axis=0)
-    late_in, late_out, token_pieces = lax.optimization_barrier((w_in, w_out, token_pieces))
+    late_in, late_out, gain_one = lax.optimization_barrier((w_in, w_out, gain_one))
     peer_in = shifted(late_in, "dp", dp_count, 1)
     peer_out = shifted(late_out, "dp", dp_count, 1)
 
@@ -805,56 +858,60 @@
     )
     parts, peer_in, peer_out, grad_rows = lax.optimization_barrier((parts, peer_in, peer_out, grad_rows))
     grad_arrived = lax.all_gather(grad_rows, "tensor", axis=0).reshape(t_count, z_count, block, width)
-    attn = swap_pieces(parts, "tensor", t_count)
+    half_rows = tok_rows // 2
+    attn = []
+    for h, (a, b) in enumerate(HOPS):
+        keep, send = parts[2 * h : 2 * h + 2]
+        got = swapped(send, "tensor", t_count, a)
+        last = swapped(added(keep[half_rows:], got[half_rows:]), "tensor", t_count, b)
+        attn += [keep, got, last]
     hidden_one, sent, gate = route(
         tokens, attn, gain_two, router, target_row, expert_index[:, None], kept_mask[:, None], count
     )
-    arrived = [
-        piece.reshape(many, block, width)
-        for group in over_expert(sent)
-        for piece in gather_pieces(group, "tensor", t_count)
-    ]
+    arrived = []
+    for k, group in enumerate(over_expert(sent)):
+        pieces = (group,) + gather_hops(group, HOPS[k % 2])
+        arrived += [piece.reshape(-1, block, width) for piece in pieces]
     back_parts, saved = expert_forward_back(
         places, arrived, grad_arrived, w_in, peer_in, w_out, peer_out, router, main, rest, chunks
     )
 
-    def summed(pieces):
-        total = pieces[0].astype(F32)
-        for piece in pieces[1:]:
-            total = total + piece.astype(F32)
-        return total.astype(BF16)
-
     size = many * block
-
-    def swap_group(group):
-        joined = [
-            jnp.concatenate([back_parts[k * t_count + j].reshape(size, width) for k in group], axis=0)
-            for j in range(t_count)
-        ]
-        return swap_pieces(joined, "tensor", t_count)
-
-    half = chunks // 2
-    far = swap_group(range(half, chunks))
+    back_parts = [piece.reshape(2 * size, width) for piece in back_parts]
+    keeps, sends = back_parts[::2], back_parts[1::2]
+    got = [swapped(sends[k], "tensor", t_count, HOPS[k % 2][0]) for k in reversed(range(chunks))][::-1]
     forward_part = expert_rows(places, saved[2], w_out, peer_out, grad_arrived.shape, main, rest, chunks)
-    far, forward_part, saved = lax.optimization_barrier((far, forward_part, saved))
-    near = swap_group(range(half))
-    in_own, in_send, out_own, out_send, router_part = expert_weights(places, saved, w_in.shape[1])
-    near, forward_part, in_send, out_send = lax.optimization_barrier((near, forward_part, in_send, out_send))
-    groups = [value[k * size : (k + 1) * size] for value in (summed(near), summed(far)) for k in range(half)]
+    got, forward_part = lax.optimization_barrier((got, forward_part))
+    groups = []
+    for k in range(chunks):
+        last = swapped(added(keeps[k][size:], got[k][size:]), "tensor", t_count, HOPS[k % 2][1])
+        total = keeps[k][:size].astype(F32) + got[k][:size].astype(F32) + last.astype(F32)
+        groups.append(total.astype(BF16))
     grad_back = back_over_expert(groups)
+    forward_part, groups = lax.optimization_barrier((forward_part, groups))
     forward_sum = lax.psum_scatter(
         forward_part.reshape(t_count * z_count * block, width), "tensor", scatter_dimension=0, tiled=True
     )
     grad_hidden, grad_attn, gain_two_part = hidden_back(target_col, grad_back, hidden_one, cotangent, gain_two)
-    grad_w_in = in_own + shifted(in_send, "dp", dp_count, 1).astype(F32)
-    grad_w_out = out_own + shifted(out_send, "dp", dp_count, 1).astype(F32)
-    grad_pieces, grad_w_in, grad_w_out, forward_sum = lax.optimization_barrier(
-        (gather_pieces(grad_attn, "tensor", t_count), grad_w_in, grad_w_out, forward_sum)
-    )
+    grad_attn, saved = lax.optimization_barrier((grad_attn, saved))
+    grad_pieces = [grad_attn]
+    for h, hops in enumerate(HOPS):
+        grad_pieces += list(gather_hops(grad_attn[h * half_rows : (h + 1) * half_rows], hops))
+    in_own, in_send, out_own, out_send, router_part = expert_weights(places, saved, w_in.shape[1])
+    grad_pieces, in_send, out_send, forward_sum = lax.optimization_barrier(
+        (grad_pieces, in_send, out_send, forward_sum)
+    )
+    in_got = shifted(in_send, "dp", dp_count, 1)
+    out_got = shifted(out_send, "dp", dp_count, 1)
     normed_parts, (weight_part, bucket_part, gain_one_part) = attend_back(
         places, bias, group_tokens, gain_one, weights, projected, mixed, logs, grad_pieces
     )
+    normed_parts, weight_part, in_got, out_got = lax.optimization_barrier(
+        (normed_parts, weight_part, in_got, out_got)
+    )
     grad_normed = swap_pieces(normed_parts, "tensor", t_count)
+    grad_w_in = in_own + in_got.astype(F32)
+    grad_w_out = out_own + out_got.astype(F32)
     forward_rows = back_over_expert(list(forward_sum.reshape(chunks, many * block, width)))
     output = output_rows(target_col, forward_rows, hidden_one, gate)
     grad_tokens = tokens_back(tokens, grad_normed, gain_one, grad_hidden)

time: 448 us -> 425 us (0.949)
  waiting for transfers between devices: 187 us -> 166 us
  other arithmetic: 25.5 us -> 20.8 us
    ppermute x58, waiting for transfers between devices: 187 us -> 166 us  [swapped(): return lax.ppermute(value, axis, [(s, s ^ bits) for s in range(count)])]
  transfers between devices with their start and end apart: 65 -> 65, of which waited for: 31 -> 37; matrix products, arithmetic and copies ran while one was open for 9% -> 9% of each run, Pallas kernels for 13% -> 20%
where the time goes in v4:
time: 425 us; the launch traced here: 422 us
  waiting for transfers between devices  166 us (39%)
  Pallas kernels  119 us (28%)
  starting transfers between devices  70.9 us (17%)
  local copies, waits for them, and re-layouts  29.6 us (7%)
  other arithmetic  20.8 us (5%)
  between operations  14.8 us (3%)
    ppermute x58, waiting for transfers between devices, swapped(): return lax.ppermute(value, axis, [(s, s ^ bits) for s in range(count)])  166 us
    ppermute x58, starting transfers between devices, swapped(): return lax.ppermute(value, axis, [(s, s ^ bits) for s in range(count)])  69.8 us
    pallas_call x1, Pallas kernels, expert_forward_back(): pl.pallas_call(functools.partial(expert_kernel, chunks, tensors, main, lo...  34.9 us
    pallas_call x1, Pallas kernels, attend_back(): pl.pallas_call(functools.partial(attend_back_kernel, heads, tensors), gri...  24 us
    pallas_call x1, Pallas kernels, expert_weights(): pl.pallas_call(expert_weights_kernel, grid_spec=pltpu.PrefetchScalarGridS...  17 us
    pallas_call x1, Pallas kernels, attend(): pl.pallas_call(functools.partial(attend_kernel, heads, tensors, len(owned...  15.4 us
    pallas_call x1, Pallas kernels, expert_rows(): pl.pallas_call(functools.partial(expert_rows_kernel, chunks, main, locals...  9.77 us
  transfers between devices with their start and end apart: 65, of which 37 were waited for; matrix products, arithmetic and copies ran while one was open for 9% of the time, Pallas kernels for 20%

profile of v4, /device:TPU:0, one launch (start us, length us, event | category | flops | bytes accessed | tf_op | source)
XLA Modules:
  0.0 421.7 jit_solution(15261023365995697257)
XLA Ops:
  20.8 8.6 %collective-permute-done.4.refs_6_ = bf16[112,768]{1,0:T(8,128)(2,1)} collective-permute-done((bf16[112,768]{1,0:T(8,128)(2,1)S(1)}, bf16[112,768]{1,0:T(8,128)(2,1)}, u32[]{:S(2)}, u32[]{:S(2)}) %collective-permute-start.4) | collective-permute-done | bytes 172064 | tf_op jit(solution)/shard_map/ppermute | solution.py:736
  54.2 7.2 %collective-permute-done.15 = bf16[144,768]{1,0:T(8,128)(2,1)S(1)} collective-permute-done((bf16[144,768]{1,0:T(8,128)(2,1)S(1)}, bf16[144,768]{1,0:T(8,128)(2,1)S(1)}, u32[]{:S(2)}, u32[]{:S(2)}) %collective-permute-start.15) | collective-permute-done | bytes 221216 | tf_op jit(solution)/shard_map/ppermute | solution.py:736
  62.0 8.5 %collective-permute-done.16 = bf16[144,768]{1,0:T(8,128)(2,1)S(1)} collective-permute-done((bf16[144,768]{1,0:T(8,128)(2,1)S(1)}, bf16[144,768]{1,0:T(8,128)(2,1)S(1)}, u32[]{:S(2)}, u32[]{:S(2)}) %collective-permute-start.16) | collective-permute-done | bytes 221216 | tf_op jit(solution)/shard_map/ppermute | solution.py:736
  77.8 15.3 %collective-permute-done.1.refs_2_ = bf16[384,768]{1,0:T(8,128)(2,1)} collective-permute-done((bf16[384,768]{1,0:T(8,128)(2,1)S(1)}, bf16[384,768]{1,0:T(8,128)(2,1)}, u32[]{:S(2)}, u32[]{:S(2)}) %collective-permute-start.1) | collective-permute-done | bytes 589856 | tf_op jit(solution)/shard_map/ppermute | solution.py:736
  93.1 15.4 %attend.1 = (bf16[384,768]{1,0:T(8,128)(2,1)}, bf16[384,768]{1,0:T(8,128)(2,1)}, bf16[384,768]{1,0:T(8,128)(2,1)}, bf16[384,768]{1,0:T(8,128)(2,1)}, bf16[1536,7...) custom-call(s32[4]{0:T(128)} %pad_add_fusion.place_ref, ...), custom_call_target="tpu_custom_call" | custom-call | flops 2415919104 | bytes 9437184 | tf_op jit(solution)/shard_map/attend/pallas_call | solution.py:171
  109.7 9.5 %collective-permute-done.20.refs_4_ = bf16[384,768]{1,0:T(8,128)(2,1)S(1)} collective-permute-done((bf16[384,768]{1,0:T(8,128)(2,1)}, bf16[384,768]{1,0:T(8,128)(2,1)S(1)}, u32[]{:S(2)}, u32[]{:S(2)}) %collective-permute-start.20) | collective-permute-done | bytes 589856 | tf_op jit(solution)/shard_map/ppermute | solution.py:736
  120.6 5.2 %collective-permute-done.18.refs_1_ = bf16[384,768]{1,0:T(8,128)(2,1)S(1)} collective-permute-done((bf16[384,768]{1,0:T(8,128)(2,1)}, bf16[384,768]{1,0:T(8,128)(2,1)S(1)}, u32[]{:S(2)}, u32[]{:S(2)}) %collective-permute-start.18) | collective-permute-done | bytes 589856 | tf_op jit(solution)/shard_map/ppermute | solution.py:736
  130.1 5.2 %collective-permute-done.21.refs_5_ = bf16[192,768]{1,0:T(8,128)(2,1)S(1)} collective-permute-done((bf16[192,768]{1,0:T(8,128)(2,1)S(1)}, bf16[192,768]{1,0:T(8,128)(2,1)S(1)}, u32[]{:S(2)}, u32[]{:S(2)}) %collective-permute-start.21) | collective-permute-done | bytes 294944 | tf_op jit(solution)/shard_map/ppermute | solution.py:736
  143.0 7.1 %collective-permute-start.30 = (bf16[144,768]{1,0:T(8,128)(2,1)S(1)}, bf16[144,768]{1,0:T(8,128)(2,1)S(1)}, u32[]{:S(2)}, u32[]{:S(2)}) collective-permute-start(bf16[144,768]{1,0:T(8,128)(2,1)S(1)} %get-tuple-element.195), channel_id=1, source_target_pairs={{0,12},{4,8},{8,4},{12,0},{1,13},{5,9},{9,5},{13,1},{2,14},{6,10},... | collective-permute-start | bytes 663560 | tf_op jit(solution)/shard_map/ppermute | solution.py:736
  151.4 5.1 %collective-permute-done.30 = bf16[144,768]{1,0:T(8,128)(2,1)S(1)} collective-permute-done((bf16[144,768]{1,0:T(8,128)(2,1)S(1)}, bf16[144,768]{1,0:T(8,128)(2,1)S(1)}, u32[]{:S(2)}, u32[]{:S(2)}) %collective-permute-start.30) | collective-permute-done | bytes 221216 | tf_op jit(solution)/shard_map/ppermute | solution.py:736
  168.8 5.7 %collective-permute-done.28 = bf16[144,768]{1,0:T(8,128)(2,1)S(1)} collective-permute-done((bf16[144,768]{1,0:T(8,128)(2,1)S(1)}, bf16[144,768]{1,0:T(8,128)(2,1)S(1)}, u32[]{:S(2)}, u32[]{:S(2)}) %collective-permute-start.28) | collective-permute-done | bytes 221216 | tf_op jit(solution)/shard_map/ppermute | solution.py:736
  175.4 8.8 %collective-permute-done.25 = bf16[144,768]{1,0:T(8,128)(2,1)S(1)} collective-permute-done((bf16[144,768]{1,0:T(8,128)(2,1)S(1)}, bf16[144,768]{1,0:T(8,128)(2,1)S(1)}, u32[]{:S(2)}, u32[]{:S(2)}) %collective-permute-start.25) | collective-permute-done | bytes 221216 | tf_op jit(solution)/shard_map/ppermute | solution.py:736
  185.9 7.0 %collective-permute-done.29 = bf16[288,768]{1,0:T(8,128)(2,1)S(1)} collective-permute-done((bf16[288,768]{1,0:T(8,128)(2,1)S(1)}, bf16[288,768]{1,0:T(8,128)(2,1)S(1)}, u32[]{:S(2)}, u32[]{:S(2)}) %collective-permute-start.29) | collective-permute-done | bytes 442400 | tf_op jit(solution)/shard_map/ppermute | solution.py:736
  195.5 34.9 %experts.1 = (bf16[2,144,768]{2,1,0:T(8,128)(2,1)}, bf16[2,144,768]{2,1,0:T(8,128)(2,1)}, bf16[2,144,768]{2,1,0:T(8,128)(2,1)}, bf16[2,144,768]{2,1,0:T(8,128)(2...) custom-call(s32[4]{0:T(128)} %pad_add_fusion.place_ref, ...), custom_call_target="tpu_custom_call" | custom-call | flops 8153726976 | bytes 24772608 | tf_op jit(solution)/shard_map/experts/pallas_call | solution.py:547
  234.6 9.8 %expert_rows.1 = bf16[4,4,144,768]{3,2,1,0:T(8,128)(2,1)} custom-call(s32[4]{0:T(128)} %pad_add_fusion.place_ref, bf16[4,576,768]{2,1,0:T(8,128)(2,1)} %get-tuple-element.126.hid_ref, bf16[4,768,384]{2,1,0:T(8,128)(2,1)} %own_out.1, bf16[4,768,384]{2,1,0:T(8,128)(2,1)} %collective-permute-done.14.refs_16_.peer_out), custom_call_target="tpu_custom_call" | custom-call | flops 2717908992 | bytes 10616832 | tf_op jit(solution)/shard_map/expert_rows/pallas_call | solution.py:593
  270.8 9.3 %collective-permute-done.41.refs_2_ = bf16[144,768]{1,0:T(8,128)(2,1)S(1)} collective-permute-done((bf16[144,768]{1,0:T(8,128)(2,1)S(1)}, bf16[144,768]{1,0:T(8,128)(2,1)S(1)}, u32[]{:S(2)}, u32[]{:S(2)}) %collective-permute-start.41) | collective-permute-done | bytes 221216 | tf_op jit(solution)/shard_map/ppermute | solution.py:736
  287.5 7.8 %collective-permute-done.46.refs_3_ = bf16[192,768]{1,0:T(8,128)(2,1)S(1)} collective-permute-done((bf16[192,768]{1,0:T(8,128)(2,1)S(1)}, bf16[192,768]{1,0:T(8,128)(2,1)S(1)}, u32[]{:S(2)}, u32[]{:S(2)}) %collective-permute-start.46) | collective-permute-done | bytes 294944 | tf_op jit(solution)/shard_map/ppermute | solution.py:736
  297.6 17.0 %expert_weights.1 = (f32[4,384,768]{2,1,0:T(8,128)}, bf16[4,384,768]{2,1,0:T(8,128)(2,1)}, f32[4,768,384]{2,1,0:T(8,128)}, bf16[4,768,384]{2,1,0:T(8,128)(2,1)}, f32[768,16]{1,0:T(8,128)}) custom-call(s32[4]{0:T(128)} %pad_add_fusion.place_ref, bf16[4,576,768]{2,1,0:T(8,128)(2,1)} %get-tuple-element.124.x_ref, ...), custom_call_target="tpu_custom_call" | custom-call | flops 5435817984 | bytes 24772608 | tf_op jit(solution)/shard_map/expert_weights/pallas_call | solution.py:632
  314.6 4.8 %collective-permute-done.47.refs_4_ = bf16[384,768]{1,0:T(8,128)(2,1)S(1)} collective-permute-done((bf16[384,768]{1,0:T(8,128)(2,1)S(1)}, bf16[384,768]{1,0:T(8,128)(2,1)S(1)}, u32[]{:S(2)}, u32[]{:S(2)}) %collective-permute-start.47) | collective-permute-done | bytes 589856 | tf_op jit(solution)/shard_map/ppermute | solution.py:736
  322.9 24.0 %attend_back.1 = (bf16[384,768]{1,0:T(8,128)(2,1)}, bf16[384,768]{1,0:T(8,128)(2,1)}, bf16[384,768]{1,0:T(8,128)(2,1)}, bf16[384,768]{1,0:T(8,128)(2,1)}, f32[76...) custom-call(s32[4]{0:T(128)} %pad_add_fusion.place_ref, f32[3,32]{1,0:T(4,128)} %convert_element_type.201.bias_ref, ...), custom_call_target="tpu_custom_call" | custom-call | flops 5586812928 | bytes 14155776 | tf_op jit(solution)/shard_map/attend_back/pallas_call | solution.py:295
  356.5 6.4 %collective-permute-done.48.refs_1_ = bf16[144,768]{1,0:T(8,128)(2,1)} collective-permute-done((bf16[144,768]{1,0:T(8,128)(2,1)}, bf16[144,768]{1,0:T(8,128)(2,1)}, u32[]{:S(2)}, u32[]{:S(2)}) %collective-permute-start.48) | collective-permute-done | bytes 221216 | tf_op jit(solution)/shard_map/ppermute | solution.py:736
  362.8 9.0 %collective-permute-done.49.refs_2_ = bf16[144,768]{1,0:T(8,128)(2,1)} collective-permute-done((bf16[144,768]{1,0:T(8,128)(2,1)}, bf16[144,768]{1,0:T(8,128)(2,1)}, u32[]{:S(2)}, u32[]{:S(2)}) %collective-permute-start.49) | collective-permute-done | bytes 221216 | tf_op jit(solution)/shard_map/ppermute | solution.py:736
  378.7 5.8 %convert_add_fusion = f32[4,768,384]{2,1,0:T(8,128)} fusion(f32[4,768,384]{2,1,0:T(8,128)} %get-tuple-element.164, bf16[4,768,384]{2,1,0:T(8,128)(2,1)} %collective-permute-done.52), kind=kLoop, calls=%fused_computation.1 | loop fusion | flops 2359296 | bytes 11796480 | tf_op jit(solution)/shard_map/add | solution.py:914
  393.9 4.5 %convert_add_fusion.1 = f32[4,384,768]{2,1,0:T(8,128)} fusion(f32[4,384,768]{2,1,0:T(8,128)S(1)} %bitcast.97, bf16[4,384,768]{2,1,0:T(8,128)(2,1)} %collective-permute-done.51), kind=kLoop, calls=%fused_computation.2 | loop fusion | flops 2359296 | bytes 11796480 | tf_op jit(solution)/shard_map/add | solution.py:913
  (321 shorter events, 165.2 us)
Async XLA Ops:
  7.2 187.5 %all-gather.3.cloned.1.call-start = ((), (), s32[]{:S(2)}) async-start(), calls=%async_computation.2 | async-start | bytes 4423680 | tf_op jit(solution)/shard_map/all_gather | solution.py:860
  44.3 64.2 %collective-permute-start.13 = (bf16[4,384,768]{2,1,0:T(8,128)(2,1)}, bf16[4,384,768]{2,1,0:T(8,128)(2,1)}, u32[]{:S(2)}, u32[]{:S(2)}) collective-permute-start(bf16[4,384,768]{2,1,0:T(8,128)(2,1)} %refs_13_.1), channel_id=1, source_target_pairs={{0,16},{16,0},{1,17},{17,1},{2,18},{18,2},{3,19},{19,3},{4,20},{20... | collective-permute-start | bytes 7077896 | tf_op jit(solution)/shard_map/ppermute | solution.py:726
  44.3 64.2 %collective-permute-start.14 = (bf16[4,768,384]{2,1,0:T(8,128)(2,1)S(1)}, bf16[4,768,384]{2,1,0:T(8,128)(2,1)}, u32[]{:S(2)}, u32[]{:S(2)}) collective-permute-start(bf16[4,768,384]{2,1,0:T(8,128)(2,1)S(1)} %copy-done.2), channel_id=1, source_target_pairs={{0,16},{16,0},{1,17},{17,1},{2,18},{18,2},{3,19},{19,3},{4,20},{20... | collective-permute-start | bytes 7077896 | tf_op jit(solution)/shard_map/ppermute | solution.py:726
  51.7 18.7 %collective-permute-start.16 = (bf16[144,768]{1,0:T(8,128)(2,1)S(1)}, bf16[144,768]{1,0:T(8,128)(2,1)S(1)}, u32[]{:S(2)}, u32[]{:S(2)}) collective-permute-start(bf16[144,768]{1,0:T(8,128)(2,1)S(1)} %get-tuple-element.202), channel_id=1, source_target_pairs={{0,8},{4,12},{8,0},{12,4},{1,9},{5,13},{9,1},{13,5},{2,10},{6,14},... | collective-permute-start | bytes 663560 | tf_op jit(solution)/shard_map/ppermute | solution.py:736
  52.8 18.1 %collective-permute-start.17 = (bf16[144,768]{1,0:T(8,128)(2,1)S(1)}, bf16[144,768]{1,0:T(8,128)(2,1)S(1)}, u32[]{:S(2)}, u32[]{:S(2)}) collective-permute-start(bf16[144,768]{1,0:T(8,128)(2,1)S(1)} %get-tuple-element.201), channel_id=1, source_target_pairs={{0,12},{4,8},{8,4},{12,0},{1,13},{5,9},{9,5},{13,1},{2,14},{6,10},... | collective-permute-start | bytes 663560 | tf_op jit(solution)/shard_map/ppermute | solution.py:736
  70.5 22.6 %collective-permute-start.1 = (bf16[384,768]{1,0:T(8,128)(2,1)S(1)}, bf16[384,768]{1,0:T(8,128)(2,1)}, u32[]{:S(2)}, u32[]{:S(2)}) collective-permute-start(bf16[384,768]{1,0:T(8,128)(2,1)S(1)} %copy-done.1), channel_id=1, source_target_pairs={{0,2},{1,3},{2,0},{3,1},{4,6},{5,7},{6,4},{7,5},{8,10},{9,11},{10,... | collective-permute-start | bytes 1769480 | tf_op jit(solution)/shard_map/ppermute | solution.py:736
  71.0 22.1 %collective-permute-start.2 = (bf16[384,768]{1,0:T(8,128)(2,1)S(1)}, bf16[384,768]{1,0:T(8,128)(2,1)}, u32[]{:S(2)}, u32[]{:S(2)}) collective-permute-start(bf16[384,768]{1,0:T(8,128)(2,1)S(1)} %copy-done.1), channel_id=1, source_target_pairs={{0,3},{1,2},{2,1},{3,0},{4,7},{5,6},{6,5},{7,4},{8,11},{9,10},{10,... | collective-permute-start | bytes 1769480 | tf_op jit(solution)/shard_map/ppermute | solution.py:736
  108.5 212.5 %reduce-scatter.2.cloned.1.call-start = ((), (), s32[]{:S(2)}) async-start(), calls=%async_computation.1 | async-start | bytes 4423680 | tf_op jit(solution)/shard_map/reduce_scatter | solution.py:892
  163.1 22.8 %collective-permute-start.23 = (bf16[288,768]{1,0:T(8,128)(2,1)S(1)}, bf16[288,768]{1,0:T(8,128)(2,1)S(1)}, u32[]{:S(2)}, u32[]{:S(2)}) collective-permute-start(bf16[288,768]{1,0:T(8,128)(2,1)S(1)} %pad_maximum_fusion.3), channel_id=1, source_target_pairs={{0,2},{1,3},{2,0},{3,1},{4,6},{5,7},{6,4},{7,5},{8,10},{9,11},{10,... | collective-permute-start | bytes 1327112 | tf_op jit(solution)/shard_map/ppermute | solution.py:736
  163.8 20.5 %collective-permute-start.25 = (bf16[144,768]{1,0:T(8,128)(2,1)S(1)}, bf16[144,768]{1,0:T(8,128)(2,1)S(1)}, u32[]{:S(2)}, u32[]{:S(2)}) collective-permute-start(bf16[144,768]{1,0:T(8,128)(2,1)S(1)} %collective-permute-done.24), channel_id=1, source_target_pairs={{0,2},{1,3},{2,0},{3,1},{4,6},{5,7},{6,4},{7,5},{8,10},{9,11},{10,... | collective-permute-start | bytes 663560 | tf_op jit(solution)/shard_map/ppermute | solution.py:736
  168.0 17.8 %collective-permute-start.32 = (bf16[288,768]{1,0:T(8,128)(2,1)S(1)}, bf16[288,768]{1,0:T(8,128)(2,1)S(1)}, u32[]{:S(2)}, u32[]{:S(2)}) collective-permute-start(bf16[288,768]{1,0:T(8,128)(2,1)S(1)} %pad_maximum_fusion.6), channel_id=1, source_target_pairs={{0,1},{1,0},{2,3},{3,2},{4,5},{5,4},{6,7},{7,6},{8,9},{9,8},{10,11... | collective-permute-start | bytes 1327112 | tf_op jit(solution)/shard_map/ppermute | solution.py:736
  174.5 18.3 %collective-permute-start.29 = (bf16[288,768]{1,0:T(8,128)(2,1)S(1)}, bf16[288,768]{1,0:T(8,128)(2,1)S(1)}, u32[]{:S(2)}, u32[]{:S(2)}) collective-permute-start(bf16[288,768]{1,0:T(8,128)(2,1)S(1)} %pad_maximum_fusion.5), channel_id=1, source_target_pairs={{0,2},{1,3},{2,0},{3,1},{4,6},{5,7},{6,4},{7,5},{8,10},{9,11},{10,... | collective-permute-start | bytes 1327112 | tf_op jit(solution)/shard_map/ppermute | solution.py:736
  232.3 17.5 %collective-permute-start.35 = (bf16[288,768]{1,0:T(8,128)(2,1)}, bf16[288,768]{1,0:T(8,128)(2,1)S(1)}, u32[]{:S(2)}, u32[]{:S(2)}) collective-permute-start(bf16[288,768]{1,0:T(8,128)(2,1)} %bitcast.128), channel_id=1, source_target_pairs={{0,1},{1,0},{2,3},{3,2},{4,5},{5,4},{6,7},{7,6},{8,9},{9,8},{10,11... | collective-permute-start | bytes 1327112 | tf_op jit(solution)/shard_map/ppermute | solution.py:736
  232.7 18.7 %collective-permute-start.36 = (bf16[288,768]{1,0:T(8,128)(2,1)}, bf16[288,768]{1,0:T(8,128)(2,1)S(1)}, u32[]{:S(2)}, u32[]{:S(2)}) collective-permute-start(bf16[288,768]{1,0:T(8,128)(2,1)} %bitcast.127), channel_id=1, source_target_pairs={{0,2},{1,3},{2,0},{3,1},{4,6},{5,7},{6,4},{7,5},{8,10},{9,11},{10,... | collective-permute-start | bytes 1327112 | tf_op jit(solution)/shard_map/ppermute | solution.py:736
  295.4 24.0 %collective-permute-start.47 = (bf16[384,768]{1,0:T(8,128)(2,1)S(1)}, bf16[384,768]{1,0:T(8,128)(2,1)S(1)}, u32[]{:S(2)}, u32[]{:S(2)}) collective-permute-start(bf16[384,768]{1,0:T(8,128)(2,1)S(1)} %pad_maximum_fusion.2), channel_id=1, source_target_pairs={{0,1},{1,0},{2,3},{3,2},{4,5},{5,4},{6,7},{7,6},{8,9},{9,8},{10,11... | collective-permute-start | bytes 1769480 | tf_op jit(solution)/shard_map/ppermute | solution.py:736
  297.0 24.0 %collective-permute-start.45 = (bf16[384,768]{1,0:T(8,128)(2,1)S(1)}, bf16[384,768]{1,0:T(8,128)(2,1)S(1)}, u32[]{:S(2)}, u32[]{:S(2)}) collective-permute-start(bf16[384,768]{1,0:T(8,128)(2,1)S(1)} %pad_maximum_fusion.1), channel_id=1, source_target_pairs={{0,2},{1,3},{2,0},{3,1},{4,6},{5,7},{6,4},{7,5},{8,10},{9,11},{10,... | collective-permute-start | bytes 1769480 | tf_op jit(solution)/shard_map/ppermute | solution.py:736
  321.1 34.5 %collective-permute-start.51 = (bf16[4,384,768]{2,1,0:T(8,128)(2,1)}, bf16[4,384,768]{2,1,0:T(8,128)(2,1)}, u32[]{:S(2)}, u32[]{:S(2)}) collective-permute-start(bf16[4,384,768]{2,1,0:T(8,128)(2,1)} %get-tuple-element.150), channel_id=1, source_target_pairs={{0,16},{16,0},{1,17},{17,1},{2,18},{18,2},{3,19},{19,3},{4,20},{20... | collective-permute-start | bytes 7077896 | tf_op jit(solution)/shard_map/ppermute | solution.py:726
  321.1 34.4 %collective-permute-start.52 = (bf16[4,768,384]{2,1,0:T(8,128)(2,1)}, bf16[4,768,384]{2,1,0:T(8,128)(2,1)}, u32[]{:S(2)}, u32[]{:S(2)}) collective-permute-start(bf16[4,768,384]{2,1,0:T(8,128)(2,1)} %get-tuple-element.151), channel_id=1, source_target_pairs={{0,16},{16,0},{1,17},{17,1},{2,18},{18,2},{3,19},{19,3},{4,20},{20... | collective-permute-start | bytes 7077896 | tf_op jit(solution)/shard_map/ppermute | solution.py:726
  352.8 19.0 %collective-permute-start.49 = (bf16[144,768]{1,0:T(8,128)(2,1)}, bf16[144,768]{1,0:T(8,128)(2,1)}, u32[]{:S(2)}, u32[]{:S(2)}) collective-permute-start(bf16[144,768]{1,0:T(8,128)(2,1)} %get-tuple-element.192), channel_id=1, source_target_pairs={{0,8},{4,12},{8,0},{12,4},{1,9},{5,13},{9,1},{13,5},{2,10},{6,14},... | collective-permute-start | bytes 663560 | tf_op jit(solution)/shard_map/ppermute | solution.py:736
  356.5 28.0 %collective-permute-start.56 = (bf16[4,112,768]{2,1,0:T(8,128)(2,1)}, bf16[4,112,768]{2,1,0:T(8,128)(2,1)S(1)}, u32[]{:S(2)}, u32[]{:S(2)}) collective-permute-start(bf16[4,112,768]{2,1,0:T(8,128)(2,1)} %fusion.5), channel_id=1, source_target_pairs={{0,16},{16,0},{1,17},{17,1},{2,18},{18,2},{3,19},{19,3},{4,20},{20... | collective-permute-start | bytes 2064392 | tf_op jit(solution)/shard_map/ppermute | solution.py:726
  376.1 25.8 %collective-permute-start.54 = (bf16[384,768]{1,0:T(8,128)(2,1)}, bf16[384,768]{1,0:T(8,128)(2,1)S(1)}, u32[]{:S(2)}, u32[]{:S(2)}) collective-permute-start(bf16[384,768]{1,0:T(8,128)(2,1)} %get-tuple-element.154), channel_id=1, source_target_pairs={{0,2},{1,3},{2,0},{3,1},{4,6},{5,7},{6,4},{7,5},{8,10},{9,11},{10,... | collective-permute-start | bytes 1769480 | tf_op jit(solution)/shard_map/ppermute | solution.py:736
  376.7 25.1 %collective-permute-start.55 = (bf16[384,768]{1,0:T(8,128)(2,1)S(1)}, bf16[384,768]{1,0:T(8,128)(2,1)S(1)}, u32[]{:S(2)}, u32[]{:S(2)}) collective-permute-start(bf16[384,768]{1,0:T(8,128)(2,1)S(1)} %copy-done.34), channel_id=1, source_target_pairs={{0,3},{1,2},{2,1},{3,0},{4,7},{5,6},{6,5},{7,4},{8,11},{9,10},{10,... | collective-permute-start | bytes 1769480 | tf_op jit(solution)/shard_map/ppermute | solution.py:736
  384.7 22.1 %collective-permute-start.57 = (bf16[112,768]{1,0:T(8,128)(2,1)S(1)}, bf16[112,768]{1,0:T(8,128)(2,1)S(1)}, u32[]{:S(2)}, u32[]{:S(2)}) collective-permute-start(bf16[112,768]{1,0:T(8,128)(2,1)S(1)} %get-tuple-element.188), channel_id=1, source_target_pairs={{0,4},{4,0},{8,12},{12,8},{1,5},{5,1},{9,13},{13,9},{2,6},{6,2},{1... | collective-permute-start | bytes 516104 | tf_op jit(solution)/shard_map/ppermute | solution.py:736
  388.9 17.9 %collective-permute-start.58 = (bf16[112,768]{1,0:T(8,128)(2,1)S(1)}, bf16[112,768]{1,0:T(8,128)(2,1)S(1)}, u32[]{:S(2)}, u32[]{:S(2)}) collective-permute-start(bf16[112,768]{1,0:T(8,128)(2,1)S(1)} %get-tuple-element.190), channel_id=1, source_target_pairs={{0,8},{4,12},{8,0},{12,4},{1,9},{5,13},{9,1},{13,5},{2,10},{6,14},... | collective-permute-start | bytes 516104 | tf_op jit(solution)/shard_map/ppermute | solution.py:736
  (84 other events, 1185.0 us)
Sparse Core Ops, SparseCore 0:
  108.7 66.3 all-gather.2
  261.4 59.6 reduce-scatter.1

commit v5 on v4

--- a/solution.py
+++ b/solution.py
@@ -334,6 +334,26 @@
     return result[:tensors], result[tensors:]
 
 
+def first_rows_kernel(count, *refs):
+    out_ref = refs[-1]
+    for k, ref in enumerate(refs[:-1]):
+        out_ref[k] = ref[:count, :]
+
+
+def first_rows(pieces, start, extra, count):
+    width = pieces[0].shape[1]
+    return pl.pallas_call(
+        functools.partial(first_rows_kernel, count),
+        grid=(1,),
+        in_specs=[pl.BlockSpec((extra, width), lambda i: (start // extra, 0))] * len(pieces),
+        out_specs=whole((len(pieces), count, width)),
+        out_shape=jax.ShapeDtypeStruct((len(pieces), count, width), BF16),
+        compiler_params=params(),
+        cost_estimate=cost(0, 4 * len(pieces) * extra * width),
+        name="first_rows",
+    )(*pieces)
+
+
 def place_kernel(target_ref, rows_ref, out_ref):
     count = out_ref.shape[0]
     rows = lax.broadcasted_iota(jnp.int32, (count, rows_ref.shape[0]), 0)
@@ -794,6 +814,7 @@
     token_pieces = gather_pieces(tokens, "tensor", t_count)
 
     small = jnp.concatenate([gain_attn[:, None], gain_moe[:, None], w_router], axis=1).reshape(-1)
+    small = jnp.concatenate(gather_pieces(small, "tensor", t_count))
     extra = -(-small.shape[0] // (16 * width)) * 16
     packed = jnp.concatenate(
         [
@@ -806,13 +827,16 @@
         [packed, jnp.pad(small, (0, extra * width - small.shape[0])).reshape(extra, width)], axis=0
     )
     owned = gather_pieces(packed, "expert", z_count)
-    ring_done = owned
+    token_pieces, owned = lax.optimization_barrier((token_pieces, owned))
     owned = owned + [swapped(piece, "dp", dp_count, 1) for piece in owned]
-    smalls = jnp.stack([piece[part:].reshape(-1)[: small.shape[0]] for piece in owned])
-    smalls = jnp.stack(gather_pieces(smalls, "tensor", t_count)).reshape(t_count * owners, -1)
+    if part % 16 or part % extra:
+        smalls = jnp.stack([piece[part:] for piece in owned])
+    else:
+        smalls = first_rows(owned, part, extra, -(-small.shape[0] // width))
+    smalls = smalls.reshape(owners, -1)[:, : small.shape[0]].reshape(owners * t_count, -1)
     owner_ids = jnp.arange(owners, dtype=jnp.int32)[:, None] ^ my_owner
     t_ids = jnp.arange(t_count, dtype=jnp.int32)[None, :] ^ my_t
-    smalls = smalls[(t_ids * owners + owner_ids).reshape(-1)].reshape(width, 2 + experts_all)
+    smalls = smalls[(owner_ids * t_count + t_ids).reshape(-1)].reshape(width, 2 + experts_all)
     if part % 16:
         order = jnp.arange(owners, dtype=jnp.int32) ^ my_owner
         owned = [jnp.stack([piece[:part] for piece in owned])[order].reshape(width, 4 * inner)]
@@ -847,9 +871,10 @@
             return pieces
         return [jnp.concatenate(pieces[k * many : (k + 1) * many], axis=0) for k in range(chunks)]
 
-    late_cotangent, _ = lax.optimization_barrier((cotangent, ring_done))
+    late_cotangent, late_in, late_out, token_pieces, owned, gain_one = lax.optimization_barrier(
+        (cotangent, w_in, w_out, token_pieces, owned, gain_one)
+    )
     grad_rows = jnp.concatenate(over_expert(place(target_row, late_cotangent, count)), axis=0)
-    late_in, late_out, gain_one = lax.optimization_barrier((w_in, w_out, gain_one))
     peer_in = shifted(late_in, "dp", dp_count, 1)
     peer_out = shifted(late_out, "dp", dp_count, 1)
 
@@ -906,13 +931,13 @@
     normed_parts, (weight_part, bucket_part, gain_one_part) = attend_back(
         places, bias, group_tokens, gain_one, weights, projected, mixed, logs, grad_pieces
     )
-    normed_parts, weight_part, in_got, out_got = lax.optimization_barrier(
-        (normed_parts, weight_part, in_got, out_got)
+    forward_rows = back_over_expert(list(forward_sum.reshape(chunks, many * block, width)))
+    normed_parts, weight_part, in_got, out_got, forward_rows = lax.optimization_barrier(
+        (normed_parts, weight_part, in_got, out_got, forward_rows)
     )
     grad_normed = swap_pieces(normed_parts, "tensor", t_count)
     grad_w_in = in_own + in_got.astype(F32)
     grad_w_out = out_own + out_got.astype(F32)
-    forward_rows = back_over_expert(list(forward_sum.reshape(chunks, many * block, width)))
     output = output_rows(target_col, forward_rows, hidden_one, gate)
     grad_tokens = tokens_back(tokens, grad_normed, gain_one, grad_hidden)
 

time: 425 us -> 394 us (0.927)
  waiting for transfers between devices: 166 us -> 130 us
  starting transfers between devices: 70.9 us -> 80.8 us
    ppermute x58, waiting for transfers between devices: 166 us -> 130 us  [swapped(): return lax.ppermute(value, axis, [(s, s ^ bits) for s in range(count)])]
    ppermute x58, starting transfers between devices: 69.8 us -> 79.7 us  [swapped(): return lax.ppermute(value, axis, [(s, s ^ bits) for s in range(count)])]
    unnamed x90 -> x99, local copies, waits for them, and re-layouts: 7.31 us -> 9.01 us
  transfers between devices with their start and end apart: 65 -> 65, of which waited for: 37 -> 33; matrix products, arithmetic and copies ran while one was open for 9% -> 8% of each run, Pallas kernels for 20% -> 21%
where the time goes in v5:
time: 394 us; the launch traced here: 393 us
  waiting for transfers between devices  130 us (33%)
  Pallas kernels  120 us (30%)
  starting transfers between devices  80.8 us (21%)
  local copies, waits for them, and re-layouts  27.3 us (7%)
  other arithmetic  19 us (5%)
  between operations  14.7 us (4%)
    ppermute x58, waiting for transfers between devices, swapped(): return lax.ppermute(value, axis, [(s, s ^ bits) for s in range(count)])  130 us
    ppermute x58, starting transfers between devices, swapped(): return lax.ppermute(value, axis, [(s, s ^ bits) for s in range(count)])  79.7 us
    pallas_call x1, Pallas kernels, expert_forward_back(): pl.pallas_call(functools.partial(expert_kernel, chunks, tensors, main, lo...  35 us
    pallas_call x1, Pallas kernels, attend_back(): pl.pallas_call(functools.partial(attend_back_kernel, heads, tensors), gri...  24 us
    pallas_call x1, Pallas kernels, expert_weights(): pl.pallas_call(expert_weights_kernel, grid_spec=pltpu.PrefetchScalarGridS...  16.4 us
    pallas_call x1, Pallas kernels, attend(): pl.pallas_call(functools.partial(attend_kernel, heads, tensors, len(owned...  15.4 us
    pallas_call x1, Pallas kernels, expert_rows(): pl.pallas_call(functools.partial(expert_rows_kernel, chunks, main, locals...  9.8 us
    unnamed x99, local copies, waits for them, and re-layouts  9.01 us
  transfers between devices with their start and end apart: 65, of which 33 were waited for; matrix products, arithmetic and copies ran while one was open for 8% of the time, Pallas kernels for 21%

profile of v5, /device:TPU:0, one launch (start us, length us, event | category | flops | bytes accessed | tf_op | source)
XLA Modules:
  0.0 392.9 jit_solution(14045930534375617074)
XLA Ops:
  17.5 19.0 %collective-permute-done.3 = bf16[432]{0:T(512)(128)(2,1)S(1)} collective-permute-done((bf16[432]{0:T(512)(128)(2,1)S(1)}, bf16[432]{0:T(512)(128)(2,1)S(1)}, u32[]{:S(2)}, u32[]{:S(2)}) %collective-permute-start.3) | collective-permute-done | bytes 896 | tf_op jit(solution)/shard_map/ppermute | solution.py:756
  48.1 3.8 collective-permute-start.8
  52.0 5.2 %collective-permute-done.7.refs_2_.refs_6_ = bf16[112,768]{1,0:T(8,128)(2,1)S(1)} collective-permute-done((bf16[112,768]{1,0:T(8,128)(2,1)S(1)}, bf16[112,768]{1,0:T(8,128)(2,1)S(1)}, u32[]{:S(2)}, u32[]{:S(2)}) %collective-permute-start.7) | collective-permute-done | bytes 172064 | tf_op jit(solution)/shard_map/ppermute | solution.py:756
  75.9 15.4 %attend.1 = (bf16[384,768]{1,0:T(8,128)(2,1)}, bf16[384,768]{1,0:T(8,128)(2,1)}, bf16[384,768]{1,0:T(8,128)(2,1)}, bf16[384,768]{1,0:T(8,128)(2,1)}, bf16[1536,7...) custom-call(s32[4]{0:T(128)} %pad_add_fusion.place_ref, ...), custom_call_target="tpu_custom_call" | custom-call | flops 2415919104 | bytes 9437184 | tf_op jit(solution)/shard_map/attend/pallas_call | solution.py:171
  96.3 13.9 %collective-permute-done.20.refs_4_ = bf16[384,768]{1,0:T(8,128)(2,1)S(1)} collective-permute-done((bf16[384,768]{1,0:T(8,128)(2,1)}, bf16[384,768]{1,0:T(8,128)(2,1)S(1)}, u32[]{:S(2)}, u32[]{:S(2)}) %collective-permute-start.20) | collective-permute-done | bytes 589856 | tf_op jit(solution)/shard_map/ppermute | solution.py:756
  118.4 6.2 %collective-permute-done.21.refs_5_ = bf16[192,768]{1,0:T(8,128)(2,1)S(1)} collective-permute-done((bf16[192,768]{1,0:T(8,128)(2,1)S(1)}, bf16[192,768]{1,0:T(8,128)(2,1)S(1)}, u32[]{:S(2)}, u32[]{:S(2)}) %collective-permute-start.21) | collective-permute-done | bytes 294944 | tf_op jit(solution)/shard_map/ppermute | solution.py:756
  126.1 4.3 %route.1 = (f32[384,768]{1,0:T(8,128)}, bf16[576,768]{1,0:T(8,128)(2,1)}, f32[384,1]{1,0:T(8,128)}) custom-call(bf16[384,768]{1,0:T(8,128)(2,1)} %tok_ref.3, bf16[384,768]{1,0:T(8,128)(2,1)} %get-tuple-element.145.refs_0_, bf16[384,768]{1,0:T(8,128)(2,1)} %copy-done.4, bf16[192,768]{1,0:T(8,128)(2,1)} %copy-done.12, ...), custom_call_target="tpu_custom_call" | custom-call | flops 339738624 | bytes 3538944 | tf_op jit(solution)/shard_map/route/pallas_call | solution.py:409
  135.0 3.9 collective-permute-start.27
  142.1 12.0 %collective-permute-done.27 = bf16[144,768]{1,0:T(8,128)(2,1)S(1)} collective-permute-done((bf16[144,768]{1,0:T(8,128)(2,1)S(1)}, bf16[144,768]{1,0:T(8,128)(2,1)S(1)}, u32[]{:S(2)}, u32[]{:S(2)}) %collective-permute-start.27) | collective-permute-done | bytes 221216 | tf_op jit(solution)/shard_map/ppermute | solution.py:756
  158.3 4.1 %collective-permute-done.28 = bf16[144,768]{1,0:T(8,128)(2,1)S(1)} collective-permute-done((bf16[144,768]{1,0:T(8,128)(2,1)S(1)}, bf16[144,768]{1,0:T(8,128)(2,1)S(1)}, u32[]{:S(2)}, u32[]{:S(2)}) %collective-permute-start.28) | collective-permute-done | bytes 221216 | tf_op jit(solution)/shard_map/ppermute | solution.py:756
  162.7 10.5 %collective-permute-done.25 = bf16[144,768]{1,0:T(8,128)(2,1)S(1)} collective-permute-done((bf16[144,768]{1,0:T(8,128)(2,1)S(1)}, bf16[144,768]{1,0:T(8,128)(2,1)S(1)}, u32[]{:S(2)}, u32[]{:S(2)}) %collective-permute-start.25) | collective-permute-done | bytes 221216 | tf_op jit(solution)/shard_map/ppermute | solution.py:756
  174.2 6.7 %collective-permute-done.29 = bf16[288,768]{1,0:T(8,128)(2,1)S(1)} collective-permute-done((bf16[288,768]{1,0:T(8,128)(2,1)S(1)}, bf16[288,768]{1,0:T(8,128)(2,1)S(1)}, u32[]{:S(2)}, u32[]{:S(2)}) %collective-permute-start.29) | collective-permute-done | bytes 442400 | tf_op jit(solution)/shard_map/ppermute | solution.py:756
  182.6 35.0 %experts.1 = (bf16[2,144,768]{2,1,0:T(8,128)(2,1)}, bf16[2,144,768]{2,1,0:T(8,128)(2,1)}, bf16[2,144,768]{2,1,0:T(8,128)(2,1)}, bf16[2,144,768]{2,1,0:T(8,128)(2...) custom-call(s32[4]{0:T(128)} %pad_add_fusion.place_ref, ...), custom_call_target="tpu_custom_call" | custom-call | flops 8153726976 | bytes 24772608 | tf_op jit(solution)/shard_map/experts/pallas_call | solution.py:567
  221.7 9.8 %expert_rows.1 = bf16[4,4,144,768]{3,2,1,0:T(8,128)(2,1)} custom-call(s32[4]{0:T(128)} %pad_add_fusion.place_ref, bf16[4,576,768]{2,1,0:T(8,128)(2,1)} %get-tuple-element.175.hid_ref, bf16[4,768,384]{2,1,0:T(8,128)(2,1)} %own_out.1, bf16[4,768,384]{2,1,0:T(8,128)(2,1)} %collective-permute-done.14.refs_16_.peer_out), custom_call_target="tpu_custom_call" | custom-call | flops 2717908992 | bytes 10616832 | tf_op jit(solution)/shard_map/expert_rows/pallas_call | solution.py:613
  232.2 4.7 %collective-permute-done.35 = bf16[288,768]{1,0:T(8,128)(2,1)S(1)} collective-permute-done((bf16[288,768]{1,0:T(8,128)(2,1)}, bf16[288,768]{1,0:T(8,128)(2,1)S(1)}, u32[]{:S(2)}, u32[]{:S(2)}) %collective-permute-start.35) | collective-permute-done | bytes 442400 | tf_op jit(solution)/shard_map/ppermute | solution.py:756
  253.3 4.4 %collective-permute-done.43.refs_3_ = bf16[144,768]{1,0:T(8,128)(2,1)S(1)} collective-permute-done((bf16[144,768]{1,0:T(8,128)(2,1)S(1)}, bf16[144,768]{1,0:T(8,128)(2,1)S(1)}, u32[]{:S(2)}, u32[]{:S(2)}) %collective-permute-start.43) | collective-permute-done | bytes 221216 | tf_op jit(solution)/shard_map/ppermute | solution.py:756
  257.7 6.9 %collective-permute-done.41.refs_2_ = bf16[144,768]{1,0:T(8,128)(2,1)S(1)} collective-permute-done((bf16[144,768]{1,0:T(8,128)(2,1)S(1)}, bf16[144,768]{1,0:T(8,128)(2,1)S(1)}, u32[]{:S(2)}, u32[]{:S(2)}) %collective-permute-start.41) | collective-permute-done | bytes 221216 | tf_op jit(solution)/shard_map/ppermute | solution.py:756
  265.4 4.3 %hidden_back.1 = (f32[384,768]{1,0:T(8,128)}, bf16[384,768]{1,0:T(8,128)(2,1)}, f32[1,768]{1,0:T(1,128)}) custom-call(s32[384,1]{1,0:T(8,128)} %broadcast_in_dim.40.target_ref, bf16[144,768]{1,0:T(8,128)(2,1)} %fusion.17.refs_0_, bf16[144,768]{1,0:T(8,128)(2,1)} %copy-done.20, bf16[144,768]{1,0:T(8,128)(2,1)} %copy-done.19, bf16[144,768]{1,0:T(8,128)(2,1)} %copy-done.18, ...), custom_call_target="tpu_custom_call" | custom-call | flops 339738624 | bytes 4718592 | tf_op jit(solution)/shard_map/hidden_back/pallas_call | solution.py:699
  272.4 8.7 %collective-permute-done.46.refs_3_ = bf16[192,768]{1,0:T(8,128)(2,1)S(1)} collective-permute-done((bf16[192,768]{1,0:T(8,128)(2,1)S(1)}, bf16[192,768]{1,0:T(8,128)(2,1)S(1)}, u32[]{:S(2)}, u32[]{:S(2)}) %collective-permute-start.46) | collective-permute-done | bytes 294944 | tf_op jit(solution)/shard_map/ppermute | solution.py:756
  283.4 16.4 %expert_weights.1 = (f32[4,384,768]{2,1,0:T(8,128)}, bf16[4,384,768]{2,1,0:T(8,128)(2,1)}, f32[4,768,384]{2,1,0:T(8,128)}, bf16[4,768,384]{2,1,0:T(8,128)(2,1)}, f32[768,16]{1,0:T(8,128)}) custom-call(s32[4]{0:T(128)} %pad_add_fusion.place_ref, bf16[4,576,768]{2,1,0:T(8,128)(2,1)} %get-tuple-element.173.x_ref, ...), custom_call_target="tpu_custom_call" | custom-call | flops 5435817984 | bytes 24772608 | tf_op jit(solution)/shard_map/expert_weights/pallas_call | solution.py:652
  299.8 4.8 %collective-permute-done.47.refs_4_ = bf16[384,768]{1,0:T(8,128)(2,1)S(1)} collective-permute-done((bf16[384,768]{1,0:T(8,128)(2,1)S(1)}, bf16[384,768]{1,0:T(8,128)(2,1)S(1)}, u32[]{:S(2)}, u32[]{:S(2)}) %collective-permute-start.47) | collective-permute-done | bytes 589856 | tf_op jit(solution)/shard_map/ppermute | solution.py:756
  315.6 24.0 %attend_back.1 = (bf16[384,768]{1,0:T(8,128)(2,1)}, bf16[384,768]{1,0:T(8,128)(2,1)}, bf16[384,768]{1,0:T(8,128)(2,1)}, bf16[384,768]{1,0:T(8,128)(2,1)}, f32[76...) custom-call(s32[4]{0:T(128)} %pad_add_fusion.place_ref, f32[3,32]{1,0:T(4,128)} %convert_element_type.201.bias_ref, ...), custom_call_target="tpu_custom_call" | custom-call | flops 5586812928 | bytes 14155776 | tf_op jit(solution)/shard_map/attend_back/pallas_call | solution.py:295
  348.1 5.9 %convert_add_fusion = f32[4,768,384]{2,1,0:T(8,128)} fusion(f32[4,768,384]{2,1,0:T(8,128)} %get-tuple-element.212, bf16[4,768,384]{2,1,0:T(8,128)(2,1)} %collective-permute-done.49), kind=kLoop, calls=%fused_computation.1 | loop fusion | flops 2359296 | bytes 11796480 | tf_op jit(solution)/shard_map/add | solution.py:940
  373.9 3.9 tokens_back.1
  (303 shorter events, 144.5 us)
Async XLA Ops:
  7.2 174.6 %all-gather.3.cloned.1.call-start = ((), (), s32[]{:S(2)}) async-start(), calls=%async_computation.2 | async-start | bytes 4423680 | tf_op jit(solution)/shard_map/all_gather | solution.py:885
  7.3 50.0 %collective-permute-start = (bf16[384,768]{1,0:T(8,128)(2,1)}, bf16[384,768]{1,0:T(8,128)(2,1)}, u32[]{:S(2)}, u32[]{:S(2)}) collective-permute-start(bf16[384,768]{1,0:T(8,128)(2,1)} %tok_ref.3), channel_id=1, source_target_pairs={{0,1},{1,0},{2,3},{3,2},{4,5},{5,4},{6,7},{7,6},{8,9},{9,8},{10,11... | collective-permute-start | bytes 1769480 | tf_op jit(solution)/shard_map/ppermute | solution.py:756
  10.3 47.0 %collective-permute-start.1 = (bf16[384,768]{1,0:T(8,128)(2,1)}, bf16[384,768]{1,0:T(8,128)(2,1)}, u32[]{:S(2)}, u32[]{:S(2)}) collective-permute-start(bf16[384,768]{1,0:T(8,128)(2,1)} %tok_ref.3), channel_id=1, source_target_pairs={{0,2},{1,3},{2,0},{3,1},{4,6},{5,7},{6,4},{7,5},{8,10},{9,11},{10,... | collective-permute-start | bytes 1769480 | tf_op jit(solution)/shard_map/ppermute | solution.py:756
  11.8 45.5 %collective-permute-start.2 = (bf16[384,768]{1,0:T(8,128)(2,1)}, bf16[384,768]{1,0:T(8,128)(2,1)}, u32[]{:S(2)}, u32[]{:S(2)}) collective-permute-start(bf16[384,768]{1,0:T(8,128)(2,1)} %tok_ref.3), channel_id=1, source_target_pairs={{0,3},{1,2},{2,1},{3,0},{4,7},{5,6},{6,5},{7,4},{8,11},{9,10},{10,... | collective-permute-start | bytes 1769480 | tf_op jit(solution)/shard_map/ppermute | solution.py:756
  12.7 23.8 %collective-permute-start.3 = (bf16[432]{0:T(512)(128)(2,1)S(1)}, bf16[432]{0:T(512)(128)(2,1)S(1)}, u32[]{:S(2)}, u32[]{:S(2)}) collective-permute-start(bf16[432]{0:T(512)(128)(2,1)S(1)} %reshape.260), channel_id=1, source_target_pairs={{0,1},{1,0},{2,3},{3,2},{4,5},{5,4},{6,7},{7,6},{8,9},{9,8},{10,11... | collective-permute-start | bytes 2600 | tf_op jit(solution)/shard_map/ppermute | solution.py:756
  14.8 25.3 %collective-permute-start.4 = (bf16[432]{0:T(512)(128)(2,1)S(1)}, bf16[432]{0:T(512)(128)(2,1)S(1)}, u32[]{:S(2)}, u32[]{:S(2)}) collective-permute-start(bf16[432]{0:T(512)(128)(2,1)S(1)} %reshape.260), channel_id=1, source_target_pairs={{0,2},{1,3},{2,0},{3,1},{4,6},{5,7},{6,4},{7,5},{8,10},{9,11},{10,... | collective-permute-start | bytes 2600 | tf_op jit(solution)/shard_map/ppermute | solution.py:756
  64.7 28.4 %collective-permute-start.13 = (bf16[4,384,768]{2,1,0:T(8,128)(2,1)}, bf16[4,384,768]{2,1,0:T(8,128)(2,1)}, u32[]{:S(2)}, u32[]{:S(2)}) collective-permute-start(bf16[4,384,768]{2,1,0:T(8,128)(2,1)} %refs_13_.1), channel_id=1, source_target_pairs={{0,16},{16,0},{1,17},{17,1},{2,18},{18,2},{3,19},{19,3},{4,20},{20... | collective-permute-start | bytes 7077896 | tf_op jit(solution)/shard_map/ppermute | solution.py:746
  65.0 28.2 %collective-permute-start.14 = (bf16[4,768,384]{2,1,0:T(8,128)(2,1)S(1)}, bf16[4,768,384]{2,1,0:T(8,128)(2,1)}, u32[]{:S(2)}, u32[]{:S(2)}) collective-permute-start(bf16[4,768,384]{2,1,0:T(8,128)(2,1)S(1)} %copy-done.1), channel_id=1, source_target_pairs={{0,16},{16,0},{1,17},{17,1},{2,18},{18,2},{3,19},{19,3},{4,20},{20... | collective-permute-start | bytes 7077896 | tf_op jit(solution)/shard_map/ppermute | solution.py:746
  71.0 20.3 %collective-permute-start.15 = (bf16[144,768]{1,0:T(8,128)(2,1)S(1)}, bf16[144,768]{1,0:T(8,128)(2,1)S(1)}, u32[]{:S(2)}, u32[]{:S(2)}) collective-permute-start(bf16[144,768]{1,0:T(8,128)(2,1)S(1)} %get-tuple-element.251), channel_id=1, source_target_pairs={{0,4},{4,0},{8,12},{12,8},{1,5},{5,1},{9,13},{13,9},{2,6},{6,2},{1... | collective-permute-start | bytes 663560 | tf_op jit(solution)/shard_map/ppermute | solution.py:756
  93.2 213.9 %reduce-scatter.2.cloned.1.call-start = ((), (), s32[]{:S(2)}) async-start(), calls=%async_computation.1 | async-start | bytes 4423680 | tf_op jit(solution)/shard_map/reduce_scatter | solution.py:917
  94.8 20.5 %collective-permute-start.18 = (bf16[384,768]{1,0:T(8,128)(2,1)}, bf16[384,768]{1,0:T(8,128)(2,1)S(1)}, u32[]{:S(2)}, u32[]{:S(2)}) collective-permute-start(bf16[384,768]{1,0:T(8,128)(2,1)} %get-tuple-element.146), channel_id=1, source_target_pairs={{0,1},{1,0},{2,3},{3,2},{4,5},{5,4},{6,7},{7,6},{8,9},{9,8},{10,11... | collective-permute-start | bytes 1769480 | tf_op jit(solution)/shard_map/ppermute | solution.py:756
  135.0 19.1 %collective-permute-start.27 = (bf16[144,768]{1,0:T(8,128)(2,1)S(1)}, bf16[144,768]{1,0:T(8,128)(2,1)S(1)}, u32[]{:S(2)}, u32[]{:S(2)}) collective-permute-start(bf16[144,768]{1,0:T(8,128)(2,1)S(1)} %get-tuple-element.245), channel_id=1, source_target_pairs={{0,8},{4,12},{8,0},{12,4},{1,9},{5,13},{9,1},{13,5},{2,10},{6,14},... | collective-permute-start | bytes 663560 | tf_op jit(solution)/shard_map/ppermute | solution.py:756
  155.3 18.8 %collective-permute-start.23 = (bf16[288,768]{1,0:T(8,128)(2,1)S(1)}, bf16[288,768]{1,0:T(8,128)(2,1)S(1)}, u32[]{:S(2)}, u32[]{:S(2)}) collective-permute-start(bf16[288,768]{1,0:T(8,128)(2,1)S(1)} %pad_maximum_fusion.3), channel_id=1, source_target_pairs={{0,2},{1,3},{2,0},{3,1},{4,6},{5,7},{6,4},{7,5},{8,10},{9,11},{10,... | collective-permute-start | bytes 1327112 | tf_op jit(solution)/shard_map/ppermute | solution.py:756
  281.2 23.4 %collective-permute-start.47 = (bf16[384,768]{1,0:T(8,128)(2,1)S(1)}, bf16[384,768]{1,0:T(8,128)(2,1)S(1)}, u32[]{:S(2)}, u32[]{:S(2)}) collective-permute-start(bf16[384,768]{1,0:T(8,128)(2,1)S(1)} %pad_maximum_fusion.2), channel_id=1, source_target_pairs={{0,1},{1,0},{2,3},{3,2},{4,5},{5,4},{6,7},{7,6},{8,9},{9,8},{10,11... | collective-permute-start | bytes 1769480 | tf_op jit(solution)/shard_map/ppermute | solution.py:756
  282.8 23.7 %collective-permute-start.45 = (bf16[384,768]{1,0:T(8,128)(2,1)S(1)}, bf16[384,768]{1,0:T(8,128)(2,1)}, u32[]{:S(2)}, u32[]{:S(2)}) collective-permute-start(bf16[384,768]{1,0:T(8,128)(2,1)S(1)} %pad_maximum_fusion.1), channel_id=1, source_target_pairs={{0,2},{1,3},{2,0},{3,1},{4,6},{5,7},{6,4},{7,5},{8,10},{9,11},{10,... | collective-permute-start | bytes 1769480 | tf_op jit(solution)/shard_map/ppermute | solution.py:756
  307.1 34.5 %collective-permute-start.48 = (bf16[4,384,768]{2,1,0:T(8,128)(2,1)}, bf16[4,384,768]{2,1,0:T(8,128)(2,1)S(1)}, u32[]{:S(2)}, u32[]{:S(2)}) collective-permute-start(bf16[4,384,768]{2,1,0:T(8,128)(2,1)} %get-tuple-element.192), channel_id=1, source_target_pairs={{0,16},{16,0},{1,17},{17,1},{2,18},{18,2},{3,19},{19,3},{4,20},{20... | collective-permute-start | bytes 7077896 | tf_op jit(solution)/shard_map/ppermute | solution.py:746
  307.2 34.5 %collective-permute-start.49 = (bf16[4,768,384]{2,1,0:T(8,128)(2,1)}, bf16[4,768,384]{2,1,0:T(8,128)(2,1)}, u32[]{:S(2)}, u32[]{:S(2)}) collective-permute-start(bf16[4,768,384]{2,1,0:T(8,128)(2,1)} %get-tuple-element.193), channel_id=1, source_target_pairs={{0,16},{16,0},{1,17},{17,1},{2,18},{18,2},{3,19},{19,3},{4,20},{20... | collective-permute-start | bytes 7077896 | tf_op jit(solution)/shard_map/ppermute | solution.py:746
  311.2 30.4 %collective-permute-start.50 = (bf16[144,768]{1,0:T(8,128)(2,1)}, bf16[144,768]{1,0:T(8,128)(2,1)S(1)}, u32[]{:S(2)}, u32[]{:S(2)}) collective-permute-start(bf16[144,768]{1,0:T(8,128)(2,1)} %get-tuple-element.241), channel_id=1, source_target_pairs={{0,4},{4,0},{8,12},{12,8},{1,5},{5,1},{9,13},{13,9},{2,6},{6,2},{1... | collective-permute-start | bytes 663560 | tf_op jit(solution)/shard_map/ppermute | solution.py:756
  312.8 28.8 %collective-permute-start.51 = (bf16[144,768]{1,0:T(8,128)(2,1)}, bf16[144,768]{1,0:T(8,128)(2,1)S(1)}, u32[]{:S(2)}, u32[]{:S(2)}) collective-permute-start(bf16[144,768]{1,0:T(8,128)(2,1)} %get-tuple-element.240), channel_id=1, source_target_pairs={{0,8},{4,12},{8,0},{12,4},{1,9},{5,13},{9,1},{13,5},{2,10},{6,14},... | collective-permute-start | bytes 663560 | tf_op jit(solution)/shard_map/ppermute | solution.py:756
  315.2 26.4 %collective-permute-start.52 = (bf16[144,768]{1,0:T(8,128)(2,1)}, bf16[144,768]{1,0:T(8,128)(2,1)S(1)}, u32[]{:S(2)}, u32[]{:S(2)}) collective-permute-start(bf16[144,768]{1,0:T(8,128)(2,1)} %get-tuple-element.239), channel_id=1, source_target_pairs={{0,12},{4,8},{8,4},{12,0},{1,13},{5,9},{9,5},{13,1},{2,14},{6,10},... | collective-permute-start | bytes 663560 | tf_op jit(solution)/shard_map/ppermute | solution.py:756
  345.4 28.4 %collective-permute-start.54 = (bf16[384,768]{1,0:T(8,128)(2,1)}, bf16[384,768]{1,0:T(8,128)(2,1)}, u32[]{:S(2)}, u32[]{:S(2)}) collective-permute-start(bf16[384,768]{1,0:T(8,128)(2,1)} %get-tuple-element.202), channel_id=1, source_target_pairs={{0,2},{1,3},{2,0},{3,1},{4,6},{5,7},{6,4},{7,5},{8,10},{9,11},{10,... | collective-permute-start | bytes 1769480 | tf_op jit(solution)/shard_map/ppermute | solution.py:756
  346.1 27.7 %collective-permute-start.55 = (bf16[384,768]{1,0:T(8,128)(2,1)}, bf16[384,768]{1,0:T(8,128)(2,1)}, u32[]{:S(2)}, u32[]{:S(2)}) collective-permute-start(bf16[384,768]{1,0:T(8,128)(2,1)} %get-tuple-element.203), channel_id=1, source_target_pairs={{0,3},{1,2},{2,1},{3,0},{4,7},{5,6},{6,5},{7,4},{8,11},{9,10},{10,... | collective-permute-start | bytes 1769480 | tf_op jit(solution)/shard_map/ppermute | solution.py:756
  354.2 23.6 %collective-permute-start.57 = (bf16[112,768]{1,0:T(8,128)(2,1)S(1)}, bf16[112,768]{1,0:T(8,128)(2,1)S(1)}, u32[]{:S(2)}, u32[]{:S(2)}) collective-permute-start(bf16[112,768]{1,0:T(8,128)(2,1)S(1)} %get-tuple-element.236), channel_id=1, source_target_pairs={{0,4},{4,0},{8,12},{12,8},{1,5},{5,1},{9,13},{13,9},{2,6},{6,2},{1... | collective-permute-start | bytes 516104 | tf_op jit(solution)/shard_map/ppermute | solution.py:756
  354.9 22.9 %collective-permute-start.58 = (bf16[112,768]{1,0:T(8,128)(2,1)S(1)}, bf16[112,768]{1,0:T(8,128)(2,1)S(1)}, u32[]{:S(2)}, u32[]{:S(2)}) collective-permute-start(bf16[112,768]{1,0:T(8,128)(2,1)S(1)} %get-tuple-element.238), channel_id=1, source_target_pairs={{0,8},{4,12},{8,0},{12,4},{1,9},{5,13},{9,1},{13,5},{2,10},{6,14},... | collective-permute-start | bytes 516104 | tf_op jit(solution)/shard_map/ppermute | solution.py:756
  (88 other events, 1204.5 us)
Sparse Core Ops, SparseCore 0:
  93.3 61.9 all-gather.2
  248.2 58.8 reduce-scatter.1

commit v6 on v5

--- a/solution.py
+++ b/solution.py
@@ -81,13 +81,6 @@
 HOPS = ((1, 2), (2, 1))
 
 
-def group_rows(place_ref, out, pieces):
-    rows = pieces[0].shape[0]
-    for j, piece in enumerate(pieces):
-        at = pl.multiple_of((place_ref[2] ^ j) * rows, rows)
-        out[pl.ds(at, rows), :] = piece[...]
-
-
 def group_halves(place_ref, out, pieces):
     rows = pieces[0].shape[0]
     half = rows // 2
@@ -119,7 +112,7 @@
 def attend_kernel(heads, tensors, owners, part, place_ref, bias_ref, *refs):
     refs = list(refs)
     take = lambda n: [refs.pop(0) for _ in range(n)]
-    pieces, owned, (gain_ref,), parts = take(tensors), take(owners), take(1), take(tensors)
+    pieces, owned, (gain_ref,), parts = take(5), take(owners), take(1), take(tensors)
     tok_ref, qkv_ref, mixed_ref, log_ref, w_ref, table, wo, group, result = refs
     inner = heads * HEAD_DIM
     step_id = pl.program_id(0)
@@ -127,8 +120,9 @@
     @pl.when(step_id == 0)
     def _():
         fill_bias(bias_ref, table, heads)
-        group_rows(place_ref, group, pieces)
-        for k, piece in enumerate(owned):
+        group_halves(place_ref, group, pieces)
+        blocks = [piece.at[n] for piece in owned for n in range(piece.shape[0])]
+        for k, piece in enumerate(blocks):
             at = pl.multiple_of((place_ref[3] ^ k) * part, part) if owners > 1 else 0
             w_ref[pl.ds(at, part), :] = piece[:part, :]
         wo[...] = w_ref[:, 3 * inner :]
@@ -161,7 +155,7 @@
 
 
 def attend(places, bias, pieces, owned, part, gain):
-    tensors = len(pieces)
+    tensors = 4
     piece_rows, width = pieces[0].shape
     rows = tensors * piece_rows
     heads = bias.shape[0]
@@ -174,7 +168,7 @@
             num_scalar_prefetch=1,
             grid=(seqs,),
             in_specs=[pl.BlockSpec(memory_space=pltpu.SMEM)]
-            + [whole((piece_rows, width))] * tensors
+            + [whole(p.shape) for p in pieces]
             + [whole(o.shape) for o in owned]
             + [whole((1, width))],
             out_specs=[whole((piece_rows, width))] * tensors
@@ -202,12 +196,13 @@
 
 
 def attend_back_kernel(
-    heads, tensors, place_ref, bias_ref, tok_ref, gain_ref, w_ref, qkv_ref, mixed_ref, log_ref, *refs
+    heads, tensors, part, place_ref, bias_ref, tok_ref, gain_ref, w_ref, qkv_ref, mixed_ref, log_ref, *refs
 ):
     refs = list(refs)
     pieces = [refs.pop(0) for _ in range(5)]
+    gain_two_ref, router_ref = refs.pop(0), refs.pop(0)
     parts = [refs.pop(0) for _ in range(tensors)]
-    weight_ref, buckets_ref, gain_out, table, wo, gmix, gproj, near, far, rows_s, group, result = refs
+    own_ref, other_ref, weight_ref, gain_out, table, wo, gmix, gproj, near, far, rows_s, group, result = refs
     inner = heads * HEAD_DIM
     blocks = LENGTH // TILE
     step_id = pl.program_id(0)
@@ -281,10 +276,36 @@
                     total = total + far[head * 2 + 1]
                 at = head * BUCKETS + k
                 rows_s[at : at + 1, :] = jnp.sum(total, axis=0, keepdims=True)
-        buckets_ref[...] = jnp.sum(rows_s[...], axis=1, keepdims=True)
-
-
-def attend_back(places, bias, tokens, gain, weights, projected, mixed, logs, pieces):
+        sums = jnp.sum(rows_s[...], axis=1, keepdims=True)
+        experts = router_ref.shape[0]
+        if part % 16:
+            own_ref[...] = jnp.broadcast_to(sums, own_ref.shape)
+            return
+        count = sums.shape[0]
+        diagonal = lax.broadcasted_iota(jnp.int32, (count, TILE), 0) == lax.broadcasted_iota(
+            jnp.int32, (count, TILE), 1
+        )
+        sums = jnp.sum(jnp.where(diagonal, sums, 0.0), axis=0, keepdims=True)
+        width = gain_out.shape[1]
+        sums = jnp.concatenate([sums, jnp.zeros((1, width - TILE), F32)], axis=1)
+        head_rows = jnp.concatenate(
+            [gain_out[...], gain_two_ref[...], sums, jnp.zeros((13, width), F32)], axis=0
+        ).astype(BF16)
+        tail = jnp.concatenate(
+            [router_ref[...].astype(BF16)]
+            + ([jnp.zeros((-experts % 16, width), BF16)] if experts % 16 else []),
+            axis=0,
+        )
+        z_count = own_ref.shape[0]
+        for n, ref in enumerate((own_ref, other_ref)):
+            for k in range(z_count):
+                at = pl.multiple_of((place_ref[3] ^ (n * z_count + k)) * part, part)
+                ref[k, :part, :] = weight_ref[pl.ds(at, part), :].astype(BF16)
+                ref[k, part : part + 16, :] = head_rows
+                ref[k, part + 16 :, :] = tail
+
+
+def attend_back(places, bias, tokens, gain, weights, projected, mixed, logs, pieces, gain_two, router, part, z_count):
     rows, width = tokens.shape
     tensors = rows // pieces[0].shape[0]
     piece = whole(pieces[0].shape)
@@ -292,8 +313,12 @@
     inner = heads * HEAD_DIM
     seqs = rows // LENGTH
     by_seq = lambda cols: pl.BlockSpec((LENGTH, cols), lambda s, *_: (s, 0))
+    experts = router.shape[0]
+    sent = (z_count, part + 16 + experts + -experts % 16, width)
+    if part % 16:
+        sent = (heads * BUCKETS, 1)
     result = pl.pallas_call(
-        functools.partial(attend_back_kernel, heads, tensors),
+        functools.partial(attend_back_kernel, heads, tensors, part),
         grid_spec=pltpu.PrefetchScalarGridSpec(
             num_scalar_prefetch=1,
             grid=(seqs,),
@@ -306,9 +331,10 @@
                 by_seq(inner),
                 by_seq(TILE),
             ]
-            + [whole(p.shape) for p in pieces],
+            + [whole(p.shape) for p in pieces]
+            + [whole((1, width)), whole((experts, width))],
             out_specs=[piece] * tensors
-            + [whole((width, 4 * inner)), whole((heads * BUCKETS, 1)), whole((1, width))],
+            + [whole(sent), whole(sent), whole((width, 4 * inner)), whole((1, width))],
             scratch_shapes=[
                 pltpu.VMEM((heads, LENGTH, LENGTH), F32),
                 pltpu.VMEM((width, inner), BF16),
@@ -323,50 +349,64 @@
         ),
         out_shape=[jax.ShapeDtypeStruct(pieces[0].shape, BF16)] * tensors
         + [
+            jax.ShapeDtypeStruct(sent, F32 if part % 16 else BF16),
+            jax.ShapeDtypeStruct(sent, F32 if part % 16 else BF16),
             jax.ShapeDtypeStruct((width, 4 * inner), F32),
-            jax.ShapeDtypeStruct((heads * BUCKETS, 1), F32),
             jax.ShapeDtypeStruct((1, width), F32),
         ],
         compiler_params=params(),
         cost_estimate=cost(18 * rows * width * inner + 10 * rows * LENGTH * inner, rows * width * 12, rows * LENGTH * heads),
         name="attend_back",
-    )(places, bias, tokens, gain, weights, projected, mixed, logs, *pieces)
+    )(places, bias, tokens, gain, weights, projected, mixed, logs, *pieces, gain_two, router)
     return result[:tensors], result[tensors:]
 
 
 def first_rows_kernel(count, *refs):
     out_ref = refs[-1]
-    for k, ref in enumerate(refs[:-1]):
-        out_ref[k] = ref[:count, :]
+    at = 0
+    for ref in refs[:-1]:
+        for n in range(ref.shape[0]):
+            out_ref[at] = ref[n, :count, :]
+            at += 1
 
 
 def first_rows(pieces, start, extra, count):
-    width = pieces[0].shape[1]
+    width = pieces[0].shape[-1]
+    total = sum(piece.shape[0] for piece in pieces)
     return pl.pallas_call(
         functools.partial(first_rows_kernel, count),
         grid=(1,),
-        in_specs=[pl.BlockSpec((extra, width), lambda i: (start // extra, 0))] * len(pieces),
-        out_specs=whole((len(pieces), count, width)),
-        out_shape=jax.ShapeDtypeStruct((len(pieces), count, width), BF16),
+        in_specs=[
+            pl.BlockSpec((piece.shape[0], extra, width), lambda i: (0, start // extra, 0)) for piece in pieces
+        ],
+        out_specs=whole((total, count, width)),
+        out_shape=jax.ShapeDtypeStruct((total, count, width), BF16),
         compiler_params=params(),
-        cost_estimate=cost(0, 4 * len(pieces) * extra * width),
+        cost_estimate=cost(0, 4 * total * extra * width),
         name="first_rows",
     )(*pieces)
 
 
-def place_kernel(target_ref, rows_ref, out_ref):
-    count = out_ref.shape[0]
-    rows = lax.broadcasted_iota(jnp.int32, (count, rows_ref.shape[0]), 0)
-    chosen = jnp.where(rows == target_ref[...], 1.0, 0.0).astype(BF16)
-    out_ref[...] = dot(chosen, rows_ref[...]).astype(BF16)
-
-
-def place(target_row, rows, count):
+def place_rows(target_ref, rows, out_refs):
+    at = 0
+    for ref in out_refs:
+        count = ref.shape[0]
+        index = lax.broadcasted_iota(jnp.int32, (count, rows.shape[0]), 0) + at
+        chosen = jnp.where(index == target_ref[...], 1.0, 0.0).astype(BF16)
+        ref[...] = dot(chosen, rows).astype(BF16)
+        at += count
+
+
+def place_kernel(target_ref, rows_ref, *out_refs):
+    place_rows(target_ref, rows_ref[...], out_refs)
+
+
+def place(target_row, rows, counts):
     return pl.pallas_call(
         place_kernel,
-        out_shape=jax.ShapeDtypeStruct((count, rows.shape[1]), BF16),
+        out_shape=[jax.ShapeDtypeStruct((count, rows.shape[1]), BF16) for count in counts],
         compiler_params=params(),
-        cost_estimate=cost(2 * count * rows.size, 4 * rows.size),
+        cost_estimate=cost(2 * sum(counts) * rows.size, 4 * rows.size),
         name="place",
     )(target_row, rows)
 
@@ -384,7 +424,7 @@
 
 
 def route_kernel(tok_ref, *refs):
-    gain_ref, router_ref, target_ref, index_ref, kept_ref, hidden_ref, sent_ref, gate_ref = refs[6:]
+    gain_ref, router_ref, target_ref, index_ref, kept_ref, hidden_ref, gate_ref = refs[6:13]
     half = tok_ref.shape[0] // 2
     for h in range(2):
         keep, got, last = refs[3 * h : 3 * h + 3]
@@ -394,29 +434,27 @@
     hidden = hidden_ref[...]
     unit, _ = unit_rows(hidden)
     moe_in = (unit * gain_ref[...]).astype(BF16)
-    count = sent_ref.shape[0]
-    rows = lax.broadcasted_iota(jnp.int32, (count, hidden.shape[0]), 0)
-    chosen = jnp.where(rows == target_ref[...], 1.0, 0.0).astype(BF16)
-    sent_ref[...] = dot(chosen, moe_in).astype(BF16)
+    place_rows(target_ref, moe_in, refs[13:])
     probs = softmax_rows(dot(moe_in, router_ref[...]))
     lanes = lax.broadcasted_iota(jnp.int32, probs.shape, 1)
     picked = jnp.sum(jnp.where(lanes == index_ref[...], probs, 0.0), axis=-1, keepdims=True)
     gate_ref[...] = picked * kept_ref[...].astype(F32)
 
 
-def route(tokens, attn, gain, router, target_row, index_col, kept_col, count):
+def route(tokens, attn, gain, router, target_row, index_col, kept_col, counts):
     rows, width = tokens.shape
-    return pl.pallas_call(
+    result = pl.pallas_call(
         route_kernel,
         out_shape=[
             jax.ShapeDtypeStruct((rows, width), F32),
-            jax.ShapeDtypeStruct((count, width), BF16),
             jax.ShapeDtypeStruct((rows, 1), F32),
-        ],
+        ]
+        + [jax.ShapeDtypeStruct((count, width), BF16) for count in counts],
         compiler_params=params(),
-        cost_estimate=cost(2 * count * rows * width, 12 * rows * width),
+        cost_estimate=cost(2 * sum(counts) * rows * width, 12 * rows * width),
         name="route",
     )(tokens, *attn, gain, router, target_row, index_col, kept_col)
+    return result[0], result[1], result[2:]
 
 
 def rest_choice(blocks, locals_, rest, expert):
@@ -640,7 +678,7 @@
     def _():
         router_ref[...] = jnp.zeros_like(router_ref)
 
-    router_ref[...] += dot(x_ref[0], gl_ref[0], ROWS_TN)
+    router_ref[...] += dot(gl_ref[0], x_ref[0], ROWS_TN)
 
 
 def expert_weights(places, saved, half):
@@ -655,14 +693,14 @@
             num_scalar_prefetch=1,
             grid=(locals_,),
             in_specs=[per(rows, width), per(rows, width), per(rows, wide), per(rows, wide), per(rows, experts)],
-            out_specs=[per(half, wide), per(half, wide), per(wide, half), per(wide, half), whole((width, experts))],
+            out_specs=[per(half, wide), per(half, wide), per(wide, half), per(wide, half), whole((experts, width))],
         ),
         out_shape=[
             jax.ShapeDtypeStruct((locals_, half, wide), F32),
             jax.ShapeDtypeStruct((locals_, half, wide), BF16),
             jax.ShapeDtypeStruct((locals_, wide, half), F32),
             jax.ShapeDtypeStruct((locals_, wide, half), BF16),
-            jax.ShapeDtypeStruct((width, experts), F32),
+            jax.ShapeDtypeStruct((experts, width), F32),
         ],
         compiler_params=params(),
         cost_estimate=cost(4 * locals_ * rows * width * wide, locals_ * rows * width * 14),
@@ -811,10 +849,12 @@
     owners = dp_count * z_count
     my_owner = my_dp * z_count + my_z
     places = jnp.stack([my_dp, my_z, my_t, my_owner]).astype(jnp.int32)
-    token_pieces = gather_pieces(tokens, "tensor", t_count)
+    half_rows = tok_rows // 2
+    token_pieces = [tokens]
+    for h, hops in enumerate(HOPS):
+        token_pieces += list(gather_hops(tokens[h * half_rows : (h + 1) * half_rows], hops))
 
     small = jnp.concatenate([gain_attn[:, None], gain_moe[:, None], w_router], axis=1).reshape(-1)
-    small = jnp.concatenate(gather_pieces(small, "tensor", t_count))
     extra = -(-small.shape[0] // (16 * width)) * 16
     packed = jnp.concatenate(
         [
@@ -826,44 +866,43 @@
     packed = jnp.concatenate(
         [packed, jnp.pad(small, (0, extra * width - small.shape[0])).reshape(extra, width)], axis=0
     )
-    owned = gather_pieces(packed, "expert", z_count)
-    token_pieces, owned = lax.optimization_barrier((token_pieces, owned))
-    owned = owned + [swapped(piece, "dp", dp_count, 1) for piece in owned]
+    owned = gather_pieces(packed[None], "expert", z_count)
+    owned = owned + [swapped(jnp.concatenate(owned, axis=0), "dp", dp_count, 1)]
     if part % 16 or part % extra:
-        smalls = jnp.stack([piece[part:] for piece in owned])
+        smalls = jnp.concatenate(owned, axis=0)[:, part:]
     else:
         smalls = first_rows(owned, part, extra, -(-small.shape[0] // width))
-    smalls = smalls.reshape(owners, -1)[:, : small.shape[0]].reshape(owners * t_count, -1)
+    smalls = smalls.reshape(owners, -1)[:, : small.shape[0]]
+    small_pieces = gather_pieces(smalls, "tensor", t_count)
+
+    z_of = expert_index // locals_
+    local = expert_index - z_of * locals_
+    inside = jnp.where(
+        slot_index < main, local * main + slot_index, locals_ * main + local * rest + slot_index - main
+    )
+    target = (z_of ^ my_z) * block + inside
+    target = jnp.where(kept_mask > 0, target, -1)
+    target_row, target_col = target[None, :], target[:, None]
+    chunks = min(z_count, 4)
+    many = z_count // chunks
+    counts = [many * block] * chunks
+    grad_sent = place(target_row, cotangent, counts)
+    token_pieces, owned, small_pieces, grad_sent = lax.optimization_barrier(
+        (token_pieces, owned, small_pieces, grad_sent)
+    )
+    smalls = jnp.stack(small_pieces).reshape(t_count * owners, -1)
     owner_ids = jnp.arange(owners, dtype=jnp.int32)[:, None] ^ my_owner
     t_ids = jnp.arange(t_count, dtype=jnp.int32)[None, :] ^ my_t
-    smalls = smalls[(owner_ids * t_count + t_ids).reshape(-1)].reshape(width, 2 + experts_all)
+    smalls = smalls[(t_ids * owners + owner_ids).reshape(-1)].reshape(width, 2 + experts_all)
     if part % 16:
         order = jnp.arange(owners, dtype=jnp.int32) ^ my_owner
-        owned = [jnp.stack([piece[:part] for piece in owned])[order].reshape(width, 4 * inner)]
+        owned = [jnp.concatenate(owned, axis=0)[:, :part][order].reshape(1, width, 4 * inner)]
     rows_owned = part if len(owned) > 1 else width
     gain_one = smalls[:, 0].astype(F32)[None]
     gain_two = smalls[:, 1].astype(F32)[None]
     router = smalls[:, 2:]
 
-    z_of = expert_index // locals_
-    local = expert_index - z_of * locals_
-    inside = jnp.where(
-        slot_index < main, local * main + slot_index, locals_ * main + local * rest + slot_index - main
-    )
-    target = (z_of ^ my_z) * block + inside
-    target = jnp.where(kept_mask > 0, target, -1)
-    target_row, target_col = target[None, :], target[:, None]
-    count = z_count * block
-    chunks = min(z_count, 4)
-    many = z_count // chunks
-
-    def over_expert(rows):
-        pieces = swap_pieces(list(rows.reshape(z_count, block, width)), "expert", z_count)
-        if many == 1:
-            return pieces
-        return [jnp.concatenate(pieces[k * many : (k + 1) * many], axis=0) for k in range(chunks)]
-
-    def back_over_expert(groups):
+    def over_expert(groups):
         if many > 1:
             groups = [g[i * block : (i + 1) * block] for g in groups for i in range(many)]
         pieces = swap_pieces(groups, "expert", z_count)
@@ -871,27 +910,23 @@
             return pieces
         return [jnp.concatenate(pieces[k * many : (k + 1) * many], axis=0) for k in range(chunks)]
 
-    late_cotangent, late_in, late_out, token_pieces, owned, gain_one = lax.optimization_barrier(
-        (cotangent, w_in, w_out, token_pieces, owned, gain_one)
-    )
-    grad_rows = jnp.concatenate(over_expert(place(target_row, late_cotangent, count)), axis=0)
+    grad_rows = jnp.concatenate(over_expert(grad_sent), axis=0)
+    parts, (group_tokens, projected, mixed, logs, weights) = attend(
+        places, bias, token_pieces, owned, rows_owned, gain_one
+    )
+    parts, late_in, late_out, grad_rows = lax.optimization_barrier((parts, w_in, w_out, grad_rows))
     peer_in = shifted(late_in, "dp", dp_count, 1)
     peer_out = shifted(late_out, "dp", dp_count, 1)
-
-    parts, (group_tokens, projected, mixed, logs, weights) = attend(
-        places, bias, token_pieces, owned, rows_owned, gain_one
-    )
-    parts, peer_in, peer_out, grad_rows = lax.optimization_barrier((parts, peer_in, peer_out, grad_rows))
     grad_arrived = lax.all_gather(grad_rows, "tensor", axis=0).reshape(t_count, z_count, block, width)
-    half_rows = tok_rows // 2
     attn = []
     for h, (a, b) in enumerate(HOPS):
         keep, send = parts[2 * h : 2 * h + 2]
         got = swapped(send, "tensor", t_count, a)
         last = swapped(added(keep[half_rows:], got[half_rows:]), "tensor", t_count, b)
         attn += [keep, got, last]
-    hidden_one, sent, gate = route(
-        tokens, attn, gain_two, router, target_row, expert_index[:, None], kept_mask[:, None], count
+    attn, peer_in, peer_out = lax.optimization_barrier((attn, peer_in, peer_out))
+    hidden_one, gate, sent = route(
+        tokens, attn, gain_two, router, target_row, expert_index[:, None], kept_mask[:, None], counts
     )
     arrived = []
     for k, group in enumerate(over_expert(sent)):
@@ -912,77 +947,75 @@
         last = swapped(added(keeps[k][size:], got[k][size:]), "tensor", t_count, HOPS[k % 2][1])
         total = keeps[k][:size].astype(F32) + got[k][:size].astype(F32) + last.astype(F32)
         groups.append(total.astype(BF16))
-    grad_back = back_over_expert(groups)
-    forward_part, groups = lax.optimization_barrier((forward_part, groups))
+    forward_part, groups, saved = lax.optimization_barrier((forward_part, groups, saved))
     forward_sum = lax.psum_scatter(
         forward_part.reshape(t_count * z_count * block, width), "tensor", scatter_dimension=0, tiled=True
     )
+    in_own, in_send, out_own, out_send, router_part = expert_weights(places, saved, w_in.shape[1])
+    grad_back, in_send, out_send = lax.optimization_barrier((over_expert(groups), in_send, out_send))
+    in_got = shifted(in_send, "dp", dp_count, 1)
+    out_got = shifted(out_send, "dp", dp_count, 1)
     grad_hidden, grad_attn, gain_two_part = hidden_back(target_col, grad_back, hidden_one, cotangent, gain_two)
-    grad_attn, saved = lax.optimization_barrier((grad_attn, saved))
     grad_pieces = [grad_attn]
     for h, hops in enumerate(HOPS):
         grad_pieces += list(gather_hops(grad_attn[h * half_rows : (h + 1) * half_rows], hops))
-    in_own, in_send, out_own, out_send, router_part = expert_weights(places, saved, w_in.shape[1])
-    grad_pieces, in_send, out_send, forward_sum = lax.optimization_barrier(
-        (grad_pieces, in_send, out_send, forward_sum)
-    )
-    in_got = shifted(in_send, "dp", dp_count, 1)
-    out_got = shifted(out_send, "dp", dp_count, 1)
-    normed_parts, (weight_part, bucket_part, gain_one_part) = attend_back(
-        places, bias, group_tokens, gain_one, weights, projected, mixed, logs, grad_pieces
-    )
-    forward_rows = back_over_expert(list(forward_sum.reshape(chunks, many * block, width)))
-    normed_parts, weight_part, in_got, out_got, forward_rows = lax.optimization_barrier(
-        (normed_parts, weight_part, in_got, out_got, forward_rows)
-    )
-    grad_normed = swap_pieces(normed_parts, "tensor", t_count)
     grad_w_in = in_own + in_got.astype(F32)
     grad_w_out = out_own + out_got.astype(F32)
+    grad_pieces, grad_w_in, grad_w_out, forward_sum = lax.optimization_barrier(
+        (grad_pieces, grad_w_in, grad_w_out, forward_sum)
+    )
+    normed_parts, (own_part, other_part, weight_part, gain_one_part) = attend_back(
+        places, bias, group_tokens, gain_one, weights, projected, mixed, logs, grad_pieces,
+        gain_two_part, router_part, part, z_count,
+    )
+    forward_rows = over_expert(list(forward_sum.reshape(chunks, many * block, width)))
+    normed_parts, own_part, other_part, forward_rows = lax.optimization_barrier(
+        (normed_parts, own_part, other_part, forward_rows)
+    )
+    grad_normed = swap_pieces(normed_parts, "tensor", t_count)
     output = output_rows(target_col, forward_rows, hidden_one, gate)
     grad_tokens = tokens_back(tokens, grad_normed, gain_one, grad_hidden)
 
-    smalls = jnp.concatenate(
-        [
-            gain_one_part.reshape(owners, part),
-            gain_two_part.reshape(owners, part),
-            router_part.reshape(owners, part * experts_all),
-            jnp.broadcast_to(bucket_part.reshape(1, heads * BUCKETS), (owners, heads * BUCKETS)),
-        ],
-        axis=1,
-    )
-    extra = -(-smalls.shape[1] // (16 * width)) * 16
-    smalls = jnp.pad(smalls, ((0, 0), (0, extra * width - smalls.shape[1]))).reshape(owners, extra, width)
-    payload = jnp.concatenate([weight_part.reshape(owners, part, width), smalls], axis=1)
-    payload = payload.reshape(dp_count, z_count, part + extra, width)
-    own = lax.dynamic_index_in_dim(payload, my_dp, 0, keepdims=False)
-    other = lax.dynamic_index_in_dim(payload, 1 - my_dp, 0, keepdims=False)
-    summed_half = own + shifted(other.astype(BF16), "dp", dp_count, 1).astype(F32)
-    turned = [lax.dynamic_index_in_dim(summed_half, my_z ^ k, 0, keepdims=False) for k in range(z_count)]
-    pieces = swap_pieces([turned[0]] + [t.astype(BF16) for t in turned[1:]], "expert", z_count)
-    total = pieces[0]
+    if part % 16:
+        head_rows = jnp.concatenate(
+            [
+                gain_one_part,
+                gain_two_part,
+                jnp.pad(own_part.reshape(1, -1), ((0, 0), (0, width - own_part.shape[0]))),
+                jnp.zeros((13, width), F32),
+                router_part,
+                jnp.zeros((-experts_all % 16, width), F32),
+            ]
+        )
+        order = jnp.arange(owners, dtype=jnp.int32) ^ my_owner
+        payload = jnp.concatenate(
+            [
+                weight_part.reshape(owners, part, width)[order],
+                jnp.broadcast_to(head_rows[None], (owners,) + head_rows.shape),
+            ],
+            axis=1,
+        ).astype(BF16)
+        own_part, other_part = payload[:z_count], payload[z_count:]
+    other_got = shifted(other_part, "dp", dp_count, 1)
+    pieces = swap_pieces([added(own_part[k], other_got[k]) for k in range(z_count)], "expert", z_count)
+    total = pieces[0].astype(F32)
     for piece in pieces[1:]:
         total = total + piece.astype(F32)
     weight_total = total[:part].reshape(part, 4, inner)
     grad_w_qkv = weight_total[:, :3].transpose(1, 0, 2)
     grad_w_attn_out = weight_total[:, 3].T
-    flat = total[part:].reshape(-1)
-    ends = [part, 2 * part, 2 * part + part * experts_all]
-    grad_rel_bias = flat[ends[2] : ends[2] + heads * BUCKETS].reshape(heads, BUCKETS)
-    rows_left = jnp.concatenate(
-        [
-            flat[: ends[0]].reshape(t_count, fine),
-            flat[ends[0] : ends[1]].reshape(t_count, fine),
-            flat[ends[1] : ends[2]].reshape(t_count, fine * experts_all),
-        ],
-        axis=1,
-    )
-    turned = [lax.dynamic_index_in_dim(rows_left, my_t ^ k, 0, keepdims=False) for k in range(t_count)]
+    grad_rel_bias = total[part + 2, : heads * BUCKETS].reshape(heads, BUCKETS)
+    mine = lax.dynamic_slice_in_dim(total[part:], my_owner * part, part, axis=1)
+    mine = jnp.concatenate([mine[:2], mine[16 : 16 + experts_all]], axis=0)
+    turned = [
+        lax.dynamic_slice_in_dim(mine, (my_t ^ k) * fine, fine, axis=1).reshape(-1) for k in range(t_count)
+    ]
     left = turned[0]
     for piece in swap_pieces(turned, "tensor", t_count)[1:]:
         left = left + piece
     grad_gain_attn = left[:fine]
     grad_gain_moe = left[fine : 2 * fine]
-    grad_w_router = left[2 * fine :].reshape(fine, experts_all)
+    grad_w_router = left[2 * fine :].reshape(experts_all, fine).T
     return (
         output,
         grad_tokens,

time: 394 us -> 368 us (0.934)
  waiting for transfers between devices: 130 us -> 113 us
  local copies, waits for them, and re-layouts: 27.3 us -> 22.4 us
  starting transfers between devices: 80.8 us -> 75.9 us
    ppermute x58 -> x56, waiting for transfers between devices: 130 us -> 113 us  [swapped(): return lax.ppermute(value, axis, [(s, s ^ bits) for s in range(count)])]
    ppermute x58 -> x56, starting transfers between devices: 79.7 us -> 75.1 us  [swapped(): return lax.ppermute(value, axis, [(s, s ^ bits) for s in range(count)])]
    unnamed x99 -> x100, local copies, waits for them, and re-layouts: 9.01 us -> 7.48 us
  transfers between devices with their start and end apart: 65 -> 63, of which waited for: 33 -> 20; matrix products, arithmetic and copies ran while one was open for 8% -> 7% of each run, Pallas kernels for 21% -> 23%
where the time goes in v6:
time: 368 us; the launch traced here: 367 us
  Pallas kernels  120 us (33%)
  waiting for transfers between devices  113 us (31%)
  starting transfers between devices  75.9 us (21%)
  local copies, waits for them, and re-layouts  22.4 us (6%)
  other arithmetic  20.6 us (6%)
  between operations  14.8 us (4%)
    ppermute x56, waiting for transfers between devices, swapped(): return lax.ppermute(value, axis, [(s, s ^ bits) for s in range(count)])  113 us
    ppermute x56, starting transfers between devices, swapped(): return lax.ppermute(value, axis, [(s, s ^ bits) for s in range(count)])  75.1 us
    pallas_call x1, Pallas kernels, expert_forward_back(): pl.pallas_call(functools.partial(expert_kernel, chunks, tensors, main, lo...  35 us
    pallas_call x1, Pallas kernels, attend_back(): pl.pallas_call(functools.partial(attend_back_kernel, heads, tensors, part...  24.5 us
    pallas_call x1, Pallas kernels, attend(): pl.pallas_call(functools.partial(attend_kernel, heads, tensors, len(owned...  15.4 us
    pallas_call x1, Pallas kernels, expert_weights(): pl.pallas_call(expert_weights_kernel, grid_spec=pltpu.PrefetchScalarGridS...  15.2 us
    pallas_call x1, Pallas kernels, expert_rows(): pl.pallas_call(functools.partial(expert_rows_kernel, chunks, main, locals...  9.84 us
    unnamed x100, local copies, waits for them, and re-layouts  7.48 us
  transfers between devices with their start and end apart: 63, of which 20 were waited for; matrix products, arithmetic and copies ran while one was open for 7% of the time, Pallas kernels for 23%

profile of v6, /device:TPU:0, one launch (start us, length us, event | category | flops | bytes accessed | tf_op | source)
XLA Modules:
  0.0 367.4 jit_solution(11694381857313688832)
XLA Ops:
  10.4 5.1 %collective-permute-start.6 = (bf16[1,112,768]{2,1,0:T(8,128)(2,1)S(1)}, bf16[1,112,768]{2,1,0:T(8,128)(2,1)S(1)}, u32[]{:S(2)}, u32[]{:S(2)}) collective-permute-start(bf16[1,112,768]{2,1,0:T(8,128)(2,1)S(1)} %maximum_bitcast_fusion.refs_0_.refs_5_), channel_id=1, source_target_pairs={{0,12},{4,8},{8,4},{12,0},{1,13},{5,9},{9,5},{13,1},{2,14},{6,10},... | collective-permute-start | bytes 516104 | tf_op jit(solution)/shard_map/ppermute | solution.py:794
  21.3 8.9 %collective-permute-done.5.refs_2_.refs_7_ = bf16[1,112,768]{2,1,0:T(8,128)(2,1)S(1)} collective-permute-done((bf16[1,112,768]{2,1,0:T(8,128)(2,1)S(1)}, bf16[1,112,768]{2,1,0:T(8,128)(2,1)S(1)}, u32[]{:S(2)}, u32[]{:S(2)}) %collective-permute-start.5) | collective-permute-done | bytes 172064 | tf_op jit(solution)/shard_map/ppermute | solution.py:794
  46.4 3.3 collective-permute-done.10
  56.0 15.4 %attend.1 = (bf16[384,768]{1,0:T(8,128)(2,1)}, bf16[384,768]{1,0:T(8,128)(2,1)}, bf16[384,768]{1,0:T(8,128)(2,1)}, bf16[384,768]{1,0:T(8,128)(2,1)}, bf16[1536,7...) custom-call(s32[4]{0:T(128)} %pad_add_fusion.place_ref, ...), custom_call_target="tpu_custom_call" | custom-call | flops 2415919104 | bytes 9437184 | tf_op jit(solution)/shard_map/attend/pallas_call | solution.py:165
  76.2 19.0 %collective-permute-done.14.refs_1_ = bf16[384,768]{1,0:T(8,128)(2,1)S(1)} collective-permute-done((bf16[384,768]{1,0:T(8,128)(2,1)}, bf16[384,768]{1,0:T(8,128)(2,1)S(1)}, u32[]{:S(2)}, u32[]{:S(2)}) %collective-permute-start.14) | collective-permute-done | bytes 589856 | tf_op jit(solution)/shard_map/ppermute | solution.py:794
  107.1 4.9 %route.1 = (f32[384,768]{1,0:T(8,128)}, f32[384,1]{1,0:T(8,128)}, bf16[144,768]{1,0:T(8,128)(2,1)}, bf16[144,768]{1,0:T(8,128)(2,1)}, bf16[144,768]{1,0:T(8,128)(2,1)}, /*index=5*/bf16[144,768]{1,0:T(8,128)(2,1)}) custom-call(bf16[384,768]{1,0:T(8,128)(2,1)} %tok_ref.3, bf16[384,768]{1,0:T(8,128)(2,1)} %get-tuple-element.165.refs_0_, ...), custom_call_target="tpu_custom_call" | custom-call | flops 339738624 | bytes 3538944 | tf_op jit(solution)/shard_map/route/pallas_call | solution.py:446
  117.7 4.5 %collective-permute-done.22 = bf16[144,768]{1,0:T(8,128)(2,1)S(1)} collective-permute-done((bf16[144,768]{1,0:T(8,128)(2,1)}, bf16[144,768]{1,0:T(8,128)(2,1)S(1)}, u32[]{:S(2)}, u32[]{:S(2)}) %collective-permute-start.22) | collective-permute-done | bytes 221216 | tf_op jit(solution)/shard_map/ppermute | solution.py:794
  124.2 9.0 %collective-permute-done.25 = bf16[144,768]{1,0:T(8,128)(2,1)S(1)} collective-permute-done((bf16[144,768]{1,0:T(8,128)(2,1)}, bf16[144,768]{1,0:T(8,128)(2,1)S(1)}, u32[]{:S(2)}, u32[]{:S(2)}) %collective-permute-start.25) | collective-permute-done | bytes 221216 | tf_op jit(solution)/shard_map/ppermute | solution.py:794
  142.7 9.0 %collective-permute-done.29 = bf16[144,768]{1,0:T(8,128)(2,1)S(1)} collective-permute-done((bf16[144,768]{1,0:T(8,128)(2,1)S(1)}, bf16[144,768]{1,0:T(8,128)(2,1)S(1)}, u32[]{:S(2)}, u32[]{:S(2)}) %collective-permute-start.29) | collective-permute-done | bytes 221216 | tf_op jit(solution)/shard_map/ppermute | solution.py:794
  156.5 3.7 collective-permute-done.30
  160.9 35.0 %experts.1 = (bf16[2,144,768]{2,1,0:T(8,128)(2,1)}, bf16[2,144,768]{2,1,0:T(8,128)(2,1)}, bf16[2,144,768]{2,1,0:T(8,128)(2,1)}, bf16[2,144,768]{2,1,0:T(8,128)(2...) custom-call(s32[4]{0:T(128)} %pad_add_fusion.place_ref, ...), custom_call_target="tpu_custom_call" | custom-call | flops 8153726976 | bytes 24772608 | tf_op jit(solution)/shard_map/experts/pallas_call | solution.py:605
  200.0 9.8 %expert_rows.1 = bf16[4,4,144,768]{3,2,1,0:T(8,128)(2,1)} custom-call(s32[4]{0:T(128)} %pad_add_fusion.place_ref, bf16[4,576,768]{2,1,0:T(8,128)(2,1)} %get-tuple-element.202.hid_ref, bf16[4,768,384]{2,1,0:T(8,128)(2,1)} %own_out.1, bf16[4,768,384]{2,1,0:T(8,128)(2,1)} %collective-permute-done.19.refs_16_.peer_out), custom_call_target="tpu_custom_call" | custom-call | flops 2717908992 | bytes 10616832 | tf_op jit(solution)/shard_map/expert_rows/pallas_call | solution.py:651
  209.8 5.5 %collective-permute-done.33 = bf16[288,768]{1,0:T(8,128)(2,1)S(1)} collective-permute-done((bf16[288,768]{1,0:T(8,128)(2,1)}, bf16[288,768]{1,0:T(8,128)(2,1)S(1)}, u32[]{:S(2)}, u32[]{:S(2)}) %collective-permute-start.33) | collective-permute-done | bytes 442400 | tf_op jit(solution)/shard_map/ppermute | solution.py:794
  230.0 15.2 %expert_weights.1 = (f32[4,384,768]{2,1,0:T(8,128)}, bf16[4,384,768]{2,1,0:T(8,128)(2,1)}, f32[4,768,384]{2,1,0:T(8,128)}, bf16[4,768,384]{2,1,0:T(8,128)(2,1)}, f32[16,768]{1,0:T(8,128)}) custom-call(s32[4]{0:T(128)} %pad_add_fusion.place_ref, bf16[4,576,768]{2,1,0:T(8,128)(2,1)} %get-tuple-element.200.x_ref, ...), custom_call_target="tpu_custom_call" | custom-call | flops 5435817984 | bytes 24772608 | tf_op jit(solution)/shard_map/expert_weights/pallas_call | solution.py:690
  246.7 4.4 %hidden_back.1 = (f32[384,768]{1,0:T(8,128)}, bf16[384,768]{1,0:T(8,128)(2,1)}, f32[1,768]{1,0:T(1,128)}) custom-call(s32[384,1]{1,0:T(8,128)} %broadcast_in_dim.35.target_ref, bf16[144,768]{1,0:T(8,128)(2,1)} %fusion.11.refs_0_, bf16[144,768]{1,0:T(8,128)(2,1)} %copy-done.25, bf16[144,768]{1,0:T(8,128)(2,1)} %copy-done.26, bf16[144,768]{1,0:T(8,128)(2,1)} %copy-done.27, ...), custom_call_target="tpu_custom_call" | custom-call | flops 339738624 | bytes 4718592 | tf_op jit(solution)/shard_map/hidden_back/pallas_call | solution.py:737
  254.3 6.9 %collective-permute-done.42.refs_1_ = bf16[192,768]{1,0:T(8,128)(2,1)S(1)} collective-permute-done((bf16[192,768]{1,0:T(8,128)(2,1)S(1)}, bf16[192,768]{1,0:T(8,128)(2,1)S(1)}, u32[]{:S(2)}, u32[]{:S(2)}) %collective-permute-start.42) | collective-permute-done | bytes 294944 | tf_op jit(solution)/shard_map/ppermute | solution.py:794
  263.6 4.5 %convert_add_fusion.1 = f32[4,384,768]{2,1,0:T(8,128)} fusion(f32[4,384,768]{2,1,0:T(8,128)S(1)} %copy-done, bf16[4,384,768]{2,1,0:T(8,128)(2,1)} %collective-permute-done.46), kind=kLoop, calls=%fused_computation.2 | loop fusion | flops 2359296 | bytes 11796480 | tf_op jit(solution)/shard_map/add | solution.py:962
  270.8 13.9 %collective-permute-done.43.refs_2_ = bf16[384,768]{1,0:T(8,128)(2,1)S(1)} collective-permute-done((bf16[384,768]{1,0:T(8,128)(2,1)S(1)}, bf16[384,768]{1,0:T(8,128)(2,1)S(1)}, u32[]{:S(2)}, u32[]{:S(2)}) %collective-permute-start.43) | collective-permute-done | bytes 589856 | tf_op jit(solution)/shard_map/ppermute | solution.py:794
  287.2 3.3 collective-permute-start.50
  291.6 24.5 %attend_back.1 = (bf16[384,768]{1,0:T(8,128)(2,1)}, bf16[384,768]{1,0:T(8,128)(2,1)}, bf16[384,768]{1,0:T(8,128)(2,1)}, bf16[384,768]{1,0:T(8,128)(2,1)}, bf16[4...) custom-call(s32[4]{0:T(128)} %pad_add_fusion.place_ref, ...), custom_call_target="tpu_custom_call" | custom-call | flops 5586812928 | bytes 14155776 | tf_op jit(solution)/shard_map/attend_back/pallas_call | solution.py:320
  325.1 7.5 %collective-permute-done.51.refs_1_ = bf16[384,768]{1,0:T(8,128)(2,1)S(1)} collective-permute-done((bf16[384,768]{1,0:T(8,128)(2,1)}, bf16[384,768]{1,0:T(8,128)(2,1)S(1)}, u32[]{:S(2)}, u32[]{:S(2)}) %collective-permute-start.51) | collective-permute-done | bytes 589856 | tf_op jit(solution)/shard_map/ppermute | solution.py:794
  334.5 3.4 output_rows.1
  337.9 8.1 %collective-permute-done.52.refs_2_ = bf16[384,768]{1,0:T(8,128)(2,1)S(1)} collective-permute-done((bf16[384,768]{1,0:T(8,128)(2,1)}, bf16[384,768]{1,0:T(8,128)(2,1)S(1)}, u32[]{:S(2)}, u32[]{:S(2)}) %collective-permute-start.52) | collective-permute-done | bytes 589856 | tf_op jit(solution)/shard_map/ppermute | solution.py:794
  347.1 3.9 %tokens_back.1 = f32[384,768]{1,0:T(8,128)} custom-call(bf16[384,768]{1,0:T(8,128)(2,1)} %tok_ref.3, bf16[384,768]{1,0:T(8,128)(2,1)} %get-tuple-element.237.refs_0_, bf16[384,768]{1,0:T(8,128)(2,1)} %copy-done.10, bf16[384,768]{1,0:T(8,128)(2,1)} %copy-done.11, bf16[384,768]{1,0:T(8,128)(2,1)} %copy-done.12, f32[1,768]{1,0:T(1,128)} %reshape.266.refs_10_.gain_ref.refs_4_, ...), custom_call_target="tpu_custom_call" | custom-call | flops 2949120 | bytes 3538944 | tf_op jit(solution)/shard_map/tokens_back/pallas_call | solution.py:774
  (289 shorter events, 123.9 us)
Async XLA Ops:
  7.2 152.9 %all-gather.3.cloned.1.call-start = ((), (), s32[]{:S(2)}) async-start(), calls=%async_computation.2 | async-start | bytes 4423680 | tf_op jit(solution)/shard_map/all_gather | solution.py:920
  31.3 18.5 %collective-permute-start.1 = (bf16[384,768]{1,0:T(8,128)(2,1)S(1)}, bf16[384,768]{1,0:T(8,128)(2,1)}, u32[]{:S(2)}, u32[]{:S(2)}) collective-permute-start(bf16[384,768]{1,0:T(8,128)(2,1)S(1)} %pad_maximum_fusion.2), channel_id=1, source_target_pairs={{0,2},{1,3},{2,0},{3,1},{4,6},{5,7},{6,4},{7,5},{8,10},{9,11},{10,... | collective-permute-start | bytes 1769480 | tf_op jit(solution)/shard_map/ppermute | solution.py:794
  51.6 19.8 %collective-permute-start.11 = (bf16[144,768]{1,0:T(8,128)(2,1)}, bf16[144,768]{1,0:T(8,128)(2,1)S(1)}, u32[]{:S(2)}, u32[]{:S(2)}) collective-permute-start(bf16[144,768]{1,0:T(8,128)(2,1)} %get-tuple-element.156), channel_id=1, source_target_pairs={{0,4},{4,0},{8,12},{12,8},{1,5},{5,1},{9,13},{13,9},{2,6},{6,2},{1... | collective-permute-start | bytes 663560 | tf_op jit(solution)/shard_map/ppermute | solution.py:794
  51.6 19.8 %collective-permute-start.12 = (bf16[144,768]{1,0:T(8,128)(2,1)}, bf16[144,768]{1,0:T(8,128)(2,1)S(1)}, u32[]{:S(2)}, u32[]{:S(2)}) collective-permute-start(bf16[144,768]{1,0:T(8,128)(2,1)} %get-tuple-element.157), channel_id=1, source_target_pairs={{0,8},{4,12},{8,0},{12,4},{1,9},{5,13},{9,1},{13,5},{2,10},{6,14},... | collective-permute-start | bytes 663560 | tf_op jit(solution)/shard_map/ppermute | solution.py:794
  72.4 212.3 %reduce-scatter.2.cloned.1.call-start = ((), (), s32[]{:S(2)}) async-start(), calls=%async_computation.1 | async-start | bytes 4423680 | tf_op jit(solution)/shard_map/reduce_scatter | solution.py:951
  72.5 33.8 %collective-permute-start.18 = (bf16[4,384,768]{2,1,0:T(8,128)(2,1)}, bf16[4,384,768]{2,1,0:T(8,128)(2,1)S(1)}, u32[]{:S(2)}, u32[]{:S(2)}) collective-permute-start(bf16[4,384,768]{2,1,0:T(8,128)(2,1)} %refs_13_.1), channel_id=1, source_target_pairs={{0,16},{16,0},{1,17},{17,1},{2,18},{18,2},{3,19},{19,3},{4,20},{20... | collective-permute-start | bytes 7077896 | tf_op jit(solution)/shard_map/ppermute | solution.py:784
  73.3 33.0 %collective-permute-start.19 = (bf16[4,768,384]{2,1,0:T(8,128)(2,1)S(1)}, bf16[4,768,384]{2,1,0:T(8,128)(2,1)}, u32[]{:S(2)}, u32[]{:S(2)}) collective-permute-start(bf16[4,768,384]{2,1,0:T(8,128)(2,1)S(1)} %copy-done.1), channel_id=1, source_target_pairs={{0,16},{16,0},{1,17},{17,1},{2,18},{18,2},{3,19},{19,3},{4,20},{20... | collective-permute-start | bytes 7077896 | tf_op jit(solution)/shard_map/ppermute | solution.py:784
  73.4 21.9 %collective-permute-start.14 = (bf16[384,768]{1,0:T(8,128)(2,1)}, bf16[384,768]{1,0:T(8,128)(2,1)S(1)}, u32[]{:S(2)}, u32[]{:S(2)}) collective-permute-start(bf16[384,768]{1,0:T(8,128)(2,1)} %get-tuple-element.160), channel_id=1, source_target_pairs={{0,1},{1,0},{2,3},{3,2},{4,5},{5,4},{6,7},{7,6},{8,9},{9,8},{10,11... | collective-permute-start | bytes 1769480 | tf_op jit(solution)/shard_map/ppermute | solution.py:794
  74.8 22.8 %collective-permute-start.16 = (bf16[384,768]{1,0:T(8,128)(2,1)}, bf16[384,768]{1,0:T(8,128)(2,1)S(1)}, u32[]{:S(2)}, u32[]{:S(2)}) collective-permute-start(bf16[384,768]{1,0:T(8,128)(2,1)} %get-tuple-element.162), channel_id=1, source_target_pairs={{0,2},{1,3},{2,0},{3,1},{4,6},{5,7},{6,4},{7,5},{8,10},{9,11},{10,... | collective-permute-start | bytes 1769480 | tf_op jit(solution)/shard_map/ppermute | solution.py:794
  114.3 19.0 %collective-permute-start.25 = (bf16[144,768]{1,0:T(8,128)(2,1)}, bf16[144,768]{1,0:T(8,128)(2,1)S(1)}, u32[]{:S(2)}, u32[]{:S(2)}) collective-permute-start(bf16[144,768]{1,0:T(8,128)(2,1)} %get-tuple-element.173), channel_id=1, source_target_pairs={{0,8},{4,12},{8,0},{12,4},{1,9},{5,13},{9,1},{13,5},{2,10},{6,14},... | collective-permute-start | bytes 663560 | tf_op jit(solution)/shard_map/ppermute | solution.py:794
  116.1 19.4 %collective-permute-start.28 = (bf16[144,768]{1,0:T(8,128)(2,1)}, bf16[144,768]{1,0:T(8,128)(2,1)S(1)}, u32[]{:S(2)}, u32[]{:S(2)}) collective-permute-start(bf16[144,768]{1,0:T(8,128)(2,1)} %get-tuple-element.174), channel_id=1, source_target_pairs={{0,12},{4,8},{8,4},{12,0},{1,13},{5,9},{9,5},{13,1},{2,14},{6,10},... | collective-permute-start | bytes 663560 | tf_op jit(solution)/shard_map/ppermute | solution.py:794
  134.4 18.9 %collective-permute-start.21 = (bf16[288,768]{1,0:T(8,128)(2,1)S(1)}, bf16[288,768]{1,0:T(8,128)(2,1)S(1)}, u32[]{:S(2)}, u32[]{:S(2)}) collective-permute-start(bf16[288,768]{1,0:T(8,128)(2,1)S(1)} %pad_maximum_fusion.6), channel_id=1, source_target_pairs={{0,2},{1,3},{2,0},{3,1},{4,6},{5,7},{6,4},{7,5},{8,10},{9,11},{10,... | collective-permute-start | bytes 1327112 | tf_op jit(solution)/shard_map/ppermute | solution.py:794
  225.3 19.9 %collective-permute-start.39 = (bf16[144,768]{1,0:T(8,128)(2,1)S(1)}, bf16[144,768]{1,0:T(8,128)(2,1)S(1)}, u32[]{:S(2)}, u32[]{:S(2)}) collective-permute-start(bf16[144,768]{1,0:T(8,128)(2,1)S(1)} %fusion.8), channel_id=1, source_target_pairs={{0,4},{4,0},{8,12},{12,8},{1,5},{5,1},{9,13},{13,9},{2,6},{6,2},{1... | collective-permute-start | bytes 663560 | tf_op jit(solution)/shard_map/ppermute | solution.py:794
  245.4 22.7 %collective-permute-start.47 = (bf16[4,768,384]{2,1,0:T(8,128)(2,1)}, bf16[4,768,384]{2,1,0:T(8,128)(2,1)S(1)}, u32[]{:S(2)}, u32[]{:S(2)}) collective-permute-start(bf16[4,768,384]{2,1,0:T(8,128)(2,1)} %get-tuple-element.216), channel_id=1, source_target_pairs={{0,16},{16,0},{1,17},{17,1},{2,18},{18,2},{3,19},{19,3},{4,20},{20... | collective-permute-start | bytes 7077896 | tf_op jit(solution)/shard_map/ppermute | solution.py:784
  261.3 23.4 %collective-permute-start.43 = (bf16[384,768]{1,0:T(8,128)(2,1)S(1)}, bf16[384,768]{1,0:T(8,128)(2,1)S(1)}, u32[]{:S(2)}, u32[]{:S(2)}) collective-permute-start(bf16[384,768]{1,0:T(8,128)(2,1)S(1)} %pad_maximum_fusion.4), channel_id=1, source_target_pairs={{0,2},{1,3},{2,0},{3,1},{4,6},{5,7},{6,4},{7,5},{8,10},{9,11},{10,... | collective-permute-start | bytes 1769480 | tf_op jit(solution)/shard_map/ppermute | solution.py:794
  262.6 22.1 %collective-permute-start.45 = (bf16[384,768]{1,0:T(8,128)(2,1)S(1)}, bf16[384,768]{1,0:T(8,128)(2,1)S(1)}, u32[]{:S(2)}, u32[]{:S(2)}) collective-permute-start(bf16[384,768]{1,0:T(8,128)(2,1)S(1)} %pad_maximum_fusion.5), channel_id=1, source_target_pairs={{0,1},{1,0},{2,3},{3,2},{4,5},{5,4},{6,7},{7,6},{8,9},{9,8},{10,11... | collective-permute-start | bytes 1769480 | tf_op jit(solution)/shard_map/ppermute | solution.py:794
  287.2 28.9 %collective-permute-start.50 = (bf16[144,768]{1,0:T(8,128)(2,1)S(1)}, bf16[144,768]{1,0:T(8,128)(2,1)S(1)}, u32[]{:S(2)}, u32[]{:S(2)}) collective-permute-start(bf16[144,768]{1,0:T(8,128)(2,1)S(1)} %get-tuple-element.251), channel_id=1, source_target_pairs={{0,12},{4,8},{8,4},{12,0},{1,13},{5,9},{9,5},{13,1},{2,14},{6,10},... | collective-permute-start | bytes 663560 | tf_op jit(solution)/shard_map/ppermute | solution.py:794
  290.5 25.6 %collective-permute-start.49 = (bf16[144,768]{1,0:T(8,128)(2,1)S(1)}, bf16[144,768]{1,0:T(8,128)(2,1)S(1)}, u32[]{:S(2)}, u32[]{:S(2)}) collective-permute-start(bf16[144,768]{1,0:T(8,128)(2,1)S(1)} %get-tuple-element.252), channel_id=1, source_target_pairs={{0,8},{4,12},{8,0},{12,4},{1,9},{5,13},{9,1},{13,5},{2,10},{6,14},... | collective-permute-start | bytes 663560 | tf_op jit(solution)/shard_map/ppermute | solution.py:794
  290.5 25.6 %collective-permute-start.48 = (bf16[144,768]{1,0:T(8,128)(2,1)S(1)}, bf16[144,768]{1,0:T(8,128)(2,1)S(1)}, u32[]{:S(2)}, u32[]{:S(2)}) collective-permute-start(bf16[144,768]{1,0:T(8,128)(2,1)S(1)} %get-tuple-element.253), channel_id=1, source_target_pairs={{0,4},{4,0},{8,12},{12,8},{1,5},{5,1},{9,13},{13,9},{2,6},{6,2},{1... | collective-permute-start | bytes 663560 | tf_op jit(solution)/shard_map/ppermute | solution.py:794
  317.8 28.2 %collective-permute-start.52 = (bf16[384,768]{1,0:T(8,128)(2,1)}, bf16[384,768]{1,0:T(8,128)(2,1)S(1)}, u32[]{:S(2)}, u32[]{:S(2)}) collective-permute-start(bf16[384,768]{1,0:T(8,128)(2,1)} %get-tuple-element.239), channel_id=1, source_target_pairs={{0,2},{1,3},{2,0},{3,1},{4,6},{5,7},{6,4},{7,5},{8,10},{9,11},{10,... | collective-permute-start | bytes 1769480 | tf_op jit(solution)/shard_map/ppermute | solution.py:794
  318.3 27.7 %collective-permute-start.53 = (bf16[384,768]{1,0:T(8,128)(2,1)}, bf16[384,768]{1,0:T(8,128)(2,1)S(1)}, u32[]{:S(2)}, u32[]{:S(2)}) collective-permute-start(bf16[384,768]{1,0:T(8,128)(2,1)} %get-tuple-element.240), channel_id=1, source_target_pairs={{0,3},{1,2},{2,1},{3,0},{4,7},{5,6},{6,5},{7,4},{8,11},{9,10},{10,... | collective-permute-start | bytes 1769480 | tf_op jit(solution)/shard_map/ppermute | solution.py:794
  321.8 29.2 %collective-permute-start.55 = (bf16[128,768]{1,0:T(8,128)(2,1)}, bf16[128,768]{1,0:T(8,128)(2,1)}, u32[]{:S(2)}, u32[]{:S(2)}) collective-permute-start(bf16[128,768]{1,0:T(8,128)(2,1)} %get-tuple-element.248), channel_id=1, source_target_pairs={{0,4},{4,0},{8,12},{12,8},{1,5},{5,1},{9,13},{13,9},{2,6},{6,2},{1... | collective-permute-start | bytes 589832 | tf_op jit(solution)/shard_map/ppermute | solution.py:794
  322.8 28.3 %collective-permute-start.57 = (bf16[128,768]{1,0:T(8,128)(2,1)}, bf16[128,768]{1,0:T(8,128)(2,1)}, u32[]{:S(2)}, u32[]{:S(2)}) collective-permute-start(bf16[128,768]{1,0:T(8,128)(2,1)} %get-tuple-element.249), channel_id=1, source_target_pairs={{0,12},{4,8},{8,4},{12,0},{1,13},{5,9},{9,5},{13,1},{2,14},{6,10},... | collective-permute-start | bytes 589832 | tf_op jit(solution)/shard_map/ppermute | solution.py:794
  332.6 18.4 %collective-permute-start.56 = (bf16[128,768]{1,0:T(8,128)(2,1)}, bf16[128,768]{1,0:T(8,128)(2,1)}, u32[]{:S(2)}, u32[]{:S(2)}) collective-permute-start(bf16[128,768]{1,0:T(8,128)(2,1)} %get-tuple-element.250), channel_id=1, source_target_pairs={{0,8},{4,12},{8,0},{12,4},{1,9},{5,13},{9,1},{13,5},{2,10},{6,14},... | collective-permute-start | bytes 589832 | tf_op jit(solution)/shard_map/ppermute | solution.py:794
  (87 other events, 1072.7 us)
Sparse Core Ops, SparseCore 0:
  72.6 63.0 all-gather.2
  225.4 56.7 reduce-scatter.1

commit v7 on v6

--- a/solution.py
+++ b/solution.py
@@ -195,14 +195,11 @@
     return result[:tensors], result[tensors:]
 
 
-def attend_back_kernel(
-    heads, tensors, part, place_ref, bias_ref, tok_ref, gain_ref, w_ref, qkv_ref, mixed_ref, log_ref, *refs
-):
+def attend_back_kernel(heads, place_ref, bias_ref, tok_ref, gain_ref, w_ref, qkv_ref, log_ref, *refs):
     refs = list(refs)
     pieces = [refs.pop(0) for _ in range(5)]
-    gain_two_ref, router_ref = refs.pop(0), refs.pop(0)
-    parts = [refs.pop(0) for _ in range(tensors)]
-    own_ref, other_ref, weight_ref, gain_out, table, wo, gmix, gproj, near, far, rows_s, group, result = refs
+    parts = [refs.pop(0) for _ in range(4)]
+    gproj, group_ref, near, far, gain_out, table, wo, gmix, group, result = refs
     inner = heads * HEAD_DIM
     blocks = LENGTH // TILE
     step_id = pl.program_id(0)
@@ -213,12 +210,12 @@
         wo[...] = w_ref[:, 3 * inner :]
         near[...] = jnp.zeros_like(near)
         far[...] = jnp.zeros_like(far)
-        weight_ref[...] = jnp.zeros_like(weight_ref)
         gain_out[...] = jnp.zeros_like(gain_out)
         group_halves(place_ref, group, pieces)
 
     here = pl.ds(pl.multiple_of(step_id * LENGTH, LENGTH), LENGTH)
-    gmix[...] = dot(group[here, :], wo[...]).astype(BF16)
+    group_ref[...] = group[here, :]
+    gmix[...] = dot(group_ref[...], wo[...]).astype(BF16)
     for head in range(heads):
         at = head * HEAD_DIM
         query = (qkv_ref[:, at : at + HEAD_DIM] * HEAD_DIM ** (-0.5)).astype(BF16)
@@ -253,16 +250,79 @@
             attention.astype(BF16), grad_rows, ROWS_TN
         ).astype(BF16)
     unit, _ = unit_rows(tok_ref[...].astype(F32))
-    normed = (unit * gain_ref[...]).astype(BF16)
     grad_normed = dot(gproj[...], w_ref[:, : 3 * inner], ROWS_NT)
     result[here, :] = grad_normed.astype(BF16)
     gain_out[...] += jnp.sum(grad_normed * unit, axis=0, keepdims=True)
-    weight_ref[:, : 3 * inner] += dot(normed, gproj[...], ROWS_TN)
-    weight_ref[:, 3 * inner :] += dot(group[here, :], mixed_ref[...], ROWS_TN)
 
     @pl.when(step_id == pl.num_programs(0) - 1)
     def _():
-        part_rows(place_ref, parts, result)
+        part_halves(place_ref, parts, result)
+
+
+def attend_back(places, bias, tokens, gain, weights, projected, logs, pieces):
+    rows, width = tokens.shape
+    piece = whole(pieces[0].shape)
+    heads = bias.shape[0]
+    inner = heads * HEAD_DIM
+    seqs = rows // LENGTH
+    by_seq = lambda cols: pl.BlockSpec((LENGTH, cols), lambda s, *_: (s, 0))
+    near, far = (heads * 3, TILE, TILE), (heads * 2, TILE, TILE)
+    result = pl.pallas_call(
+        functools.partial(attend_back_kernel, heads),
+        grid_spec=pltpu.PrefetchScalarGridSpec(
+            num_scalar_prefetch=1,
+            grid=(seqs,),
+            in_specs=[
+                pl.BlockSpec(memory_space=pltpu.SMEM),
+                by_seq(width),
+                whole((1, width)),
+                whole((width, 4 * inner)),
+                by_seq(3 * inner),
+                by_seq(TILE),
+            ]
+            + [whole(p.shape) for p in pieces],
+            out_specs=[piece] * 4
+            + [by_seq(3 * inner), by_seq(width), whole(near), whole(far), whole((1, width))],
+            scratch_shapes=[
+                pltpu.VMEM((heads, LENGTH, LENGTH), F32),
+                pltpu.VMEM((width, inner), BF16),
+                pltpu.VMEM((LENGTH, inner), BF16),
+                pltpu.VMEM((rows, width), BF16),
+                pltpu.VMEM((rows, width), BF16),
+            ],
+        ),
+        out_shape=[jax.ShapeDtypeStruct(pieces[0].shape, BF16)] * 4
+        + [
+            jax.ShapeDtypeStruct((rows, 3 * inner), BF16),
+            jax.ShapeDtypeStruct((rows, width), BF16),
+            jax.ShapeDtypeStruct(near, F32),
+            jax.ShapeDtypeStruct(far, F32),
+            jax.ShapeDtypeStruct((1, width), F32),
+        ],
+        compiler_params=params(),
+        cost_estimate=cost(8 * rows * width * inner + 10 * rows * LENGTH * inner, rows * width * 12, rows * LENGTH * heads),
+        name="attend_back",
+    )(places, bias, tokens, gain, weights, projected, logs, *pieces)
+    return result[:4], result[4:]
+
+
+def attend_weights_kernel(
+    heads, part, place_ref, tok_ref, gain_ref, gproj, group_ref, mixed_ref, near, far,
+    gain_out, gain_two_ref, router_ref, own_ref, other_ref, weight_ref, rows_s,
+):
+    inner = heads * HEAD_DIM
+
+    @pl.when(pl.program_id(0) == 0)
+    def _():
+        weight_ref[...] = jnp.zeros_like(weight_ref)
+
+    unit, _ = unit_rows(tok_ref[...].astype(F32))
+    normed = (unit * gain_ref[...]).astype(BF16)
+    weight_ref[:, : 3 * inner] += dot(normed, gproj[...], ROWS_TN)
+    weight_ref[:, 3 * inner :] += dot(group_ref[...], mixed_ref[...], ROWS_TN)
+
+    @pl.when(pl.program_id(0) == pl.num_programs(0) - 1)
+    def _():
         ids = [tile_bucket(step) for step in (-1, 0, 1)]
         for head in range(heads):
             for k in range(BUCKETS):
@@ -305,11 +365,9 @@
                 ref[k, part + 16 :, :] = tail
 
 
-def attend_back(places, bias, tokens, gain, weights, projected, mixed, logs, pieces, gain_two, router, part, z_count):
+def attend_weights(places, tokens, gain, grads, mixed, gain_two, router, heads, part, z_count):
+    gproj, group, near, far, gain_one = grads
     rows, width = tokens.shape
-    tensors = rows // pieces[0].shape[0]
-    piece = whole(pieces[0].shape)
-    heads = bias.shape[0]
     inner = heads * HEAD_DIM
     seqs = rows // LENGTH
     by_seq = lambda cols: pl.BlockSpec((LENGTH, cols), lambda s, *_: (s, 0))
@@ -317,48 +375,36 @@
     sent = (z_count, part + 16 + experts + -experts % 16, width)
     if part % 16:
         sent = (heads * BUCKETS, 1)
-    result = pl.pallas_call(
-        functools.partial(attend_back_kernel, heads, tensors, part),
+    kind = F32 if part % 16 else BF16
+    return pl.pallas_call(
+        functools.partial(attend_weights_kernel, heads, part),
         grid_spec=pltpu.PrefetchScalarGridSpec(
             num_scalar_prefetch=1,
             grid=(seqs,),
             in_specs=[
-                pl.BlockSpec(memory_space=pltpu.SMEM),
                 by_seq(width),
                 whole((1, width)),
-                whole((width, 4 * inner)),
                 by_seq(3 * inner),
+                by_seq(width),
                 by_seq(inner),
-                by_seq(TILE),
-            ]
-            + [whole(p.shape) for p in pieces]
-            + [whole((1, width)), whole((experts, width))],
-            out_specs=[piece] * tensors
-            + [whole(sent), whole(sent), whole((width, 4 * inner)), whole((1, width))],
-            scratch_shapes=[
-                pltpu.VMEM((heads, LENGTH, LENGTH), F32),
-                pltpu.VMEM((width, inner), BF16),
-                pltpu.VMEM((LENGTH, inner), BF16),
-                pltpu.VMEM((LENGTH, 3 * inner), BF16),
-                pltpu.VMEM((heads * 3, TILE, TILE), F32),
-                pltpu.VMEM((heads * 2, TILE, TILE), F32),
-                pltpu.VMEM((heads * BUCKETS, TILE), F32),
-                pltpu.VMEM((rows, width), BF16),
-                pltpu.VMEM((rows, width), BF16),
+                whole(near.shape),
+                whole(far.shape),
+                whole((1, width)),
+                whole((1, width)),
+                whole((experts, width)),
             ],
+            out_specs=[whole(sent), whole(sent), whole((width, 4 * inner))],
+            scratch_shapes=[pltpu.VMEM((heads * BUCKETS, TILE), F32)],
         ),
-        out_shape=[jax.ShapeDtypeStruct(pieces[0].shape, BF16)] * tensors
-        + [
-            jax.ShapeDtypeStruct(sent, F32 if part % 16 else BF16),
-            jax.ShapeDtypeStruct(sent, F32 if part % 16 else BF16),
+        out_shape=[
+            jax.ShapeDtypeStruct(sent, kind),
+            jax.ShapeDtypeStruct(sent, kind),
             jax.ShapeDtypeStruct((width, 4 * inner), F32),
-            jax.ShapeDtypeStruct((1, width), F32),
         ],
         compiler_params=params(),
-        cost_estimate=cost(18 * rows * width * inner + 10 * rows * LENGTH * inner, rows * width * 12, rows * LENGTH * heads),
-        name="attend_back",
-    )(places, bias, tokens, gain, weights, projected, mixed, logs, *pieces, gain_two, router)
-    return result[:tensors], result[tensors:]
+        cost_estimate=cost(8 * rows * width * inner, rows * width * 12),
+        name="attend_weights",
+    )(places, tokens, gain, gproj, group, mixed, near, far, gain_one, gain_two, router)
 
 
 def first_rows_kernel(count, *refs):
@@ -493,13 +539,8 @@
         part = spread[rest_at : rest_at + blocks * locals_ * rest].reshape(blocks, locals_ * rest, width)
         rest_at += blocks * locals_ * rest
 
-        @pl.when(expert == 0)
-        def _():
-            view[:, locals_ * main :, :] = part
-
-        @pl.when(expert > 0)
-        def _():
-            view[:, locals_ * main :, :] = view[:, locals_ * main :, :] + part
+        before = view[:, locals_ * main :, :]
+        view[:, locals_ * main :, :] = part + jnp.where(expert > 0, before, jnp.zeros_like(before))
 
 
 def group_views(place_ref, ref, tensors, chunks):
@@ -548,8 +589,6 @@
     pick_rows(x_ref.at[0], xs, choice, main_rows, main, expert)
     pick_rows(grows, group_views(place_ref, g_ref, tensors, chunks), choice, main_rows, main, expert)
     join_halves(place_ref, own_in, peer_in, own_out, peer_out, win, wout)
-    inner[...] = dot(x_ref[0], win[...])
-    gunits[...] = dot(grows[...], wout[...], ROWS_NT)
     probs = softmax_rows(dot(x_ref[0], router[...]))
     lanes = lax.broadcasted_iota(jnp.int32, probs.shape, 1)
     mine = lanes == place_ref[1] * locals_ + expert
@@ -557,37 +596,57 @@
     gate_s[...] = jnp.broadcast_to(picked, gate_s.shape)
     chunk = 16
     half_wide = wide // 2 if wide % (2 * TILE) == 0 else wide
-
-    def body(step, _):
-        at = pl.ds(pl.multiple_of(step * chunk, chunk), chunk)
-        gate_tile = gate_s[at, :]
-        gate = jnp.concatenate([gate_tile] * (half_wide // TILE), axis=1)
-        total = None
-        for start in range(0, wide, half_wide):
-            lanes_at = slice(start, start + half_wide)
-            value = inner[at, lanes_at]
-            square = value * value
-            wave = jnp.tanh(value * (GELU_A + (GELU_A * GELU_B) * square))
-            half = 0.5 + 0.5 * wave
-            hidden = (value * half).astype(BF16)
-            bend = value * (0.5 * GELU_A + (1.5 * GELU_A * GELU_B) * square)
-            slope = half + bend * (1.0 - wave * wave)
-            units = gunits[at, lanes_at]
-            hid_ref[0, at, lanes_at] = hidden
-            gi_ref[0, at, lanes_at] = (gate * (units * slope)).astype(BF16)
-            product = hidden.astype(F32) * units
-            for tile in range(0, half_wide, TILE):
-                part = product[:, tile : tile + TILE]
-                total = part if total is None else total + part
-        dots[at, :] = total
-        gate = jnp.concatenate([gate_tile] * (width // TILE), axis=1)
-        ge_ref[0, at, :] = (gate * grows[at, :].astype(F32)).astype(BF16)
-        return 0
-
-    lax.fori_loop(0, rows // chunk, body, 0, unroll=4)
-    grad_logits = (jnp.sum(dots[...], axis=-1, keepdims=True) * probs * (jnp.where(mine, 1.0, 0.0) - picked)).astype(BF16)
-    gl_ref[0] = grad_logits
-    back[...] = (dot(gi_ref[0], win[...], ROWS_NT) + dot(grad_logits, router[...], ROWS_NT)).astype(BF16)
+    half_rows = rows // 2
+
+    def multiply(part):
+        at = slice(part * half_rows, (part + 1) * half_rows)
+        inner[at, :] = dot(x_ref[0, at, :], win[...])
+        gunits[at, :] = dot(grows[at, :], wout[...], ROWS_NT)
+
+    def activate(part):
+        for row in range(part * half_rows, (part + 1) * half_rows, chunk):
+            at = slice(row, row + chunk)
+            gate_tile = gate_s[at, :]
+            gate = jnp.concatenate([gate_tile] * (half_wide // TILE), axis=1)
+            total = None
+            for start in range(0, wide, half_wide):
+                lanes_at = slice(start, start + half_wide)
+                value = inner[at, lanes_at]
+                square = value * value
+                wave = jnp.tanh(value * (GELU_A + (GELU_A * GELU_B) * square))
+                half = 0.5 + 0.5 * wave
+                hidden = (value * half).astype(BF16)
+                bend = value * (0.5 * GELU_A + (1.5 * GELU_A * GELU_B) * square)
+                slope = half + bend * (1.0 - wave * wave)
+                units = gunits[at, lanes_at]
+                hid_ref[0, at, lanes_at] = hidden
+                gi_ref[0, at, lanes_at] = (gate * (units * slope)).astype(BF16)
+                product = hidden.astype(F32) * units
+                for tile in range(0, half_wide, TILE):
+                    part_sum = product[:, tile : tile + TILE]
+                    total = part_sum if total is None else total + part_sum
+            dots[at, :] = total
+            gate = jnp.concatenate([gate_tile] * (width // TILE), axis=1)
+            ge_ref[0, at, :] = (gate * grows[at, :].astype(F32)).astype(BF16)
+
+    def finish(part):
+        at = slice(part * half_rows, (part + 1) * half_rows)
+        grad_logits = (
+            jnp.sum(dots[at, :], axis=-1, keepdims=True)
+            * probs[at]
+            * (jnp.where(mine[at], 1.0, 0.0) - picked[at])
+        ).astype(BF16)
+        gl_ref[0, at, :] = grad_logits
+        back[at, :] = (
+            dot(gi_ref[0, at, :], win[...], ROWS_NT) + dot(grad_logits, router[...], ROWS_NT)
+        ).astype(BF16)
+
+    multiply(0)
+    multiply(1)
+    activate(0)
+    finish(0)
+    activate(1)
+    finish(1)
     put_rows(back_refs, back, choice, main_rows, main, locals_, rest, expert)
 
 
@@ -763,11 +822,16 @@
 
 
 def tokens_back_kernel(tok_ref, *refs):
-    gain_ref, hidden_ref, out_ref = refs[-3:]
-    unit, scale = unit_rows(tok_ref[...].astype(F32))
-    scaled = sum_pieces(refs[:-3]) * gain_ref[...]
-    inside = jnp.mean(unit * scaled, axis=-1, keepdims=True)
-    out_ref[...] = hidden_ref[...] + scale * (scaled - unit * inside)
+    gain_ref, hidden_ref, out_ref = refs[6:]
+    half = tok_ref.shape[0] // 2
+    for h in range(2):
+        keep, got, last = refs[3 * h : 3 * h + 3]
+        here = slice(h * half, (h + 1) * half)
+        unit, scale = unit_rows(tok_ref[here, :].astype(F32))
+        grad = keep[:half, :].astype(F32) + got[:half, :].astype(F32) + last[...].astype(F32)
+        scaled = grad * gain_ref[...]
+        inside = jnp.mean(unit * scaled, axis=-1, keepdims=True)
+        out_ref[here, :] = hidden_ref[here, :] + scale * (scaled - unit * inside)
 
 
 def tokens_back(tokens, grad_normed, gain, grad_hidden):
@@ -803,6 +867,17 @@
     first = swapped(value, "tensor", 4, a)
     second = swapped(jnp.concatenate([value, first], axis=0), "tensor", 4, b)
     return first, second
+
+
+def sum_hops(parts):
+    half = parts[0].shape[0] // 2
+    result = []
+    for h, (a, b) in enumerate(HOPS):
+        keep, send = parts[2 * h : 2 * h + 2]
+        got = swapped(send, "tensor", 4, a)
+        last = swapped(added(keep[half:], got[half:]), "tensor", 4, b)
+        result += [keep, got, last]
+    return result
 
 
 def added(a, b):
@@ -867,6 +942,29 @@
         [packed, jnp.pad(small, (0, extra * width - small.shape[0])).reshape(extra, width)], axis=0
     )
     owned = gather_pieces(packed[None], "expert", z_count)
+
+    chunks = min(z_count, 4)
+    many = z_count // chunks
+
+    def over_expert(groups):
+        if many > 1:
+            groups = [g[i * block : (i + 1) * block] for g in groups for i in range(many)]
+        pieces = swap_pieces(groups, "expert", z_count)
+        if many == 1:
+            return pieces
+        return [jnp.concatenate(pieces[k * many : (k + 1) * many], axis=0) for k in range(chunks)]
+
+    z_of = expert_index // locals_
+    local = expert_index - z_of * locals_
+    inside = jnp.where(
+        slot_index < main, local * main + slot_index, locals_ * main + local * rest + slot_index - main
+    )
+    target = (z_of ^ my_z) * block + inside
+    target = jnp.where(kept_mask > 0, target, -1)
+    target_row, target_col = target[None, :], target[:, None]
+    counts = [many * block] * chunks
+    grad_sent = place(target_row, cotangent, counts)
+    owned, grad_sent = lax.optimization_barrier((owned, grad_sent))
     owned = owned + [swapped(jnp.concatenate(owned, axis=0), "dp", dp_count, 1)]
     if part % 16 or part % extra:
         smalls = jnp.concatenate(owned, axis=0)[:, part:]
@@ -875,21 +973,11 @@
     smalls = smalls.reshape(owners, -1)[:, : small.shape[0]]
     small_pieces = gather_pieces(smalls, "tensor", t_count)
 
-    z_of = expert_index // locals_
-    local = expert_index - z_of * locals_
-    inside = jnp.where(
-        slot_index < main, local * main + slot_index, locals_ * main + local * rest + slot_index - main
-    )
-    target = (z_of ^ my_z) * block + inside
-    target = jnp.where(kept_mask > 0, target, -1)
-    target_row, target_col = target[None, :], target[:, None]
-    chunks = min(z_count, 4)
-    many = z_count // chunks
-    counts = [many * block] * chunks
-    grad_sent = place(target_row, cotangent, counts)
-    token_pieces, owned, small_pieces, grad_sent = lax.optimization_barrier(
-        (token_pieces, owned, small_pieces, grad_sent)
-    )
+    grad_rows = jnp.concatenate(over_expert(grad_sent), axis=0)
+    token_pieces, owned, small_pieces, grad_rows = lax.optimization_barrier(
+        (token_pieces, owned, small_pieces, grad_rows)
+    )
+    grad_arrived = lax.all_gather(grad_rows, "tensor", axis=0).reshape(t_count, z_count, block, width)
     smalls = jnp.stack(small_pieces).reshape(t_count * owners, -1)
     owner_ids = jnp.arange(owners, dtype=jnp.int32)[:, None] ^ my_owner
     t_ids = jnp.arange(t_count, dtype=jnp.int32)[None, :] ^ my_t
@@ -902,28 +990,15 @@
     gain_two = smalls[:, 1].astype(F32)[None]
     router = smalls[:, 2:]
 
-    def over_expert(groups):
-        if many > 1:
-            groups = [g[i * block : (i + 1) * block] for g in groups for i in range(many)]
-        pieces = swap_pieces(groups, "expert", z_count)
-        if many == 1:
-            return pieces
-        return [jnp.concatenate(pieces[k * many : (k + 1) * many], axis=0) for k in range(chunks)]
 
     grad_rows = jnp.concatenate(over_expert(grad_sent), axis=0)
     parts, (group_tokens, projected, mixed, logs, weights) = attend(
         places, bias, token_pieces, owned, rows_owned, gain_one
     )
-    parts, late_in, late_out, grad_rows = lax.optimization_barrier((parts, w_in, w_out, grad_rows))
+    parts, late_in, late_out = lax.optimization_barrier((parts, w_in, w_out))
     peer_in = shifted(late_in, "dp", dp_count, 1)
     peer_out = shifted(late_out, "dp", dp_count, 1)
-    grad_arrived = lax.all_gather(grad_rows, "tensor", axis=0).reshape(t_count, z_count, block, width)
-    attn = []
-    for h, (a, b) in enumerate(HOPS):
-        keep, send = parts[2 * h : 2 * h + 2]
-        got = swapped(send, "tensor", t_count, a)
-        last = swapped(added(keep[half_rows:], got[half_rows:]), "tensor", t_count, b)
-        attn += [keep, got, last]
+    attn = sum_hops(parts)
     attn, peer_in, peer_out = lax.optimization_barrier((attn, peer_in, peer_out))
     hidden_one, gate, sent = route(
         tokens, attn, gain_two, router, target_row, expert_index[:, None], kept_mask[:, None], counts
@@ -942,15 +1017,15 @@
     got = [swapped(sends[k], "tensor", t_count, HOPS[k % 2][0]) for k in reversed(range(chunks))][::-1]
     forward_part = expert_rows(places, saved[2], w_out, peer_out, grad_arrived.shape, main, rest, chunks)
     got, forward_part = lax.optimization_barrier((got, forward_part))
+    forward_sum = lax.psum_scatter(
+        forward_part.reshape(t_count * z_count * block, width), "tensor", scatter_dimension=0, tiled=True
+    )
     groups = []
     for k in range(chunks):
         last = swapped(added(keeps[k][size:], got[k][size:]), "tensor", t_count, HOPS[k % 2][1])
         total = keeps[k][:size].astype(F32) + got[k][:size].astype(F32) + last.astype(F32)
         groups.append(total.astype(BF16))
-    forward_part, groups, saved = lax.optimization_barrier((forward_part, groups, saved))
-    forward_sum = lax.psum_scatter(
-        forward_part.reshape(t_count * z_count * block, width), "tensor", scatter_dimension=0, tiled=True
-    )
+    groups, saved = lax.optimization_barrier((groups, saved))
     in_own, in_send, out_own, out_send, router_part = expert_weights(places, saved, w_in.shape[1])
     grad_back, in_send, out_send = lax.optimization_barrier((over_expert(groups), in_send, out_send))
     in_got = shifted(in_send, "dp", dp_count, 1)
@@ -964,15 +1039,16 @@
     grad_pieces, grad_w_in, grad_w_out, forward_sum = lax.optimization_barrier(
         (grad_pieces, grad_w_in, grad_w_out, forward_sum)
     )
-    normed_parts, (own_part, other_part, weight_part, gain_one_part) = attend_back(
-        places, bias, group_tokens, gain_one, weights, projected, mixed, logs, grad_pieces,
-        gain_two_part, router_part, part, z_count,
+    normed_parts, grads = attend_back(
+        places, bias, group_tokens, gain_one, weights, projected, logs, grad_pieces
     )
     forward_rows = over_expert(list(forward_sum.reshape(chunks, many * block, width)))
-    normed_parts, own_part, other_part, forward_rows = lax.optimization_barrier(
-        (normed_parts, own_part, other_part, forward_rows)
-    )
-    grad_normed = swap_pieces(normed_parts, "tensor", t_count)
+    normed_parts, grads, forward_rows = lax.optimization_barrier((normed_parts, grads, forward_rows))
+    own_part, other_part, weight_part = attend_weights(
+        places, group_tokens, gain_one, grads, mixed, gain_two_part, router_part, heads, part, z_count
+    )
+    gain_one_part = grads[4]
+    grad_normed = sum_hops(normed_parts)
     output = output_rows(target_col, forward_rows, hidden_one, gate)
     grad_tokens = tokens_back(tokens, grad_normed, gain_one, grad_hidden)
 

time: 368 us -> 373 us (1.014)
  waiting for transfers between devices: 113 us -> 126 us
  Pallas kernels: 120 us -> 115 us
    ppermute x56 -> x57, waiting for transfers between devices: 113 us -> 126 us  [swapped(): return lax.ppermute(value, axis, [(s, s ^ bits) for s in range(count)])]
    pallas_call x1, Pallas kernels: 35 us -> 23.3 us  [expert_forward_back(): pl.pallas_call(functools.partial(expert_kernel, chunks, tensors, main, lo...]
    pallas_call x1 -> x2, Pallas kernels: 24.5 us -> 30.6 us  [the longest x1 19.8 us: attend_back(): pl.pallas_call(functools.partial(attend_back_kernel, heads), grid_spec=pl...]
    unnamed x100 -> x116, local copies, waits for them, and re-layouts: 7.48 us -> 6.31 us
    ppermute x56 -> x57, starting transfers between devices: 75.1 us -> 74.5 us  [swapped(): return lax.ppermute(value, axis, [(s, s ^ bits) for s in range(count)])]
  transfers between devices with their start and end apart: 63 -> 64, of which waited for: 20 -> 27; matrix products, arithmetic and copies ran while one was open for 7% -> 8% of each run, Pallas kernels for 23% -> 25%
where the time goes in v7:
time: 373 us; the launch traced here: 372 us
  waiting for transfers between devices  126 us (34%)
  Pallas kernels  115 us (31%)
  starting transfers between devices  75.8 us (20%)
  local copies, waits for them, and re-layouts  21 us (6%)
  other arithmetic  19.9 us (5%)
  between operations  14.8 us (4%)
    ppermute x57, waiting for transfers between devices, swapped(): return lax.ppermute(value, axis, [(s, s ^ bits) for s in range(count)])  126 us
    ppermute x57, starting transfers between devices, swapped(): return lax.ppermute(value, axis, [(s, s ^ bits) for s in range(count)])  74.5 us
    pallas_call x1, Pallas kernels, expert_forward_back(): pl.pallas_call(functools.partial(expert_kernel, chunks, tensors, main, lo...  23.3 us
    pallas_call x1, Pallas kernels, attend_back(): pl.pallas_call(functools.partial(attend_back_kernel, heads), grid_spec=pl...  19.8 us
    pallas_call x1, Pallas kernels, attend(): pl.pallas_call(functools.partial(attend_kernel, heads, tensors, len(owned...  16.3 us
    pallas_call x1, Pallas kernels, expert_weights(): pl.pallas_call(expert_weights_kernel, grid_spec=pltpu.PrefetchScalarGridS...  15.2 us
    pallas_call x1, Pallas kernels, attend_weights(): pl.pallas_call(functools.partial(attend_weights_kernel, heads, part), gri...  10.9 us
    pallas_call x1, Pallas kernels, expert_rows(): pl.pallas_call(functools.partial(expert_rows_kernel, chunks, main, locals...  9.7 us
  transfers between devices with their start and end apart: 64, of which 27 were waited for; matrix products, arithmetic and copies ran while one was open for 8% of the time, Pallas kernels for 25%

profile of v7, /device:TPU:0, one launch (start us, length us, event | category | flops | bytes accessed | tf_op | source)
XLA Modules:
  0.0 372.5 jit_solution(17123186016571083160)
XLA Ops:
  10.4 5.1 %collective-permute-start.6 = (bf16[1,112,768]{2,1,0:T(8,128)(2,1)S(1)}, bf16[1,112,768]{2,1,0:T(8,128)(2,1)S(1)}, u32[]{:S(2)}, u32[]{:S(2)}) collective-permute-start(bf16[1,112,768]{2,1,0:T(8,128)(2,1)S(1)} %maximum_bitcast_fusion.refs_0_.refs_5_), channel_id=1, source_target_pairs={{0,12},{4,8},{8,4},{12,0},{1,13},{5,9},{9,5},{13,1},{2,14},{6,10},... | collective-permute-start | bytes 516104 | tf_op jit(solution)/shard_map/ppermute | solution.py:858
  22.7 7.4 %collective-permute-done.5.refs_2_.refs_7_ = bf16[1,112,768]{2,1,0:T(8,128)(2,1)S(1)} collective-permute-done((bf16[1,112,768]{2,1,0:T(8,128)(2,1)S(1)}, bf16[1,112,768]{2,1,0:T(8,128)(2,1)S(1)}, u32[]{:S(2)}, u32[]{:S(2)}) %collective-permute-start.5) | collective-permute-done | bytes 172064 | tf_op jit(solution)/shard_map/ppermute | solution.py:858
  32.6 7.6 %collective-permute-done.2.refs_3_ = bf16[192,768]{1,0:T(8,128)(2,1)S(1)} collective-permute-done((bf16[192,768]{1,0:T(8,128)(2,1)S(1)}, bf16[192,768]{1,0:T(8,128)(2,1)S(1)}, u32[]{:S(2)}, u32[]{:S(2)}) %collective-permute-start.2) | collective-permute-done | bytes 294944 | tf_op jit(solution)/shard_map/ppermute | solution.py:858
  53.2 7.5 %collective-permute-done.12 = bf16[144,768]{1,0:T(8,128)(2,1)S(1)} collective-permute-done((bf16[144,768]{1,0:T(8,128)(2,1)S(1)}, bf16[144,768]{1,0:T(8,128)(2,1)S(1)}, u32[]{:S(2)}, u32[]{:S(2)}) %collective-permute-start.12) | collective-permute-done | bytes 221216 | tf_op jit(solution)/shard_map/ppermute | solution.py:858
  69.1 16.3 %attend.1 = (bf16[384,768]{1,0:T(8,128)(2,1)}, bf16[384,768]{1,0:T(8,128)(2,1)}, bf16[384,768]{1,0:T(8,128)(2,1)}, bf16[384,768]{1,0:T(8,128)(2,1)}, bf16[1536,7...) custom-call(s32[4]{0:T(128)} %pad_add_fusion.place_ref, ...), custom_call_target="tpu_custom_call" | custom-call | flops 2415919104 | bytes 9437184 | tf_op jit(solution)/shard_map/attend/pallas_call | solution.py:165
  86.8 23.6 %collective-permute-done.14.refs_1_ = bf16[384,768]{1,0:T(8,128)(2,1)S(1)} collective-permute-done((bf16[384,768]{1,0:T(8,128)(2,1)}, bf16[384,768]{1,0:T(8,128)(2,1)S(1)}, u32[]{:S(2)}, u32[]{:S(2)}) %collective-permute-start.14) | collective-permute-done | bytes 589856 | tf_op jit(solution)/shard_map/ppermute | solution.py:858
  117.3 9.5 %collective-permute-done.15.refs_2_ = bf16[192,768]{1,0:T(8,128)(2,1)S(1)} collective-permute-done((bf16[192,768]{1,0:T(8,128)(2,1)S(1)}, bf16[192,768]{1,0:T(8,128)(2,1)S(1)}, u32[]{:S(2)}, u32[]{:S(2)}) %collective-permute-start.15) | collective-permute-done | bytes 294944 | tf_op jit(solution)/shard_map/ppermute | solution.py:858
  128.4 4.3 %route.1 = (f32[384,768]{1,0:T(8,128)}, f32[384,1]{1,0:T(8,128)}, bf16[144,768]{1,0:T(8,128)(2,1)}, bf16[144,768]{1,0:T(8,128)(2,1)}, bf16[144,768]{1,0:T(8,128)(2,1)}, /*index=5*/bf16[144,768]{1,0:T(8,128)(2,1)}) custom-call(bf16[384,768]{1,0:T(8,128)(2,1)} %tok_ref.3, bf16[384,768]{1,0:T(8,128)(2,1)} %get-tuple-element.179.refs_0_, ...), custom_call_target="tpu_custom_call" | custom-call | flops 339738624 | bytes 3538944 | tf_op jit(solution)/shard_map/route/pallas_call | solution.py:492
  137.4 5.0 %collective-permute-done.22 = bf16[144,768]{1,0:T(8,128)(2,1)S(1)} collective-permute-done((bf16[144,768]{1,0:T(8,128)(2,1)}, bf16[144,768]{1,0:T(8,128)(2,1)S(1)}, u32[]{:S(2)}, u32[]{:S(2)}) %collective-permute-start.22) | collective-permute-done | bytes 221216 | tf_op jit(solution)/shard_map/ppermute | solution.py:858
  143.1 10.3 %collective-permute-done.25 = bf16[144,768]{1,0:T(8,128)(2,1)S(1)} collective-permute-done((bf16[144,768]{1,0:T(8,128)(2,1)}, bf16[144,768]{1,0:T(8,128)(2,1)S(1)}, u32[]{:S(2)}, u32[]{:S(2)}) %collective-permute-start.25) | collective-permute-done | bytes 221216 | tf_op jit(solution)/shard_map/ppermute | solution.py:858
  162.8 3.7 collective-permute-done.29
  175.7 23.3 %experts.1 = (bf16[2,144,768]{2,1,0:T(8,128)(2,1)}, bf16[2,144,768]{2,1,0:T(8,128)(2,1)}, bf16[2,144,768]{2,1,0:T(8,128)(2,1)}, bf16[2,144,768]{2,1,0:T(8,128)(2...) custom-call(s32[4]{0:T(128)} %pad_add_fusion.place_ref, ...), custom_call_target="tpu_custom_call" | custom-call | flops 8153726976 | bytes 24772608 | tf_op jit(solution)/shard_map/experts/pallas_call | solution.py:664
  203.1 9.7 %expert_rows.1 = bf16[4,4,144,768]{3,2,1,0:T(8,128)(2,1)} custom-call(s32[4]{0:T(128)} %pad_add_fusion.place_ref, bf16[4,576,768]{2,1,0:T(8,128)(2,1)} %get-tuple-element.215.hid_ref, bf16[4,768,384]{2,1,0:T(8,128)(2,1)} %own_out.1, bf16[4,768,384]{2,1,0:T(8,128)(2,1)} %collective-permute-done.19.refs_16_.peer_out), custom_call_target="tpu_custom_call" | custom-call | flops 2717908992 | bytes 10616832 | tf_op jit(solution)/shard_map/expert_rows/pallas_call | solution.py:710
  212.8 5.3 %collective-permute-done.33 = bf16[288,768]{1,0:T(8,128)(2,1)S(1)} collective-permute-done((bf16[288,768]{1,0:T(8,128)(2,1)}, bf16[288,768]{1,0:T(8,128)(2,1)S(1)}, u32[]{:S(2)}, u32[]{:S(2)}) %collective-permute-start.33) | collective-permute-done | bytes 442400 | tf_op jit(solution)/shard_map/ppermute | solution.py:858
  228.4 10.6 %collective-permute-start.39 = (bf16[144,768]{1,0:T(8,128)(2,1)S(1)}, bf16[144,768]{1,0:T(8,128)(2,1)S(1)}, u32[]{:S(2)}, u32[]{:S(2)}) collective-permute-start(bf16[144,768]{1,0:T(8,128)(2,1)S(1)} %fusion.8), channel_id=1, source_target_pairs={{0,4},{4,0},{8,12},{12,8},{1,5},{5,1},{9,13},{13,9},{2,6},{6,2},{1... | collective-permute-start | bytes 663560 | tf_op jit(solution)/shard_map/ppermute | solution.py:858
  241.5 15.2 %expert_weights.1 = (f32[4,384,768]{2,1,0:T(8,128)}, bf16[4,384,768]{2,1,0:T(8,128)(2,1)}, f32[4,768,384]{2,1,0:T(8,128)}, bf16[4,768,384]{2,1,0:T(8,128)(2,1)}, f32[16,768]{1,0:T(8,128)}) custom-call(s32[4]{0:T(128)} %pad_add_fusion.place_ref, bf16[4,576,768]{2,1,0:T(8,128)(2,1)} %get-tuple-element.213.x_ref, ...), custom_call_target="tpu_custom_call" | custom-call | flops 5435817984 | bytes 24772608 | tf_op jit(solution)/shard_map/expert_weights/pallas_call | solution.py:749
  258.1 4.3 %hidden_back.1 = (f32[384,768]{1,0:T(8,128)}, bf16[384,768]{1,0:T(8,128)(2,1)}, f32[1,768]{1,0:T(1,128)}) custom-call(s32[384,1]{1,0:T(8,128)} %broadcast_in_dim.35.target_ref, bf16[144,768]{1,0:T(8,128)(2,1)} %fusion.11.refs_0_, bf16[144,768]{1,0:T(8,128)(2,1)} %copy-done.28, bf16[144,768]{1,0:T(8,128)(2,1)} %copy-done.29, bf16[144,768]{1,0:T(8,128)(2,1)} %copy-done.30, ...), custom_call_target="tpu_custom_call" | custom-call | flops 339738624 | bytes 4718592 | tf_op jit(solution)/shard_map/hidden_back/pallas_call | solution.py:796
  266.4 8.1 %collective-permute-done.42.refs_1_ = bf16[192,768]{1,0:T(8,128)(2,1)S(1)} collective-permute-done((bf16[192,768]{1,0:T(8,128)(2,1)S(1)}, bf16[192,768]{1,0:T(8,128)(2,1)S(1)}, u32[]{:S(2)}, u32[]{:S(2)}) %collective-permute-start.42) | collective-permute-done | bytes 294944 | tf_op jit(solution)/shard_map/ppermute | solution.py:858
  276.8 4.5 %convert_add_fusion.1 = f32[4,384,768]{2,1,0:T(8,128)} fusion(f32[4,384,768]{2,1,0:T(8,128)S(1)} %copy-done, bf16[4,384,768]{2,1,0:T(8,128)(2,1)} %collective-permute-done.46), kind=kLoop, calls=%fused_computation.2 | loop fusion | flops 2359296 | bytes 11796480 | tf_op jit(solution)/shard_map/add | solution.py:1037
  284.0 5.6 %collective-permute-done.43.refs_2_ = bf16[384,768]{1,0:T(8,128)(2,1)S(1)} collective-permute-done((bf16[384,768]{1,0:T(8,128)(2,1)S(1)}, bf16[384,768]{1,0:T(8,128)(2,1)S(1)}, u32[]{:S(2)}, u32[]{:S(2)}) %collective-permute-start.43) | collective-permute-done | bytes 589856 | tf_op jit(solution)/shard_map/ppermute | solution.py:858
  297.7 19.8 %attend_back.1 = (bf16[384,768]{1,0:T(8,128)(2,1)}, bf16[384,768]{1,0:T(8,128)(2,1)}, bf16[384,768]{1,0:T(8,128)(2,1)}, bf16[384,768]{1,0:T(8,128)(2,1)}, bf16[1...) custom-call(s32[4]{0:T(128)} %pad_add_fusion.place_ref, ...), custom_call_target="tpu_custom_call" | custom-call | flops 3321888768 | bytes 14155776 | tf_op jit(solution)/shard_map/attend_back/pallas_call | solution.py:270
  318.5 10.9 %attend_weights.1 = (bf16[4,128,768]{2,1,0:T(8,128)(2,1)}, bf16[4,128,768]{2,1,0:T(8,128)(2,1)}, f32[768,768]{1,0:T(8,128)}) custom-call(s32[4]{0:T(128)} %pad_add_fusion.place_ref, bf16[1536,768]{1,0:T(8,128)(2,1)} %get-tuple-element.165.tok_ref, f32[1,768]{1,0:T(1,128)} %reshape.266.refs_10_.gain_ref.refs_6_, bf16[1536,576]{1,0:T(8,128)(2,1)} %get-tuple-element.256.gproj, ...), custom_call_target="tpu_custom_call" | custom-call | flops 1811939328 | bytes 14155776 | tf_op jit(solution)/shard_map/attend_weights/pallas_call | solution.py:379
  342.9 4.0 %tokens_back.1 = f32[384,768]{1,0:T(8,128)} custom-call(bf16[384,768]{1,0:T(8,128)(2,1)} %tok_ref.3, bf16[384,768]{1,0:T(8,128)(2,1)} %get-tuple-element.251.refs_0_, bf16[384,768]{1,0:T(8,128)(2,1)} %copy-done.5, bf16[192,768]{1,0:T(8,128)(2,1)} %copy-done.17, bf16[384,768]{1,0:T(8,128)(2,1)} %get-tuple-element.253.refs_3_, bf16[384,768]{1,0:T(8,128)(2,1)} %copy-done.6, ...), custom_call_target="tpu_custom_call" | custom-call | flops 2949120 | bytes 3538944 | tf_op jit(solution)/shard_map/tokens_back/pallas_call | solution.py:838
  348.6 7.5 %collective-permute-done.57 = bf16[128,768]{1,0:T(8,128)(2,1)} collective-permute-done((bf16[128,768]{1,0:T(8,128)(2,1)S(1)}, bf16[128,768]{1,0:T(8,128)(2,1)}, u32[]{:S(2)}, u32[]{:S(2)}) %collective-permute-start.57) | collective-permute-done | bytes 196640 | tf_op jit(solution)/shard_map/ppermute | solution.py:858
  (310 shorter events, 128.2 us)
Async XLA Ops:
  7.2 167.8 %all-gather.3.cloned.1.call-start = ((), (), s32[]{:S(2)}) async-start(), calls=%async_computation.2 | async-start | bytes 4423680 | tf_op jit(solution)/shard_map/all_gather | solution.py:980
  32.0 33.9 %collective-permute-start.1 = (bf16[384,768]{1,0:T(8,128)(2,1)S(1)}, bf16[384,768]{1,0:T(8,128)(2,1)S(1)}, u32[]{:S(2)}, u32[]{:S(2)}) collective-permute-start(bf16[384,768]{1,0:T(8,128)(2,1)S(1)} %pad_maximum_fusion.2), channel_id=1, source_target_pairs={{0,2},{1,3},{2,0},{3,1},{4,6},{5,7},{6,4},{7,5},{8,10},{9,11},{10,... | collective-permute-start | bytes 1769480 | tf_op jit(solution)/shard_map/ppermute | solution.py:858
  40.2 25.6 %collective-permute-start.3 = (bf16[384,768]{1,0:T(8,128)(2,1)S(1)}, bf16[384,768]{1,0:T(8,128)(2,1)}, u32[]{:S(2)}, u32[]{:S(2)}) collective-permute-start(bf16[384,768]{1,0:T(8,128)(2,1)S(1)} %pad_maximum_fusion.3), channel_id=1, source_target_pairs={{0,1},{1,0},{2,3},{3,2},{4,5},{5,4},{6,7},{7,6},{8,9},{9,8},{10,11... | collective-permute-start | bytes 1769480 | tf_op jit(solution)/shard_map/ppermute | solution.py:858
  41.8 18.9 %collective-permute-start.12 = (bf16[144,768]{1,0:T(8,128)(2,1)S(1)}, bf16[144,768]{1,0:T(8,128)(2,1)S(1)}, u32[]{:S(2)}, u32[]{:S(2)}) collective-permute-start(bf16[144,768]{1,0:T(8,128)(2,1)S(1)} %copy-done.52), channel_id=1, source_target_pairs={{0,8},{4,12},{8,0},{12,4},{1,9},{5,13},{9,1},{13,5},{2,10},{6,14},... | collective-permute-start | bytes 663560 | tf_op jit(solution)/shard_map/ppermute | solution.py:858
  44.9 17.3 %collective-permute-start.13 = (bf16[144,768]{1,0:T(8,128)(2,1)S(1)}, bf16[144,768]{1,0:T(8,128)(2,1)S(1)}, u32[]{:S(2)}, u32[]{:S(2)}) collective-permute-start(bf16[144,768]{1,0:T(8,128)(2,1)S(1)} %copy-done.51), channel_id=1, source_target_pairs={{0,12},{4,8},{8,4},{12,0},{1,13},{5,9},{9,5},{13,1},{2,14},{6,10},... | collective-permute-start | bytes 663560 | tf_op jit(solution)/shard_map/ppermute | solution.py:858
  65.9 225.2 %reduce-scatter.2.cloned.1.call-start = ((), (), s32[]{:S(2)}) async-start(), calls=%async_computation.1 | async-start | bytes 4423680 | tf_op jit(solution)/shard_map/reduce_scatter | solution.py:1020
  85.5 41.4 %collective-permute-start.18 = (bf16[4,384,768]{2,1,0:T(8,128)(2,1)S(1)}, bf16[4,384,768]{2,1,0:T(8,128)(2,1)S(1)}, u32[]{:S(2)}, u32[]{:S(2)}) collective-permute-start(bf16[4,384,768]{2,1,0:T(8,128)(2,1)S(1)} %copy-done.42), channel_id=1, source_target_pairs={{0,16},{16,0},{1,17},{17,1},{2,18},{18,2},{3,19},{19,3},{4,20},{20... | collective-permute-start | bytes 7077896 | tf_op jit(solution)/shard_map/ppermute | solution.py:848
  85.6 42.8 %collective-permute-start.19 = (bf16[4,768,384]{2,1,0:T(8,128)(2,1)S(1)}, bf16[4,768,384]{2,1,0:T(8,128)(2,1)}, u32[]{:S(2)}, u32[]{:S(2)}) collective-permute-start(bf16[4,768,384]{2,1,0:T(8,128)(2,1)S(1)} %copy-done.1), channel_id=1, source_target_pairs={{0,16},{16,0},{1,17},{17,1},{2,18},{18,2},{3,19},{19,3},{4,20},{20... | collective-permute-start | bytes 7077896 | tf_op jit(solution)/shard_map/ppermute | solution.py:848
  86.0 24.4 %collective-permute-start.14 = (bf16[384,768]{1,0:T(8,128)(2,1)}, bf16[384,768]{1,0:T(8,128)(2,1)S(1)}, u32[]{:S(2)}, u32[]{:S(2)}) collective-permute-start(bf16[384,768]{1,0:T(8,128)(2,1)} %get-tuple-element.174), channel_id=1, source_target_pairs={{0,1},{1,0},{2,3},{3,2},{4,5},{5,4},{6,7},{7,6},{8,9},{9,8},{10,11... | collective-permute-start | bytes 1769480 | tf_op jit(solution)/shard_map/ppermute | solution.py:858
  86.3 25.4 %collective-permute-start.16 = (bf16[384,768]{1,0:T(8,128)(2,1)}, bf16[384,768]{1,0:T(8,128)(2,1)S(1)}, u32[]{:S(2)}, u32[]{:S(2)}) collective-permute-start(bf16[384,768]{1,0:T(8,128)(2,1)} %get-tuple-element.176), channel_id=1, source_target_pairs={{0,2},{1,3},{2,0},{3,1},{4,6},{5,7},{6,4},{7,5},{8,10},{9,11},{10,... | collective-permute-start | bytes 1769480 | tf_op jit(solution)/shard_map/ppermute | solution.py:858
  134.4 19.0 %collective-permute-start.25 = (bf16[144,768]{1,0:T(8,128)(2,1)}, bf16[144,768]{1,0:T(8,128)(2,1)S(1)}, u32[]{:S(2)}, u32[]{:S(2)}) collective-permute-start(bf16[144,768]{1,0:T(8,128)(2,1)} %get-tuple-element.187), channel_id=1, source_target_pairs={{0,8},{4,12},{8,0},{12,4},{1,9},{5,13},{9,1},{13,5},{2,10},{6,14},... | collective-permute-start | bytes 663560 | tf_op jit(solution)/shard_map/ppermute | solution.py:858
  135.5 18.2 %collective-permute-start.20 = (bf16[144,768]{1,0:T(8,128)(2,1)}, bf16[144,768]{1,0:T(8,128)(2,1)S(1)}, u32[]{:S(2)}, u32[]{:S(2)}) collective-permute-start(bf16[144,768]{1,0:T(8,128)(2,1)} %get-tuple-element.185), channel_id=1, source_target_pairs={{0,1},{1,0},{2,3},{3,2},{4,5},{5,4},{6,7},{7,6},{8,9},{9,8},{10,11... | collective-permute-start | bytes 663560 | tf_op jit(solution)/shard_map/ppermute | solution.py:858
  135.8 20.2 %collective-permute-start.28 = (bf16[144,768]{1,0:T(8,128)(2,1)}, bf16[144,768]{1,0:T(8,128)(2,1)S(1)}, u32[]{:S(2)}, u32[]{:S(2)}) collective-permute-start(bf16[144,768]{1,0:T(8,128)(2,1)} %get-tuple-element.188), channel_id=1, source_target_pairs={{0,12},{4,8},{8,4},{12,0},{1,13},{5,9},{9,5},{13,1},{2,14},{6,10},... | collective-permute-start | bytes 663560 | tf_op jit(solution)/shard_map/ppermute | solution.py:858
  201.0 17.2 %collective-permute-start.33 = (bf16[288,768]{1,0:T(8,128)(2,1)}, bf16[288,768]{1,0:T(8,128)(2,1)S(1)}, u32[]{:S(2)}, u32[]{:S(2)}) collective-permute-start(bf16[288,768]{1,0:T(8,128)(2,1)} %bitcast.113), channel_id=1, source_target_pairs={{0,1},{1,0},{2,3},{3,2},{4,5},{5,4},{6,7},{7,6},{8,9},{9,8},{10,11... | collective-permute-start | bytes 1327112 | tf_op jit(solution)/shard_map/ppermute | solution.py:858
  201.5 16.7 %collective-permute-start.34 = (bf16[288,768]{1,0:T(8,128)(2,1)}, bf16[288,768]{1,0:T(8,128)(2,1)S(1)}, u32[]{:S(2)}, u32[]{:S(2)}) collective-permute-start(bf16[288,768]{1,0:T(8,128)(2,1)} %bitcast.112), channel_id=1, source_target_pairs={{0,2},{1,3},{2,0},{3,1},{4,6},{5,7},{6,4},{7,5},{8,10},{9,11},{10,... | collective-permute-start | bytes 1327112 | tf_op jit(solution)/shard_map/ppermute | solution.py:858
  228.4 28.3 %collective-permute-start.39 = (bf16[144,768]{1,0:T(8,128)(2,1)S(1)}, bf16[144,768]{1,0:T(8,128)(2,1)S(1)}, u32[]{:S(2)}, u32[]{:S(2)}) collective-permute-start(bf16[144,768]{1,0:T(8,128)(2,1)S(1)} %fusion.8), channel_id=1, source_target_pairs={{0,4},{4,0},{8,12},{12,8},{1,5},{5,1},{9,13},{13,9},{2,6},{6,2},{1... | collective-permute-start | bytes 663560 | tf_op jit(solution)/shard_map/ppermute | solution.py:858
  239.1 17.6 %collective-permute-start.40 = (bf16[144,768]{1,0:T(8,128)(2,1)S(1)}, bf16[144,768]{1,0:T(8,128)(2,1)S(1)}, u32[]{:S(2)}, u32[]{:S(2)}) collective-permute-start(bf16[144,768]{1,0:T(8,128)(2,1)S(1)} %fusion.5), channel_id=1, source_target_pairs={{0,8},{4,12},{8,0},{12,4},{1,9},{5,13},{9,1},{13,5},{2,10},{6,14},... | collective-permute-start | bytes 663560 | tf_op jit(solution)/shard_map/ppermute | solution.py:858
  239.3 17.4 %collective-permute-start.41 = (bf16[144,768]{1,0:T(8,128)(2,1)S(1)}, bf16[144,768]{1,0:T(8,128)(2,1)S(1)}, u32[]{:S(2)}, u32[]{:S(2)}) collective-permute-start(bf16[144,768]{1,0:T(8,128)(2,1)S(1)} %fusion.2), channel_id=1, source_target_pairs={{0,12},{4,8},{8,4},{12,0},{1,13},{5,9},{9,5},{13,1},{2,14},{6,10},... | collective-permute-start | bytes 663560 | tf_op jit(solution)/shard_map/ppermute | solution.py:858
  256.8 20.0 %collective-permute-start.46 = (bf16[4,384,768]{2,1,0:T(8,128)(2,1)}, bf16[4,384,768]{2,1,0:T(8,128)(2,1)}, u32[]{:S(2)}, u32[]{:S(2)}) collective-permute-start(bf16[4,384,768]{2,1,0:T(8,128)(2,1)} %get-tuple-element.227), channel_id=1, source_target_pairs={{0,16},{16,0},{1,17},{17,1},{2,18},{18,2},{3,19},{19,3},{4,20},{20... | collective-permute-start | bytes 7077896 | tf_op jit(solution)/shard_map/ppermute | solution.py:848
  256.8 24.5 %collective-permute-start.47 = (bf16[4,768,384]{2,1,0:T(8,128)(2,1)}, bf16[4,768,384]{2,1,0:T(8,128)(2,1)S(1)}, u32[]{:S(2)}, u32[]{:S(2)}) collective-permute-start(bf16[4,768,384]{2,1,0:T(8,128)(2,1)} %get-tuple-element.229), channel_id=1, source_target_pairs={{0,16},{16,0},{1,17},{17,1},{2,18},{18,2},{3,19},{19,3},{4,20},{20... | collective-permute-start | bytes 7077896 | tf_op jit(solution)/shard_map/ppermute | solution.py:848
  293.3 24.2 %collective-permute-start.50 = (bf16[144,768]{1,0:T(8,128)(2,1)S(1)}, bf16[144,768]{1,0:T(8,128)(2,1)S(1)}, u32[]{:S(2)}, u32[]{:S(2)}) collective-permute-start(bf16[144,768]{1,0:T(8,128)(2,1)S(1)} %get-tuple-element.273), channel_id=1, source_target_pairs={{0,12},{4,8},{8,4},{12,0},{1,13},{5,9},{9,5},{13,1},{2,14},{6,10},... | collective-permute-start | bytes 663560 | tf_op jit(solution)/shard_map/ppermute | solution.py:858
  296.6 20.9 %collective-permute-start.49 = (bf16[144,768]{1,0:T(8,128)(2,1)S(1)}, bf16[144,768]{1,0:T(8,128)(2,1)S(1)}, u32[]{:S(2)}, u32[]{:S(2)}) collective-permute-start(bf16[144,768]{1,0:T(8,128)(2,1)S(1)} %get-tuple-element.274), channel_id=1, source_target_pairs={{0,8},{4,12},{8,0},{12,4},{1,9},{5,13},{9,1},{13,5},{2,10},{6,14},... | collective-permute-start | bytes 663560 | tf_op jit(solution)/shard_map/ppermute | solution.py:858
  296.6 20.9 %collective-permute-start.48 = (bf16[144,768]{1,0:T(8,128)(2,1)S(1)}, bf16[144,768]{1,0:T(8,128)(2,1)S(1)}, u32[]{:S(2)}, u32[]{:S(2)}) collective-permute-start(bf16[144,768]{1,0:T(8,128)(2,1)S(1)} %get-tuple-element.275), channel_id=1, source_target_pairs={{0,4},{4,0},{8,12},{12,8},{1,5},{5,1},{9,13},{13,9},{2,6},{6,2},{1... | collective-permute-start | bytes 663560 | tf_op jit(solution)/shard_map/ppermute | solution.py:858
  338.2 17.9 %collective-permute-start.57 = (bf16[128,768]{1,0:T(8,128)(2,1)S(1)}, bf16[128,768]{1,0:T(8,128)(2,1)}, u32[]{:S(2)}, u32[]{:S(2)}) collective-permute-start(bf16[128,768]{1,0:T(8,128)(2,1)S(1)} %get-tuple-element.272), channel_id=1, source_target_pairs={{0,8},{4,12},{8,0},{12,4},{1,9},{5,13},{9,1},{13,5},{2,10},{6,14},... | collective-permute-start | bytes 589832 | tf_op jit(solution)/shard_map/ppermute | solution.py:858
  (96 other events, 1119.7 us)
Sparse Core Ops, SparseCore 0:
  66.0 61.1 all-gather.2
  218.3 53.0 reduce-scatter.1

commit v8 on v6

--- a/solution.py
+++ b/solution.py
@@ -100,13 +100,6 @@
             for n, j in enumerate(order):
                 at = pl.multiple_of((place_ref[2] ^ j) * 2 * half + h * half, half)
                 piece[n * half : (n + 1) * half, :] = source[pl.ds(at, half), :]
-
-
-def part_rows(place_ref, pieces, source):
-    rows = pieces[0].shape[0]
-    for j, piece in enumerate(pieces):
-        at = pl.multiple_of((place_ref[2] ^ j) * rows, rows)
-        piece[...] = source[pl.ds(at, rows), :]
 
 
 def attend_kernel(heads, tensors, owners, part, place_ref, bias_ref, *refs):
@@ -202,7 +195,7 @@
     pieces = [refs.pop(0) for _ in range(5)]
     gain_two_ref, router_ref = refs.pop(0), refs.pop(0)
     parts = [refs.pop(0) for _ in range(tensors)]
-    own_ref, other_ref, weight_ref, gain_out, table, wo, gmix, gproj, near, far, rows_s, group, result = refs
+    own_ref, other_ref, weight_ref, gain_out, table, wo, gmix, gproj, near, far, rows_s, group, result, extras = refs
     inner = heads * HEAD_DIM
     blocks = LENGTH // TILE
     step_id = pl.program_id(0)
@@ -262,7 +255,7 @@
 
     @pl.when(step_id == pl.num_programs(0) - 1)
     def _():
-        part_rows(place_ref, parts, result)
+        part_halves(place_ref, parts, result)
         ids = [tile_bucket(step) for step in (-1, 0, 1)]
         for head in range(heads):
             for k in range(BUCKETS):
@@ -278,7 +271,7 @@
                 rows_s[at : at + 1, :] = jnp.sum(total, axis=0, keepdims=True)
         sums = jnp.sum(rows_s[...], axis=1, keepdims=True)
         experts = router_ref.shape[0]
-        if part % 16:
+        if part % 16 or part > TILE or experts % 16:
             own_ref[...] = jnp.broadcast_to(sums, own_ref.shape)
             return
         count = sums.shape[0]
@@ -286,23 +279,24 @@
             jnp.int32, (count, TILE), 1
         )
         sums = jnp.sum(jnp.where(diagonal, sums, 0.0), axis=0, keepdims=True)
-        width = gain_out.shape[1]
-        sums = jnp.concatenate([sums, jnp.zeros((1, width - TILE), F32)], axis=1)
-        head_rows = jnp.concatenate(
-            [gain_out[...], gain_two_ref[...], sums, jnp.zeros((13, width), F32)], axis=0
-        ).astype(BF16)
-        tail = jnp.concatenate(
-            [router_ref[...].astype(BF16)]
-            + ([jnp.zeros((-experts % 16, width), BF16)] if experts % 16 else []),
-            axis=0,
+        z_count = own_ref.shape[0]
+        owners = 2 * z_count
+        gap = jnp.zeros((experts, TILE - part), F32)
+        low = jnp.zeros((experts - 1, TILE), F32)
+        rows = jnp.concatenate(
+            [gain_out[...], gain_two_ref[...], jnp.zeros((experts - 2, gain_out.shape[1]), F32)], axis=0
         )
-        z_count = own_ref.shape[0]
+        for n in range(owners):
+            cut = slice(n * part, (n + 1) * part)
+            tiles = [router_ref[:, cut], gap, rows[:, cut], gap, jnp.concatenate([sums, low], axis=0)]
+            tiles.append(jnp.zeros((experts, gain_out.shape[1] - 3 * TILE), F32))
+            extras[n] = jnp.concatenate(tiles, axis=1).astype(BF16)
         for n, ref in enumerate((own_ref, other_ref)):
             for k in range(z_count):
-                at = pl.multiple_of((place_ref[3] ^ (n * z_count + k)) * part, part)
+                owner = place_ref[3] ^ (n * z_count + k)
+                at = pl.multiple_of(owner * part, part)
                 ref[k, :part, :] = weight_ref[pl.ds(at, part), :].astype(BF16)
-                ref[k, part : part + 16, :] = head_rows
-                ref[k, part + 16 :, :] = tail
+                ref[k, part:, :] = extras[owner]
 
 
 def attend_back(places, bias, tokens, gain, weights, projected, mixed, logs, pieces, gain_two, router, part, z_count):
@@ -314,8 +308,9 @@
     seqs = rows // LENGTH
     by_seq = lambda cols: pl.BlockSpec((LENGTH, cols), lambda s, *_: (s, 0))
     experts = router.shape[0]
-    sent = (z_count, part + 16 + experts + -experts % 16, width)
-    if part % 16:
+    sent = (z_count, part + experts, width)
+    plain = part % 16 or part > TILE or experts % 16
+    if plain:
         sent = (heads * BUCKETS, 1)
     result = pl.pallas_call(
         functools.partial(attend_back_kernel, heads, tensors, part),
@@ -345,12 +340,13 @@
                 pltpu.VMEM((heads * BUCKETS, TILE), F32),
                 pltpu.VMEM((rows, width), BF16),
                 pltpu.VMEM((rows, width), BF16),
+                pltpu.VMEM((2 * z_count, experts, width), BF16),
             ],
         ),
         out_shape=[jax.ShapeDtypeStruct(pieces[0].shape, BF16)] * tensors
         + [
-            jax.ShapeDtypeStruct(sent, F32 if part % 16 else BF16),
-            jax.ShapeDtypeStruct(sent, F32 if part % 16 else BF16),
+            jax.ShapeDtypeStruct(sent, F32 if plain else BF16),
+            jax.ShapeDtypeStruct(sent, F32 if plain else BF16),
             jax.ShapeDtypeStruct((width, 4 * inner), F32),
             jax.ShapeDtypeStruct((1, width), F32),
         ],
@@ -493,13 +489,8 @@
         part = spread[rest_at : rest_at + blocks * locals_ * rest].reshape(blocks, locals_ * rest, width)
         rest_at += blocks * locals_ * rest
 
-        @pl.when(expert == 0)
-        def _():
-            view[:, locals_ * main :, :] = part
-
-        @pl.when(expert > 0)
-        def _():
-            view[:, locals_ * main :, :] = view[:, locals_ * main :, :] + part
+        before = view[:, locals_ * main :, :]
+        view[:, locals_ * main :, :] = part + jnp.where(expert > 0, before, jnp.zeros_like(before))
 
 
 def group_views(place_ref, ref, tensors, chunks):
@@ -548,8 +539,6 @@
     pick_rows(x_ref.at[0], xs, choice, main_rows, main, expert)
     pick_rows(grows, group_views(place_ref, g_ref, tensors, chunks), choice, main_rows, main, expert)
     join_halves(place_ref, own_in, peer_in, own_out, peer_out, win, wout)
-    inner[...] = dot(x_ref[0], win[...])
-    gunits[...] = dot(grows[...], wout[...], ROWS_NT)
     probs = softmax_rows(dot(x_ref[0], router[...]))
     lanes = lax.broadcasted_iota(jnp.int32, probs.shape, 1)
     mine = lanes == place_ref[1] * locals_ + expert
@@ -557,37 +546,57 @@
     gate_s[...] = jnp.broadcast_to(picked, gate_s.shape)
     chunk = 16
     half_wide = wide // 2 if wide % (2 * TILE) == 0 else wide
-
-    def body(step, _):
-        at = pl.ds(pl.multiple_of(step * chunk, chunk), chunk)
-        gate_tile = gate_s[at, :]
-        gate = jnp.concatenate([gate_tile] * (half_wide // TILE), axis=1)
-        total = None
-        for start in range(0, wide, half_wide):
-            lanes_at = slice(start, start + half_wide)
-            value = inner[at, lanes_at]
-            square = value * value
-            wave = jnp.tanh(value * (GELU_A + (GELU_A * GELU_B) * square))
-            half = 0.5 + 0.5 * wave
-            hidden = (value * half).astype(BF16)
-            bend = value * (0.5 * GELU_A + (1.5 * GELU_A * GELU_B) * square)
-            slope = half + bend * (1.0 - wave * wave)
-            units = gunits[at, lanes_at]
-            hid_ref[0, at, lanes_at] = hidden
-            gi_ref[0, at, lanes_at] = (gate * (units * slope)).astype(BF16)
-            product = hidden.astype(F32) * units
-            for tile in range(0, half_wide, TILE):
-                part = product[:, tile : tile + TILE]
-                total = part if total is None else total + part
-        dots[at, :] = total
-        gate = jnp.concatenate([gate_tile] * (width // TILE), axis=1)
-        ge_ref[0, at, :] = (gate * grows[at, :].astype(F32)).astype(BF16)
-        return 0
-
-    lax.fori_loop(0, rows // chunk, body, 0, unroll=4)
-    grad_logits = (jnp.sum(dots[...], axis=-1, keepdims=True) * probs * (jnp.where(mine, 1.0, 0.0) - picked)).astype(BF16)
-    gl_ref[0] = grad_logits
-    back[...] = (dot(gi_ref[0], win[...], ROWS_NT) + dot(grad_logits, router[...], ROWS_NT)).astype(BF16)
+    half_rows = rows // 2
+
+    def multiply(part):
+        at = slice(part * half_rows, (part + 1) * half_rows)
+        inner[at, :] = dot(x_ref[0, at, :], win[...])
+        gunits[at, :] = dot(grows[at, :], wout[...], ROWS_NT)
+
+    def activate(part):
+        for row in range(part * half_rows, (part + 1) * half_rows, chunk):
+            at = slice(row, row + chunk)
+            gate_tile = gate_s[at, :]
+            gate = jnp.concatenate([gate_tile] * (half_wide // TILE), axis=1)
+            total = None
+            for start in range(0, wide, half_wide):
+                lanes_at = slice(start, start + half_wide)
+                value = inner[at, lanes_at]
+                square = value * value
+                wave = jnp.tanh(value * (GELU_A + (GELU_A * GELU_B) * square))
+                half = 0.5 + 0.5 * wave
+                hidden = (value * half).astype(BF16)
+                bend = value * (0.5 * GELU_A + (1.5 * GELU_A * GELU_B) * square)
+                slope = half + bend * (1.0 - wave * wave)
+                units = gunits[at, lanes_at]
+                hid_ref[0, at, lanes_at] = hidden
+                gi_ref[0, at, lanes_at] = (gate * (units * slope)).astype(BF16)
+                product = hidden.astype(F32) * units
+                for tile in range(0, half_wide, TILE):
+                    part_sum = product[:, tile : tile + TILE]
+                    total = part_sum if total is None else total + part_sum
+            dots[at, :] = total
+            gate = jnp.concatenate([gate_tile] * (width // TILE), axis=1)
+            ge_ref[0, at, :] = (gate * grows[at, :].astype(F32)).astype(BF16)
+
+    def finish(part):
+        at = slice(part * half_rows, (part + 1) * half_rows)
+        grad_logits = (
+            jnp.sum(dots[at, :], axis=-1, keepdims=True)
+            * probs[at]
+            * (jnp.where(mine[at], 1.0, 0.0) - picked[at])
+        ).astype(BF16)
+        gl_ref[0, at, :] = grad_logits
+        back[at, :] = (
+            dot(gi_ref[0, at, :], win[...], ROWS_NT) + dot(grad_logits, router[...], ROWS_NT)
+        ).astype(BF16)
+
+    multiply(0)
+    multiply(1)
+    activate(0)
+    finish(0)
+    activate(1)
+    finish(1)
     put_rows(back_refs, back, choice, main_rows, main, locals_, rest, expert)
 
 
@@ -724,7 +733,8 @@
     hidden_ref, cot_ref, gain_ref, grad_ref, attn_ref, gain_out = refs[-6:]
     grad_in = take_rows(target_ref, refs[:-6])
     unit, scale = unit_rows(hidden_ref[...])
-    gain_out[...] = jnp.sum(grad_in * unit, axis=0, keepdims=True)
+    gained = jnp.sum(grad_in * unit, axis=0, keepdims=True)
+    gain_out[...] = gained + jnp.where(pl.program_id(0) > 0, gain_out[...], jnp.zeros_like(gained))
     scaled = grad_in * gain_ref[...]
     inside = jnp.mean(unit * scaled, axis=-1, keepdims=True)
     grad = cot_ref[...].astype(F32) + scale * (scaled - unit * inside)
@@ -734,8 +744,13 @@
 
 def hidden_back(target_col, back, hidden, cotangent, gain):
     rows, width = hidden.shape
+    steps = 3 if rows % 48 == 0 else 1
+    by_row = lambda cols: pl.BlockSpec((rows // steps, cols), lambda i: (i, 0))
     return pl.pallas_call(
         hidden_back_kernel,
+        grid=(steps,),
+        in_specs=[by_row(1)] + [whole(b.shape) for b in back] + [by_row(width), by_row(width), whole((1, width))],
+        out_specs=[by_row(width), by_row(width), whole((1, width))],
         out_shape=[
             jax.ShapeDtypeStruct((rows, width), F32),
             jax.ShapeDtypeStruct((rows, width), BF16),
@@ -763,11 +778,16 @@
 
 
 def tokens_back_kernel(tok_ref, *refs):
-    gain_ref, hidden_ref, out_ref = refs[-3:]
-    unit, scale = unit_rows(tok_ref[...].astype(F32))
-    scaled = sum_pieces(refs[:-3]) * gain_ref[...]
-    inside = jnp.mean(unit * scaled, axis=-1, keepdims=True)
-    out_ref[...] = hidden_ref[...] + scale * (scaled - unit * inside)
+    gain_ref, hidden_ref, out_ref = refs[6:]
+    half = tok_ref.shape[0] // 2
+    for h in range(2):
+        keep, got, last = refs[3 * h : 3 * h + 3]
+        here = slice(h * half, (h + 1) * half)
+        unit, scale = unit_rows(tok_ref[here, :].astype(F32))
+        grad = keep[:half, :].astype(F32) + got[:half, :].astype(F32) + last[...].astype(F32)
+        scaled = grad * gain_ref[...]
+        inside = jnp.mean(unit * scaled, axis=-1, keepdims=True)
+        out_ref[here, :] = hidden_ref[here, :] + scale * (scaled - unit * inside)
 
 
 def tokens_back(tokens, grad_normed, gain, grad_hidden):
@@ -803,6 +823,17 @@
     first = swapped(value, "tensor", 4, a)
     second = swapped(jnp.concatenate([value, first], axis=0), "tensor", 4, b)
     return first, second
+
+
+def sum_hops(parts):
+    half = parts[0].shape[0] // 2
+    result = []
+    for h, (a, b) in enumerate(HOPS):
+        keep, send = parts[2 * h : 2 * h + 2]
+        got = swapped(send, "tensor", 4, a)
+        last = swapped(added(keep[half:], got[half:]), "tensor", 4, b)
+        result += [keep, got, last]
+    return result
 
 
 def added(a, b):
@@ -918,12 +949,7 @@
     peer_in = shifted(late_in, "dp", dp_count, 1)
     peer_out = shifted(late_out, "dp", dp_count, 1)
     grad_arrived = lax.all_gather(grad_rows, "tensor", axis=0).reshape(t_count, z_count, block, width)
-    attn = []
-    for h, (a, b) in enumerate(HOPS):
-        keep, send = parts[2 * h : 2 * h + 2]
-        got = swapped(send, "tensor", t_count, a)
-        last = swapped(added(keep[half_rows:], got[half_rows:]), "tensor", t_count, b)
-        attn += [keep, got, last]
+    attn = sum_hops(parts)
     attn, peer_in, peer_out = lax.optimization_barrier((attn, peer_in, peer_out))
     hidden_one, gate, sent = route(
         tokens, attn, gain_two, router, target_row, expert_index[:, None], kept_mask[:, None], counts
@@ -972,29 +998,22 @@
     normed_parts, own_part, other_part, forward_rows = lax.optimization_barrier(
         (normed_parts, own_part, other_part, forward_rows)
     )
-    grad_normed = swap_pieces(normed_parts, "tensor", t_count)
+    grad_normed = sum_hops(normed_parts)
     output = output_rows(target_col, forward_rows, hidden_one, gate)
     grad_tokens = tokens_back(tokens, grad_normed, gain_one, grad_hidden)
 
-    if part % 16:
-        head_rows = jnp.concatenate(
-            [
-                gain_one_part,
-                gain_two_part,
-                jnp.pad(own_part.reshape(1, -1), ((0, 0), (0, width - own_part.shape[0]))),
-                jnp.zeros((13, width), F32),
-                router_part,
-                jnp.zeros((-experts_all % 16, width), F32),
-            ]
-        )
+    if part % 16 or part > TILE or experts_all % 16:
+        pad = lambda value, lanes: jnp.pad(value, ((0, 0), (0, lanes - value.shape[1])))
+        gains = jnp.concatenate([gain_one_part, gain_two_part, jnp.zeros((experts_all - 2, width), F32)])
+        sums = jnp.pad(own_part.reshape(1, -1), ((0, experts_all - 1), (0, TILE - own_part.shape[0])))
+        extras = [
+            pad(jnp.concatenate([pad(router_part[:, cut], TILE), pad(gains[:, cut], TILE), sums], axis=1), width)
+            for cut in (slice(n * part, (n + 1) * part) for n in range(owners))
+        ]
         order = jnp.arange(owners, dtype=jnp.int32) ^ my_owner
         payload = jnp.concatenate(
-            [
-                weight_part.reshape(owners, part, width)[order],
-                jnp.broadcast_to(head_rows[None], (owners,) + head_rows.shape),
-            ],
-            axis=1,
-        ).astype(BF16)
+            [weight_part.astype(BF16).reshape(owners, part, width), jnp.stack(extras).astype(BF16)], axis=1
+        )[order]
         own_part, other_part = payload[:z_count], payload[z_count:]
     other_got = shifted(other_part, "dp", dp_count, 1)
     pieces = swap_pieces([added(own_part[k], other_got[k]) for k in range(z_count)], "expert", z_count)
@@ -1004,9 +1023,8 @@
     weight_total = total[:part].reshape(part, 4, inner)
     grad_w_qkv = weight_total[:, :3].transpose(1, 0, 2)
     grad_w_attn_out = weight_total[:, 3].T
-    grad_rel_bias = total[part + 2, : heads * BUCKETS].reshape(heads, BUCKETS)
-    mine = lax.dynamic_slice_in_dim(total[part:], my_owner * part, part, axis=1)
-    mine = jnp.concatenate([mine[:2], mine[16 : 16 + experts_all]], axis=0)
+    grad_rel_bias = total[part, 2 * TILE : 2 * TILE + heads * BUCKETS].reshape(heads, BUCKETS)
+    mine = jnp.concatenate([total[part : part + 2, TILE : TILE + part], total[part:, :part]], axis=0)
     turned = [
         lax.dynamic_slice_in_dim(mine, (my_t ^ k) * fine, fine, axis=1).reshape(-1) for k in range(t_count)
     ]

time: 368 us -> 360 us (0.978)
  Pallas kernels: 120 us -> 110 us
  waiting for transfers between devices: 113 us -> 118 us
    pallas_call x1, Pallas kernels: 35 us -> 23.5 us  [expert_forward_back(): pl.pallas_call(functools.partial(expert_kernel, chunks, tensors, main, lo...]
    ppermute x56 -> x57, waiting for transfers between devices: 113 us -> 118 us  [swapped(): return lax.ppermute(value, axis, [(s, s ^ bits) for s in range(count)])]
    ppermute x56 -> x57, starting transfers between devices: 75.1 us -> 74.8 us  [swapped(): return lax.ppermute(value, axis, [(s, s ^ bits) for s in range(count)])]
    unnamed x100 -> x104, local copies, waits for them, and re-layouts: 7.48 us -> 7.83 us
  transfers between devices with their start and end apart: 63 -> 64, of which waited for: 20 -> 22; matrix products, arithmetic and copies ran while one was open for 7% -> 8% of each run, Pallas kernels for 23% -> 23%
where the time goes in v8:
time: 360 us; the launch traced here: 359 us
  waiting for transfers between devices  118 us (33%)
  Pallas kernels  110 us (31%)
  starting transfers between devices  75.5 us (21%)
  local copies, waits for them, and re-layouts  22.3 us (6%)
  other arithmetic  19.2 us (5%)
  between operations  14.8 us (4%)
    ppermute x57, waiting for transfers between devices, swapped(): return lax.ppermute(value, axis, [(s, s ^ bits) for s in range(count)])  118 us
    ppermute x57, starting transfers between devices, swapped(): return lax.ppermute(value, axis, [(s, s ^ bits) for s in range(count)])  74.8 us
    pallas_call x1, Pallas kernels, attend_back(): pl.pallas_call(functools.partial(attend_back_kernel, heads, tensors, part...  24.5 us
    pallas_call x1, Pallas kernels, expert_forward_back(): pl.pallas_call(functools.partial(expert_kernel, chunks, tensors, main, lo...  23.5 us
    pallas_call x1, Pallas kernels, attend(): pl.pallas_call(functools.partial(attend_kernel, heads, tensors, len(owned...  15.4 us
    pallas_call x1, Pallas kernels, expert_weights(): pl.pallas_call(expert_weights_kernel, grid_spec=pltpu.PrefetchScalarGridS...  15.2 us
    pallas_call x1, Pallas kernels, expert_rows(): pl.pallas_call(functools.partial(expert_rows_kernel, chunks, main, locals...  9.63 us
    unnamed x104, local copies, waits for them, and re-layouts  7.83 us
  transfers between devices with their start and end apart: 64, of which 22 were waited for; matrix products, arithmetic and copies ran while one was open for 8% of the time, Pallas kernels for 23%

profile of v8, /device:TPU:0, one launch (start us, length us, event | category | flops | bytes accessed | tf_op | source)
XLA Modules:
  0.0 359.0 jit_solution(294985532574368542)
XLA Ops:
  10.4 5.1 %collective-permute-start.6 = (bf16[1,112,768]{2,1,0:T(8,128)(2,1)S(1)}, bf16[1,112,768]{2,1,0:T(8,128)(2,1)S(1)}, u32[]{:S(2)}, u32[]{:S(2)}) collective-permute-start(bf16[1,112,768]{2,1,0:T(8,128)(2,1)S(1)} %maximum_bitcast_fusion.refs_0_.refs_5_), channel_id=1, source_target_pairs={{0,12},{4,8},{8,4},{12,0},{1,13},{5,9},{9,5},{13,1},{2,14},{6,10},... | collective-permute-start | bytes 516104 | tf_op jit(solution)/shard_map/ppermute | solution.py:814
  21.3 8.9 %collective-permute-done.5.refs_2_.refs_7_ = bf16[1,112,768]{2,1,0:T(8,128)(2,1)S(1)} collective-permute-done((bf16[1,112,768]{2,1,0:T(8,128)(2,1)S(1)}, bf16[1,112,768]{2,1,0:T(8,128)(2,1)S(1)}, u32[]{:S(2)}, u32[]{:S(2)}) %collective-permute-start.5) | collective-permute-done | bytes 172064 | tf_op jit(solution)/shard_map/ppermute | solution.py:814
  56.0 15.4 %attend.1 = (bf16[384,768]{1,0:T(8,128)(2,1)}, bf16[384,768]{1,0:T(8,128)(2,1)}, bf16[384,768]{1,0:T(8,128)(2,1)}, bf16[384,768]{1,0:T(8,128)(2,1)}, bf16[1536,7...) custom-call(s32[4]{0:T(128)} %pad_add_fusion.place_ref, ...), custom_call_target="tpu_custom_call" | custom-call | flops 2415919104 | bytes 9437184 | tf_op jit(solution)/shard_map/attend/pallas_call | solution.py:158
  76.2 19.0 %collective-permute-done.14.refs_1_ = bf16[384,768]{1,0:T(8,128)(2,1)S(1)} collective-permute-done((bf16[384,768]{1,0:T(8,128)(2,1)}, bf16[384,768]{1,0:T(8,128)(2,1)S(1)}, u32[]{:S(2)}, u32[]{:S(2)}) %collective-permute-start.14) | collective-permute-done | bytes 589856 | tf_op jit(solution)/shard_map/ppermute | solution.py:814
  107.1 4.9 %route.1 = (f32[384,768]{1,0:T(8,128)}, f32[384,1]{1,0:T(8,128)}, bf16[144,768]{1,0:T(8,128)(2,1)}, bf16[144,768]{1,0:T(8,128)(2,1)}, bf16[144,768]{1,0:T(8,128)(2,1)}, /*index=5*/bf16[144,768]{1,0:T(8,128)(2,1)}) custom-call(bf16[384,768]{1,0:T(8,128)(2,1)} %tok_ref.3, bf16[384,768]{1,0:T(8,128)(2,1)} %get-tuple-element.165.refs_0_, ...), custom_call_target="tpu_custom_call" | custom-call | flops 339738624 | bytes 3538944 | tf_op jit(solution)/shard_map/route/pallas_call | solution.py:442
  117.7 4.5 %collective-permute-done.22 = bf16[144,768]{1,0:T(8,128)(2,1)S(1)} collective-permute-done((bf16[144,768]{1,0:T(8,128)(2,1)}, bf16[144,768]{1,0:T(8,128)(2,1)S(1)}, u32[]{:S(2)}, u32[]{:S(2)}) %collective-permute-start.22) | collective-permute-done | bytes 221216 | tf_op jit(solution)/shard_map/ppermute | solution.py:814
  124.2 9.0 %collective-permute-done.25 = bf16[144,768]{1,0:T(8,128)(2,1)S(1)} collective-permute-done((bf16[144,768]{1,0:T(8,128)(2,1)}, bf16[144,768]{1,0:T(8,128)(2,1)S(1)}, u32[]{:S(2)}, u32[]{:S(2)}) %collective-permute-start.25) | collective-permute-done | bytes 221216 | tf_op jit(solution)/shard_map/ppermute | solution.py:814
  142.7 9.0 %collective-permute-done.29 = bf16[144,768]{1,0:T(8,128)(2,1)S(1)} collective-permute-done((bf16[144,768]{1,0:T(8,128)(2,1)S(1)}, bf16[144,768]{1,0:T(8,128)(2,1)S(1)}, u32[]{:S(2)}, u32[]{:S(2)}) %collective-permute-start.29) | collective-permute-done | bytes 221216 | tf_op jit(solution)/shard_map/ppermute | solution.py:814
  156.5 3.7 %collective-permute-done.30 = bf16[288,768]{1,0:T(8,128)(2,1)S(1)} collective-permute-done((bf16[288,768]{1,0:T(8,128)(2,1)S(1)}, bf16[288,768]{1,0:T(8,128)(2,1)S(1)}, u32[]{:S(2)}, u32[]{:S(2)}) %collective-permute-start.30) | collective-permute-done | bytes 442400 | tf_op jit(solution)/shard_map/ppermute | solution.py:814
  160.9 23.5 %experts.1 = (bf16[2,144,768]{2,1,0:T(8,128)(2,1)}, bf16[2,144,768]{2,1,0:T(8,128)(2,1)}, bf16[2,144,768]{2,1,0:T(8,128)(2,1)}, bf16[2,144,768]{2,1,0:T(8,128)(2...) custom-call(s32[4]{0:T(128)} %pad_add_fusion.place_ref, ...), custom_call_target="tpu_custom_call" | custom-call | flops 8153726976 | bytes 24772608 | tf_op jit(solution)/shard_map/experts/pallas_call | solution.py:614
  188.5 9.6 %expert_rows.1 = bf16[4,4,144,768]{3,2,1,0:T(8,128)(2,1)} custom-call(s32[4]{0:T(128)} %pad_add_fusion.place_ref, bf16[4,576,768]{2,1,0:T(8,128)(2,1)} %get-tuple-element.202.hid_ref, bf16[4,768,384]{2,1,0:T(8,128)(2,1)} %own_out.1, bf16[4,768,384]{2,1,0:T(8,128)(2,1)} %collective-permute-done.19.refs_16_.peer_out), custom_call_target="tpu_custom_call" | custom-call | flops 2717908992 | bytes 10616832 | tf_op jit(solution)/shard_map/expert_rows/pallas_call | solution.py:660
  198.1 5.7 %collective-permute-done.33 = bf16[288,768]{1,0:T(8,128)(2,1)S(1)} collective-permute-done((bf16[288,768]{1,0:T(8,128)(2,1)}, bf16[288,768]{1,0:T(8,128)(2,1)S(1)}, u32[]{:S(2)}, u32[]{:S(2)}) %collective-permute-start.33) | collective-permute-done | bytes 442400 | tf_op jit(solution)/shard_map/ppermute | solution.py:814
  218.5 15.2 %expert_weights.1 = (f32[4,384,768]{2,1,0:T(8,128)}, bf16[4,384,768]{2,1,0:T(8,128)(2,1)}, f32[4,768,384]{2,1,0:T(8,128)}, bf16[4,768,384]{2,1,0:T(8,128)(2,1)}, f32[16,768]{1,0:T(8,128)}) custom-call(s32[4]{0:T(128)} %pad_add_fusion.place_ref, bf16[4,576,768]{2,1,0:T(8,128)(2,1)} %get-tuple-element.200.x_ref, ...), custom_call_target="tpu_custom_call" | custom-call | flops 5435817984 | bytes 24772608 | tf_op jit(solution)/shard_map/expert_weights/pallas_call | solution.py:699
  235.2 4.9 %hidden_back.1 = (f32[384,768]{1,0:T(8,128)}, bf16[384,768]{1,0:T(8,128)(2,1)}, f32[1,768]{1,0:T(1,128)}) custom-call(s32[384,1]{1,0:T(8,128)} %broadcast_in_dim.35.target_ref, bf16[144,768]{1,0:T(8,128)(2,1)} %fusion.11.refs_0_, bf16[144,768]{1,0:T(8,128)(2,1)} %copy-done.28, bf16[144,768]{1,0:T(8,128)(2,1)} %copy-done.29, bf16[144,768]{1,0:T(8,128)(2,1)} %copy-done.30, ...), custom_call_target="tpu_custom_call" | custom-call | flops 339738624 | bytes 4718592 | tf_op jit(solution)/shard_map/hidden_back/pallas_call | solution.py:749
  243.4 7.0 %collective-permute-done.42.refs_1_ = bf16[192,768]{1,0:T(8,128)(2,1)S(1)} collective-permute-done((bf16[192,768]{1,0:T(8,128)(2,1)S(1)}, bf16[192,768]{1,0:T(8,128)(2,1)S(1)}, u32[]{:S(2)}, u32[]{:S(2)}) %collective-permute-start.42) | collective-permute-done | bytes 294944 | tf_op jit(solution)/shard_map/ppermute | solution.py:814
  252.7 4.5 %convert_add_fusion.1 = f32[4,384,768]{2,1,0:T(8,128)} fusion(f32[4,384,768]{2,1,0:T(8,128)S(1)} %copy-done, bf16[4,384,768]{2,1,0:T(8,128)(2,1)} %collective-permute-done.46), kind=kLoop, calls=%fused_computation.2 | loop fusion | flops 2359296 | bytes 11796480 | tf_op jit(solution)/shard_map/add | solution.py:988
  260.0 13.3 %collective-permute-done.43.refs_2_ = bf16[384,768]{1,0:T(8,128)(2,1)S(1)} collective-permute-done((bf16[384,768]{1,0:T(8,128)(2,1)S(1)}, bf16[384,768]{1,0:T(8,128)(2,1)S(1)}, u32[]{:S(2)}, u32[]{:S(2)}) %collective-permute-start.43) | collective-permute-done | bytes 589856 | tf_op jit(solution)/shard_map/ppermute | solution.py:814
  275.6 3.7 %collective-permute-start.50 = (bf16[144,768]{1,0:T(8,128)(2,1)S(1)}, bf16[144,768]{1,0:T(8,128)(2,1)S(1)}, u32[]{:S(2)}, u32[]{:S(2)}) collective-permute-start(bf16[144,768]{1,0:T(8,128)(2,1)S(1)} %get-tuple-element.251), channel_id=1, source_target_pairs={{0,12},{4,8},{8,4},{12,0},{1,13},{5,9},{9,5},{13,1},{2,14},{6,10},... | collective-permute-start | bytes 663560 | tf_op jit(solution)/shard_map/ppermute | solution.py:814
  280.0 24.5 %attend_back.1 = (bf16[384,768]{1,0:T(8,128)(2,1)}, bf16[384,768]{1,0:T(8,128)(2,1)}, bf16[384,768]{1,0:T(8,128)(2,1)}, bf16[384,768]{1,0:T(8,128)(2,1)}, bf16[4...) custom-call(s32[4]{0:T(128)} %pad_add_fusion.place_ref, ...), custom_call_target="tpu_custom_call" | custom-call | flops 5586812928 | bytes 14155776 | tf_op jit(solution)/shard_map/attend_back/pallas_call | solution.py:315
  307.4 3.4 output_rows.1
  310.9 8.8 %collective-permute-done.51.refs_1_ = bf16[384,768]{1,0:T(8,128)(2,1)S(1)} collective-permute-done((bf16[384,768]{1,0:T(8,128)(2,1)}, bf16[384,768]{1,0:T(8,128)(2,1)S(1)}, u32[]{:S(2)}, u32[]{:S(2)}) %collective-permute-start.51) | collective-permute-done | bytes 589856 | tf_op jit(solution)/shard_map/ppermute | solution.py:814
  330.0 3.7 %collective-permute-done.58 = bf16[112,768]{1,0:T(8,128)(2,1)S(1)} collective-permute-done((bf16[112,768]{1,0:T(8,128)(2,1)S(1)}, bf16[112,768]{1,0:T(8,128)(2,1)S(1)}, u32[]{:S(2)}, u32[]{:S(2)}) %collective-permute-start.58) | collective-permute-done | bytes 172064 | tf_op jit(solution)/shard_map/ppermute | solution.py:814
  333.7 5.6 %collective-permute-done.57 = bf16[112,768]{1,0:T(8,128)(2,1)S(1)} collective-permute-done((bf16[112,768]{1,0:T(8,128)(2,1)S(1)}, bf16[112,768]{1,0:T(8,128)(2,1)S(1)}, u32[]{:S(2)}, u32[]{:S(2)}) %collective-permute-start.57) | collective-permute-done | bytes 172064 | tf_op jit(solution)/shard_map/ppermute | solution.py:814
  348.1 4.0 %tokens_back.1 = f32[384,768]{1,0:T(8,128)} custom-call(bf16[384,768]{1,0:T(8,128)(2,1)} %tok_ref.3, bf16[384,768]{1,0:T(8,128)(2,1)} %get-tuple-element.237.refs_0_, bf16[384,768]{1,0:T(8,128)(2,1)} %copy-done.5, bf16[192,768]{1,0:T(8,128)(2,1)} %copy-done.19, bf16[384,768]{1,0:T(8,128)(2,1)} %get-tuple-element.239.refs_3_, bf16[384,768]{1,0:T(8,128)(2,1)} %copy-done.6, ...), custom_call_target="tpu_custom_call" | custom-call | flops 2949120 | bytes 3538944 | tf_op jit(solution)/shard_map/tokens_back/pallas_call | solution.py:794
  (296 shorter events, 127.2 us)
Async XLA Ops:
  7.2 152.9 %all-gather.3.cloned.1.call-start = ((), (), s32[]{:S(2)}) async-start(), calls=%async_computation.2 | async-start | bytes 4423680 | tf_op jit(solution)/shard_map/all_gather | solution.py:951
  31.3 18.5 %collective-permute-start.1 = (bf16[384,768]{1,0:T(8,128)(2,1)S(1)}, bf16[384,768]{1,0:T(8,128)(2,1)}, u32[]{:S(2)}, u32[]{:S(2)}) collective-permute-start(bf16[384,768]{1,0:T(8,128)(2,1)S(1)} %pad_maximum_fusion.2), channel_id=1, source_target_pairs={{0,2},{1,3},{2,0},{3,1},{4,6},{5,7},{6,4},{7,5},{8,10},{9,11},{10,... | collective-permute-start | bytes 1769480 | tf_op jit(solution)/shard_map/ppermute | solution.py:814
  51.6 19.8 %collective-permute-start.11 = (bf16[144,768]{1,0:T(8,128)(2,1)}, bf16[144,768]{1,0:T(8,128)(2,1)S(1)}, u32[]{:S(2)}, u32[]{:S(2)}) collective-permute-start(bf16[144,768]{1,0:T(8,128)(2,1)} %get-tuple-element.156), channel_id=1, source_target_pairs={{0,4},{4,0},{8,12},{12,8},{1,5},{5,1},{9,13},{13,9},{2,6},{6,2},{1... | collective-permute-start | bytes 663560 | tf_op jit(solution)/shard_map/ppermute | solution.py:814
  51.6 19.8 %collective-permute-start.12 = (bf16[144,768]{1,0:T(8,128)(2,1)}, bf16[144,768]{1,0:T(8,128)(2,1)S(1)}, u32[]{:S(2)}, u32[]{:S(2)}) collective-permute-start(bf16[144,768]{1,0:T(8,128)(2,1)} %get-tuple-element.157), channel_id=1, source_target_pairs={{0,8},{4,12},{8,0},{12,4},{1,9},{5,13},{9,1},{13,5},{2,10},{6,14},... | collective-permute-start | bytes 663560 | tf_op jit(solution)/shard_map/ppermute | solution.py:814
  72.4 200.9 %reduce-scatter.2.cloned.1.call-start = ((), (), s32[]{:S(2)}) async-start(), calls=%async_computation.1 | async-start | bytes 4423680 | tf_op jit(solution)/shard_map/reduce_scatter | solution.py:977
  72.5 33.8 %collective-permute-start.18 = (bf16[4,384,768]{2,1,0:T(8,128)(2,1)}, bf16[4,384,768]{2,1,0:T(8,128)(2,1)S(1)}, u32[]{:S(2)}, u32[]{:S(2)}) collective-permute-start(bf16[4,384,768]{2,1,0:T(8,128)(2,1)} %refs_13_.1), channel_id=1, source_target_pairs={{0,16},{16,0},{1,17},{17,1},{2,18},{18,2},{3,19},{19,3},{4,20},{20... | collective-permute-start | bytes 7077896 | tf_op jit(solution)/shard_map/ppermute | solution.py:804
  73.3 33.0 %collective-permute-start.19 = (bf16[4,768,384]{2,1,0:T(8,128)(2,1)S(1)}, bf16[4,768,384]{2,1,0:T(8,128)(2,1)}, u32[]{:S(2)}, u32[]{:S(2)}) collective-permute-start(bf16[4,768,384]{2,1,0:T(8,128)(2,1)S(1)} %copy-done.1), channel_id=1, source_target_pairs={{0,16},{16,0},{1,17},{17,1},{2,18},{18,2},{3,19},{19,3},{4,20},{20... | collective-permute-start | bytes 7077896 | tf_op jit(solution)/shard_map/ppermute | solution.py:804
  73.3 21.9 %collective-permute-start.14 = (bf16[384,768]{1,0:T(8,128)(2,1)}, bf16[384,768]{1,0:T(8,128)(2,1)S(1)}, u32[]{:S(2)}, u32[]{:S(2)}) collective-permute-start(bf16[384,768]{1,0:T(8,128)(2,1)} %get-tuple-element.160), channel_id=1, source_target_pairs={{0,1},{1,0},{2,3},{3,2},{4,5},{5,4},{6,7},{7,6},{8,9},{9,8},{10,11... | collective-permute-start | bytes 1769480 | tf_op jit(solution)/shard_map/ppermute | solution.py:814
  74.8 22.8 %collective-permute-start.16 = (bf16[384,768]{1,0:T(8,128)(2,1)}, bf16[384,768]{1,0:T(8,128)(2,1)S(1)}, u32[]{:S(2)}, u32[]{:S(2)}) collective-permute-start(bf16[384,768]{1,0:T(8,128)(2,1)} %get-tuple-element.162), channel_id=1, source_target_pairs={{0,2},{1,3},{2,0},{3,1},{4,6},{5,7},{6,4},{7,5},{8,10},{9,11},{10,... | collective-permute-start | bytes 1769480 | tf_op jit(solution)/shard_map/ppermute | solution.py:814
  114.3 19.0 %collective-permute-start.25 = (bf16[144,768]{1,0:T(8,128)(2,1)}, bf16[144,768]{1,0:T(8,128)(2,1)S(1)}, u32[]{:S(2)}, u32[]{:S(2)}) collective-permute-start(bf16[144,768]{1,0:T(8,128)(2,1)} %get-tuple-element.173), channel_id=1, source_target_pairs={{0,8},{4,12},{8,0},{12,4},{1,9},{5,13},{9,1},{13,5},{2,10},{6,14},... | collective-permute-start | bytes 663560 | tf_op jit(solution)/shard_map/ppermute | solution.py:814
  116.1 19.4 %collective-permute-start.28 = (bf16[144,768]{1,0:T(8,128)(2,1)}, bf16[144,768]{1,0:T(8,128)(2,1)S(1)}, u32[]{:S(2)}, u32[]{:S(2)}) collective-permute-start(bf16[144,768]{1,0:T(8,128)(2,1)} %get-tuple-element.174), channel_id=1, source_target_pairs={{0,12},{4,8},{8,4},{12,0},{1,13},{5,9},{9,5},{13,1},{2,14},{6,10},... | collective-permute-start | bytes 663560 | tf_op jit(solution)/shard_map/ppermute | solution.py:814
  134.4 18.9 %collective-permute-start.21 = (bf16[288,768]{1,0:T(8,128)(2,1)S(1)}, bf16[288,768]{1,0:T(8,128)(2,1)S(1)}, u32[]{:S(2)}, u32[]{:S(2)}) collective-permute-start(bf16[288,768]{1,0:T(8,128)(2,1)S(1)} %pad_maximum_fusion.6), channel_id=1, source_target_pairs={{0,2},{1,3},{2,0},{3,1},{4,6},{5,7},{6,4},{7,5},{8,10},{9,11},{10,... | collective-permute-start | bytes 1327112 | tf_op jit(solution)/shard_map/ppermute | solution.py:814
  213.8 19.9 %collective-permute-start.39 = (bf16[144,768]{1,0:T(8,128)(2,1)S(1)}, bf16[144,768]{1,0:T(8,128)(2,1)S(1)}, u32[]{:S(2)}, u32[]{:S(2)}) collective-permute-start(bf16[144,768]{1,0:T(8,128)(2,1)S(1)} %fusion.8), channel_id=1, source_target_pairs={{0,4},{4,0},{8,12},{12,8},{1,5},{5,1},{9,13},{13,9},{2,6},{6,2},{1... | collective-permute-start | bytes 663560 | tf_op jit(solution)/shard_map/ppermute | solution.py:814
  215.5 18.2 %collective-permute-start.40 = (bf16[144,768]{1,0:T(8,128)(2,1)S(1)}, bf16[144,768]{1,0:T(8,128)(2,1)S(1)}, u32[]{:S(2)}, u32[]{:S(2)}) collective-permute-start(bf16[144,768]{1,0:T(8,128)(2,1)S(1)} %fusion.5), channel_id=1, source_target_pairs={{0,8},{4,12},{8,0},{12,4},{1,9},{5,13},{9,1},{13,5},{2,10},{6,14},... | collective-permute-start | bytes 663560 | tf_op jit(solution)/shard_map/ppermute | solution.py:814
  233.8 18.9 %collective-permute-start.46 = (bf16[4,384,768]{2,1,0:T(8,128)(2,1)}, bf16[4,384,768]{2,1,0:T(8,128)(2,1)}, u32[]{:S(2)}, u32[]{:S(2)}) collective-permute-start(bf16[4,384,768]{2,1,0:T(8,128)(2,1)} %get-tuple-element.214), channel_id=1, source_target_pairs={{0,16},{16,0},{1,17},{17,1},{2,18},{18,2},{3,19},{19,3},{4,20},{20... | collective-permute-start | bytes 7077896 | tf_op jit(solution)/shard_map/ppermute | solution.py:804
  233.9 23.4 %collective-permute-start.47 = (bf16[4,768,384]{2,1,0:T(8,128)(2,1)}, bf16[4,768,384]{2,1,0:T(8,128)(2,1)S(1)}, u32[]{:S(2)}, u32[]{:S(2)}) collective-permute-start(bf16[4,768,384]{2,1,0:T(8,128)(2,1)} %get-tuple-element.216), channel_id=1, source_target_pairs={{0,16},{16,0},{1,17},{17,1},{2,18},{18,2},{3,19},{19,3},{4,20},{20... | collective-permute-start | bytes 7077896 | tf_op jit(solution)/shard_map/ppermute | solution.py:804
  250.4 22.9 %collective-permute-start.43 = (bf16[384,768]{1,0:T(8,128)(2,1)S(1)}, bf16[384,768]{1,0:T(8,128)(2,1)S(1)}, u32[]{:S(2)}, u32[]{:S(2)}) collective-permute-start(bf16[384,768]{1,0:T(8,128)(2,1)S(1)} %pad_maximum_fusion.4), channel_id=1, source_target_pairs={{0,2},{1,3},{2,0},{3,1},{4,6},{5,7},{6,4},{7,5},{8,10},{9,11},{10,... | collective-permute-start | bytes 1769480 | tf_op jit(solution)/shard_map/ppermute | solution.py:814
  251.8 21.6 %collective-permute-start.45 = (bf16[384,768]{1,0:T(8,128)(2,1)S(1)}, bf16[384,768]{1,0:T(8,128)(2,1)}, u32[]{:S(2)}, u32[]{:S(2)}) collective-permute-start(bf16[384,768]{1,0:T(8,128)(2,1)S(1)} %pad_maximum_fusion.5), channel_id=1, source_target_pairs={{0,1},{1,0},{2,3},{3,2},{4,5},{5,4},{6,7},{7,6},{8,9},{9,8},{10,11... | collective-permute-start | bytes 1769480 | tf_op jit(solution)/shard_map/ppermute | solution.py:814
  275.6 28.9 %collective-permute-start.50 = (bf16[144,768]{1,0:T(8,128)(2,1)S(1)}, bf16[144,768]{1,0:T(8,128)(2,1)S(1)}, u32[]{:S(2)}, u32[]{:S(2)}) collective-permute-start(bf16[144,768]{1,0:T(8,128)(2,1)S(1)} %get-tuple-element.251), channel_id=1, source_target_pairs={{0,12},{4,8},{8,4},{12,0},{1,13},{5,9},{9,5},{13,1},{2,14},{6,10},... | collective-permute-start | bytes 663560 | tf_op jit(solution)/shard_map/ppermute | solution.py:814
  279.3 25.2 %collective-permute-start.49 = (bf16[144,768]{1,0:T(8,128)(2,1)S(1)}, bf16[144,768]{1,0:T(8,128)(2,1)S(1)}, u32[]{:S(2)}, u32[]{:S(2)}) collective-permute-start(bf16[144,768]{1,0:T(8,128)(2,1)S(1)} %get-tuple-element.252), channel_id=1, source_target_pairs={{0,8},{4,12},{8,0},{12,4},{1,9},{5,13},{9,1},{13,5},{2,10},{6,14},... | collective-permute-start | bytes 663560 | tf_op jit(solution)/shard_map/ppermute | solution.py:814
  279.3 25.3 %collective-permute-start.48 = (bf16[144,768]{1,0:T(8,128)(2,1)S(1)}, bf16[144,768]{1,0:T(8,128)(2,1)S(1)}, u32[]{:S(2)}, u32[]{:S(2)}) collective-permute-start(bf16[144,768]{1,0:T(8,128)(2,1)S(1)} %get-tuple-element.253), channel_id=1, source_target_pairs={{0,4},{4,0},{8,12},{12,8},{1,5},{5,1},{9,13},{13,9},{2,6},{6,2},{1... | collective-permute-start | bytes 663560 | tf_op jit(solution)/shard_map/ppermute | solution.py:814
  306.6 19.6 %collective-permute-start.53 = (bf16[384,768]{1,0:T(8,128)(2,1)}, bf16[384,768]{1,0:T(8,128)(2,1)S(1)}, u32[]{:S(2)}, u32[]{:S(2)}) collective-permute-start(bf16[384,768]{1,0:T(8,128)(2,1)} %get-tuple-element.240), channel_id=1, source_target_pairs={{0,2},{1,3},{2,0},{3,1},{4,6},{5,7},{6,4},{7,5},{8,10},{9,11},{10,... | collective-permute-start | bytes 1769480 | tf_op jit(solution)/shard_map/ppermute | solution.py:814
  320.6 26.9 %collective-permute-start.52 = (bf16[192,768]{1,0:T(8,128)(2,1)}, bf16[192,768]{1,0:T(8,128)(2,1)S(1)}, u32[]{:S(2)}, u32[]{:S(2)}) collective-permute-start(bf16[192,768]{1,0:T(8,128)(2,1)} %add_convert_fusion.1), channel_id=1, source_target_pairs={{0,2},{1,3},{2,0},{3,1},{4,6},{5,7},{6,4},{7,5},{8,10},{9,11},{10,... | collective-permute-start | bytes 884744 | tf_op jit(solution)/shard_map/ppermute | solution.py:814
  327.1 20.4 %collective-permute-start.54 = (bf16[192,768]{1,0:T(8,128)(2,1)}, bf16[192,768]{1,0:T(8,128)(2,1)}, u32[]{:S(2)}, u32[]{:S(2)}) collective-permute-start(bf16[192,768]{1,0:T(8,128)(2,1)} %add_convert_fusion), channel_id=1, source_target_pairs={{0,1},{1,0},{2,3},{3,2},{4,5},{5,4},{6,7},{7,6},{8,9},{9,8},{10,11... | collective-permute-start | bytes 884744 | tf_op jit(solution)/shard_map/ppermute | solution.py:814
  (90 other events, 1101.3 us)
Sparse Core Ops, SparseCore 0:
  72.6 63.0 all-gather.2
  213.9 56.0 reduce-scatter.1

commit v9 on v8

--- a/solution.py
+++ b/solution.py
@@ -11,6 +11,7 @@
 BUCKETS = 32
 LENGTH = 512
 TILE = 128
+BLOCK = 32
 EPSILON = 1e-06
 BORDERS = (12, 16, 23, 32, 46, 64, 91)
 F32 = jnp.float32
@@ -106,7 +107,7 @@
     refs = list(refs)
     take = lambda n: [refs.pop(0) for _ in range(n)]
     pieces, owned, (gain_ref,), parts = take(5), take(owners), take(1), take(tensors)
-    tok_ref, qkv_ref, mixed_ref, log_ref, w_ref, table, wo, group, result = refs
+    tok_ref, qkv_ref, mixed_ref, log_ref, w_ref, table, wo, group, result, raw, soft = refs
     inner = heads * HEAD_DIM
     step_id = pl.program_id(0)
 
@@ -125,21 +126,24 @@
     unit, _ = unit_rows(tok_ref[...].astype(F32))
     normed = (unit * gain_ref[...]).astype(BF16)
     qkv_ref[...] = dot(normed, w_ref[:, : 3 * inner]).astype(BF16)
-    lanes = lax.broadcasted_iota(jnp.int32, (LENGTH, TILE), 1)
-    logs = jnp.zeros((LENGTH, TILE), F32)
+    lanes = lax.broadcasted_iota(jnp.int32, (BLOCK, TILE), 1)
     for head in range(heads):
         at = head * HEAD_DIM
-        query = qkv_ref[:, at : at + HEAD_DIM] * HEAD_DIM ** (-0.5)
-        key = qkv_ref[:, inner + at : inner + at + HEAD_DIM]
+        query = (qkv_ref[:, at : at + HEAD_DIM] * HEAD_DIM ** (-0.5)).astype(BF16)
+        raw[head] = dot(query, qkv_ref[:, inner + at : inner + at + HEAD_DIM], ROWS_NT)
+    for head in range(heads):
+        at = head * HEAD_DIM
+        for row in range(0, LENGTH, BLOCK):
+            cut = slice(row, row + BLOCK)
+            scores = raw[head, cut, :] + table[head, cut, :]
+            top = jnp.max(scores, axis=-1, keepdims=True)
+            exponent = jnp.exp(scores - top)
+            total = jnp.sum(exponent, axis=-1, keepdims=True)
+            soft[head, cut, :] = (exponent * (1.0 / total)).astype(BF16)
+            logs = jnp.broadcast_to(top + jnp.log(total), (BLOCK, TILE))
+            log_ref[cut, :] = logs if head == 0 else jnp.where(lanes >= head, logs, log_ref[cut, :])
         value = qkv_ref[:, 2 * inner + at : 2 * inner + at + HEAD_DIM]
-        scores = dot(query.astype(BF16), key, ROWS_NT) + table[head]
-        top = jnp.max(scores, axis=-1, keepdims=True)
-        exponent = jnp.exp(scores - top)
-        total = jnp.sum(exponent, axis=-1, keepdims=True)
-        attention = (exponent * (1.0 / total)).astype(BF16)
-        mixed_ref[:, at : at + HEAD_DIM] = dot(attention, value).astype(BF16)
-        logs = jnp.where(lanes == head, top + jnp.log(total), logs)
-    log_ref[...] = logs
+        mixed_ref[:, at : at + HEAD_DIM] = dot(soft[head], value).astype(BF16)
     result[here, :] = dot(mixed_ref[...], wo[...], ROWS_NT).astype(BF16)
 
     @pl.when(step_id == pl.num_programs(0) - 1)
@@ -171,6 +175,8 @@
                 pltpu.VMEM((width, inner), BF16),
                 pltpu.VMEM((rows, width), BF16),
                 pltpu.VMEM((rows, width), BF16),
+                pltpu.VMEM((heads, LENGTH, LENGTH), F32),
+                pltpu.VMEM((heads, LENGTH, LENGTH), BF16),
             ],
         ),
         out_shape=[jax.ShapeDtypeStruct((piece_rows, width), BF16)] * tensors
@@ -195,7 +201,7 @@
     pieces = [refs.pop(0) for _ in range(5)]
     gain_two_ref, router_ref = refs.pop(0), refs.pop(0)
     parts = [refs.pop(0) for _ in range(tensors)]
-    own_ref, other_ref, weight_ref, gain_out, table, wo, gmix, gproj, near, far, rows_s, group, result, extras = refs
+    own_ref, other_ref, weight_ref, gain_out, table, wo, gmix, gproj, near, far, rows_s, group, result, extras, raw, raw_grad, soft, soft_grad = refs
     inner = heads * HEAD_DIM
     blocks = LENGTH // TILE
     step_id = pl.program_id(0)
@@ -215,35 +221,39 @@
     for head in range(heads):
         at = head * HEAD_DIM
         query = (qkv_ref[:, at : at + HEAD_DIM] * HEAD_DIM ** (-0.5)).astype(BF16)
+        raw[head] = dot(query, qkv_ref[:, inner + at : inner + at + HEAD_DIM], ROWS_NT)
+        value = qkv_ref[:, 2 * inner + at : 2 * inner + at + HEAD_DIM]
+        raw_grad[head] = dot(gmix[:, at : at + HEAD_DIM], value, ROWS_NT)
+    for head in range(heads):
+        at = head * HEAD_DIM
+        for row in range(0, LENGTH, BLOCK):
+            cut = slice(row, row + BLOCK)
+            attention = jnp.exp(raw[head, cut, :] + table[head, cut, :] - log_ref[cut, head : head + 1])
+            grad_weights = raw_grad[head, cut, :]
+            inner_sum = jnp.sum(attention * grad_weights, axis=-1, keepdims=True)
+            grad_scores = attention * (grad_weights - inner_sum)
+            soft[head, cut, :] = attention.astype(BF16)
+            soft_grad[head, cut, :] = grad_scores.astype(BF16)
+            i, inside = row // TILE, slice(row % TILE, row % TILE + BLOCK)
+            low, high = None, None
+            for j in range(blocks):
+                piece = grad_scores[:, j * TILE : (j + 1) * TILE]
+                if abs(j - i) <= 1:
+                    near[head * 3 + j - i + 1, inside, :] += piece
+                elif j < i:
+                    low = piece if low is None else low + piece
+                else:
+                    high = piece if high is None else high + piece
+            if low is not None:
+                far[head * 2, inside, :] += low
+            if high is not None:
+                far[head * 2 + 1, inside, :] += high
+        query = (qkv_ref[:, at : at + HEAD_DIM] * HEAD_DIM ** (-0.5)).astype(BF16)
         key = qkv_ref[:, inner + at : inner + at + HEAD_DIM]
-        value = qkv_ref[:, 2 * inner + at : 2 * inner + at + HEAD_DIM]
-        grad_rows = gmix[:, at : at + HEAD_DIM]
-        scores = dot(query, key, ROWS_NT) + table[head]
-        attention = jnp.exp(scores - log_ref[:, head : head + 1])
-        grad_weights = dot(grad_rows, value, ROWS_NT)
-        inner_sum = jnp.sum(attention * grad_weights, axis=-1, keepdims=True)
-        grad_scores = attention * (grad_weights - inner_sum)
-        low = jnp.zeros((TILE, TILE), F32)
-        high = jnp.zeros((TILE, TILE), F32)
-        mid = [jnp.zeros((TILE, TILE), F32) for _ in range(3)]
-        for i in range(blocks):
-            for j in range(blocks):
-                piece = grad_scores[i * TILE : (i + 1) * TILE, j * TILE : (j + 1) * TILE]
-                if abs(j - i) <= 1:
-                    mid[j - i + 1] = mid[j - i + 1] + piece
-                elif j < i:
-                    low = low + piece
-                else:
-                    high = high + piece
-        for k in range(3):
-            near[head * 3 + k] += mid[k]
-        far[head * 2] += low
-        far[head * 2 + 1] += high
-        rounded = grad_scores.astype(BF16)
-        gproj[:, at : at + HEAD_DIM] = (dot(rounded, key) * HEAD_DIM ** (-0.5)).astype(BF16)
-        gproj[:, inner + at : inner + at + HEAD_DIM] = dot(rounded, query, ROWS_TN).astype(BF16)
+        gproj[:, at : at + HEAD_DIM] = (dot(soft_grad[head], key) * HEAD_DIM ** (-0.5)).astype(BF16)
+        gproj[:, inner + at : inner + at + HEAD_DIM] = dot(soft_grad[head], query, ROWS_TN).astype(BF16)
         gproj[:, 2 * inner + at : 2 * inner + at + HEAD_DIM] = dot(
-            attention.astype(BF16), grad_rows, ROWS_TN
+            soft[head], gmix[:, at : at + HEAD_DIM], ROWS_TN
         ).astype(BF16)
     unit, _ = unit_rows(tok_ref[...].astype(F32))
     normed = (unit * gain_ref[...]).astype(BF16)
@@ -341,6 +351,10 @@
                 pltpu.VMEM((rows, width), BF16),
                 pltpu.VMEM((rows, width), BF16),
                 pltpu.VMEM((2 * z_count, experts, width), BF16),
+                pltpu.VMEM((heads, LENGTH, LENGTH), F32),
+                pltpu.VMEM((heads, LENGTH, LENGTH), F32),
+                pltpu.VMEM((heads, LENGTH, LENGTH), BF16),
+                pltpu.VMEM((heads, LENGTH, LENGTH), BF16),
             ],
         ),
         out_shape=[jax.ShapeDtypeStruct(pieces[0].shape, BF16)] * tensors
@@ -998,10 +1012,6 @@
     normed_parts, own_part, other_part, forward_rows = lax.optimization_barrier(
         (normed_parts, own_part, other_part, forward_rows)
     )
-    grad_normed = sum_hops(normed_parts)
-    output = output_rows(target_col, forward_rows, hidden_one, gate)
-    grad_tokens = tokens_back(tokens, grad_normed, gain_one, grad_hidden)
-
     if part % 16 or part > TILE or experts_all % 16:
         pad = lambda value, lanes: jnp.pad(value, ((0, 0), (0, lanes - value.shape[1])))
         gains = jnp.concatenate([gain_one_part, gain_two_part, jnp.zeros((experts_all - 2, width), F32)])
@@ -1016,7 +1026,13 @@
         )[order]
         own_part, other_part = payload[:z_count], payload[z_count:]
     other_got = shifted(other_part, "dp", dp_count, 1)
+    normed_parts, other_got = lax.optimization_barrier((normed_parts, other_got))
+    grad_normed = sum_hops(normed_parts)
+    output = output_rows(target_col, forward_rows, hidden_one, gate)
+    grad_tokens = tokens_back(tokens, grad_normed, gain_one, grad_hidden)
+
     pieces = swap_pieces([added(own_part[k], other_got[k]) for k in range(z_count)], "expert", z_count)
+    pieces, grad_tokens = lax.optimization_barrier((pieces, grad_tokens))
     total = pieces[0].astype(F32)
     for piece in pieces[1:]:
         total = total + piece.astype(F32)

time: 360 us -> 364 us (1.011)
    unnamed x104 -> x102, local copies, waits for them, and re-layouts: 7.83 us -> 7.17 us
  transfers between devices with their start and end apart: 64 -> 64, of which waited for: 22 -> 21; matrix products, arithmetic and copies ran while one was open for 8% -> 8% of each run, Pallas kernels for 23% -> 24%
where the time goes in v9:
time: 364 us; the launch traced here: 363 us
  waiting for transfers between devices  118 us (32%)
  Pallas kernels  109 us (30%)
  starting transfers between devices  76 us (21%)
  other arithmetic  22.8 us (6%)
  local copies, waits for them, and re-layouts  21.8 us (6%)
  between operations  14.9 us (4%)
    ppermute x57, waiting for transfers between devices, swapped(): return lax.ppermute(value, axis, [(s, s ^ bits) for s in range(count)])  116 us
    ppermute x57, starting transfers between devices, swapped(): return lax.ppermute(value, axis, [(s, s ^ bits) for s in range(count)])  75.2 us
    pallas_call x1, Pallas kernels, attend_back(): pl.pallas_call(functools.partial(attend_back_kernel, heads, tensors, part...  24.7 us
    pallas_call x1, Pallas kernels, expert_forward_back(): pl.pallas_call(functools.partial(expert_kernel, chunks, tensors, main, lo...  23.5 us
    pallas_call x1, Pallas kernels, expert_weights(): pl.pallas_call(expert_weights_kernel, grid_spec=pltpu.PrefetchScalarGridS...  15.2 us
    pallas_call x1, Pallas kernels, attend(): pl.pallas_call(functools.partial(attend_kernel, heads, tensors, len(owned...  14.9 us
    pallas_call x1, Pallas kernels, expert_rows(): pl.pallas_call(functools.partial(expert_rows_kernel, chunks, main, locals...  9.63 us
  transfers between devices with their start and end apart: 64, of which 21 were waited for; matrix products, arithmetic and copies ran while one was open for 8% of the time, Pallas kernels for 24%

profile of v9, /device:TPU:0, one launch (start us, length us, event | category | flops | bytes accessed | tf_op | source)
XLA Modules:
  0.0 362.9 jit_solution(11873411999818775135)
XLA Ops:
  10.4 5.1 %collective-permute-start.6 = (bf16[1,112,768]{2,1,0:T(8,128)(2,1)S(1)}, bf16[1,112,768]{2,1,0:T(8,128)(2,1)S(1)}, u32[]{:S(2)}, u32[]{:S(2)}) collective-permute-start(bf16[1,112,768]{2,1,0:T(8,128)(2,1)S(1)} %maximum_bitcast_fusion.refs_0_.refs_5_), channel_id=1, source_target_pairs={{0,12},{4,8},{8,4},{12,0},{1,13},{5,9},{9,5},{13,1},{2,14},{6,10},... | collective-permute-start | bytes 516104 | tf_op jit(solution)/shard_map/ppermute | solution.py:828
  21.3 8.9 %collective-permute-done.5.refs_2_.refs_7_ = bf16[1,112,768]{2,1,0:T(8,128)(2,1)S(1)} collective-permute-done((bf16[1,112,768]{2,1,0:T(8,128)(2,1)S(1)}, bf16[1,112,768]{2,1,0:T(8,128)(2,1)S(1)}, u32[]{:S(2)}, u32[]{:S(2)}) %collective-permute-start.5) | collective-permute-done | bytes 172064 | tf_op jit(solution)/shard_map/ppermute | solution.py:828
  56.0 14.9 %attend.1 = (bf16[384,768]{1,0:T(8,128)(2,1)}, bf16[384,768]{1,0:T(8,128)(2,1)}, bf16[384,768]{1,0:T(8,128)(2,1)}, bf16[384,768]{1,0:T(8,128)(2,1)}, bf16[1536,7...) custom-call(s32[4]{0:T(128)} %pad_add_fusion.place_ref, ...), custom_call_target="tpu_custom_call" | custom-call | flops 2415919104 | bytes 9437184 | tf_op jit(solution)/shard_map/attend/pallas_call | solution.py:162
  75.8 18.6 %collective-permute-done.14.refs_1_ = bf16[384,768]{1,0:T(8,128)(2,1)S(1)} collective-permute-done((bf16[384,768]{1,0:T(8,128)(2,1)}, bf16[384,768]{1,0:T(8,128)(2,1)S(1)}, u32[]{:S(2)}, u32[]{:S(2)}) %collective-permute-start.14) | collective-permute-done | bytes 589856 | tf_op jit(solution)/shard_map/ppermute | solution.py:828
  102.2 3.6 %collective-permute-done.15.refs_2_ = bf16[192,768]{1,0:T(8,128)(2,1)S(1)} collective-permute-done((bf16[192,768]{1,0:T(8,128)(2,1)S(1)}, bf16[192,768]{1,0:T(8,128)(2,1)S(1)}, u32[]{:S(2)}, u32[]{:S(2)}) %collective-permute-start.15) | collective-permute-done | bytes 294944 | tf_op jit(solution)/shard_map/ppermute | solution.py:828
  106.7 4.8 %route.1 = (f32[384,768]{1,0:T(8,128)}, f32[384,1]{1,0:T(8,128)}, bf16[144,768]{1,0:T(8,128)(2,1)}, bf16[144,768]{1,0:T(8,128)(2,1)}, bf16[144,768]{1,0:T(8,128)(2,1)}, /*index=5*/bf16[144,768]{1,0:T(8,128)(2,1)}) custom-call(bf16[384,768]{1,0:T(8,128)(2,1)} %tok_ref.3, bf16[384,768]{1,0:T(8,128)(2,1)} %get-tuple-element.175.refs_0_, ...), custom_call_target="tpu_custom_call" | custom-call | flops 339738624 | bytes 3538944 | tf_op jit(solution)/shard_map/route/pallas_call | solution.py:456
  117.6 4.7 %collective-permute-done.22 = bf16[144,768]{1,0:T(8,128)(2,1)S(1)} collective-permute-done((bf16[144,768]{1,0:T(8,128)(2,1)}, bf16[144,768]{1,0:T(8,128)(2,1)S(1)}, u32[]{:S(2)}, u32[]{:S(2)}) %collective-permute-start.22) | collective-permute-done | bytes 221216 | tf_op jit(solution)/shard_map/ppermute | solution.py:828
  123.9 9.3 %collective-permute-done.25 = bf16[144,768]{1,0:T(8,128)(2,1)S(1)} collective-permute-done((bf16[144,768]{1,0:T(8,128)(2,1)}, bf16[144,768]{1,0:T(8,128)(2,1)S(1)}, u32[]{:S(2)}, u32[]{:S(2)}) %collective-permute-start.25) | collective-permute-done | bytes 221216 | tf_op jit(solution)/shard_map/ppermute | solution.py:828
  142.7 9.0 %collective-permute-done.29 = bf16[144,768]{1,0:T(8,128)(2,1)S(1)} collective-permute-done((bf16[144,768]{1,0:T(8,128)(2,1)S(1)}, bf16[144,768]{1,0:T(8,128)(2,1)S(1)}, u32[]{:S(2)}, u32[]{:S(2)}) %collective-permute-start.29) | collective-permute-done | bytes 221216 | tf_op jit(solution)/shard_map/ppermute | solution.py:828
  156.5 3.7 %collective-permute-done.30 = bf16[288,768]{1,0:T(8,128)(2,1)S(1)} collective-permute-done((bf16[288,768]{1,0:T(8,128)(2,1)S(1)}, bf16[288,768]{1,0:T(8,128)(2,1)S(1)}, u32[]{:S(2)}, u32[]{:S(2)}) %collective-permute-start.30) | collective-permute-done | bytes 442400 | tf_op jit(solution)/shard_map/ppermute | solution.py:828
  160.9 23.5 %experts.1 = (bf16[2,144,768]{2,1,0:T(8,128)(2,1)}, bf16[2,144,768]{2,1,0:T(8,128)(2,1)}, bf16[2,144,768]{2,1,0:T(8,128)(2,1)}, bf16[2,144,768]{2,1,0:T(8,128)(2...) custom-call(s32[4]{0:T(128)} %pad_add_fusion.place_ref, ...), custom_call_target="tpu_custom_call" | custom-call | flops 8153726976 | bytes 24772608 | tf_op jit(solution)/shard_map/experts/pallas_call | solution.py:628
  188.5 9.6 %expert_rows.1 = bf16[4,4,144,768]{3,2,1,0:T(8,128)(2,1)} custom-call(s32[4]{0:T(128)} %pad_add_fusion.place_ref, bf16[4,576,768]{2,1,0:T(8,128)(2,1)} %get-tuple-element.212.hid_ref, bf16[4,768,384]{2,1,0:T(8,128)(2,1)} %own_out.1, bf16[4,768,384]{2,1,0:T(8,128)(2,1)} %collective-permute-done.19.refs_16_.peer_out), custom_call_target="tpu_custom_call" | custom-call | flops 2717908992 | bytes 10616832 | tf_op jit(solution)/shard_map/expert_rows/pallas_call | solution.py:674
  198.1 5.7 %collective-permute-done.33 = bf16[288,768]{1,0:T(8,128)(2,1)S(1)} collective-permute-done((bf16[288,768]{1,0:T(8,128)(2,1)}, bf16[288,768]{1,0:T(8,128)(2,1)S(1)}, u32[]{:S(2)}, u32[]{:S(2)}) %collective-permute-start.33) | collective-permute-done | bytes 442400 | tf_op jit(solution)/shard_map/ppermute | solution.py:828
  218.5 15.2 %expert_weights.1 = (f32[4,384,768]{2,1,0:T(8,128)}, bf16[4,384,768]{2,1,0:T(8,128)(2,1)}, f32[4,768,384]{2,1,0:T(8,128)}, bf16[4,768,384]{2,1,0:T(8,128)(2,1)}, f32[16,768]{1,0:T(8,128)}) custom-call(s32[4]{0:T(128)} %pad_add_fusion.place_ref, bf16[4,576,768]{2,1,0:T(8,128)(2,1)} %get-tuple-element.210.x_ref, ...), custom_call_target="tpu_custom_call" | custom-call | flops 5435817984 | bytes 24772608 | tf_op jit(solution)/shard_map/expert_weights/pallas_call | solution.py:713
  235.2 4.9 %hidden_back.1 = (f32[384,768]{1,0:T(8,128)}, bf16[384,768]{1,0:T(8,128)(2,1)}, f32[1,768]{1,0:T(1,128)}) custom-call(s32[384,1]{1,0:T(8,128)} %broadcast_in_dim.35.target_ref, bf16[144,768]{1,0:T(8,128)(2,1)} %fusion.11.refs_0_, bf16[144,768]{1,0:T(8,128)(2,1)} %copy-done.26, bf16[144,768]{1,0:T(8,128)(2,1)} %copy-done.27, bf16[144,768]{1,0:T(8,128)(2,1)} %copy-done.28, ...), custom_call_target="tpu_custom_call" | custom-call | flops 339738624 | bytes 4718592 | tf_op jit(solution)/shard_map/hidden_back/pallas_call | solution.py:763
  243.4 7.0 %collective-permute-done.42.refs_1_ = bf16[192,768]{1,0:T(8,128)(2,1)S(1)} collective-permute-done((bf16[192,768]{1,0:T(8,128)(2,1)S(1)}, bf16[192,768]{1,0:T(8,128)(2,1)S(1)}, u32[]{:S(2)}, u32[]{:S(2)}) %collective-permute-start.42) | collective-permute-done | bytes 294944 | tf_op jit(solution)/shard_map/ppermute | solution.py:828
  252.7 4.5 %convert_add_fusion.1 = f32[4,384,768]{2,1,0:T(8,128)} fusion(f32[4,384,768]{2,1,0:T(8,128)S(1)} %copy-done, bf16[4,384,768]{2,1,0:T(8,128)(2,1)} %collective-permute-done.46), kind=kLoop, calls=%fused_computation.2 | loop fusion | flops 2359296 | bytes 11796480 | tf_op jit(solution)/shard_map/add | solution.py:1002
  260.0 13.3 %collective-permute-done.43.refs_2_ = bf16[384,768]{1,0:T(8,128)(2,1)S(1)} collective-permute-done((bf16[384,768]{1,0:T(8,128)(2,1)S(1)}, bf16[384,768]{1,0:T(8,128)(2,1)S(1)}, u32[]{:S(2)}, u32[]{:S(2)}) %collective-permute-start.43) | collective-permute-done | bytes 589856 | tf_op jit(solution)/shard_map/ppermute | solution.py:828
  275.7 3.8 %collective-permute-start.50 = (bf16[144,768]{1,0:T(8,128)(2,1)S(1)}, bf16[144,768]{1,0:T(8,128)(2,1)S(1)}, u32[]{:S(2)}, u32[]{:S(2)}) collective-permute-start(bf16[144,768]{1,0:T(8,128)(2,1)S(1)} %get-tuple-element.272), channel_id=1, source_target_pairs={{0,12},{4,8},{8,4},{12,0},{1,13},{5,9},{9,5},{13,1},{2,14},{6,10},... | collective-permute-start | bytes 663560 | tf_op jit(solution)/shard_map/ppermute | solution.py:828
  280.1 24.7 %attend_back.1 = (bf16[384,768]{1,0:T(8,128)(2,1)}, bf16[384,768]{1,0:T(8,128)(2,1)}, bf16[384,768]{1,0:T(8,128)(2,1)}, bf16[384,768]{1,0:T(8,128)(2,1)}, bf16[4...) custom-call(s32[4]{0:T(128)} %pad_add_fusion.place_ref, ...), custom_call_target="tpu_custom_call" | custom-call | flops 5586812928 | bytes 14155776 | tf_op jit(solution)/shard_map/attend_back/pallas_call | solution.py:325
  309.5 13.4 %collective-permute-done.55.refs_1_ = bf16[384,768]{1,0:T(8,128)(2,1)S(1)} collective-permute-done((bf16[384,768]{1,0:T(8,128)(2,1)}, bf16[384,768]{1,0:T(8,128)(2,1)S(1)}, u32[]{:S(2)}, u32[]{:S(2)}) %collective-permute-start.55) | collective-permute-done | bytes 589856 | tf_op jit(solution)/shard_map/ppermute | solution.py:828
  329.7 3.7 %collective-permute-start.54 = (bf16[112,768]{1,0:T(8,128)(2,1)}, bf16[112,768]{1,0:T(8,128)(2,1)S(1)}, u32[]{:S(2)}, u32[]{:S(2)}) collective-permute-start(bf16[112,768]{1,0:T(8,128)(2,1)} %get-tuple-element.268), channel_id=1, source_target_pairs={{0,12},{4,8},{8,4},{12,0},{1,13},{5,9},{9,5},{13,1},{2,14},{6,10},... | collective-permute-start | bytes 516104 | tf_op jit(solution)/shard_map/ppermute | solution.py:828
  338.2 4.0 %tokens_back.1 = f32[384,768]{1,0:T(8,128)} custom-call(bf16[384,768]{1,0:T(8,128)(2,1)} %tok_ref.3, bf16[384,768]{1,0:T(8,128)(2,1)} %get-tuple-element.254.refs_0_, bf16[384,768]{1,0:T(8,128)(2,1)} %copy-done.4, bf16[192,768]{1,0:T(8,128)(2,1)} %copy-done.16, bf16[384,768]{1,0:T(8,128)(2,1)} %get-tuple-element.256.refs_3_, bf16[384,768]{1,0:T(8,128)(2,1)} %copy-done.5, ...), custom_call_target="tpu_custom_call" | custom-call | flops 2949120 | bytes 3538944 | tf_op jit(solution)/shard_map/tokens_back/pallas_call | solution.py:808
  342.3 4.6 %collective-permute-done.53 = bf16[112,768]{1,0:T(8,128)(2,1)} collective-permute-done((bf16[112,768]{1,0:T(8,128)(2,1)}, bf16[112,768]{1,0:T(8,128)(2,1)}, u32[]{:S(2)}, u32[]{:S(2)}) %collective-permute-start.53) | collective-permute-done | bytes 172064 | tf_op jit(solution)/shard_map/ppermute | solution.py:828
  (294 shorter events, 127.4 us)
Async XLA Ops:
  7.2 152.9 %all-gather.3.cloned.1.call-start = ((), (), s32[]{:S(2)}) async-start(), calls=%async_computation.2 | async-start | bytes 4423680 | tf_op jit(solution)/shard_map/all_gather | solution.py:965
  31.3 18.5 %collective-permute-start.1 = (bf16[384,768]{1,0:T(8,128)(2,1)S(1)}, bf16[384,768]{1,0:T(8,128)(2,1)}, u32[]{:S(2)}, u32[]{:S(2)}) collective-permute-start(bf16[384,768]{1,0:T(8,128)(2,1)S(1)} %pad_maximum_fusion.2), channel_id=1, source_target_pairs={{0,2},{1,3},{2,0},{3,1},{4,6},{5,7},{6,4},{7,5},{8,10},{9,11},{10,... | collective-permute-start | bytes 1769480 | tf_op jit(solution)/shard_map/ppermute | solution.py:828
  51.6 19.4 %collective-permute-start.11 = (bf16[144,768]{1,0:T(8,128)(2,1)}, bf16[144,768]{1,0:T(8,128)(2,1)S(1)}, u32[]{:S(2)}, u32[]{:S(2)}) collective-permute-start(bf16[144,768]{1,0:T(8,128)(2,1)} %get-tuple-element.166), channel_id=1, source_target_pairs={{0,4},{4,0},{8,12},{12,8},{1,5},{5,1},{9,13},{13,9},{2,6},{6,2},{1... | collective-permute-start | bytes 663560 | tf_op jit(solution)/shard_map/ppermute | solution.py:828
  51.6 19.4 %collective-permute-start.12 = (bf16[144,768]{1,0:T(8,128)(2,1)}, bf16[144,768]{1,0:T(8,128)(2,1)S(1)}, u32[]{:S(2)}, u32[]{:S(2)}) collective-permute-start(bf16[144,768]{1,0:T(8,128)(2,1)} %get-tuple-element.167), channel_id=1, source_target_pairs={{0,8},{4,12},{8,0},{12,4},{1,9},{5,13},{9,1},{13,5},{2,10},{6,14},... | collective-permute-start | bytes 663560 | tf_op jit(solution)/shard_map/ppermute | solution.py:828
  72.0 201.3 %reduce-scatter.2.cloned.1.call-start = ((), (), s32[]{:S(2)}) async-start(), calls=%async_computation.1 | async-start | bytes 4423680 | tf_op jit(solution)/shard_map/reduce_scatter | solution.py:991
  72.0 33.8 %collective-permute-start.18 = (bf16[4,384,768]{2,1,0:T(8,128)(2,1)}, bf16[4,384,768]{2,1,0:T(8,128)(2,1)S(1)}, u32[]{:S(2)}, u32[]{:S(2)}) collective-permute-start(bf16[4,384,768]{2,1,0:T(8,128)(2,1)} %refs_13_.1), channel_id=1, source_target_pairs={{0,16},{16,0},{1,17},{17,1},{2,18},{18,2},{3,19},{19,3},{4,20},{20... | collective-permute-start | bytes 7077896 | tf_op jit(solution)/shard_map/ppermute | solution.py:818
  72.9 33.0 %collective-permute-start.19 = (bf16[4,768,384]{2,1,0:T(8,128)(2,1)S(1)}, bf16[4,768,384]{2,1,0:T(8,128)(2,1)}, u32[]{:S(2)}, u32[]{:S(2)}) collective-permute-start(bf16[4,768,384]{2,1,0:T(8,128)(2,1)S(1)} %copy-done.1), channel_id=1, source_target_pairs={{0,16},{16,0},{1,17},{17,1},{2,18},{18,2},{3,19},{19,3},{4,20},{20... | collective-permute-start | bytes 7077896 | tf_op jit(solution)/shard_map/ppermute | solution.py:818
  72.9 21.4 %collective-permute-start.14 = (bf16[384,768]{1,0:T(8,128)(2,1)}, bf16[384,768]{1,0:T(8,128)(2,1)S(1)}, u32[]{:S(2)}, u32[]{:S(2)}) collective-permute-start(bf16[384,768]{1,0:T(8,128)(2,1)} %get-tuple-element.170), channel_id=1, source_target_pairs={{0,1},{1,0},{2,3},{3,2},{4,5},{5,4},{6,7},{7,6},{8,9},{9,8},{10,11... | collective-permute-start | bytes 1769480 | tf_op jit(solution)/shard_map/ppermute | solution.py:828
  74.4 22.3 %collective-permute-start.16 = (bf16[384,768]{1,0:T(8,128)(2,1)}, bf16[384,768]{1,0:T(8,128)(2,1)S(1)}, u32[]{:S(2)}, u32[]{:S(2)}) collective-permute-start(bf16[384,768]{1,0:T(8,128)(2,1)} %get-tuple-element.172), channel_id=1, source_target_pairs={{0,2},{1,3},{2,0},{3,1},{4,6},{5,7},{6,4},{7,5},{8,10},{9,11},{10,... | collective-permute-start | bytes 1769480 | tf_op jit(solution)/shard_map/ppermute | solution.py:828
  114.3 19.0 %collective-permute-start.25 = (bf16[144,768]{1,0:T(8,128)(2,1)}, bf16[144,768]{1,0:T(8,128)(2,1)S(1)}, u32[]{:S(2)}, u32[]{:S(2)}) collective-permute-start(bf16[144,768]{1,0:T(8,128)(2,1)} %get-tuple-element.183), channel_id=1, source_target_pairs={{0,8},{4,12},{8,0},{12,4},{1,9},{5,13},{9,1},{13,5},{2,10},{6,14},... | collective-permute-start | bytes 663560 | tf_op jit(solution)/shard_map/ppermute | solution.py:828
  115.3 18.0 %collective-permute-start.20 = (bf16[144,768]{1,0:T(8,128)(2,1)}, bf16[144,768]{1,0:T(8,128)(2,1)S(1)}, u32[]{:S(2)}, u32[]{:S(2)}) collective-permute-start(bf16[144,768]{1,0:T(8,128)(2,1)} %get-tuple-element.181), channel_id=1, source_target_pairs={{0,1},{1,0},{2,3},{3,2},{4,5},{5,4},{6,7},{7,6},{8,9},{9,8},{10,11... | collective-permute-start | bytes 663560 | tf_op jit(solution)/shard_map/ppermute | solution.py:828
  116.1 19.4 %collective-permute-start.28 = (bf16[144,768]{1,0:T(8,128)(2,1)}, bf16[144,768]{1,0:T(8,128)(2,1)S(1)}, u32[]{:S(2)}, u32[]{:S(2)}) collective-permute-start(bf16[144,768]{1,0:T(8,128)(2,1)} %get-tuple-element.184), channel_id=1, source_target_pairs={{0,12},{4,8},{8,4},{12,0},{1,13},{5,9},{9,5},{13,1},{2,14},{6,10},... | collective-permute-start | bytes 663560 | tf_op jit(solution)/shard_map/ppermute | solution.py:828
  134.4 18.9 %collective-permute-start.21 = (bf16[288,768]{1,0:T(8,128)(2,1)S(1)}, bf16[288,768]{1,0:T(8,128)(2,1)S(1)}, u32[]{:S(2)}, u32[]{:S(2)}) collective-permute-start(bf16[288,768]{1,0:T(8,128)(2,1)S(1)} %pad_maximum_fusion.6), channel_id=1, source_target_pairs={{0,2},{1,3},{2,0},{3,1},{4,6},{5,7},{6,4},{7,5},{8,10},{9,11},{10,... | collective-permute-start | bytes 1327112 | tf_op jit(solution)/shard_map/ppermute | solution.py:828
  186.4 17.4 %collective-permute-start.33 = (bf16[288,768]{1,0:T(8,128)(2,1)}, bf16[288,768]{1,0:T(8,128)(2,1)S(1)}, u32[]{:S(2)}, u32[]{:S(2)}) collective-permute-start(bf16[288,768]{1,0:T(8,128)(2,1)} %bitcast.110), channel_id=1, source_target_pairs={{0,1},{1,0},{2,3},{3,2},{4,5},{5,4},{6,7},{7,6},{8,9},{9,8},{10,11... | collective-permute-start | bytes 1327112 | tf_op jit(solution)/shard_map/ppermute | solution.py:828
  186.8 17.1 %collective-permute-start.34 = (bf16[288,768]{1,0:T(8,128)(2,1)}, bf16[288,768]{1,0:T(8,128)(2,1)S(1)}, u32[]{:S(2)}, u32[]{:S(2)}) collective-permute-start(bf16[288,768]{1,0:T(8,128)(2,1)} %bitcast.109), channel_id=1, source_target_pairs={{0,2},{1,3},{2,0},{3,1},{4,6},{5,7},{6,4},{7,5},{8,10},{9,11},{10,... | collective-permute-start | bytes 1327112 | tf_op jit(solution)/shard_map/ppermute | solution.py:828
  213.8 19.9 %collective-permute-start.39 = (bf16[144,768]{1,0:T(8,128)(2,1)S(1)}, bf16[144,768]{1,0:T(8,128)(2,1)S(1)}, u32[]{:S(2)}, u32[]{:S(2)}) collective-permute-start(bf16[144,768]{1,0:T(8,128)(2,1)S(1)} %fusion.8), channel_id=1, source_target_pairs={{0,4},{4,0},{8,12},{12,8},{1,5},{5,1},{9,13},{13,9},{2,6},{6,2},{1... | collective-permute-start | bytes 663560 | tf_op jit(solution)/shard_map/ppermute | solution.py:828
  215.5 18.2 %collective-permute-start.40 = (bf16[144,768]{1,0:T(8,128)(2,1)S(1)}, bf16[144,768]{1,0:T(8,128)(2,1)S(1)}, u32[]{:S(2)}, u32[]{:S(2)}) collective-permute-start(bf16[144,768]{1,0:T(8,128)(2,1)S(1)} %fusion.5), channel_id=1, source_target_pairs={{0,8},{4,12},{8,0},{12,4},{1,9},{5,13},{9,1},{13,5},{2,10},{6,14},... | collective-permute-start | bytes 663560 | tf_op jit(solution)/shard_map/ppermute | solution.py:828
  233.8 18.9 %collective-permute-start.46 = (bf16[4,384,768]{2,1,0:T(8,128)(2,1)}, bf16[4,384,768]{2,1,0:T(8,128)(2,1)}, u32[]{:S(2)}, u32[]{:S(2)}) collective-permute-start(bf16[4,384,768]{2,1,0:T(8,128)(2,1)} %get-tuple-element.224), channel_id=1, source_target_pairs={{0,16},{16,0},{1,17},{17,1},{2,18},{18,2},{3,19},{19,3},{4,20},{20... | collective-permute-start | bytes 7077896 | tf_op jit(solution)/shard_map/ppermute | solution.py:818
  233.9 23.3 %collective-permute-start.47 = (bf16[4,768,384]{2,1,0:T(8,128)(2,1)}, bf16[4,768,384]{2,1,0:T(8,128)(2,1)S(1)}, u32[]{:S(2)}, u32[]{:S(2)}) collective-permute-start(bf16[4,768,384]{2,1,0:T(8,128)(2,1)} %get-tuple-element.226), channel_id=1, source_target_pairs={{0,16},{16,0},{1,17},{17,1},{2,18},{18,2},{3,19},{19,3},{4,20},{20... | collective-permute-start | bytes 7077896 | tf_op jit(solution)/shard_map/ppermute | solution.py:818
  250.4 22.9 %collective-permute-start.43 = (bf16[384,768]{1,0:T(8,128)(2,1)S(1)}, bf16[384,768]{1,0:T(8,128)(2,1)S(1)}, u32[]{:S(2)}, u32[]{:S(2)}) collective-permute-start(bf16[384,768]{1,0:T(8,128)(2,1)S(1)} %pad_maximum_fusion.4), channel_id=1, source_target_pairs={{0,2},{1,3},{2,0},{3,1},{4,6},{5,7},{6,4},{7,5},{8,10},{9,11},{10,... | collective-permute-start | bytes 1769480 | tf_op jit(solution)/shard_map/ppermute | solution.py:828
  251.7 21.6 %collective-permute-start.45 = (bf16[384,768]{1,0:T(8,128)(2,1)S(1)}, bf16[384,768]{1,0:T(8,128)(2,1)S(1)}, u32[]{:S(2)}, u32[]{:S(2)}) collective-permute-start(bf16[384,768]{1,0:T(8,128)(2,1)S(1)} %pad_maximum_fusion.5), channel_id=1, source_target_pairs={{0,1},{1,0},{2,3},{3,2},{4,5},{5,4},{6,7},{7,6},{8,9},{9,8},{10,11... | collective-permute-start | bytes 1769480 | tf_op jit(solution)/shard_map/ppermute | solution.py:828
  275.7 29.1 %collective-permute-start.50 = (bf16[144,768]{1,0:T(8,128)(2,1)S(1)}, bf16[144,768]{1,0:T(8,128)(2,1)S(1)}, u32[]{:S(2)}, u32[]{:S(2)}) collective-permute-start(bf16[144,768]{1,0:T(8,128)(2,1)S(1)} %get-tuple-element.272), channel_id=1, source_target_pairs={{0,12},{4,8},{8,4},{12,0},{1,13},{5,9},{9,5},{13,1},{2,14},{6,10},... | collective-permute-start | bytes 663560 | tf_op jit(solution)/shard_map/ppermute | solution.py:828
  279.5 25.4 %collective-permute-start.49 = (bf16[144,768]{1,0:T(8,128)(2,1)S(1)}, bf16[144,768]{1,0:T(8,128)(2,1)S(1)}, u32[]{:S(2)}, u32[]{:S(2)}) collective-permute-start(bf16[144,768]{1,0:T(8,128)(2,1)S(1)} %get-tuple-element.273), channel_id=1, source_target_pairs={{0,8},{4,12},{8,0},{12,4},{1,9},{5,13},{9,1},{13,5},{2,10},{6,14},... | collective-permute-start | bytes 663560 | tf_op jit(solution)/shard_map/ppermute | solution.py:828
  279.5 25.4 %collective-permute-start.48 = (bf16[144,768]{1,0:T(8,128)(2,1)S(1)}, bf16[144,768]{1,0:T(8,128)(2,1)S(1)}, u32[]{:S(2)}, u32[]{:S(2)}) collective-permute-start(bf16[144,768]{1,0:T(8,128)(2,1)S(1)} %get-tuple-element.274), channel_id=1, source_target_pairs={{0,4},{4,0},{8,12},{12,8},{1,5},{5,1},{9,13},{13,9},{2,6},{6,2},{1... | collective-permute-start | bytes 663560 | tf_op jit(solution)/shard_map/ppermute | solution.py:828
  (89 other events, 1107.0 us)
Sparse Core Ops, SparseCore 0:
  72.1 63.7 all-gather.2
  213.9 56.0 reduce-scatter.1

commit v10 on v8

--- a/solution.py
+++ b/solution.py
@@ -733,8 +733,7 @@
     hidden_ref, cot_ref, gain_ref, grad_ref, attn_ref, gain_out = refs[-6:]
     grad_in = take_rows(target_ref, refs[:-6])
     unit, scale = unit_rows(hidden_ref[...])
-    gained = jnp.sum(grad_in * unit, axis=0, keepdims=True)
-    gain_out[...] = gained + jnp.where(pl.program_id(0) > 0, gain_out[...], jnp.zeros_like(gained))
+    gain_out[...] = jnp.sum(grad_in * unit, axis=0, keepdims=True)
     scaled = grad_in * gain_ref[...]
     inside = jnp.mean(unit * scaled, axis=-1, keepdims=True)
     grad = cot_ref[...].astype(F32) + scale * (scaled - unit * inside)
@@ -744,13 +743,8 @@
 
 def hidden_back(target_col, back, hidden, cotangent, gain):
     rows, width = hidden.shape
-    steps = 3 if rows % 48 == 0 else 1
-    by_row = lambda cols: pl.BlockSpec((rows // steps, cols), lambda i: (i, 0))
     return pl.pallas_call(
         hidden_back_kernel,
-        grid=(steps,),
-        in_specs=[by_row(1)] + [whole(b.shape) for b in back] + [by_row(width), by_row(width), whole((1, width))],
-        out_specs=[by_row(width), by_row(width), whole((1, width))],
         out_shape=[
             jax.ShapeDtypeStruct((rows, width), F32),
             jax.ShapeDtypeStruct((rows, width), BF16),
@@ -1017,6 +1011,7 @@
         own_part, other_part = payload[:z_count], payload[z_count:]
     other_got = shifted(other_part, "dp", dp_count, 1)
     pieces = swap_pieces([added(own_part[k], other_got[k]) for k in range(z_count)], "expert", z_count)
+    pieces, grad_tokens = lax.optimization_barrier((pieces, grad_tokens))
     total = pieces[0].astype(F32)
     for piece in pieces[1:]:
         total = total + piece.astype(F32)

time: 360 us -> 358 us (level)
  waiting for transfers between devices: 118 us -> 113 us
  other arithmetic: 19.2 us -> 22.8 us
    ppermute x57, waiting for transfers between devices: 118 us -> 113 us  [swapped(): return lax.ppermute(value, axis, [(s, s ^ bits) for s in range(count)])]
    unnamed x104 -> x102, local copies, waits for them, and re-layouts: 7.83 us -> 7.17 us
  transfers between devices with their start and end apart: 64 -> 64, of which waited for: 22 -> 20; matrix products, arithmetic and copies ran while one was open for 8% -> 8% of each run, Pallas kernels for 23% -> 24%
where the time goes in v10:
time: 358 us; the launch traced here: 357 us
  waiting for transfers between devices  113 us (32%)
  Pallas kernels  109 us (30%)
  starting transfers between devices  75.7 us (21%)
  other arithmetic  22.8 us (6%)
  local copies, waits for them, and re-layouts  21.8 us (6%)
  between operations  14.8 us (4%)
    ppermute x57, waiting for transfers between devices, swapped(): return lax.ppermute(value, axis, [(s, s ^ bits) for s in range(count)])  113 us
    ppermute x57, starting transfers between devices, swapped(): return lax.ppermute(value, axis, [(s, s ^ bits) for s in range(count)])  75 us
    pallas_call x1, Pallas kernels, attend_back(): pl.pallas_call(functools.partial(attend_back_kernel, heads, tensors, part...  24.4 us
    pallas_call x1, Pallas kernels, expert_forward_back(): pl.pallas_call(functools.partial(expert_kernel, chunks, tensors, main, lo...  23.5 us
    pallas_call x1, Pallas kernels, attend(): pl.pallas_call(functools.partial(attend_kernel, heads, tensors, len(owned...  15.4 us
    pallas_call x1, Pallas kernels, expert_weights(): pl.pallas_call(expert_weights_kernel, grid_spec=pltpu.PrefetchScalarGridS...  15.2 us
    pallas_call x1, Pallas kernels, expert_rows(): pl.pallas_call(functools.partial(expert_rows_kernel, chunks, main, locals...  9.63 us
    unnamed x102, local copies, waits for them, and re-layouts  7.17 us
  transfers between devices with their start and end apart: 64, of which 20 were waited for; matrix products, arithmetic and copies ran while one was open for 8% of the time, Pallas kernels for 24%

profile of v10, /device:TPU:0, one launch (start us, length us, event | category | flops | bytes accessed | tf_op | source)
XLA Modules:
  0.0 357.1 jit_solution(16719743589013055535)
XLA Ops:
  10.4 5.1 %collective-permute-start.6 = (bf16[1,112,768]{2,1,0:T(8,128)(2,1)S(1)}, bf16[1,112,768]{2,1,0:T(8,128)(2,1)S(1)}, u32[]{:S(2)}, u32[]{:S(2)}) collective-permute-start(bf16[1,112,768]{2,1,0:T(8,128)(2,1)S(1)} %maximum_bitcast_fusion.refs_0_.refs_5_), channel_id=1, source_target_pairs={{0,12},{4,8},{8,4},{12,0},{1,13},{5,9},{9,5},{13,1},{2,14},{6,10},... | collective-permute-start | bytes 516104 | tf_op jit(solution)/shard_map/ppermute | solution.py:808
  21.3 8.9 %collective-permute-done.5.refs_2_.refs_7_ = bf16[1,112,768]{2,1,0:T(8,128)(2,1)S(1)} collective-permute-done((bf16[1,112,768]{2,1,0:T(8,128)(2,1)S(1)}, bf16[1,112,768]{2,1,0:T(8,128)(2,1)S(1)}, u32[]{:S(2)}, u32[]{:S(2)}) %collective-permute-start.5) | collective-permute-done | bytes 172064 | tf_op jit(solution)/shard_map/ppermute | solution.py:808
  46.3 3.4 collective-permute-done.10
  56.0 15.4 %attend.1 = (bf16[384,768]{1,0:T(8,128)(2,1)}, bf16[384,768]{1,0:T(8,128)(2,1)}, bf16[384,768]{1,0:T(8,128)(2,1)}, bf16[384,768]{1,0:T(8,128)(2,1)}, bf16[1536,7...) custom-call(s32[4]{0:T(128)} %pad_add_fusion.place_ref, ...), custom_call_target="tpu_custom_call" | custom-call | flops 2415919104 | bytes 9437184 | tf_op jit(solution)/shard_map/attend/pallas_call | solution.py:158
  76.2 19.0 %collective-permute-done.14.refs_1_ = bf16[384,768]{1,0:T(8,128)(2,1)S(1)} collective-permute-done((bf16[384,768]{1,0:T(8,128)(2,1)}, bf16[384,768]{1,0:T(8,128)(2,1)S(1)}, u32[]{:S(2)}, u32[]{:S(2)}) %collective-permute-start.14) | collective-permute-done | bytes 589856 | tf_op jit(solution)/shard_map/ppermute | solution.py:808
  107.1 4.9 %route.1 = (f32[384,768]{1,0:T(8,128)}, f32[384,1]{1,0:T(8,128)}, bf16[144,768]{1,0:T(8,128)(2,1)}, bf16[144,768]{1,0:T(8,128)(2,1)}, bf16[144,768]{1,0:T(8,128)(2,1)}, /*index=5*/bf16[144,768]{1,0:T(8,128)(2,1)}) custom-call(bf16[384,768]{1,0:T(8,128)(2,1)} %tok_ref.3, bf16[384,768]{1,0:T(8,128)(2,1)} %get-tuple-element.170.refs_0_, ...), custom_call_target="tpu_custom_call" | custom-call | flops 339738624 | bytes 3538944 | tf_op jit(solution)/shard_map/route/pallas_call | solution.py:442
  117.7 4.5 %collective-permute-done.22 = bf16[144,768]{1,0:T(8,128)(2,1)S(1)} collective-permute-done((bf16[144,768]{1,0:T(8,128)(2,1)}, bf16[144,768]{1,0:T(8,128)(2,1)S(1)}, u32[]{:S(2)}, u32[]{:S(2)}) %collective-permute-start.22) | collective-permute-done | bytes 221216 | tf_op jit(solution)/shard_map/ppermute | solution.py:808
  124.2 9.0 %collective-permute-done.25 = bf16[144,768]{1,0:T(8,128)(2,1)S(1)} collective-permute-done((bf16[144,768]{1,0:T(8,128)(2,1)}, bf16[144,768]{1,0:T(8,128)(2,1)S(1)}, u32[]{:S(2)}, u32[]{:S(2)}) %collective-permute-start.25) | collective-permute-done | bytes 221216 | tf_op jit(solution)/shard_map/ppermute | solution.py:808
  142.7 9.0 %collective-permute-done.29 = bf16[144,768]{1,0:T(8,128)(2,1)S(1)} collective-permute-done((bf16[144,768]{1,0:T(8,128)(2,1)S(1)}, bf16[144,768]{1,0:T(8,128)(2,1)S(1)}, u32[]{:S(2)}, u32[]{:S(2)}) %collective-permute-start.29) | collective-permute-done | bytes 221216 | tf_op jit(solution)/shard_map/ppermute | solution.py:808
  156.5 3.7 %collective-permute-done.30 = bf16[288,768]{1,0:T(8,128)(2,1)S(1)} collective-permute-done((bf16[288,768]{1,0:T(8,128)(2,1)S(1)}, bf16[288,768]{1,0:T(8,128)(2,1)S(1)}, u32[]{:S(2)}, u32[]{:S(2)}) %collective-permute-start.30) | collective-permute-done | bytes 442400 | tf_op jit(solution)/shard_map/ppermute | solution.py:808
  160.9 23.5 %experts.1 = (bf16[2,144,768]{2,1,0:T(8,128)(2,1)}, bf16[2,144,768]{2,1,0:T(8,128)(2,1)}, bf16[2,144,768]{2,1,0:T(8,128)(2,1)}, bf16[2,144,768]{2,1,0:T(8,128)(2...) custom-call(s32[4]{0:T(128)} %pad_add_fusion.place_ref, ...), custom_call_target="tpu_custom_call" | custom-call | flops 8153726976 | bytes 24772608 | tf_op jit(solution)/shard_map/experts/pallas_call | solution.py:614
  188.5 9.6 %expert_rows.1 = bf16[4,4,144,768]{3,2,1,0:T(8,128)(2,1)} custom-call(s32[4]{0:T(128)} %pad_add_fusion.place_ref, bf16[4,576,768]{2,1,0:T(8,128)(2,1)} %get-tuple-element.207.hid_ref, bf16[4,768,384]{2,1,0:T(8,128)(2,1)} %own_out.1, bf16[4,768,384]{2,1,0:T(8,128)(2,1)} %collective-permute-done.19.refs_16_.peer_out), custom_call_target="tpu_custom_call" | custom-call | flops 2717908992 | bytes 10616832 | tf_op jit(solution)/shard_map/expert_rows/pallas_call | solution.py:660
  198.1 5.7 %collective-permute-done.33 = bf16[288,768]{1,0:T(8,128)(2,1)S(1)} collective-permute-done((bf16[288,768]{1,0:T(8,128)(2,1)}, bf16[288,768]{1,0:T(8,128)(2,1)S(1)}, u32[]{:S(2)}, u32[]{:S(2)}) %collective-permute-start.33) | collective-permute-done | bytes 442400 | tf_op jit(solution)/shard_map/ppermute | solution.py:808
  218.5 15.2 %expert_weights.1 = (f32[4,384,768]{2,1,0:T(8,128)}, bf16[4,384,768]{2,1,0:T(8,128)(2,1)}, f32[4,768,384]{2,1,0:T(8,128)}, bf16[4,768,384]{2,1,0:T(8,128)(2,1)}, f32[16,768]{1,0:T(8,128)}) custom-call(s32[4]{0:T(128)} %pad_add_fusion.place_ref, bf16[4,576,768]{2,1,0:T(8,128)(2,1)} %get-tuple-element.205.x_ref, ...), custom_call_target="tpu_custom_call" | custom-call | flops 5435817984 | bytes 24772608 | tf_op jit(solution)/shard_map/expert_weights/pallas_call | solution.py:699
  235.2 4.4 %hidden_back.1 = (f32[384,768]{1,0:T(8,128)}, bf16[384,768]{1,0:T(8,128)(2,1)}, f32[1,768]{1,0:T(1,128)}) custom-call(s32[384,1]{1,0:T(8,128)} %broadcast_in_dim.35.target_ref, bf16[144,768]{1,0:T(8,128)(2,1)} %fusion.11.refs_0_, bf16[144,768]{1,0:T(8,128)(2,1)} %copy-done.26, bf16[144,768]{1,0:T(8,128)(2,1)} %copy-done.27, bf16[144,768]{1,0:T(8,128)(2,1)} %copy-done.28, ...), custom_call_target="tpu_custom_call" | custom-call | flops 339738624 | bytes 4718592 | tf_op jit(solution)/shard_map/hidden_back/pallas_call | solution.py:746
  242.8 6.9 %collective-permute-done.42.refs_1_ = bf16[192,768]{1,0:T(8,128)(2,1)S(1)} collective-permute-done((bf16[192,768]{1,0:T(8,128)(2,1)S(1)}, bf16[192,768]{1,0:T(8,128)(2,1)S(1)}, u32[]{:S(2)}, u32[]{:S(2)}) %collective-permute-start.42) | collective-permute-done | bytes 294944 | tf_op jit(solution)/shard_map/ppermute | solution.py:808
  252.1 4.5 %convert_add_fusion.1 = f32[4,384,768]{2,1,0:T(8,128)} fusion(f32[4,384,768]{2,1,0:T(8,128)S(1)} %copy-done, bf16[4,384,768]{2,1,0:T(8,128)(2,1)} %collective-permute-done.46), kind=kLoop, calls=%fused_computation.2 | loop fusion | flops 2359296 | bytes 11796480 | tf_op jit(solution)/shard_map/add | solution.py:982
  259.3 13.9 %collective-permute-done.43.refs_2_ = bf16[384,768]{1,0:T(8,128)(2,1)S(1)} collective-permute-done((bf16[384,768]{1,0:T(8,128)(2,1)S(1)}, bf16[384,768]{1,0:T(8,128)(2,1)S(1)}, u32[]{:S(2)}, u32[]{:S(2)}) %collective-permute-start.43) | collective-permute-done | bytes 589856 | tf_op jit(solution)/shard_map/ppermute | solution.py:808
  275.7 3.3 collective-permute-start.50
  280.1 24.4 %attend_back.1 = (bf16[384,768]{1,0:T(8,128)(2,1)}, bf16[384,768]{1,0:T(8,128)(2,1)}, bf16[384,768]{1,0:T(8,128)(2,1)}, bf16[384,768]{1,0:T(8,128)(2,1)}, bf16[4...) custom-call(s32[4]{0:T(128)} %pad_add_fusion.place_ref, ...), custom_call_target="tpu_custom_call" | custom-call | flops 5586812928 | bytes 14155776 | tf_op jit(solution)/shard_map/attend_back/pallas_call | solution.py:315
  306.7 12.0 %collective-permute-done.55.refs_1_ = bf16[384,768]{1,0:T(8,128)(2,1)S(1)} collective-permute-done((bf16[384,768]{1,0:T(8,128)(2,1)}, bf16[384,768]{1,0:T(8,128)(2,1)S(1)}, u32[]{:S(2)}, u32[]{:S(2)}) %collective-permute-start.55) | collective-permute-done | bytes 589856 | tf_op jit(solution)/shard_map/ppermute | solution.py:808
  325.4 3.4 collective-permute-start.54
  329.7 3.4 output_rows.1
  333.9 4.0 %tokens_back.1 = f32[384,768]{1,0:T(8,128)} custom-call(bf16[384,768]{1,0:T(8,128)(2,1)} %tok_ref.3, bf16[384,768]{1,0:T(8,128)(2,1)} %get-tuple-element.244.refs_0_, bf16[384,768]{1,0:T(8,128)(2,1)} %copy-done.3, bf16[192,768]{1,0:T(8,128)(2,1)} %copy-done.16, bf16[384,768]{1,0:T(8,128)(2,1)} %get-tuple-element.246.refs_3_, bf16[384,768]{1,0:T(8,128)(2,1)} %copy-done.4, ...), custom_call_target="tpu_custom_call" | custom-call | flops 2949120 | bytes 3538944 | tf_op jit(solution)/shard_map/tokens_back/pallas_call | solution.py:788
  (294 shorter events, 125.2 us)
Async XLA Ops:
  7.2 152.9 %all-gather.3.cloned.1.call-start = ((), (), s32[]{:S(2)}) async-start(), calls=%async_computation.2 | async-start | bytes 4423680 | tf_op jit(solution)/shard_map/all_gather | solution.py:945
  31.3 18.5 %collective-permute-start.1 = (bf16[384,768]{1,0:T(8,128)(2,1)S(1)}, bf16[384,768]{1,0:T(8,128)(2,1)}, u32[]{:S(2)}, u32[]{:S(2)}) collective-permute-start(bf16[384,768]{1,0:T(8,128)(2,1)S(1)} %pad_maximum_fusion.2), channel_id=1, source_target_pairs={{0,2},{1,3},{2,0},{3,1},{4,6},{5,7},{6,4},{7,5},{8,10},{9,11},{10,... | collective-permute-start | bytes 1769480 | tf_op jit(solution)/shard_map/ppermute | solution.py:808
  51.6 19.8 %collective-permute-start.11 = (bf16[144,768]{1,0:T(8,128)(2,1)}, bf16[144,768]{1,0:T(8,128)(2,1)S(1)}, u32[]{:S(2)}, u32[]{:S(2)}) collective-permute-start(bf16[144,768]{1,0:T(8,128)(2,1)} %get-tuple-element.161), channel_id=1, source_target_pairs={{0,4},{4,0},{8,12},{12,8},{1,5},{5,1},{9,13},{13,9},{2,6},{6,2},{1... | collective-permute-start | bytes 663560 | tf_op jit(solution)/shard_map/ppermute | solution.py:808
  51.6 19.8 %collective-permute-start.12 = (bf16[144,768]{1,0:T(8,128)(2,1)}, bf16[144,768]{1,0:T(8,128)(2,1)S(1)}, u32[]{:S(2)}, u32[]{:S(2)}) collective-permute-start(bf16[144,768]{1,0:T(8,128)(2,1)} %get-tuple-element.162), channel_id=1, source_target_pairs={{0,8},{4,12},{8,0},{12,4},{1,9},{5,13},{9,1},{13,5},{2,10},{6,14},... | collective-permute-start | bytes 663560 | tf_op jit(solution)/shard_map/ppermute | solution.py:808
  72.4 200.8 %reduce-scatter.2.cloned.1.call-start = ((), (), s32[]{:S(2)}) async-start(), calls=%async_computation.1 | async-start | bytes 4423680 | tf_op jit(solution)/shard_map/reduce_scatter | solution.py:971
  72.5 33.8 %collective-permute-start.18 = (bf16[4,384,768]{2,1,0:T(8,128)(2,1)}, bf16[4,384,768]{2,1,0:T(8,128)(2,1)S(1)}, u32[]{:S(2)}, u32[]{:S(2)}) collective-permute-start(bf16[4,384,768]{2,1,0:T(8,128)(2,1)} %refs_13_.1), channel_id=1, source_target_pairs={{0,16},{16,0},{1,17},{17,1},{2,18},{18,2},{3,19},{19,3},{4,20},{20... | collective-permute-start | bytes 7077896 | tf_op jit(solution)/shard_map/ppermute | solution.py:798
  73.3 33.0 %collective-permute-start.19 = (bf16[4,768,384]{2,1,0:T(8,128)(2,1)S(1)}, bf16[4,768,384]{2,1,0:T(8,128)(2,1)}, u32[]{:S(2)}, u32[]{:S(2)}) collective-permute-start(bf16[4,768,384]{2,1,0:T(8,128)(2,1)S(1)} %copy-done.1), channel_id=1, source_target_pairs={{0,16},{16,0},{1,17},{17,1},{2,18},{18,2},{3,19},{19,3},{4,20},{20... | collective-permute-start | bytes 7077896 | tf_op jit(solution)/shard_map/ppermute | solution.py:798
  73.4 21.9 %collective-permute-start.14 = (bf16[384,768]{1,0:T(8,128)(2,1)}, bf16[384,768]{1,0:T(8,128)(2,1)S(1)}, u32[]{:S(2)}, u32[]{:S(2)}) collective-permute-start(bf16[384,768]{1,0:T(8,128)(2,1)} %get-tuple-element.165), channel_id=1, source_target_pairs={{0,1},{1,0},{2,3},{3,2},{4,5},{5,4},{6,7},{7,6},{8,9},{9,8},{10,11... | collective-permute-start | bytes 1769480 | tf_op jit(solution)/shard_map/ppermute | solution.py:808
  74.8 22.8 %collective-permute-start.16 = (bf16[384,768]{1,0:T(8,128)(2,1)}, bf16[384,768]{1,0:T(8,128)(2,1)S(1)}, u32[]{:S(2)}, u32[]{:S(2)}) collective-permute-start(bf16[384,768]{1,0:T(8,128)(2,1)} %get-tuple-element.167), channel_id=1, source_target_pairs={{0,2},{1,3},{2,0},{3,1},{4,6},{5,7},{6,4},{7,5},{8,10},{9,11},{10,... | collective-permute-start | bytes 1769480 | tf_op jit(solution)/shard_map/ppermute | solution.py:808
  114.3 19.0 %collective-permute-start.25 = (bf16[144,768]{1,0:T(8,128)(2,1)}, bf16[144,768]{1,0:T(8,128)(2,1)S(1)}, u32[]{:S(2)}, u32[]{:S(2)}) collective-permute-start(bf16[144,768]{1,0:T(8,128)(2,1)} %get-tuple-element.178), channel_id=1, source_target_pairs={{0,8},{4,12},{8,0},{12,4},{1,9},{5,13},{9,1},{13,5},{2,10},{6,14},... | collective-permute-start | bytes 663560 | tf_op jit(solution)/shard_map/ppermute | solution.py:808
  115.3 18.0 %collective-permute-start.20 = (bf16[144,768]{1,0:T(8,128)(2,1)}, bf16[144,768]{1,0:T(8,128)(2,1)S(1)}, u32[]{:S(2)}, u32[]{:S(2)}) collective-permute-start(bf16[144,768]{1,0:T(8,128)(2,1)} %get-tuple-element.176), channel_id=1, source_target_pairs={{0,1},{1,0},{2,3},{3,2},{4,5},{5,4},{6,7},{7,6},{8,9},{9,8},{10,11... | collective-permute-start | bytes 663560 | tf_op jit(solution)/shard_map/ppermute | solution.py:808
  116.1 19.4 %collective-permute-start.28 = (bf16[144,768]{1,0:T(8,128)(2,1)}, bf16[144,768]{1,0:T(8,128)(2,1)S(1)}, u32[]{:S(2)}, u32[]{:S(2)}) collective-permute-start(bf16[144,768]{1,0:T(8,128)(2,1)} %get-tuple-element.179), channel_id=1, source_target_pairs={{0,12},{4,8},{8,4},{12,0},{1,13},{5,9},{9,5},{13,1},{2,14},{6,10},... | collective-permute-start | bytes 663560 | tf_op jit(solution)/shard_map/ppermute | solution.py:808
  134.4 18.9 %collective-permute-start.21 = (bf16[288,768]{1,0:T(8,128)(2,1)S(1)}, bf16[288,768]{1,0:T(8,128)(2,1)S(1)}, u32[]{:S(2)}, u32[]{:S(2)}) collective-permute-start(bf16[288,768]{1,0:T(8,128)(2,1)S(1)} %pad_maximum_fusion.6), channel_id=1, source_target_pairs={{0,2},{1,3},{2,0},{3,1},{4,6},{5,7},{6,4},{7,5},{8,10},{9,11},{10,... | collective-permute-start | bytes 1327112 | tf_op jit(solution)/shard_map/ppermute | solution.py:808
  186.4 17.4 %collective-permute-start.33 = (bf16[288,768]{1,0:T(8,128)(2,1)}, bf16[288,768]{1,0:T(8,128)(2,1)S(1)}, u32[]{:S(2)}, u32[]{:S(2)}) collective-permute-start(bf16[288,768]{1,0:T(8,128)(2,1)} %bitcast.110), channel_id=1, source_target_pairs={{0,1},{1,0},{2,3},{3,2},{4,5},{5,4},{6,7},{7,6},{8,9},{9,8},{10,11... | collective-permute-start | bytes 1327112 | tf_op jit(solution)/shard_map/ppermute | solution.py:808
  186.8 17.1 %collective-permute-start.34 = (bf16[288,768]{1,0:T(8,128)(2,1)}, bf16[288,768]{1,0:T(8,128)(2,1)S(1)}, u32[]{:S(2)}, u32[]{:S(2)}) collective-permute-start(bf16[288,768]{1,0:T(8,128)(2,1)} %bitcast.109), channel_id=1, source_target_pairs={{0,2},{1,3},{2,0},{3,1},{4,6},{5,7},{6,4},{7,5},{8,10},{9,11},{10,... | collective-permute-start | bytes 1327112 | tf_op jit(solution)/shard_map/ppermute | solution.py:808
  213.8 20.0 %collective-permute-start.39 = (bf16[144,768]{1,0:T(8,128)(2,1)S(1)}, bf16[144,768]{1,0:T(8,128)(2,1)S(1)}, u32[]{:S(2)}, u32[]{:S(2)}) collective-permute-start(bf16[144,768]{1,0:T(8,128)(2,1)S(1)} %fusion.8), channel_id=1, source_target_pairs={{0,4},{4,0},{8,12},{12,8},{1,5},{5,1},{9,13},{13,9},{2,6},{6,2},{1... | collective-permute-start | bytes 663560 | tf_op jit(solution)/shard_map/ppermute | solution.py:808
  215.5 18.2 %collective-permute-start.40 = (bf16[144,768]{1,0:T(8,128)(2,1)S(1)}, bf16[144,768]{1,0:T(8,128)(2,1)S(1)}, u32[]{:S(2)}, u32[]{:S(2)}) collective-permute-start(bf16[144,768]{1,0:T(8,128)(2,1)S(1)} %fusion.5), channel_id=1, source_target_pairs={{0,8},{4,12},{8,0},{12,4},{1,9},{5,13},{9,1},{13,5},{2,10},{6,14},... | collective-permute-start | bytes 663560 | tf_op jit(solution)/shard_map/ppermute | solution.py:808
  233.8 18.3 %collective-permute-start.46 = (bf16[4,384,768]{2,1,0:T(8,128)(2,1)}, bf16[4,384,768]{2,1,0:T(8,128)(2,1)}, u32[]{:S(2)}, u32[]{:S(2)}) collective-permute-start(bf16[4,384,768]{2,1,0:T(8,128)(2,1)} %get-tuple-element.219), channel_id=1, source_target_pairs={{0,16},{16,0},{1,17},{17,1},{2,18},{18,2},{3,19},{19,3},{4,20},{20... | collective-permute-start | bytes 7077896 | tf_op jit(solution)/shard_map/ppermute | solution.py:798
  233.9 22.7 %collective-permute-start.47 = (bf16[4,768,384]{2,1,0:T(8,128)(2,1)}, bf16[4,768,384]{2,1,0:T(8,128)(2,1)S(1)}, u32[]{:S(2)}, u32[]{:S(2)}) collective-permute-start(bf16[4,768,384]{2,1,0:T(8,128)(2,1)} %get-tuple-element.221), channel_id=1, source_target_pairs={{0,16},{16,0},{1,17},{17,1},{2,18},{18,2},{3,19},{19,3},{4,20},{20... | collective-permute-start | bytes 7077896 | tf_op jit(solution)/shard_map/ppermute | solution.py:798
  249.8 23.4 %collective-permute-start.43 = (bf16[384,768]{1,0:T(8,128)(2,1)S(1)}, bf16[384,768]{1,0:T(8,128)(2,1)S(1)}, u32[]{:S(2)}, u32[]{:S(2)}) collective-permute-start(bf16[384,768]{1,0:T(8,128)(2,1)S(1)} %pad_maximum_fusion.4), channel_id=1, source_target_pairs={{0,2},{1,3},{2,0},{3,1},{4,6},{5,7},{6,4},{7,5},{8,10},{9,11},{10,... | collective-permute-start | bytes 1769480 | tf_op jit(solution)/shard_map/ppermute | solution.py:808
  251.2 22.1 %collective-permute-start.45 = (bf16[384,768]{1,0:T(8,128)(2,1)S(1)}, bf16[384,768]{1,0:T(8,128)(2,1)S(1)}, u32[]{:S(2)}, u32[]{:S(2)}) collective-permute-start(bf16[384,768]{1,0:T(8,128)(2,1)S(1)} %pad_maximum_fusion.5), channel_id=1, source_target_pairs={{0,1},{1,0},{2,3},{3,2},{4,5},{5,4},{6,7},{7,6},{8,9},{9,8},{10,11... | collective-permute-start | bytes 1769480 | tf_op jit(solution)/shard_map/ppermute | solution.py:808
  275.7 28.8 %collective-permute-start.50 = (bf16[144,768]{1,0:T(8,128)(2,1)S(1)}, bf16[144,768]{1,0:T(8,128)(2,1)S(1)}, u32[]{:S(2)}, u32[]{:S(2)}) collective-permute-start(bf16[144,768]{1,0:T(8,128)(2,1)S(1)} %get-tuple-element.262), channel_id=1, source_target_pairs={{0,12},{4,8},{8,4},{12,0},{1,13},{5,9},{9,5},{13,1},{2,14},{6,10},... | collective-permute-start | bytes 663560 | tf_op jit(solution)/shard_map/ppermute | solution.py:808
  279.0 25.5 %collective-permute-start.49 = (bf16[144,768]{1,0:T(8,128)(2,1)S(1)}, bf16[144,768]{1,0:T(8,128)(2,1)S(1)}, u32[]{:S(2)}, u32[]{:S(2)}) collective-permute-start(bf16[144,768]{1,0:T(8,128)(2,1)S(1)} %get-tuple-element.263), channel_id=1, source_target_pairs={{0,8},{4,12},{8,0},{12,4},{1,9},{5,13},{9,1},{13,5},{2,10},{6,14},... | collective-permute-start | bytes 663560 | tf_op jit(solution)/shard_map/ppermute | solution.py:808
  279.0 25.6 %collective-permute-start.48 = (bf16[144,768]{1,0:T(8,128)(2,1)S(1)}, bf16[144,768]{1,0:T(8,128)(2,1)S(1)}, u32[]{:S(2)}, u32[]{:S(2)}) collective-permute-start(bf16[144,768]{1,0:T(8,128)(2,1)S(1)} %get-tuple-element.264), channel_id=1, source_target_pairs={{0,4},{4,0},{8,12},{12,8},{1,5},{5,1},{9,13},{13,9},{2,6},{6,2},{1... | collective-permute-start | bytes 663560 | tf_op jit(solution)/shard_map/ppermute | solution.py:808
  (89 other events, 1102.2 us)
Sparse Core Ops, SparseCore 0:
  72.6 63.0 all-gather.2
  213.9 56.7 reduce-scatter.1

commit v11 on v10

--- a/solution.py
+++ b/solution.py
@@ -981,17 +981,15 @@
         grad_pieces += list(gather_hops(grad_attn[h * half_rows : (h + 1) * half_rows], hops))
     grad_w_in = in_own + in_got.astype(F32)
     grad_w_out = out_own + out_got.astype(F32)
-    grad_pieces, grad_w_in, grad_w_out, forward_sum = lax.optimization_barrier(
-        (grad_pieces, grad_w_in, grad_w_out, forward_sum)
-    )
+    grad_pieces, grad_w_in, grad_w_out = lax.optimization_barrier((grad_pieces, grad_w_in, grad_w_out))
     normed_parts, (own_part, other_part, weight_part, gain_one_part) = attend_back(
         places, bias, group_tokens, gain_one, weights, projected, mixed, logs, grad_pieces,
         gain_two_part, router_part, part, z_count,
     )
+    normed_parts, own_part, other_part, forward_sum = lax.optimization_barrier(
+        (normed_parts, own_part, other_part, forward_sum)
+    )
     forward_rows = over_expert(list(forward_sum.reshape(chunks, many * block, width)))
-    normed_parts, own_part, other_part, forward_rows = lax.optimization_barrier(
-        (normed_parts, own_part, other_part, forward_rows)
-    )
     grad_normed = sum_hops(normed_parts)
     output = output_rows(target_col, forward_rows, hidden_one, gate)
     grad_tokens = tokens_back(tokens, grad_normed, gain_one, grad_hidden)

time: 358 us -> 358 us (level)
    unnamed x102 -> x100, local copies, waits for them, and re-layouts: 7.17 us -> 8.21 us
  transfers between devices with their start and end apart: 64 -> 64, of which waited for: 20 -> 21; matrix products, arithmetic and copies ran while one was open for 8% -> 8% of each run, Pallas kernels for 24% -> 24%
where the time goes in v11:
time: 358 us; the launch traced here: 357 us
  waiting for transfers between devices  114 us (32%)
  Pallas kernels  109 us (30%)
  starting transfers between devices  76.9 us (21%)
  local copies, waits for them, and re-layouts  22.5 us (6%)
  other arithmetic  20.2 us (6%)
  between operations  14.8 us (4%)
    ppermute x57, waiting for transfers between devices, swapped(): return lax.ppermute(value, axis, [(s, s ^ bits) for s in range(count)])  114 us
    ppermute x57, starting transfers between devices, swapped(): return lax.ppermute(value, axis, [(s, s ^ bits) for s in range(count)])  76.2 us
    pallas_call x1, Pallas kernels, attend_back(): pl.pallas_call(functools.partial(attend_back_kernel, heads, tensors, part...  24.5 us
    pallas_call x1, Pallas kernels, expert_forward_back(): pl.pallas_call(functools.partial(expert_kernel, chunks, tensors, main, lo...  23.5 us
    pallas_call x1, Pallas kernels, attend(): pl.pallas_call(functools.partial(attend_kernel, heads, tensors, len(owned...  15.4 us
    pallas_call x1, Pallas kernels, expert_weights(): pl.pallas_call(expert_weights_kernel, grid_spec=pltpu.PrefetchScalarGridS...  15.2 us
    pallas_call x1, Pallas kernels, expert_rows(): pl.pallas_call(functools.partial(expert_rows_kernel, chunks, main, locals...  9.61 us
    unnamed x100, local copies, waits for them, and re-layouts  8.21 us
  transfers between devices with their start and end apart: 64, of which 21 were waited for; matrix products, arithmetic and copies ran while one was open for 8% of the time, Pallas kernels for 24%

profile of v11, /device:TPU:0, one launch (start us, length us, event | category | flops | bytes accessed | tf_op | source)
XLA Modules:
  0.0 357.2 jit_solution(5278516587440875484)
XLA Ops:
  10.4 5.1 %collective-permute-start.6 = (bf16[1,112,768]{2,1,0:T(8,128)(2,1)S(1)}, bf16[1,112,768]{2,1,0:T(8,128)(2,1)S(1)}, u32[]{:S(2)}, u32[]{:S(2)}) collective-permute-start(bf16[1,112,768]{2,1,0:T(8,128)(2,1)S(1)} %maximum_bitcast_fusion.refs_0_.refs_5_), channel_id=1, source_target_pairs={{0,12},{4,8},{8,4},{12,0},{1,13},{5,9},{9,5},{13,1},{2,14},{6,10},... | collective-permute-start | bytes 516104 | tf_op jit(solution)/shard_map/ppermute | solution.py:808
  21.3 8.9 %collective-permute-done.5.refs_2_.refs_7_ = bf16[1,112,768]{2,1,0:T(8,128)(2,1)S(1)} collective-permute-done((bf16[1,112,768]{2,1,0:T(8,128)(2,1)S(1)}, bf16[1,112,768]{2,1,0:T(8,128)(2,1)S(1)}, u32[]{:S(2)}, u32[]{:S(2)}) %collective-permute-start.5) | collective-permute-done | bytes 172064 | tf_op jit(solution)/shard_map/ppermute | solution.py:808
  47.3 3.4 collective-permute-done.10
  56.9 15.4 %attend.1 = (bf16[384,768]{1,0:T(8,128)(2,1)}, bf16[384,768]{1,0:T(8,128)(2,1)}, bf16[384,768]{1,0:T(8,128)(2,1)}, bf16[384,768]{1,0:T(8,128)(2,1)}, bf16[1536,7...) custom-call(s32[4]{0:T(128)} %pad_add_fusion.place_ref, ...), custom_call_target="tpu_custom_call" | custom-call | flops 2415919104 | bytes 9437184 | tf_op jit(solution)/shard_map/attend/pallas_call | solution.py:158
  77.2 19.0 %collective-permute-done.14.refs_1_ = bf16[384,768]{1,0:T(8,128)(2,1)S(1)} collective-permute-done((bf16[384,768]{1,0:T(8,128)(2,1)}, bf16[384,768]{1,0:T(8,128)(2,1)S(1)}, u32[]{:S(2)}, u32[]{:S(2)}) %collective-permute-start.14) | collective-permute-done | bytes 589856 | tf_op jit(solution)/shard_map/ppermute | solution.py:808
  108.1 4.9 %route.1 = (f32[384,768]{1,0:T(8,128)}, f32[384,1]{1,0:T(8,128)}, bf16[144,768]{1,0:T(8,128)(2,1)}, bf16[144,768]{1,0:T(8,128)(2,1)}, bf16[144,768]{1,0:T(8,128)(2,1)}, /*index=5*/bf16[144,768]{1,0:T(8,128)(2,1)}) custom-call(bf16[384,768]{1,0:T(8,128)(2,1)} %tok_ref.3, bf16[384,768]{1,0:T(8,128)(2,1)} %get-tuple-element.166.refs_0_, ...), custom_call_target="tpu_custom_call" | custom-call | flops 339738624 | bytes 3538944 | tf_op jit(solution)/shard_map/route/pallas_call | solution.py:442
  118.7 4.6 %collective-permute-done.22 = bf16[144,768]{1,0:T(8,128)(2,1)S(1)} collective-permute-done((bf16[144,768]{1,0:T(8,128)(2,1)}, bf16[144,768]{1,0:T(8,128)(2,1)S(1)}, u32[]{:S(2)}, u32[]{:S(2)}) %collective-permute-start.22) | collective-permute-done | bytes 221216 | tf_op jit(solution)/shard_map/ppermute | solution.py:808
  125.1 8.9 %collective-permute-done.25 = bf16[144,768]{1,0:T(8,128)(2,1)S(1)} collective-permute-done((bf16[144,768]{1,0:T(8,128)(2,1)}, bf16[144,768]{1,0:T(8,128)(2,1)S(1)}, u32[]{:S(2)}, u32[]{:S(2)}) %collective-permute-start.25) | collective-permute-done | bytes 221216 | tf_op jit(solution)/shard_map/ppermute | solution.py:808
  143.6 9.0 %collective-permute-done.29 = bf16[144,768]{1,0:T(8,128)(2,1)S(1)} collective-permute-done((bf16[144,768]{1,0:T(8,128)(2,1)S(1)}, bf16[144,768]{1,0:T(8,128)(2,1)S(1)}, u32[]{:S(2)}, u32[]{:S(2)}) %collective-permute-start.29) | collective-permute-done | bytes 221216 | tf_op jit(solution)/shard_map/ppermute | solution.py:808
  157.4 3.7 %collective-permute-done.30 = bf16[288,768]{1,0:T(8,128)(2,1)S(1)} collective-permute-done((bf16[288,768]{1,0:T(8,128)(2,1)S(1)}, bf16[288,768]{1,0:T(8,128)(2,1)S(1)}, u32[]{:S(2)}, u32[]{:S(2)}) %collective-permute-start.30) | collective-permute-done | bytes 442400 | tf_op jit(solution)/shard_map/ppermute | solution.py:808
  161.8 23.5 %experts.1 = (bf16[2,144,768]{2,1,0:T(8,128)(2,1)}, bf16[2,144,768]{2,1,0:T(8,128)(2,1)}, bf16[2,144,768]{2,1,0:T(8,128)(2,1)}, bf16[2,144,768]{2,1,0:T(8,128)(2...) custom-call(s32[4]{0:T(128)} %pad_add_fusion.place_ref, ...), custom_call_target="tpu_custom_call" | custom-call | flops 8153726976 | bytes 24772608 | tf_op jit(solution)/shard_map/experts/pallas_call | solution.py:614
  189.4 9.6 %expert_rows.1 = bf16[4,4,144,768]{3,2,1,0:T(8,128)(2,1)} custom-call(s32[4]{0:T(128)} %pad_add_fusion.place_ref, bf16[4,576,768]{2,1,0:T(8,128)(2,1)} %get-tuple-element.203.hid_ref, bf16[4,768,384]{2,1,0:T(8,128)(2,1)} %own_out.1, bf16[4,768,384]{2,1,0:T(8,128)(2,1)} %collective-permute-done.19.refs_16_.peer_out), custom_call_target="tpu_custom_call" | custom-call | flops 2717908992 | bytes 10616832 | tf_op jit(solution)/shard_map/expert_rows/pallas_call | solution.py:660
  199.0 5.7 %collective-permute-done.33 = bf16[288,768]{1,0:T(8,128)(2,1)S(1)} collective-permute-done((bf16[288,768]{1,0:T(8,128)(2,1)}, bf16[288,768]{1,0:T(8,128)(2,1)S(1)}, u32[]{:S(2)}, u32[]{:S(2)}) %collective-permute-start.33) | collective-permute-done | bytes 442400 | tf_op jit(solution)/shard_map/ppermute | solution.py:808
  219.4 15.2 %expert_weights.1 = (f32[4,384,768]{2,1,0:T(8,128)}, bf16[4,384,768]{2,1,0:T(8,128)(2,1)}, f32[4,768,384]{2,1,0:T(8,128)}, bf16[4,768,384]{2,1,0:T(8,128)(2,1)}, f32[16,768]{1,0:T(8,128)}) custom-call(s32[4]{0:T(128)} %pad_add_fusion.place_ref, bf16[4,576,768]{2,1,0:T(8,128)(2,1)} %get-tuple-element.201.x_ref, ...), custom_call_target="tpu_custom_call" | custom-call | flops 5435817984 | bytes 24772608 | tf_op jit(solution)/shard_map/expert_weights/pallas_call | solution.py:699
  236.1 4.4 %hidden_back.1 = (f32[384,768]{1,0:T(8,128)}, bf16[384,768]{1,0:T(8,128)(2,1)}, f32[1,768]{1,0:T(1,128)}) custom-call(s32[384,1]{1,0:T(8,128)} %broadcast_in_dim.35.target_ref, bf16[144,768]{1,0:T(8,128)(2,1)} %fusion.11.refs_0_, bf16[144,768]{1,0:T(8,128)(2,1)} %copy-done.24, bf16[144,768]{1,0:T(8,128)(2,1)} %copy-done.25, bf16[144,768]{1,0:T(8,128)(2,1)} %copy-done.26, ...), custom_call_target="tpu_custom_call" | custom-call | flops 339738624 | bytes 4718592 | tf_op jit(solution)/shard_map/hidden_back/pallas_call | solution.py:746
  243.7 6.9 %collective-permute-done.42.refs_1_ = bf16[192,768]{1,0:T(8,128)(2,1)S(1)} collective-permute-done((bf16[192,768]{1,0:T(8,128)(2,1)S(1)}, bf16[192,768]{1,0:T(8,128)(2,1)S(1)}, u32[]{:S(2)}, u32[]{:S(2)}) %collective-permute-start.42) | collective-permute-done | bytes 294944 | tf_op jit(solution)/shard_map/ppermute | solution.py:808
  253.0 4.5 %convert_add_fusion.1 = f32[4,384,768]{2,1,0:T(8,128)} fusion(f32[4,384,768]{2,1,0:T(8,128)S(1)} %copy-done, bf16[4,384,768]{2,1,0:T(8,128)(2,1)} %collective-permute-done.46), kind=kLoop, calls=%fused_computation.2 | loop fusion | flops 2359296 | bytes 11796480 | tf_op jit(solution)/shard_map/add | solution.py:982
  260.2 13.9 %collective-permute-done.43.refs_2_ = bf16[384,768]{1,0:T(8,128)(2,1)S(1)} collective-permute-done((bf16[384,768]{1,0:T(8,128)(2,1)S(1)}, bf16[384,768]{1,0:T(8,128)(2,1)S(1)}, u32[]{:S(2)}, u32[]{:S(2)}) %collective-permute-start.43) | collective-permute-done | bytes 589856 | tf_op jit(solution)/shard_map/ppermute | solution.py:808
  275.2 24.5 %attend_back.1 = (bf16[384,768]{1,0:T(8,128)(2,1)}, bf16[384,768]{1,0:T(8,128)(2,1)}, bf16[384,768]{1,0:T(8,128)(2,1)}, bf16[384,768]{1,0:T(8,128)(2,1)}, bf16[4...) custom-call(s32[4]{0:T(128)} %pad_add_fusion.place_ref, ...), custom_call_target="tpu_custom_call" | custom-call | flops 5586812928 | bytes 14155776 | tf_op jit(solution)/shard_map/attend_back/pallas_call | solution.py:315
  303.8 3.3 collective-permute-start.50
  307.2 7.5 %collective-permute-done.55.refs_1_ = bf16[384,768]{1,0:T(8,128)(2,1)S(1)} collective-permute-done((bf16[384,768]{1,0:T(8,128)(2,1)}, bf16[384,768]{1,0:T(8,128)(2,1)S(1)}, u32[]{:S(2)}, u32[]{:S(2)}) %collective-permute-start.55) | collective-permute-done | bytes 589856 | tf_op jit(solution)/shard_map/ppermute | solution.py:808
  322.6 8.2 %collective-permute-done.49.refs_2_ = bf16[144,768]{1,0:T(8,128)(2,1)} collective-permute-done((bf16[144,768]{1,0:T(8,128)(2,1)S(1)}, bf16[144,768]{1,0:T(8,128)(2,1)}, u32[]{:S(2)}, u32[]{:S(2)}) %collective-permute-start.49) | collective-permute-done | bytes 221216 | tf_op jit(solution)/shard_map/ppermute | solution.py:808
  333.8 3.4 output_rows.1
  337.9 4.0 %tokens_back.1 = f32[384,768]{1,0:T(8,128)} custom-call(bf16[384,768]{1,0:T(8,128)(2,1)} %tok_ref.3, bf16[384,768]{1,0:T(8,128)(2,1)} %get-tuple-element.236.refs_0_, bf16[384,768]{1,0:T(8,128)(2,1)} %copy-done.4, bf16[192,768]{1,0:T(8,128)(2,1)} %copy-done.18, bf16[384,768]{1,0:T(8,128)(2,1)} %get-tuple-element.238.refs_3_, bf16[384,768]{1,0:T(8,128)(2,1)} %copy-done.5, ...), custom_call_target="tpu_custom_call" | custom-call | flops 2949120 | bytes 3538944 | tf_op jit(solution)/shard_map/tokens_back/pallas_call | solution.py:788
  (292 shorter events, 124.9 us)
Async XLA Ops:
  7.2 153.9 %all-gather.3.cloned.1.call-start = ((), (), s32[]{:S(2)}) async-start(), calls=%async_computation.2 | async-start | bytes 4423680 | tf_op jit(solution)/shard_map/all_gather | solution.py:945
  31.3 19.4 %collective-permute-start.1 = (bf16[384,768]{1,0:T(8,128)(2,1)S(1)}, bf16[384,768]{1,0:T(8,128)(2,1)}, u32[]{:S(2)}, u32[]{:S(2)}) collective-permute-start(bf16[384,768]{1,0:T(8,128)(2,1)S(1)} %pad_maximum_fusion.2), channel_id=1, source_target_pairs={{0,2},{1,3},{2,0},{3,1},{4,6},{5,7},{6,4},{7,5},{8,10},{9,11},{10,... | collective-permute-start | bytes 1769480 | tf_op jit(solution)/shard_map/ppermute | solution.py:808
  52.5 19.8 %collective-permute-start.11 = (bf16[144,768]{1,0:T(8,128)(2,1)}, bf16[144,768]{1,0:T(8,128)(2,1)S(1)}, u32[]{:S(2)}, u32[]{:S(2)}) collective-permute-start(bf16[144,768]{1,0:T(8,128)(2,1)} %get-tuple-element.157), channel_id=1, source_target_pairs={{0,4},{4,0},{8,12},{12,8},{1,5},{5,1},{9,13},{13,9},{2,6},{6,2},{1... | collective-permute-start | bytes 663560 | tf_op jit(solution)/shard_map/ppermute | solution.py:808
  52.5 19.8 %collective-permute-start.12 = (bf16[144,768]{1,0:T(8,128)(2,1)}, bf16[144,768]{1,0:T(8,128)(2,1)S(1)}, u32[]{:S(2)}, u32[]{:S(2)}) collective-permute-start(bf16[144,768]{1,0:T(8,128)(2,1)} %get-tuple-element.158), channel_id=1, source_target_pairs={{0,8},{4,12},{8,0},{12,4},{1,9},{5,13},{9,1},{13,5},{2,10},{6,14},... | collective-permute-start | bytes 663560 | tf_op jit(solution)/shard_map/ppermute | solution.py:808
  73.4 226.4 %reduce-scatter.2.cloned.1.call-start = ((), (), s32[]{:S(2)}) async-start(), calls=%async_computation.1 | async-start | bytes 4423680 | tf_op jit(solution)/shard_map/reduce_scatter | solution.py:971
  73.4 33.8 %collective-permute-start.18 = (bf16[4,384,768]{2,1,0:T(8,128)(2,1)}, bf16[4,384,768]{2,1,0:T(8,128)(2,1)S(1)}, u32[]{:S(2)}, u32[]{:S(2)}) collective-permute-start(bf16[4,384,768]{2,1,0:T(8,128)(2,1)} %refs_13_.1), channel_id=1, source_target_pairs={{0,16},{16,0},{1,17},{17,1},{2,18},{18,2},{3,19},{19,3},{4,20},{20... | collective-permute-start | bytes 7077896 | tf_op jit(solution)/shard_map/ppermute | solution.py:798
  74.3 33.0 %collective-permute-start.19 = (bf16[4,768,384]{2,1,0:T(8,128)(2,1)S(1)}, bf16[4,768,384]{2,1,0:T(8,128)(2,1)}, u32[]{:S(2)}, u32[]{:S(2)}) collective-permute-start(bf16[4,768,384]{2,1,0:T(8,128)(2,1)S(1)} %copy-done.1), channel_id=1, source_target_pairs={{0,16},{16,0},{1,17},{17,1},{2,18},{18,2},{3,19},{19,3},{4,20},{20... | collective-permute-start | bytes 7077896 | tf_op jit(solution)/shard_map/ppermute | solution.py:798
  74.3 21.9 %collective-permute-start.14 = (bf16[384,768]{1,0:T(8,128)(2,1)}, bf16[384,768]{1,0:T(8,128)(2,1)S(1)}, u32[]{:S(2)}, u32[]{:S(2)}) collective-permute-start(bf16[384,768]{1,0:T(8,128)(2,1)} %get-tuple-element.161), channel_id=1, source_target_pairs={{0,1},{1,0},{2,3},{3,2},{4,5},{5,4},{6,7},{7,6},{8,9},{9,8},{10,11... | collective-permute-start | bytes 1769480 | tf_op jit(solution)/shard_map/ppermute | solution.py:808
  75.8 22.8 %collective-permute-start.16 = (bf16[384,768]{1,0:T(8,128)(2,1)}, bf16[384,768]{1,0:T(8,128)(2,1)S(1)}, u32[]{:S(2)}, u32[]{:S(2)}) collective-permute-start(bf16[384,768]{1,0:T(8,128)(2,1)} %get-tuple-element.163), channel_id=1, source_target_pairs={{0,2},{1,3},{2,0},{3,1},{4,6},{5,7},{6,4},{7,5},{8,10},{9,11},{10,... | collective-permute-start | bytes 1769480 | tf_op jit(solution)/shard_map/ppermute | solution.py:808
  115.1 19.0 %collective-permute-start.25 = (bf16[144,768]{1,0:T(8,128)(2,1)}, bf16[144,768]{1,0:T(8,128)(2,1)S(1)}, u32[]{:S(2)}, u32[]{:S(2)}) collective-permute-start(bf16[144,768]{1,0:T(8,128)(2,1)} %get-tuple-element.174), channel_id=1, source_target_pairs={{0,8},{4,12},{8,0},{12,4},{1,9},{5,13},{9,1},{13,5},{2,10},{6,14},... | collective-permute-start | bytes 663560 | tf_op jit(solution)/shard_map/ppermute | solution.py:808
  116.2 17.9 %collective-permute-start.20 = (bf16[144,768]{1,0:T(8,128)(2,1)}, bf16[144,768]{1,0:T(8,128)(2,1)S(1)}, u32[]{:S(2)}, u32[]{:S(2)}) collective-permute-start(bf16[144,768]{1,0:T(8,128)(2,1)} %get-tuple-element.172), channel_id=1, source_target_pairs={{0,1},{1,0},{2,3},{3,2},{4,5},{5,4},{6,7},{7,6},{8,9},{9,8},{10,11... | collective-permute-start | bytes 663560 | tf_op jit(solution)/shard_map/ppermute | solution.py:808
  117.0 19.4 %collective-permute-start.28 = (bf16[144,768]{1,0:T(8,128)(2,1)}, bf16[144,768]{1,0:T(8,128)(2,1)S(1)}, u32[]{:S(2)}, u32[]{:S(2)}) collective-permute-start(bf16[144,768]{1,0:T(8,128)(2,1)} %get-tuple-element.175), channel_id=1, source_target_pairs={{0,12},{4,8},{8,4},{12,0},{1,13},{5,9},{9,5},{13,1},{2,14},{6,10},... | collective-permute-start | bytes 663560 | tf_op jit(solution)/shard_map/ppermute | solution.py:808
  135.2 19.0 %collective-permute-start.21 = (bf16[288,768]{1,0:T(8,128)(2,1)S(1)}, bf16[288,768]{1,0:T(8,128)(2,1)S(1)}, u32[]{:S(2)}, u32[]{:S(2)}) collective-permute-start(bf16[288,768]{1,0:T(8,128)(2,1)S(1)} %pad_maximum_fusion.6), channel_id=1, source_target_pairs={{0,2},{1,3},{2,0},{3,1},{4,6},{5,7},{6,4},{7,5},{8,10},{9,11},{10,... | collective-permute-start | bytes 1327112 | tf_op jit(solution)/shard_map/ppermute | solution.py:808
  187.4 17.4 %collective-permute-start.33 = (bf16[288,768]{1,0:T(8,128)(2,1)}, bf16[288,768]{1,0:T(8,128)(2,1)S(1)}, u32[]{:S(2)}, u32[]{:S(2)}) collective-permute-start(bf16[288,768]{1,0:T(8,128)(2,1)} %bitcast.110), channel_id=1, source_target_pairs={{0,1},{1,0},{2,3},{3,2},{4,5},{5,4},{6,7},{7,6},{8,9},{9,8},{10,11... | collective-permute-start | bytes 1327112 | tf_op jit(solution)/shard_map/ppermute | solution.py:808
  214.7 19.9 %collective-permute-start.39 = (bf16[144,768]{1,0:T(8,128)(2,1)S(1)}, bf16[144,768]{1,0:T(8,128)(2,1)S(1)}, u32[]{:S(2)}, u32[]{:S(2)}) collective-permute-start(bf16[144,768]{1,0:T(8,128)(2,1)S(1)} %fusion.8), channel_id=1, source_target_pairs={{0,4},{4,0},{8,12},{12,8},{1,5},{5,1},{9,13},{13,9},{2,6},{6,2},{1... | collective-permute-start | bytes 663560 | tf_op jit(solution)/shard_map/ppermute | solution.py:808
  216.4 18.2 %collective-permute-start.40 = (bf16[144,768]{1,0:T(8,128)(2,1)S(1)}, bf16[144,768]{1,0:T(8,128)(2,1)S(1)}, u32[]{:S(2)}, u32[]{:S(2)}) collective-permute-start(bf16[144,768]{1,0:T(8,128)(2,1)S(1)} %fusion.5), channel_id=1, source_target_pairs={{0,8},{4,12},{8,0},{12,4},{1,9},{5,13},{9,1},{13,5},{2,10},{6,14},... | collective-permute-start | bytes 663560 | tf_op jit(solution)/shard_map/ppermute | solution.py:808
  234.7 18.3 %collective-permute-start.46 = (bf16[4,384,768]{2,1,0:T(8,128)(2,1)}, bf16[4,384,768]{2,1,0:T(8,128)(2,1)}, u32[]{:S(2)}, u32[]{:S(2)}) collective-permute-start(bf16[4,384,768]{2,1,0:T(8,128)(2,1)} %get-tuple-element.215), channel_id=1, source_target_pairs={{0,16},{16,0},{1,17},{17,1},{2,18},{18,2},{3,19},{19,3},{4,20},{20... | collective-permute-start | bytes 7077896 | tf_op jit(solution)/shard_map/ppermute | solution.py:798
  234.8 22.7 %collective-permute-start.47 = (bf16[4,768,384]{2,1,0:T(8,128)(2,1)}, bf16[4,768,384]{2,1,0:T(8,128)(2,1)S(1)}, u32[]{:S(2)}, u32[]{:S(2)}) collective-permute-start(bf16[4,768,384]{2,1,0:T(8,128)(2,1)} %get-tuple-element.217), channel_id=1, source_target_pairs={{0,16},{16,0},{1,17},{17,1},{2,18},{18,2},{3,19},{19,3},{4,20},{20... | collective-permute-start | bytes 7077896 | tf_op jit(solution)/shard_map/ppermute | solution.py:798
  250.7 23.4 %collective-permute-start.43 = (bf16[384,768]{1,0:T(8,128)(2,1)S(1)}, bf16[384,768]{1,0:T(8,128)(2,1)S(1)}, u32[]{:S(2)}, u32[]{:S(2)}) collective-permute-start(bf16[384,768]{1,0:T(8,128)(2,1)S(1)} %pad_maximum_fusion.4), channel_id=1, source_target_pairs={{0,2},{1,3},{2,0},{3,1},{4,6},{5,7},{6,4},{7,5},{8,10},{9,11},{10,... | collective-permute-start | bytes 1769480 | tf_op jit(solution)/shard_map/ppermute | solution.py:808
  252.0 22.1 %collective-permute-start.45 = (bf16[384,768]{1,0:T(8,128)(2,1)S(1)}, bf16[384,768]{1,0:T(8,128)(2,1)S(1)}, u32[]{:S(2)}, u32[]{:S(2)}) collective-permute-start(bf16[384,768]{1,0:T(8,128)(2,1)S(1)} %pad_maximum_fusion.5), channel_id=1, source_target_pairs={{0,1},{1,0},{2,3},{3,2},{4,5},{5,4},{6,7},{7,6},{8,9},{9,8},{10,11... | collective-permute-start | bytes 1769480 | tf_op jit(solution)/shard_map/ppermute | solution.py:808
  307.2 23.6 %collective-permute-start.49 = (bf16[144,768]{1,0:T(8,128)(2,1)S(1)}, bf16[144,768]{1,0:T(8,128)(2,1)}, u32[]{:S(2)}, u32[]{:S(2)}) collective-permute-start(bf16[144,768]{1,0:T(8,128)(2,1)S(1)} %get-tuple-element.255), channel_id=1, source_target_pairs={{0,8},{4,12},{8,0},{12,4},{1,9},{5,13},{9,1},{13,5},{2,10},{6,14},... | collective-permute-start | bytes 663560 | tf_op jit(solution)/shard_map/ppermute | solution.py:808
  317.0 20.2 %collective-permute-start.56 = (bf16[192,768]{1,0:T(8,128)(2,1)S(1)}, bf16[192,768]{1,0:T(8,128)(2,1)S(1)}, u32[]{:S(2)}, u32[]{:S(2)}) collective-permute-start(bf16[192,768]{1,0:T(8,128)(2,1)S(1)} %add_convert_fusion.1), channel_id=1, source_target_pairs={{0,2},{1,3},{2,0},{3,1},{4,6},{5,7},{6,4},{7,5},{8,10},{9,11},{10,... | collective-permute-start | bytes 884744 | tf_op jit(solution)/shard_map/ppermute | solution.py:808
  318.7 18.5 %collective-permute-start.58 = (bf16[192,768]{1,0:T(8,128)(2,1)S(1)}, bf16[192,768]{1,0:T(8,128)(2,1)S(1)}, u32[]{:S(2)}, u32[]{:S(2)}) collective-permute-start(bf16[192,768]{1,0:T(8,128)(2,1)S(1)} %add_convert_fusion), channel_id=1, source_target_pairs={{0,1},{1,0},{2,3},{3,2},{4,5},{5,4},{6,7},{7,6},{8,9},{9,8},{10,11... | collective-permute-start | bytes 884744 | tf_op jit(solution)/shard_map/ppermute | solution.py:808
  320.1 21.9 %collective-permute-start.54 = (bf16[112,768]{1,0:T(8,128)(2,1)}, bf16[112,768]{1,0:T(8,128)(2,1)S(1)}, u32[]{:S(2)}, u32[]{:S(2)}) collective-permute-start(bf16[112,768]{1,0:T(8,128)(2,1)} %get-tuple-element.250), channel_id=1, source_target_pairs={{0,12},{4,8},{8,4},{12,0},{1,13},{5,9},{9,5},{13,1},{2,14},{6,10},... | collective-permute-start | bytes 516104 | tf_op jit(solution)/shard_map/ppermute | solution.py:808
  (88 other events, 1074.9 us)
Sparse Core Ops, SparseCore 0:
  73.5 63.0 all-gather.2
  214.8 56.7 reduce-scatter.1
